TPU v7x, 32 devices: a whole 2x2x4 slice. The times are simulated.
32 devices in a mesh: event: 2 (over x), cuts: 16 (over z, y, core).
Axes of the slice: x: 2, y: 2, z: 4, core: 2. Of those that a mesh axis runs over, the one named last changes fastest.
Arguments:
- forward_displacement: float32 [2, 278784], P('event', 'cuts'), may hold values from -6 to 6
- forward_velocity: float32 [2, 278784], P('event', 'cuts'), may hold values from -6 to 6
- adjoint_displacement: float32 [2, 278784], P('event', 'cuts'), may hold values from -6 to 6
- adjoint_velocity: float32 [2, 278784], P('event', 'cuts'), may hold values from -6 to 6
- inverse_mass: float32 [278784], P('cuts'), may hold values from 0.3 to 3
- shear_modulus: float32 [125, 4096], P(None, 'cuts'), may hold values from 0.5 to 4
- connectivity: int32 [125, 4096], P(None, 'cuts'), may hold values from 0 to 18512, as said below
- face_points: int32 [16, 1152], P('cuts'), may hold values from 0 to 1088, as said below
- element_count: int32 [16], P('cuts'), may hold values from 128 to 256, as said below
Outputs:
- forward_displacement_next: float32 [2, 278784], P('event', 'cuts')
- forward_velocity_next: float32 [2, 278784], P('event', 'cuts')
- adjoint_displacement_next: float32 [2, 278784], P('event', 'cuts')
- adjoint_velocity_next: float32 [2, 278784], P('event', 'cuts')
- shear_kernel: float32 [256, 1089], P('cuts')
Inputs may be any that keep to these rules, and one draw needn't show every extreme that they name: `connectivity`: slot n of slice s is the element (ex, ey, ez) of a structured block of 4 x 8 x 8 elements, in an order drawn per slice; its point (i, j, k) has coordinates x = 4 ex + i, y = 4 ey + j, z = 4 ez + k and index x 1089 + y * 33 + z for x < 16; points with x = 16 lie on the next slice's first plane and have index 17424 + g, where g is their slot in the next slice's face list. `face_points`: row s lists in slots 0 to 1088 each point of slice s with x = 0 once; slots 1089 to 1151 hold 0. `element_count`: some slice has all 256 slots live in every draw.
All inputs are finite; a program needn't handle non-finite values.
Results may differ from a plain program's by a relative error of at most 0.0001.
Values sent between devices are 32-bit elements; how exact they have to be, the bound alone decides.
No kernel may reach another device: no remote copies, remote signals or barrier semaphores. Data moves between devices by JAX's collectives and lax.ppermute only.
A program may use at most 128 MiB of HBM per device.

v0:
```python
import jax
import jax.numpy as jnp
import numpy as np
from jax import lax
from jax.sharding import PartitionSpec as P

NGLL = 5
PXU = 16
PY = 33
PZ = 33
PYZ = 1089
NPTS = 17424
NBUF = 1152


time_step = 0.02
cross_sigma = 1.5
cross_reach = 4


def from_behind(block, axis, distance):
    devices = range(lax.axis_size(axis))
    route = [((i - distance) % len(devices), i) for i in devices]
    return lax.ppermute(block, axis, route)


def with_halo(cells, sides, width):
    for axis, dim in sides:
        count = lax.axis_size(axis)
        head = lax.slice_in_dim(cells, 0, width, axis=dim)
        tail = lax.slice_in_dim(cells, cells.shape[dim] - width, cells.shape[dim], axis=dim)
        cells = jnp.concatenate(
            [
                lax.ppermute(tail, axis, [(i, (i + 1) % count) for i in range(count)]),
                cells,
                lax.ppermute(head, axis, [((i + 1) % count, i) for i in range(count)]),
            ],
            axis=dim,
        )
    return cells


def gll_tables():
    nodes = np.array([-1.0, -np.sqrt(3.0 / 7.0), 0.0, np.sqrt(3.0 / 7.0), 1.0])
    quad_weights = np.array([0.1, 49.0 / 90.0, 32.0 / 45.0, 49.0 / 90.0, 0.1])
    barycentric = np.array(
        [
            1.0
            / np.prod(
                [
                    nodes[node_row] - nodes[node_column]
                    for node_column in range(5)
                    if node_column != node_row
                ]
            )
            for node_row in range(5)
        ]
    )
    derivative = np.zeros((5, 5))
    for node_row in range(5):
        for node_column in range(5):
            if node_column != node_row:
                derivative[node_row, node_column] = (
                    barycentric[node_column]
                    / barycentric[node_row]
                    / (nodes[node_row] - nodes[node_column])
                )
        derivative[node_row, node_row] = -np.sum(derivative[node_row])
    weights_cube = (
        quad_weights[:, None, None] * quad_weights[None, :, None] * quad_weights[None, None, :]
    ).reshape(125)
    return (
        jnp.asarray(derivative, dtype=jnp.float32),
        jnp.asarray(weights_cube, dtype=jnp.float32),
    )


def gradients(cube, derivative):
    grad_x = jnp.einsum("il,ljkn->ijkn", derivative, cube, precision=lax.Precision.HIGHEST)
    grad_y = jnp.einsum("jl,ilkn->ijkn", derivative, cube, precision=lax.Precision.HIGHEST)
    grad_z = jnp.einsum("kl,ijln->ijkn", derivative, cube, precision=lax.Precision.HIGHEST)
    return (grad_x, grad_y, grad_z)


def stiffness(grads, flux_cube, derivative):
    term_x = jnp.einsum(
        "li,ljkn->ijkn", derivative, flux_cube * grads[0], precision=lax.Precision.HIGHEST
    )
    term_y = jnp.einsum(
        "lj,ilkn->ijkn", derivative, flux_cube * grads[1], precision=lax.Precision.HIGHEST
    )
    term_z = jnp.einsum(
        "lk,ijln->ijkn", derivative, flux_cube * grads[2], precision=lax.Precision.HIGHEST
    )
    return -(term_x + term_y + term_z)


def along_weight(offset):
    sigma = PXU / 4.0
    return jnp.exp(-offset * offset / (2.0 * sigma * sigma))


def along_band():
    offsets = jnp.arange(-PXU, PXU + 1, dtype=jnp.int32).astype(jnp.float32)
    norm_total = jnp.sum(along_weight(offsets))
    row_index = jnp.arange(PXU, dtype=jnp.int32)
    rim_index = jnp.arange(3 * PXU, dtype=jnp.int32)
    spread = rim_index[None, :] - PXU - row_index[:, None]
    inside = (jnp.abs(spread) <= PXU).astype(jnp.float32)
    return along_weight(spread.astype(jnp.float32)) * inside / norm_total


def cross_matrix(count):
    point_index = jnp.arange(count, dtype=jnp.int32)
    offset = (point_index[:, None] - point_index[None, :]).astype(jnp.float32)
    kept = jnp.exp(-offset * offset / (2.0 * cross_sigma * cross_sigma)) * (
        jnp.abs(offset) <= cross_reach
    ).astype(jnp.float32)
    return kept / jnp.sum(kept, axis=1, keepdims=True)


def on_device(
    forward_displacement,
    forward_velocity,
    adjoint_displacement,
    adjoint_velocity,
    inverse_mass,
    shear_modulus,
    connectivity,
    face_points,
    element_count,
):
    derivative, weights_cube = gll_tables()
    faces = face_points[0]
    elements = connectivity.shape[1]
    active = (jnp.arange(elements, dtype=jnp.int32) < element_count[0]).astype(jnp.float32)
    flux = weights_cube[:, None] * shear_modulus * active[None, :]
    flux_cube = flux.reshape(NGLL, NGLL, NGLL, elements)
    forward_now = forward_displacement[0]
    adjoint_now = adjoint_displacement[0]
    both_now = jnp.stack([forward_now, adjoint_now])
    both_ghost = from_behind(both_now[:, faces], "cuts", -1)
    both_ext = jnp.concatenate([both_now, both_ghost], axis=1)
    gathered = both_ext[:, connectivity]
    cubes = gathered.transpose(1, 0, 2).reshape(NGLL, NGLL, NGLL, 2 * elements)
    both_grads = gradients(cubes, derivative)
    both_flux = jnp.concatenate([flux_cube, flux_cube], axis=3)
    both_force = stiffness(both_grads, both_flux, derivative)
    forward_term = both_force[..., :elements]
    adjoint_term = both_force[..., elements:]
    product = (
        both_grads[0][..., :elements] * both_grads[0][..., elements:]
        + both_grads[1][..., :elements] * both_grads[1][..., elements:]
        + both_grads[2][..., :elements] * both_grads[2][..., elements:]
    )
    kernel_term = -flux_cube * product
    stacked_terms = jnp.stack(
        [forward_term.reshape(-1), adjoint_term.reshape(-1), kernel_term.reshape(-1)], axis=1
    )
    point_ids = connectivity.reshape(-1)
    total = NPTS + NBUF
    summed_terms = jax.ops.segment_sum(stacked_terms, point_ids, num_segments=total)
    forward_force = summed_terms[:, 0]
    adjoint_force = summed_terms[:, 1]
    kernel_ext = summed_terms[:, 2]
    back_forward, back_adjoint, back_kernel = from_behind(
        (forward_force[NPTS:], adjoint_force[NPTS:], kernel_ext[NPTS:]), "cuts", 1
    )
    forward_force = forward_force[:NPTS].at[faces].add(back_forward)
    adjoint_force = adjoint_force[:NPTS].at[faces].add(back_adjoint)
    kernel_points = kernel_ext[:NPTS].at[faces].add(back_kernel)
    forward_speed_next = forward_velocity[0] - time_step * inverse_mass * forward_force
    forward_now_next = forward_now - time_step * forward_speed_next
    adjoint_speed_next = adjoint_velocity[0] + time_step * inverse_mass * adjoint_force
    adjoint_now_next = adjoint_now + time_step * adjoint_speed_next
    event_kernel = kernel_points.reshape(PXU, PYZ)
    band = along_band()
    cross = jnp.kron(cross_matrix(PY), cross_matrix(PZ))
    summed = lax.psum(event_kernel, "event")
    rimmed = with_halo(summed, (("cuts", 0),), PXU)
    smoothed_along = jnp.dot(band, rimmed, precision=lax.Precision.HIGHEST)
    shear_kernel = jnp.dot(smoothed_along, cross.T, precision=lax.Precision.HIGHEST)
    return (
        forward_now_next[None, :],
        forward_speed_next[None, :],
        adjoint_now_next[None, :],
        adjoint_speed_next[None, :],
        shear_kernel,
    )


def solution(mesh):
    in_specs = (
        P("event", "cuts"),
        P("event", "cuts"),
        P("event", "cuts"),
        P("event", "cuts"),
        P("cuts"),
        P(None, "cuts"),
        P(None, "cuts"),
        P("cuts", None),
        P("cuts"),
    )
    out_specs = (
        P("event", "cuts"),
        P("event", "cuts"),
        P("event", "cuts"),
        P("event", "cuts"),
        P("cuts", None),
    )
    return jax.shard_map(
        on_device, mesh=mesh, in_specs=in_specs, out_specs=out_specs, check_vma=False
    )
```

profile of v0, /device:TPU:0, one launch (start us, length us, event | category | flops | bytes accessed | tf_op | source)
XLA Modules:
  0.0 391.2 jit_solution(7314501262075341366)
XLA Ops:
  7.2 0.7 fusion.35
  8.0 1.1 pad_maximum_fusion.2
  9.1 5.1 %copy.95 = f32[2,17424]{0,1:T(8,128)} copy(f32[2,17424]{1,0:T(2,128)S(1)} %pad_maximum_fusion.2) | data formatting | bytes 278784 | tf_op jit(solution)/shard_map/stack | solution.py:141
  14.1 6.0 %gather_fusion = f32[1152,2]{1,0:T(8,128)S(1)} fusion(f32[2,17424]{0,1:T(8,128)} %copy.95, s32[2048]{0:T(1024)S(1)} %pad_clamp_fusion.1), kind=kCustom, calls=%fused_computation | custom fusion | bytes 23040 | tf_op jit(solution)/shard_map/gather | solution.py:142
  20.3 5.5 %collective-permute-start = (f32[2,1152]{1,0:T(2,128)S(1)}, f32[2,1152]{1,0:T(2,128)S(1)}, u32[]{:S(2)}, u32[]{:S(2)}) collective-permute-start(f32[2,1152]{1,0:T(2,128)S(1)} %copy.96), channel_id=1, source_target_pairs={{1,0},{2,1},{3,2},{4,3},{5,4},{6,5},{7,6},{8,7},{9,8},{10,9},{11,1... | collective-permute-start | bytes 27656 | tf_op jit(solution)/shard_map/ppermute | solution.py:24
  26.9 8.9 %broadcast_multiply_fusion = f32[33,33,33,33]{3,2,1,0:T(8,128)} fusion(f32[33,33]{1,0:T(8,128)S(1)} %fusion.25), kind=kLoop, calls=%fused_computation.6 | loop fusion | flops 1185921 | bytes 4748040 | tf_op jit(solution)/shard_map/jit(kron)/mul | solution.py:178
  36.0 5.3 %copy.97 = f32[2,18576]{0,1:T(8,128)} copy(f32[2,18576]{1,0:T(2,128)S(1)} %pad_maximum_fusion.1) | data formatting | bytes 297216 | tf_op jit(solution)/shard_map/concatenate | solution.py:143
  41.3 63.0 %gather_fusion.1 = f32[32000,2]{1,0:T(8,128)} fusion(f32[2,18576]{0,1:T(8,128)} %copy.97, s32[32768]{0:T(1024)S(1)} %pad_clamp_fusion), kind=kCustom, calls=%fused_computation.1 | custom fusion | bytes 640000 | tf_op jit(solution)/shard_map/gather | solution.py:144
  104.3 9.1 %copy.98 = f32[125,2,256]{2,1,0:T(2,128)S(1)} copy(f32[125,2,256]{1,2,0:T(8,128)} %bitcast.37) | data formatting | bytes 512000 | tf_op jit(solution)/shard_map/transpose | solution.py:145
  117.4 0.8 fusion.3
  119.3 8.5 %copy.114 = f32[32000,3]{1,0:T(8,128)} copy(f32[32000,3]{0,1:T(4,128)S(1)} %pad_maximum_fusion) | data formatting | bytes 768000 | tf_op jit(solution)/shard_map/stack | solution.py:157
  127.8 176.6 %scatter_custom_fusion = f32[18576,3]{1,0:T(8,128)} fusion(s32[32000]{0:T(1024)S(1)} %reshape.155, f32[32000,3]{1,0:T(8,128)} %copy.114, f32[]{:T(128)} %constant.13.clone.1), kind=kCustom, calls=%fused_computation.10 | custom fusion | flops 96000 | bytes 223424 | tf_op jit(solution)/shard_map/scatter-add | solution.py:162
  304.4 2.5 slice_reduce_fusion.3
  306.9 16.4 %slice_reduce_fusion = (f32[17424]{0:T(1024)S(1)}, f32[17424]{0:T(1024)S(1)}, f32[17424]{0:T(1024)S(1)}) fusion(f32[18576,3]{1,0:T(8,128)} %scatter_custom_fusion), kind=kLoop, calls=%fused_computation.7 | loop fusion | bytes 418176 | tf_op jit(solution)/shard_map/slice | solution.py:171
  323.5 8.8 %scatter_fusion.2 = f32[17424]{0:T(1024)S(1)} fusion(f32[17424]{0:T(1024)S(1)} %get-tuple-element.8, s32[1152]{0:T(1024)S(1)} %fusion.35, f32[1152]{0:T(1024)S(1)} %collective-permute-done.3), kind=kCustom, calls=%fused_computation.5 | custom fusion | flops 1152 | bytes 18432 | tf_op jit(solution)/shard_map/scatter-add | solution.py:171
  332.3 0.7 reshape.136
  333.5 15.5 %mul.130 = f32[1089,1089]{1,0:T(8,128)} reshape(f32[33,33,33,33]{3,2,1,0:T(8,128)} %broadcast_multiply_fusion) | data formatting | bytes 9487368 | tf_op jit(solution)/shard_map/jit(kron)/mul | solution.py:178
  349.4 0.7 fusion.43
  350.1 8.8 %scatter_fusion = f32[17424]{0:T(1024)S(1)} fusion(f32[17424]{0:T(1024)S(1)} %get-tuple-element.10, s32[1152]{0:T(1024)S(1)} %fusion.35, f32[1152]{0:T(1024)S(1)} %collective-permute-done.1), kind=kCustom, calls=%fused_computation.3 | custom fusion | flops 1152 | bytes 18432 | tf_op jit(solution)/shard_map/scatter-add | solution.py:169
  358.9 8.8 %scatter_fusion.1 = f32[17424]{0:T(1024)S(1)} fusion(f32[17424]{0:T(1024)S(1)} %get-tuple-element.9, s32[1152]{0:T(1024)S(1)} %fusion.35, f32[1152]{0:T(1024)S(1)} %collective-permute-done.2), kind=kCustom, calls=%fused_computation.4 | custom fusion | flops 1152 | bytes 18432 | tf_op jit(solution)/shard_map/scatter-add | solution.py:170
  367.8 4.7 %collective-permute-start.5 = (f32[16,1089]{1,0:T(8,128)}, f32[16,1089]{1,0:T(8,128)S(1)}, u32[]{:S(2)}, u32[]{:S(2)}) collective-permute-start(f32[16,1089]{1,0:T(8,128)} %all-reduce.2.cloned.1.call-done), channel_id=1, source_target_pairs={{1,0},{2,1},{3,2},{4,3},{5,4},{6,5},{7,6},{8,7},{9,8},{10,9},{11,1... | collective-permute-start | bytes 209096 | tf_op jit(solution)/shard_map/ppermute | solution.py:36
  372.6 0.7 broadcast_in_dim.16
  375.3 1.8 fusion.13
  377.1 7.3 %fusion.52 = f32[16,1089]{1,0:T(8,128)} fusion(f32[16,1089]{1,0:T(8,128)S(1)} %fusion.13, f32[1089,1089]{1,0:T(8,128)} %mul.130), kind=kOutput, calls=%fused_computation.91 | convolution fusion | flops 227696832 | bytes 4883076 | tf_op jit(solution)/shard_map/dot_general | solution.py:182
  (71 shorter events, 8.8 us)
Async XLA Ops:
  7.2 19.4 %copy-start.8 = (f32[125]{0:T(128)S(1)}, f32[125]{0:T(128)}, u32[]{:S(2)}) copy-start(f32[125]{0:T(128)} %constant.35.clone) | copy-start | bytes 1504
  7.2 18.7 %copy-start.2 = (s32[125,256]{1,0:T(8,128)S(1)}, s32[125,256]{1,0:T(8,128)}, u32[]{:S(2)}) copy-start(s32[125,256]{1,0:T(8,128)} %param.17) | copy-start | bytes 384004
  7.2 19.4 %copy-start.4 = (f32[125,256]{1,0:T(8,128)S(1)}, f32[125,256]{1,0:T(8,128)}, u32[]{:S(2)}) copy-start(f32[125,256]{1,0:T(8,128)} %param.16) | copy-start | bytes 384004
  7.2 360.5 %all-reduce.2.cloned.1.call-start = ((), (), s32[]{:S(2)}) async-start(), calls=%async_computation | async-start | bytes 147456 | tf_op jit(solution)/shard_map/psum | solution.py:179
  20.3 15.6 %collective-permute-start = (f32[2,1152]{1,0:T(2,128)S(1)}, f32[2,1152]{1,0:T(2,128)S(1)}, u32[]{:S(2)}, u32[]{:S(2)}) collective-permute-start(f32[2,1152]{1,0:T(2,128)S(1)} %copy.96), channel_id=1, source_target_pairs={{1,0},{2,1},{3,2},{4,3},{5,4},{6,5},{7,6},{8,7},{9,8},{10,9},{11,1... | collective-permute-start | bytes 27656 | tf_op jit(solution)/shard_map/ppermute | solution.py:24
  26.8 9.0 %copy-start = (f32[1,17424]{1,0:T(1,128)S(1)}, f32[1,17424]{1,0:T(1,128)}, u32[]{:S(2)}) copy-start(f32[1,17424]{1,0:T(1,128)} %param.11) | copy-start | bytes 209092
  26.8 9.0 %copy-start.1 = (f32[1,17424]{1,0:T(1,128)S(1)}, f32[1,17424]{1,0:T(1,128)}, u32[]{:S(2)}) copy-start(f32[1,17424]{1,0:T(1,128)} %param.13) | copy-start | bytes 209092
  41.3 72.3 %copy-start.3 = (f32[5,5,1,1]{1,0,3,2:T(8,128)S(1)}, f32[5,5,1,1]{1,0,3,2:T(8,128)}, u32[]{:S(2)}) copy-start(f32[5,5,1,1]{1,0,3,2:T(8,128)} %constant.42) | copy-start | bytes 304
  306.9 16.6 %collective-permute-start.3 = (f32[1152]{0:T(1024)S(1)}, f32[1152]{0:T(1024)S(1)}, u32[]{:S(2)}, u32[]{:S(2)}) collective-permute-start(f32[1152]{0:T(1024)S(1)} %get-tuple-element.5), channel_id=1, source_target_pairs={{15,0},{0,1},{1,2},{2,3},{3,4},{4,5},{5,6},{6,7},{7,8},{8,9},{9,10... | collective-permute-start | bytes 13832 | tf_op jit(solution)/shard_map/ppermute | solution.py:24
  323.3 26.7 %collective-permute-start.1 = (f32[1152]{0:T(1024)S(1)}, f32[1152]{0:T(1024)S(1)}, u32[]{:S(2)}, u32[]{:S(2)}) collective-permute-start(f32[1152]{0:T(1024)S(1)} %get-tuple-element.7), channel_id=1, source_target_pairs={{15,0},{0,1},{1,2},{2,3},{3,4},{4,5},{5,6},{6,7},{7,8},{8,9},{9,10... | collective-permute-start | bytes 13832 | tf_op jit(solution)/shard_map/ppermute | solution.py:24
  323.4 35.5 %collective-permute-start.2 = (f32[1152]{0:T(1024)S(1)}, f32[1152]{0:T(1024)S(1)}, u32[]{:S(2)}, u32[]{:S(2)}) collective-permute-start(f32[1152]{0:T(1024)S(1)} %get-tuple-element.6), channel_id=1, source_target_pairs={{15,0},{0,1},{1,2},{2,3},{3,4},{4,5},{5,6},{6,7},{7,8},{8,9},{9,10... | collective-permute-start | bytes 13832 | tf_op jit(solution)/shard_map/ppermute | solution.py:24
  333.4 15.6 %copy-start.6 = (f32[1,17424]{1,0:T(1,128)S(1)}, f32[1,17424]{1,0:T(1,128)}, u32[]{:S(2)}) copy-start(f32[1,17424]{1,0:T(1,128)} %param.12) | copy-start | bytes 209092
  333.4 15.7 %copy-start.7 = (f32[1,17424]{1,0:T(1,128)S(1)}, f32[1,17424]{1,0:T(1,128)}, u32[]{:S(2)}) copy-start(f32[1,17424]{1,0:T(1,128)} %param.14) | copy-start | bytes 209092
  358.9 13.7 %copy-start.5 = (f32[17424]{0:T(1024)S(1)}, f32[17424]{0:T(1024)}, u32[]{:S(2)}) copy-start(f32[17424]{0:T(1024)} %param.15) | copy-start | bytes 209092
  367.7 7.6 %collective-permute-start.4 = (f32[16,1089]{1,0:T(8,128)}, f32[16,1089]{1,0:T(8,128)S(1)}, u32[]{:S(2)}, u32[]{:S(2)}) collective-permute-start(f32[16,1089]{1,0:T(8,128)} %all-reduce.2.cloned.1.call-done), channel_id=1, source_target_pairs={{0,1},{1,2},{2,3},{3,4},{4,5},{5,6},{6,7},{7,8},{8,9},{9,10},{10,1... | collective-permute-start | bytes 209096 | tf_op jit(solution)/shard_map/ppermute | solution.py:34
  367.8 7.5 %collective-permute-start.5 = (f32[16,1089]{1,0:T(8,128)}, f32[16,1089]{1,0:T(8,128)S(1)}, u32[]{:S(2)}, u32[]{:S(2)}) collective-permute-start(f32[16,1089]{1,0:T(8,128)} %all-reduce.2.cloned.1.call-done), channel_id=1, source_target_pairs={{1,0},{2,1},{3,2},{4,3},{5,4},{6,5},{7,6},{8,7},{9,8},{10,9},{11,1... | collective-permute-start | bytes 209096 | tf_op jit(solution)/shard_map/ppermute | solution.py:36
Sparse Core Ops, SparseCore 0:
  333.2 22.4 all-reduce.1
where the time goes:
time: 392 us; the launch traced here: 391 us
  other arithmetic  217 us (55%)
  local copies, waits for them, and re-layouts  136 us (35%)
  between operations  15.2 us (4%)
  matrix products  12.8 us (3%)
  starting transfers between devices  10.5 us (3%)
    scatter-add x1, other arithmetic, on_device(): jax.ops.segment_sum(stacked_terms, point_ids, num_segments=total)  177 us
    gather x1, local copies, waits for them, and re-layouts, on_device(): gathered = both_ext[:, connectivity]  63 us
    slice x1, local copies, waits for them, and re-layouts, on_device(): kernel_points = kernel_ext[:NPTS].at[faces].add(back_kernel)  16.4 us
    mul x1, local copies, waits for them, and re-layouts, on_device(): cross = jnp.kron(cross_matrix(PY), cross_matrix(PZ))  15.5 us
    transpose x1, local copies, waits for them, and re-layouts, on_device(): cubes = gathered.transpose(1, 0, 2).reshape(NGLL, NGLL, NGLL, 2 * elements)  9.08 us
    mul x1, other arithmetic, on_device(): cross = jnp.kron(cross_matrix(PY), cross_matrix(PZ))  8.92 us
    another operation x4, local copies, waits for them, and re-layouts, on_device(): jnp.stack([forward_term.reshape(-1), adjoint_term.reshape(-1), kernel_ter...  8.92 us
    scatter-add x1, other arithmetic, on_device(): kernel_points = kernel_ext[:NPTS].at[faces].add(back_kernel)  8.81 us
  transfers between devices with their start and end apart: 7, of which 0 were waited for; matrix products, arithmetic and copies ran while one was open for 19% of the time, Pallas kernels for 0%

commit v1 on v0

v1 whole, which is shorter than its diff:
```python
import numpy as np
import jax
import jax.numpy as jnp
import ml_dtypes
from jax import lax
from jax.experimental import pallas as pl
from jax.experimental.pallas import tpu as pltpu
from jax.sharding import PartitionSpec as P

NGLL = 5
EX, EY, EZ = 4, 8, 8
PXU = 16
PY = 33
PZ = 33
PYZ = 1089
NPTS = 17424
LANES = 128
ROWS = 144
TIME_STEP = 0.02
F32 = jnp.float32
BF16 = jnp.bfloat16


def gll():
    nodes = np.array([-1.0, -np.sqrt(3.0 / 7.0), 0.0, np.sqrt(3.0 / 7.0), 1.0])
    bary = np.array([1.0 / np.prod([nodes[r] - nodes[c] for c in range(5) if c != r]) for r in range(5)])
    d = np.zeros((5, 5))
    for r in range(5):
        for c in range(5):
            if c != r:
                d[r, c] = bary[c] / bary[r] / (nodes[r] - nodes[c])
        d[r, r] = -np.sum(d[r])
    return d


DERIV = gll()


def split_np(x):
    x = np.asarray(x, np.float32)
    parts = []
    for _ in range(3):
        p = x.astype(ml_dtypes.bfloat16)
        parts.append(p)
        x = x - p.astype(np.float32)
    return parts


def band_table():
    offsets = np.arange(-PXU, PXU + 1)
    w = lambda d: np.exp(-d * d / (2.0 * (PXU / 4.0) ** 2))
    total = w(offsets.astype(np.float64)).sum()
    target = np.arange(-PXU, 2 * PXU + 1)
    source = np.zeros(24, np.int64)
    for r, i in ((0, 1), (4, 0), (8, 3), (12, 2), (20, 4)):
        source[r : r + 4] = 4 * np.arange(4) + i
    spread = target[:, None] - source[None, :]
    band = np.zeros((64, 24))
    band[:49] = w(spread.astype(np.float64)) * (np.abs(spread) <= PXU) / total
    band[:, 16:20] = 0.0
    b1, b2, b3 = split_np(band)
    return np.concatenate([b1, b1, b1, b2, b2, b3], axis=1)


def cross_table():
    off = np.arange(-4, 5)
    k = np.exp(-off * off / (2.0 * 1.5 * 1.5))
    point = np.arange(33)
    inside = ((point[None, :] + off[:, None]) >= 0) & ((point[None, :] + off[:, None]) < 33)
    taps = k[:, None] * inside
    taps = taps / taps.sum(axis=0, keepdims=True)
    out = np.zeros((24, 1152), np.float32)
    out[0:9, :PYZ] = np.tile(taps, (1, PY))
    out[9:18, :PYZ] = np.repeat(taps, PZ, axis=1)
    return out


def split3(x):
    hi = x.astype(BF16)
    rest = x - hi.astype(F32)
    mid = rest.astype(BF16)
    low = (rest - mid.astype(F32)).astype(BF16)
    return hi, mid, low


def dot_nt(a, b):
    return lax.dot_general(a, b, (((1,), (1,)), ((), ())), preferred_element_type=F32)


def dot_tn(a, b):
    return lax.dot_general(a, b, (((0,), (0,)), ((), ())), preferred_element_type=F32)


def selector():
    column = lax.broadcasted_iota(jnp.int32, (8, 256), 1)
    row = lax.broadcasted_iota(jnp.int32, (8, 256), 0)
    base = column - 4 * row
    blocks = [jnp.where(base == j * PZ + k, 1.0, 0.0) for j in range(5) for k in range(5)]
    return jnp.concatenate(blocks, axis=0).astype(BF16)


def flux_kernel(count_ref, conn_ref, shear_ref, flux_ref):
    point = conn_ref[0:1, :].astype(F32)
    x = jnp.floor((point + 0.5) * (1.0 / PYZ))
    rest = point - x * PYZ
    y = jnp.floor((rest + 0.5) * (1.0 / PZ))
    z = rest - y * PZ
    code = (8.0 * z + y + 0.25 * x).astype(jnp.int32)
    slot = lax.broadcasted_iota(jnp.int32, (1, 256), 1)
    code = jnp.where(slot < count_ref[0], code, -1)
    row = lax.broadcasted_iota(jnp.int32, (LANES, 256), 0)
    member = ((row >> 3) & 7) * 4 + (row & 3)
    picks = [jnp.where(code - member == ez * 32, 1.0, 0.0).astype(BF16) for ez in range(EZ)]
    pick = jnp.concatenate(picks, axis=0)
    q = lax.broadcasted_iota(jnp.int32, (125, 256), 0)
    weight = None
    for digit in (q // 25, (q // 5) % 5, q % 5):
        w = jnp.where(digit == 2, 32.0 / 45.0, jnp.where((digit == 0) | (digit == 4), 0.1, 49.0 / 90.0))
        weight = w if weight is None else weight * w
    hi, mid, low = split3(shear_ref[...] * weight)
    moved = dot_nt(hi, pick) + (dot_nt(mid, pick) + dot_nt(low, pick))
    for ez in range(EZ):
        flux_ref[pl.ds(ez, 125, stride=8), :] = moved[:, ez * LANES : (ez + 1) * LANES]


def derive(e):
    d = DERIV
    s0, s1 = e[0] + e[4], e[1] + e[3]
    d0, d1 = e[0] - e[4], e[1] - e[3]
    out = [None] * 5
    for i in (0, 1):
        even = float((d[i, 0] - d[i, 4]) / 2) * d0 + float((d[i, 1] - d[i, 3]) / 2) * d1
        odd = float((d[i, 0] + d[i, 4]) / 2) * s0 + float((d[i, 1] + d[i, 3]) / 2) * s1 + float(d[i, 2]) * e[2]
        out[i] = odd + even
        out[4 - i] = even - odd
    out[2] = float(d[2, 0]) * d0 + float(d[2, 1]) * d1
    return out


def derive_back(t):
    d = DERIV
    s0, s1 = t[0] + t[4], t[1] + t[3]
    d0, d1 = t[0] - t[4], t[1] - t[3]
    out = [None] * 5
    for i in (0, 1):
        even = float((d[0, i] - d[4, i]) / 2) * d0 + float((d[1, i] - d[3, i]) / 2) * d1
        odd = float((d[0, i] + d[4, i]) / 2) * s0 + float((d[1, i] + d[3, i]) / 2) * s1 + float(d[2, i]) * t[2]
        out[i] = odd + even
        out[4 - i] = even - odd
    out[2] = float(d[0, 2]) * d0 + float(d[1, 2]) * d1
    return out


def shifted(tiles, distance, lane):
    skip, part = divmod(distance, LANES)
    if part == 0:
        moved = tiles
        pick = None
    else:
        moved = [pltpu.roll(t, LANES - part, 1) for t in tiles]
        pick = lane < LANES - part
    n = len(tiles)
    out = []
    for i in range(n):
        a = moved[(i + skip) % n]
        b = moved[(i + skip + 1) % n]
        out.append(a if pick is None else jnp.where(pick, a, b))
    return out


def main_kernel(
    own_ref, ghost_ref, flux_ref, band_ref, cross_ref,
    force_ref, face_ref, before_ref, here_ref, after_ref, far_ref,
    plane_ref, win_ref, elem_ref, term_ref, kern_ref,
):
    lane = lax.broadcasted_iota(jnp.int32, (8, LANES), 1)
    lane9 = lax.broadcasted_iota(jnp.int32, (9, LANES), 1)
    for x in range(PXU + 1):
        for f in range(2):
            if x < PXU:
                r0, off = divmod(PYZ * x, LANES)
                flat = own_ref[f, r0 : r0 + 9, :]
                if off:
                    flat = jnp.where(
                        lane9 < LANES - off,
                        pltpu.roll(flat, LANES - off, 1),
                        pltpu.roll(own_ref[f, r0 + 1 : r0 + 10, :], LANES - off, 1),
                    )
            else:
                flat = ghost_ref[f, 0:9, :]
            if x < PXU:
                plane_ref[pl.ds((x % 4) * 72 + f * 4 + x // 4, 9, stride=8), :] = flat
            if x % 4 == 0 and x > 0:
                plane_ref[pl.ds(4 * 72 + f * 4 + x // 4 - 1, 9, stride=8), :] = flat
    for i in range(NGLL):
        tiles = [plane_ref[i * 72 + t * 8 : i * 72 + t * 8 + 8, :] for t in range(9)]
        for ey in range(EY):
            near = [tiles[ey], tiles[ey + 1], tiles[min(ey + 2, 8)]]
            if ey:
                near = [pltpu.roll(t, LANES - 4 * ey, 1) for t in near]
                keep = lane < LANES - 4 * ey
                near = [jnp.where(keep, near[0], near[1]), jnp.where(keep, near[1], near[2])]
            for copy in range(2):
                r = i * LANES + copy * 64 + ey * 8
                win_ref[r : r + 8, 0:LANES] = near[0]
                win_ref[r : r + 8, LANES:] = near[1]
    select = selector()
    hi, mid, low = split3(win_ref[...])
    elem_ref[...] = dot_nt(select, hi) + (dot_nt(select, mid) + dot_nt(select, low))

    def at(ref, i, j, k):
        r = (j * 5 + k) * 8
        return ref[r : r + 8, i * LANES : (i + 1) * LANES]

    def put(ref, i, j, k, value):
        r = (j * 5 + k) * 8
        ref[r : r + 8, i * LANES : (i + 1) * LANES] = value

    def flux_at(i, j, k):
        r = ((i * 5 + j) * 5 + k) * 8
        return flux_ref[r : r + 8, :]

    upper = lane >= 64
    for axis in range(3):
        for p in range(5):
            for q in range(5):
                line = [((l, p, q), (p, l, q), (p, q, l))[axis] for l in range(5)]
                grads = derive([at(elem_ref, *c) for c in line])
                flux = [flux_at(*c) for c in line]
                back = derive_back([g * m for g, m in zip(grads, flux)])
                for n, c in enumerate(line):
                    prod = grads[n] * pltpu.roll(grads[n], 4, 1)
                    if axis == 0:
                        put(term_ref, *c, back[n])
                        put(kern_ref, *c, prod)
                    elif axis == 1:
                        put(term_ref, *c, at(term_ref, *c) + back[n])
                        put(kern_ref, *c, at(kern_ref, *c) + prod)
                    else:
                        total = at(term_ref, *c) + back[n]
                        kern = flux[n] * (at(kern_ref, *c) + prod)
                        put(term_ref, *c, -jnp.where(upper, kern, total))
    hi, mid, low = split3(term_ref[...])
    win_ref[...] = dot_tn(hi, select) + (dot_tn(mid, select) + dot_tn(low, select))

    def gathered(i, copy):
        tiles = [None] * 9
        for ey in range(EY):
            r = i * LANES + copy * 64 + ey * 8
            a, b = win_ref[r : r + 8, 0:LANES], win_ref[r : r + 8, LANES:]
            if ey:
                a, b = pltpu.roll(a, 4 * ey, 1), pltpu.roll(b, 4 * ey, 1)
                keep = lane >= 4 * ey
                a, b = jnp.where(keep, a, 0.0), jnp.where(keep, b, a)
            tiles[ey] = a if ey == 0 else tiles[ey] + a
            tiles[ey + 1] = b
        return tiles

    row = lax.broadcasted_iota(jnp.int32, (8, LANES), 0)
    force = [gathered(i, 0) for i in range(NGLL)]
    inner = (row != 0) & (row != 4)
    for t in range(9):
        force[0][t] = force[0][t] + jnp.where(inner, pltpu.roll(force[4][t], 1, 0), 0.0)
    for i in range(NGLL):
        for t in range(9):
            plane_ref[i * 72 + t * 8 : i * 72 + t * 8 + 8, :] = force[i][t]
    force_ref[...] = jnp.zeros(force_ref.shape, F32)
    for f in range(2):
        for x in range(PXU):
            r0, off = divmod(PYZ * x, LANES)
            flat = plane_ref[pl.ds((x % 4) * 72 + f * 4 + x // 4, 9, stride=8), :]
            if off:
                flat = pltpu.roll(flat, off, 1)
                spill = jnp.where(lane9 < off, flat, 0.0)
                flat = jnp.where(lane9 < off, 0.0, flat)
            force_ref[f, r0 : r0 + 9, :] = force_ref[f, r0 : r0 + 9, :] + flat
            if off:
                force_ref[f, r0 + 1 : r0 + 10, :] = force_ref[f, r0 + 1 : r0 + 10, :] + spill
        face_ref[f] = jnp.zeros((16, LANES), F32)
        face_ref[f, 0:9, :] = plane_ref[pl.ds(4 * 72 + f * 4 + 3, 9, stride=8), :]
    kern = [gathered(i, 1) for i in range(NGLL)]
    lower = row < 4
    rows = []
    for t in range(9):
        part = [jnp.where(lower, pltpu.roll(kern[i + 1][t], 4, 0), kern[i][t]) for i in (0, 2)]
        rows.append(jnp.concatenate(part + [jnp.where(lower, 0.0, kern[4][t])], axis=0))
    tiles = rows
    lane24 = lax.broadcasted_iota(jnp.int32, (24, LANES), 1)
    for base, step in ((0, 1), (9, PZ)):
        total = None
        for tap in range(9):
            moved = shifted(tiles, step * (tap - 4), lane24) if tap != 4 else tiles
            scaled = [m * cross_ref[base + tap : base + tap + 1, t * LANES : (t + 1) * LANES] for t, m in enumerate(moved)]
            total = scaled if total is None else [a + b for a, b in zip(total, scaled)]
        tiles = total
    flat = jnp.concatenate(tiles, axis=1)
    k1 = flat.astype(BF16).astype(F32)
    k2 = (flat - k1).astype(BF16).astype(F32)
    k3 = flat - k1 - k2
    stacked = jnp.concatenate([k1, k2, k3, k1, k2, k1], axis=0).astype(BF16)
    shares = jnp.dot(band_ref[...], stacked, preferred_element_type=F32)[:, :PYZ]
    before_ref[...] = shares[0:16]
    here_ref[...] = shares[16:32]
    after_ref[...] = shares[32:48]
    far_ref[...] = shares[48:56]


def on_device(
    forward_displacement,
    forward_velocity,
    adjoint_displacement,
    adjoint_velocity,
    inverse_mass,
    shear_modulus,
    connectivity,
    face_points,
    element_count,
):
    events = lax.axis_size("event")
    cuts = lax.axis_size("cuts")

    def from_cut(block, distance):
        return lax.ppermute(block, "cuts", [(i, (i + distance) % cuts) for i in range(cuts)])

    def from_both(block, turn, distance):
        pairs = [
            (e * cuts + i, ((e + turn) % events) * cuts + (i + distance) % cuts)
            for e in range(events)
            for i in range(cuts)
        ]
        return lax.ppermute(block, ("event", "cuts"), pairs)

    both = jnp.concatenate([forward_displacement, adjoint_displacement], axis=0)
    face = jnp.pad(both[:, :PYZ], ((0, 0), (0, 16 * LANES - PYZ))).reshape(2, 16, LANES)
    ghost = from_cut(face, -1)
    own = jnp.pad(both, ((0, 0), (0, ROWS * LANES - NPTS))).reshape(2, ROWS, LANES)

    flux = pl.pallas_call(
        flux_kernel,
        out_shape=jax.ShapeDtypeStruct((1000, LANES), F32),
        grid=(1,),
        in_specs=[
            pl.BlockSpec(memory_space=pltpu.SMEM),
            pl.BlockSpec((8, 256), lambda g: (0, 0)),
            pl.BlockSpec((125, 256), lambda g: (0, 0)),
        ],
        out_specs=pl.BlockSpec((1000, LANES), lambda g: (0, 0)),
        cost_estimate=pl.CostEstimate(flops=200000000, bytes_accessed=2000000, transcendentals=0),
        name="flux",
    )(element_count, connectivity, shear_modulus)

    share = jax.ShapeDtypeStruct((PXU, PYZ), F32)
    force, face_force, before, here, after, far = pl.pallas_call(
        main_kernel,
        out_shape=[
            jax.ShapeDtypeStruct((2, ROWS, LANES), F32),
            jax.ShapeDtypeStruct((2, 16, LANES), F32),
            share,
            share,
            share,
            jax.ShapeDtypeStruct((8, PYZ), F32),
        ],
        scratch_shapes=[
            pltpu.VMEM((5 * 72, LANES), F32),
            pltpu.VMEM((5 * LANES, 256), F32),
            pltpu.VMEM((200, 5 * LANES), F32),
            pltpu.VMEM((200, 5 * LANES), F32),
            pltpu.VMEM((200, 5 * LANES), F32),
        ],
        cost_estimate=pl.CostEstimate(flops=400000000, bytes_accessed=4000000, transcendentals=0),
        name="elements",
    )(own, ghost, flux, jnp.asarray(band_table()), jnp.asarray(cross_table()))

    face_back = from_cut(face_force, 1)
    far = far[0:1]
    if events <= 2:
        turns = range(events)
    else:
        before, here, after, far = lax.psum((before, here, after, far), "event")
        turns = range(1)
    total = None
    first = None
    for turn in turns:
        mine = here if turn == 0 else from_both(here, turn, 0)
        block = mine + from_both(before, turn, -1) + from_both(after, turn, 1)
        edge = from_both(far, turn, 2)
        total = block if total is None else total + block
        first = edge if first is None else first + edge
    shear_kernel = total + jnp.pad(first, ((0, PXU - 1), (0, 0)))

    back = jnp.pad(face_back.reshape(2, 16 * LANES)[:, :PYZ], ((0, 0), (0, NPTS - PYZ)))
    force = force.reshape(2, ROWS * LANES)[:, :NPTS] + back
    mass = inverse_mass[None, :]
    forward_velocity_next = forward_velocity - TIME_STEP * mass * force[0:1]
    forward_next = forward_displacement - TIME_STEP * forward_velocity_next
    adjoint_velocity_next = adjoint_velocity + TIME_STEP * mass * force[1:2]
    adjoint_next = adjoint_displacement + TIME_STEP * adjoint_velocity_next
    return (forward_next, forward_velocity_next, adjoint_next, adjoint_velocity_next, shear_kernel)


def solution(mesh):
    in_specs = (
        P("event", "cuts"),
        P("event", "cuts"),
        P("event", "cuts"),
        P("event", "cuts"),
        P("cuts"),
        P(None, "cuts"),
        P(None, "cuts"),
        P("cuts", None),
        P("cuts"),
    )
    out_specs = (
        P("event", "cuts"),
        P("event", "cuts"),
        P("event", "cuts"),
        P("event", "cuts"),
        P("cuts", None),
    )
    return jax.shard_map(on_device, mesh=mesh, in_specs=in_specs, out_specs=out_specs, check_vma=False)
```

time: 392 us -> 33.6 us (0.09)
  other arithmetic: 217 us -> 2.63 us
  local copies, waits for them, and re-layouts: 136 us -> 4.15 us
  between operations: 15.2 us -> 1.4 us
  matrix products: 12.8 us -> 0 us
  Pallas kernels: 0 us -> 7.27 us
  waiting for transfers between devices: 0.05 us -> 4.8 us
    scatter-add x4 -> x0, other arithmetic: 203 us -> none  [the longest x1 177 us: on_device(): jax.ops.segment_sum(stacked_terms, point_ids, num_segments=total)]
    gather x3 -> x0, local copies, waits for them, and re-layouts: 69.1 us -> none  [the longest x1 63 us: on_device(): gathered = both_ext[:, connectivity]]
    slice x5 -> x2, local copies, waits for them, and re-layouts: 19 us -> 0.81 us  [the longest x1 0.81 us: on_device(): far = far[0:1]]
    mul x2 -> x0, local copies, waits for them, and re-layouts: 15.6 us -> none  [the longest x1 15.5 us: on_device(): cross = jnp.kron(cross_matrix(PY), cross_matrix(PZ))]
    another operation x6 -> x0, local copies, waits for them, and re-layouts: 14 us -> none  [the longest x4 8.92 us: on_device(): jnp.stack([forward_term.reshape(-1), adjoint_term.reshape(-1), kernel_ter...]
    dot_general x8 -> x0, matrix products: 12.8 us -> none  [the longest x1 7.26 us: on_device(): jnp.dot(smoothed_along, cross.T, precision=lax.Precision.HIGHEST)]
    mul x3 -> x1, other arithmetic: 9.36 us -> 0.01 us  [on_device(): forward_velocity_next = forward_velocity - TIME_STEP * mass * force[0:1]]
    transpose x1 -> x0, local copies, waits for them, and re-layouts: 9.08 us -> none  [on_device(): cubes = gathered.transpose(1, 0, 2).reshape(NGLL, NGLL, NGLL, 2 * elements)]
  transfers between devices with their start and end apart: 7 -> 9, of which waited for: 0 -> 4; matrix products, arithmetic and copies ran while one was open for 19% -> 6% of each run, Pallas kernels for 0% -> 7%
where the time goes in v1:
time: 33.6 us; the launch traced here: 33.3 us
  starting transfers between devices  13 us (39%)
  Pallas kernels  7.27 us (22%)
  waiting for transfers between devices  4.8 us (14%)
  local copies, waits for them, and re-layouts  4.15 us (12%)
  other arithmetic  2.63 us (8%)
  between operations  1.4 us (4%)
    ppermute x7, starting transfers between devices, from_both(): return lax.ppermute(block, ('event', 'cuts'), pairs)  7.55 us
    ppermute x2, starting transfers between devices, from_cut(): lax.ppermute(block, 'cuts', [(i, (i + distance) % cuts) for i in range(cu...  5.5 us
    pallas_call x1, Pallas kernels, on_device(): pl.pallas_call(main_kernel, out_shape=[jax.ShapeDtypeStruct((2, ROWS, LAN...  4.83 us
    ppermute x7, waiting for transfers between devices, from_both(): return lax.ppermute(block, ('event', 'cuts'), pairs)  4.79 us
    unnamed x25, local copies, waits for them, and re-layouts  3.33 us
    pallas_call x1, Pallas kernels, on_device(): pl.pallas_call(flux_kernel, out_shape=jax.ShapeDtypeStruct((1000, LANES),...  2.44 us
    add x1, other arithmetic, on_device(): adjoint_next = adjoint_displacement + TIME_STEP * adjoint_velocity_next  1.07 us
    slice x1, local copies, waits for them, and re-layouts, on_device(): far = far[0:1]  0.81 us
  transfers between devices with their start and end apart: 9, of which 4 were waited for; matrix products, arithmetic and copies ran while one was open for 6% of the time, Pallas kernels for 7%

profile of v1, /device:TPU:0, one launch (start us, length us, event | category | flops | bytes accessed | tf_op | source)
XLA Modules:
  0.0 33.3 jit_solution(16167044952624618811)
XLA Ops:
  0.7 0.7 %copy-done.7 = pred[2048]{0:T(1024)(128)(4,1)S(1)} copy-done((pred[2048]{0:T(1024)(128)(4,1)S(1)}, pred[2048]{0:T(1024)(128)(4,1)}, u32[]{:S(2)}) %copy-start.7) | copy-done | bytes 2072
  1.3 0.7 %select_bitcast_fusion = f32[1,2,16,128]{3,1,2,0:T(2,128)S(1)} fusion(f32[1,17424]{1,0:T(1,128)} %param.13, f32[1,17424]{1,0:T(1,128)} %param.11, pred[2048]{0:T(1024)(128)(4,1)S(1)} %copy-done.7), kind=kLoop, calls=%fused_computation.18 | loop fusion | flops 8192 | bytes 157824
  2.1 5.5 %collective-permute-start = (f32[2,16,128]{2,1,0:T(8,128)S(1)}, f32[2,16,128]{2,1,0:T(8,128)S(1)}, u32[]{:S(2)}, u32[]{:S(2)}) collective-permute-start(f32[2,16,128]{2,1,0:T(8,128)S(1)} %bitcast.23), channel_id=1, source_target_pairs={{0,15},{1,0},{2,1},{3,2},{4,3},{5,4},{6,5},{7,6},{8,7},{9,8},{10,9... | collective-permute-start | bytes 49160 | tf_op jit(solution)/shard_map/ppermute | solution.py:323
  7.6 0.1 pad_maximum_fusion
  8.4 0.7 %copy.24 = f32[1,2,144,128]{3,2,1,0:T(8,128)} copy(f32[1,2,144,128]{3,1,2,0:T(2,128)S(1)} %pad_bitcast_fusion) | data formatting | bytes 294912
  9.0 2.4 %flux.1.flux_ref = f32[1000,128]{1,0:T(8,128)} custom-call(s32[1]{0:T(128)S(6)} %copy.27.count_ref, s32[125,256]{1,0:T(8,128)} %conn_ref.1, f32[125,256]{1,0:T(8,128)} %shear_ref.1), custom_call_target="tpu_custom_call" | custom-call | flops 200000000 | bytes 2000000 | tf_op jit(solution)/shard_map/flux/pallas_call | solution.py:338
  11.5 0.6 %copy-done.9 = f32[2,16,128]{2,1,0:T(8,128)} copy-done((f32[2,16,128]{2,1,0:T(8,128)}, f32[2,16,128]{2,1,0:T(8,128)S(1)}, u32[]{:S(2)}) %copy-start.9) | copy-done | bytes 16408
  12.1 4.8 %elements.1 = (f32[2,144,128]{2,1,0:T(8,128)}, f32[2,16,128]{2,1,0:T(8,128)}, f32[16,1089]{1,0:T(8,128)}, f32[16,1089]{1,0:T(8,128)}, f32[16,1089]{1,0:T(8,128)}, /*index=5*/f32[8,1089]{1,0:T(8,128)}) custom-call(f32[2,144,128]{2,1,0:T(8,128)} %bitcast.20, f32[2,16,128]{2,1,0:T(8,128)} %copy-done.9, f32[1000,128]{1,0:T(8,128)} %flux.1.flux_ref, ...), custom_call_target="tpu_custom_call" | custom-call | flops 400000000 | bytes 4000000 | tf_op jit(solution)/shard_map/elements/pallas_call | solution.py:353
  16.9 0.8 %slice.24 = f32[1,1089]{1,0:T(1,128)S(1)} slice(f32[8,1089]{1,0:T(8,128)} %get-tuple-element.16), slice={[0:1], [0:1089]} | slice | bytes 8712 | tf_op jit(solution)/shard_map/slice | solution.py:375
  17.7 0.8 %collective-permute-start.8 = (f32[1,1089]{1,0:T(1,128)S(1)}, f32[1,1089]{1,0:T(1,128)S(1)}, u32[]{:S(2)}, u32[]{:S(2)}) collective-permute-start(f32[1,1089]{1,0:T(1,128)S(1)} %slice.24), channel_id=1, source_target_pairs={{0,18},{1,19},{2,20},{3,21},{4,22},{5,23},{6,24},{7,25},{8,26},{9,... | collective-permute-start | bytes 13076 | tf_op jit(solution)/shard_map/ppermute | solution.py:331
  18.6 4.5 %collective-permute-start.2 = (f32[16,1089]{1,0:T(8,128)}, f32[16,1089]{1,0:T(8,128)S(1)}, u32[]{:S(2)}, u32[]{:S(2)}) collective-permute-start(f32[16,1089]{1,0:T(8,128)} %get-tuple-element.14), channel_id=1, source_target_pairs={{0,15},{1,0},{2,1},{3,2},{4,3},{5,4},{6,5},{7,6},{8,7},{9,8},{10,9... | collective-permute-start | bytes 209096 | tf_op jit(solution)/shard_map/ppermute | solution.py:331
  23.1 0.5 %collective-permute-start.5 = (f32[16,1089]{1,0:T(8,128)}, f32[16,1089]{1,0:T(8,128)S(1)}, u32[]{:S(2)}, u32[]{:S(2)}) collective-permute-start(f32[16,1089]{1,0:T(8,128)} %get-tuple-element.14), channel_id=1, source_target_pairs={{0,31},{1,16},{2,17},{3,18},{4,19},{5,20},{6,21},{7,22},{8,23},{9,... | collective-permute-start | bytes 209096 | tf_op jit(solution)/shard_map/ppermute | solution.py:331
  23.6 0.1 copy.23
  23.7 0.4 %collective-permute-done.7 = f32[1,1089]{1,0:T(1,128)S(1)} collective-permute-done((f32[1,1089]{1,0:T(1,128)S(1)}, f32[1,1089]{1,0:T(1,128)S(1)}, u32[]{:S(2)}, u32[]{:S(2)}) %collective-permute-start.7) | collective-permute-done | bytes 4388 | tf_op jit(solution)/shard_map/ppermute | solution.py:331
  24.1 0.4 %copy-done.8 = f32[16,1089]{1,0:T(8,128)S(1)} copy-done((f32[16,1089]{1,0:T(8,128)S(1)}, f32[16,1089]{1,0:T(8,128)}, u32[]{:S(2)}) %copy-start.8) | copy-done | bytes 69720
  24.5 0.3 collective-permute-start.3
  24.8 0.3 collective-permute-done.8
  25.1 0.6 %collective-permute-start.6 = (f32[16,1089]{1,0:T(8,128)S(1)}, f32[16,1089]{1,0:T(8,128)S(1)}, u32[]{:S(2)}, u32[]{:S(2)}) collective-permute-start(f32[16,1089]{1,0:T(8,128)S(1)} %copy-done.8), channel_id=1, source_target_pairs={{0,17},{1,18},{2,19},{3,20},{4,21},{5,22},{6,23},{7,24},{8,25},{9,... | collective-permute-start | bytes 209096 | tf_op jit(solution)/shard_map/ppermute | solution.py:331
  25.7 0.8 %collective-permute-start.4 = (f32[16,1089]{1,0:T(8,128)S(1)}, f32[16,1089]{1,0:T(8,128)S(1)}, u32[]{:S(2)}, u32[]{:S(2)}) collective-permute-start(f32[16,1089]{1,0:T(8,128)S(1)} %copy-done.3), channel_id=1, source_target_pairs={{0,16},{1,17},{2,18},{3,19},{4,20},{5,21},{6,22},{7,23},{8,24},{9,... | collective-permute-start | bytes 209096 | tf_op jit(solution)/shard_map/ppermute | solution.py:331
  26.6 0.8 %copy-done.5 = f32[1,17424]{1,0:T(1,128)S(1)} copy-done((f32[1,17424]{1,0:T(1,128)S(1)}, f32[1,17424]{1,0:T(1,128)}, u32[]{:S(2)}) %copy-start.5) | copy-done | bytes 69720
  27.5 1.1 %multiply_add_fusion = (f32[1,17424]{1,0:T(1,128)}, f32[1,17424]{1,0:T(1,128)}, f32[1,17424]{1,0:T(1,128)}, f32[1,17424]{1,0:T(1,128)}) fusion(f32[1,17424]{1,0:T(1,128)S(1)} %copy-done, f32[1,17424]{1,0:T(1,128)S(1)} %copy-done.5, f32[2,17424]{1,0:T(2,128)S(1)} %slice_add_fusion, f32[17424]{0:T(1024)S(1)} %broadcast_multiply_fusion, ...), kind=kLoop, calls=%fused_computation.12 | loop fusion | flops 139392 | bytes 766656 | tf_op jit(solution)/shard_map/add | solution.py:397
  28.6 2.4 %collective-permute-done.3 = f32[16,1089]{1,0:T(8,128)S(1)} collective-permute-done((f32[16,1089]{1,0:T(8,128)S(1)}, f32[16,1089]{1,0:T(8,128)S(1)}, u32[]{:S(2)}, u32[]{:S(2)}) %collective-permute-start.3) | collective-permute-done | bytes 69728 | tf_op jit(solution)/shard_map/ppermute | solution.py:331
  31.0 1.7 %collective-permute-done.6 = f32[16,1089]{1,0:T(8,128)S(1)} collective-permute-done((f32[16,1089]{1,0:T(8,128)S(1)}, f32[16,1089]{1,0:T(8,128)S(1)}, u32[]{:S(2)}, u32[]{:S(2)}) %collective-permute-start.6) | collective-permute-done | bytes 69728 | tf_op jit(solution)/shard_map/ppermute | solution.py:331
  32.6 0.7 %pad_add_fusion = f32[16,1089]{1,0:T(8,128)} fusion(f32[1,1089]{1,0:T(1,128)S(1)} %add.44, f32[16,1089]{1,0:T(8,128)S(1)} %collective-permute-done.6, f32[16,1089]{1,0:T(8,128)S(1)} %collective-permute-done.4, f32[16,1089]{1,0:T(8,128)S(1)} %collective-permute-done.5, f32[16,1089]{1,0:T(8,128)S(1)} %collective-permute-done.3, f32[16,1089]{1,0:T(8,128)S(1)} %copy-done.3, ...), kind=kLoop, calls=%fused_computation.7 | loop fusion | flops 104544 | bytes 492228 | tf_op jit(solution)/shard_map/add | solution.py:389
  (30 shorter events, 0.1 us)
Async XLA Ops:
  0.6 0.7 %copy-start.7 = (pred[2048]{0:T(1024)(128)(4,1)S(1)}, pred[2048]{0:T(1024)(128)(4,1)}, u32[]{:S(2)}) copy-start(pred[2048]{0:T(1024)(128)(4,1)} %constant.10.clone.1) | copy-start | bytes 6148
  0.6 6.9 %copy-start.1 = (f32[1,17424]{1,0:T(1,128)S(1)}, f32[1,17424]{1,0:T(1,128)}, u32[]{:S(2)}) copy-start(f32[1,17424]{1,0:T(1,128)} %param.11) | copy-start | bytes 209092
  0.7 6.9 %copy-start = (f32[1,17424]{1,0:T(1,128)S(1)}, f32[1,17424]{1,0:T(1,128)}, u32[]{:S(2)}) copy-start(f32[1,17424]{1,0:T(1,128)} %param.13) | copy-start | bytes 209092
  2.1 9.4 %collective-permute-start = (f32[2,16,128]{2,1,0:T(8,128)S(1)}, f32[2,16,128]{2,1,0:T(8,128)S(1)}, u32[]{:S(2)}, u32[]{:S(2)}) collective-permute-start(f32[2,16,128]{2,1,0:T(8,128)S(1)} %bitcast.23), channel_id=1, source_target_pairs={{0,15},{1,0},{2,1},{3,2},{4,3},{5,4},{6,5},{7,6},{8,7},{9,8},{10,9... | collective-permute-start | bytes 49160 | tf_op jit(solution)/shard_map/ppermute | solution.py:323
  11.5 0.6 %copy-start.9 = (f32[2,16,128]{2,1,0:T(8,128)}, f32[2,16,128]{2,1,0:T(8,128)S(1)}, u32[]{:S(2)}) copy-start(f32[2,16,128]{2,1,0:T(8,128)S(1)} %collective-permute-done.ghost_ref) | copy-start | bytes 49156
  12.1 6.5 %copy-start.4 = (f32[17424]{0:T(1024)S(1)}, f32[17424]{0:T(1024)}, u32[]{:S(2)}) copy-start(f32[17424]{0:T(1024)} %param.15) | copy-start | bytes 209092
  16.9 6.7 %copy-start.2 = (f32[2,144,128]{2,1,0:T(8,128)S(1)}, f32[2,144,128]{2,1,0:T(8,128)}, u32[]{:S(2)}) copy-start(f32[2,144,128]{2,1,0:T(8,128)} %get-tuple-element.11) | copy-start | bytes 442372
  17.7 6.3 %collective-permute-start.7 = (f32[1,1089]{1,0:T(1,128)S(1)}, f32[1,1089]{1,0:T(1,128)S(1)}, u32[]{:S(2)}, u32[]{:S(2)}) collective-permute-start(f32[1,1089]{1,0:T(1,128)S(1)} %slice.24), channel_id=1, source_target_pairs={{0,2},{1,3},{2,4},{3,5},{4,6},{5,7},{6,8},{7,9},{8,10},{9,11},{10,... | collective-permute-start | bytes 13076 | tf_op jit(solution)/shard_map/ppermute | solution.py:331
  17.7 7.4 %collective-permute-start.8 = (f32[1,1089]{1,0:T(1,128)S(1)}, f32[1,1089]{1,0:T(1,128)S(1)}, u32[]{:S(2)}, u32[]{:S(2)}) collective-permute-start(f32[1,1089]{1,0:T(1,128)S(1)} %slice.24), channel_id=1, source_target_pairs={{0,18},{1,19},{2,20},{3,21},{4,22},{5,23},{6,24},{7,25},{8,26},{9,... | collective-permute-start | bytes 13076 | tf_op jit(solution)/shard_map/ppermute | solution.py:331
  18.6 7.2 %collective-permute-start.1 = (f32[2,16,128]{2,1,0:T(8,128)}, f32[2,16,128]{2,1,0:T(8,128)S(1)}, u32[]{:S(2)}, u32[]{:S(2)}) collective-permute-start(f32[2,16,128]{2,1,0:T(8,128)} %get-tuple-element.12), channel_id=1, source_target_pairs={{0,1},{1,2},{2,3},{3,4},{4,5},{5,6},{6,7},{7,8},{8,9},{9,10},{10,1... | collective-permute-start | bytes 49160 | tf_op jit(solution)/shard_map/ppermute | solution.py:323
  18.6 10.0 %collective-permute-start.2 = (f32[16,1089]{1,0:T(8,128)}, f32[16,1089]{1,0:T(8,128)S(1)}, u32[]{:S(2)}, u32[]{:S(2)}) collective-permute-start(f32[16,1089]{1,0:T(8,128)} %get-tuple-element.14), channel_id=1, source_target_pairs={{0,15},{1,0},{2,1},{3,2},{4,3},{5,4},{6,5},{7,6},{8,7},{9,8},{10,9... | collective-permute-start | bytes 209096 | tf_op jit(solution)/shard_map/ppermute | solution.py:331
  23.1 7.9 %collective-permute-start.5 = (f32[16,1089]{1,0:T(8,128)}, f32[16,1089]{1,0:T(8,128)S(1)}, u32[]{:S(2)}, u32[]{:S(2)}) collective-permute-start(f32[16,1089]{1,0:T(8,128)} %get-tuple-element.14), channel_id=1, source_target_pairs={{0,31},{1,16},{2,17},{3,18},{4,19},{5,20},{6,21},{7,22},{8,23},{9,... | collective-permute-start | bytes 209096 | tf_op jit(solution)/shard_map/ppermute | solution.py:331
  23.6 0.9 %copy-start.8 = (f32[16,1089]{1,0:T(8,128)S(1)}, f32[16,1089]{1,0:T(8,128)}, u32[]{:S(2)}) copy-start(f32[16,1089]{1,0:T(8,128)} %get-tuple-element.15) | copy-start | bytes 209092
  23.6 2.1 %copy-start.3 = (f32[16,1089]{1,0:T(8,128)S(1)}, f32[16,1089]{1,0:T(8,128)}, u32[]{:S(2)}) copy-start(f32[16,1089]{1,0:T(8,128)} %get-tuple-element.13) | copy-start | bytes 209092
  24.5 6.5 %collective-permute-start.3 = (f32[16,1089]{1,0:T(8,128)S(1)}, f32[16,1089]{1,0:T(8,128)S(1)}, u32[]{:S(2)}, u32[]{:S(2)}) collective-permute-start(f32[16,1089]{1,0:T(8,128)S(1)} %copy-done.8), channel_id=1, source_target_pairs={{0,1},{1,2},{2,3},{3,4},{4,5},{5,6},{6,7},{7,8},{8,9},{9,10},{10,1... | collective-permute-start | bytes 209096 | tf_op jit(solution)/shard_map/ppermute | solution.py:331
  25.1 7.5 %collective-permute-start.6 = (f32[16,1089]{1,0:T(8,128)S(1)}, f32[16,1089]{1,0:T(8,128)S(1)}, u32[]{:S(2)}, u32[]{:S(2)}) collective-permute-start(f32[16,1089]{1,0:T(8,128)S(1)} %copy-done.8), channel_id=1, source_target_pairs={{0,17},{1,18},{2,19},{3,20},{4,21},{5,22},{6,23},{7,24},{8,25},{9,... | collective-permute-start | bytes 209096 | tf_op jit(solution)/shard_map/ppermute | solution.py:331
  25.7 5.2 %collective-permute-start.4 = (f32[16,1089]{1,0:T(8,128)S(1)}, f32[16,1089]{1,0:T(8,128)S(1)}, u32[]{:S(2)}, u32[]{:S(2)}) collective-permute-start(f32[16,1089]{1,0:T(8,128)S(1)} %copy-done.3), channel_id=1, source_target_pairs={{0,16},{1,17},{2,18},{3,19},{4,20},{5,21},{6,22},{7,23},{8,24},{9,... | collective-permute-start | bytes 209096 | tf_op jit(solution)/shard_map/ppermute | solution.py:331
  26.6 0.9 %copy-start.5 = (f32[1,17424]{1,0:T(1,128)S(1)}, f32[1,17424]{1,0:T(1,128)}, u32[]{:S(2)}) copy-start(f32[1,17424]{1,0:T(1,128)} %param.14) | copy-start | bytes 209092
  26.6 0.9 %copy-start.6 = (f32[1,17424]{1,0:T(1,128)S(1)}, f32[1,17424]{1,0:T(1,128)}, u32[]{:S(2)}) copy-start(f32[1,17424]{1,0:T(1,128)} %param.12) | copy-start | bytes 209092

commit v2 on v1

v2 whole, which is shorter than its diff:
```python
import numpy as np
import jax
import jax.numpy as jnp
import ml_dtypes
from jax import lax
from jax.experimental import pallas as pl
from jax.experimental.pallas import tpu as pltpu
from jax.sharding import PartitionSpec as P

NGLL = 5
EX, EY, EZ = 4, 8, 8
PXU = 16
PY = 33
PZ = 33
PYZ = 1089
NPTS = 17424
LANES = 128
ROWS = 144
TIME_STEP = 0.02
F32 = jnp.float32
BF16 = jnp.bfloat16


def gll():
    nodes = np.array([-1.0, -np.sqrt(3.0 / 7.0), 0.0, np.sqrt(3.0 / 7.0), 1.0])
    bary = np.array([1.0 / np.prod([nodes[r] - nodes[c] for c in range(5) if c != r]) for r in range(5)])
    d = np.zeros((5, 5))
    for r in range(5):
        for c in range(5):
            if c != r:
                d[r, c] = bary[c] / bary[r] / (nodes[r] - nodes[c])
        d[r, r] = -np.sum(d[r])
    return d


DERIV = gll()


def split_np(x):
    x = np.asarray(x, np.float32)
    parts = []
    for _ in range(3):
        p = x.astype(ml_dtypes.bfloat16)
        parts.append(p)
        x = x - p.astype(np.float32)
    return parts


ROW_PLANE = np.array([5, 9, 13, 0, 4, 8, 12, 1, 7, 11, 15, 2, 6, 10, 14, 3])


def band_table():
    offsets = np.arange(-PXU, PXU + 1)
    w = lambda d: np.exp(-d * d / (2.0 * (PXU / 4.0) ** 2))
    total = w(offsets.astype(np.float64)).sum()
    out = []
    for first in (-PXU, PXU):
        source = np.concatenate([ROW_PLANE, ROW_PLANE + first, ROW_PLANE - first])
        spread = np.arange(PXU)[:, None] - source[None, :]
        band = w(spread.astype(np.float64)) * (np.abs(spread) <= PXU) / total
        b1, b2, b3 = split_np(band)
        out.append(np.concatenate([b1, b1, b1, b2, b2, b3], axis=1))
    return np.stack(out)


def cross_table():
    off = np.arange(-4, 5)
    k = np.exp(-off * off / (2.0 * 1.5 * 1.5))
    point = np.arange(33)
    inside = ((point[None, :] + off[:, None]) >= 0) & ((point[None, :] + off[:, None]) < 33)
    taps = k[:, None] * inside
    taps = taps / taps.sum(axis=0, keepdims=True)
    out = np.zeros((24, 1152), np.float32)
    out[0:9, :PYZ] = np.tile(taps, (1, PY))
    out[9:18, :PYZ] = np.repeat(taps, PZ, axis=1)
    return out


def split3(x):
    hi = x.astype(BF16)
    rest = x - hi.astype(F32)
    mid = rest.astype(BF16)
    low = (rest - mid.astype(F32)).astype(BF16)
    return hi, mid, low


def dot_nt(a, b):
    return lax.dot_general(a, b, (((1,), (1,)), ((), ())), preferred_element_type=F32)


def dot_tn(a, b):
    return lax.dot_general(a, b, (((0,), (0,)), ((), ())), preferred_element_type=F32)


def selector():
    column = lax.broadcasted_iota(jnp.int32, (8, 256), 1)
    row = lax.broadcasted_iota(jnp.int32, (8, 256), 0)
    base = column - 4 * row
    blocks = [jnp.where(base == j * PZ + k, 1.0, 0.0) for j in range(5) for k in range(5)]
    return jnp.concatenate(blocks, axis=0).astype(BF16)


def slot_elements(conn_ref, count_ref):
    point = conn_ref[0:1, :].astype(F32)
    x = jnp.floor((point + 0.5) * (1.0 / PYZ))
    rest = point - x * PYZ
    y = jnp.floor((rest + 0.5) * (1.0 / PZ))
    z = rest - y * PZ
    code = (8.0 * z + y + 0.25 * x).astype(jnp.int32)
    slot = lax.broadcasted_iota(jnp.int32, (1, 256), 1)
    return jnp.where(slot < count_ref[0], code, -1000)


def weighted(shear_ref):
    q = lax.broadcasted_iota(jnp.int32, (125, 256), 0)
    weight = None
    for digit in (q // 25, (q // 5) % 5, q % 5):
        w = jnp.where(digit == 2, 32.0 / 45.0, jnp.where((digit == 0) | (digit == 4), 0.1, 49.0 / 90.0))
        weight = w if weight is None else weight * w
    return split3(shear_ref[...] * weight)


def moved_by(parts, pick):
    hi, mid, low = parts
    return dot_nt(hi, pick) + (dot_nt(mid, pick) + dot_nt(low, pick))


def pack_kernel(parity_ref, count_ref, conn_ref, shear_ref, fwd_ref, adj_ref, first_ref, second_ref, line_ref):
    code = slot_elements(conn_ref, count_ref)
    lane = lax.broadcasted_iota(jnp.int32, (LANES, 256), 0) & 63
    pick = jnp.where(code == (lane >> 3) * 32 + (lane & 7) * 4 + 3, 1.0, 0.0).astype(BF16)
    flux = moved_by(weighted(shear_ref), pick)
    flux = jnp.concatenate([flux, jnp.zeros((3, LANES), F32)], axis=0)
    low = lax.broadcasted_iota(jnp.int32, (64, LANES), 1) < 64
    flux = jnp.where(low, flux[0:64], flux[64:128])
    for f, ref in enumerate((fwd_ref, adj_ref)):
        for r in (0, 8, 16, 24, 32):
            line_ref[f, r : r + 8, :] = ref[0:1, r * LANES : (r + 8) * LANES].reshape(8, LANES)
        base = 102 * LANES
        for r in (0, 8, 16, 24):
            at = base + r * LANES
            line_ref[f, 40 + r : 48 + r, :] = ref[0:1, at : at + 8 * LANES].reshape(8, LANES)
        at = base + 32 * LANES
        line_ref[f, 72:74, :] = ref[0:1, at : at + 2 * LANES].reshape(2, LANES)
        line_ref[f, 74:80, :] = jnp.zeros((6, LANES), F32)
        line_ref[f, 74:75, 0:16] = ref[0:1, at + 2 * LANES : at + 2 * LANES + 16]
    odd = parity_ref[0] == 1
    for ref, flip in ((first_ref, odd), (second_ref, jnp.logical_not(odd))):
        for f in range(2):
            ref[40 * f : 40 * f + 40, :] = jnp.where(flip, line_ref[f, 40:80, :], line_ref[f, 0:40, :])
        ref[80:144, :] = flux


def flux_kernel(count_ref, conn_ref, shear_ref, flux_ref):
    code = slot_elements(conn_ref, count_ref)
    lane = lax.broadcasted_iota(jnp.int32, (LANES, 256), 0)
    layer = lane >> 3
    layer = jnp.where(layer >= 10, layer - 10, jnp.where(layer >= 5, layer - 5, layer)) - 1
    member = jnp.where((layer >= 0) & (layer < 4), (lane & 7) * 4 + layer, -1)
    member = jnp.where(member >= 0, member, 5000)
    pick = jnp.concatenate([jnp.where(code - member == ez * 32, 1.0, 0.0).astype(BF16) for ez in range(EZ)], axis=0)
    moved = moved_by(weighted(shear_ref), pick)
    for ez in range(EZ):
        flux_ref[pl.ds(ez, 125, stride=8), :] = moved[:, ez * LANES : (ez + 1) * LANES]


def derive(e):
    d = DERIV
    s0, s1 = e[0] + e[4], e[1] + e[3]
    d0, d1 = e[0] - e[4], e[1] - e[3]
    out = [None] * 5
    for i in (0, 1):
        even = float((d[i, 0] - d[i, 4]) / 2) * d0 + float((d[i, 1] - d[i, 3]) / 2) * d1
        odd = float((d[i, 0] + d[i, 4]) / 2) * s0 + float((d[i, 1] + d[i, 3]) / 2) * s1 + float(d[i, 2]) * e[2]
        out[i] = odd + even
        out[4 - i] = even - odd
    out[2] = float(d[2, 0]) * d0 + float(d[2, 1]) * d1
    return out


def derive_back(t):
    d = DERIV
    s0, s1 = t[0] + t[4], t[1] + t[3]
    d0, d1 = t[0] - t[4], t[1] - t[3]
    out = [None] * 5
    for i in (0, 1):
        even = float((d[0, i] - d[4, i]) / 2) * d0 + float((d[1, i] - d[3, i]) / 2) * d1
        odd = float((d[0, i] + d[4, i]) / 2) * s0 + float((d[1, i] + d[3, i]) / 2) * s1 + float(d[2, i]) * t[2]
        out[i] = odd + even
        out[4 - i] = even - odd
    out[2] = float(d[0, 2]) * d0 + float(d[1, 2]) * d1
    return out


def shifted(tiles, distance, lane):
    skip, part = divmod(distance, LANES)
    if part == 0:
        moved = tiles
        pick = None
    else:
        moved = [pltpu.roll(t, LANES - part, 1) for t in tiles]
        pick = lane < LANES - part
    n = len(tiles)
    out = []
    for i in range(n):
        a = moved[(i + skip) % n]
        b = moved[(i + skip + 1) % n]
        out.append(a if pick is None else jnp.where(pick, a, b))
    return out


def at(ref, i, j, k):
    r = (j * 5 + k) * 8
    return ref[r : r + 8, i * LANES : (i + 1) * LANES]


def put(ref, i, j, k, value):
    r = (j * 5 + k) * 8
    ref[r : r + 8, i * LANES : (i + 1) * LANES] = value


def flux_at(ref, i, j, k):
    r = ((i * 5 + j) * 5 + k) * 8
    return ref[r : r + 8, :]


def lines():
    for axis in range(3):
        for p in range(5):
            for q in range(5):
                yield axis, [((l, p, q), (p, l, q), (p, q, l))[axis] for l in range(5)]


def plane_of(ref, start, row):
    r0, off = divmod(start, LANES)
    lane9 = lax.broadcasted_iota(jnp.int32, (9, LANES), 1)
    flat = ref[row + r0 : row + r0 + 9, :]
    if off:
        flat = jnp.where(
            lane9 < LANES - off,
            pltpu.roll(flat, LANES - off, 1),
            pltpu.roll(ref[row + r0 + 1 : row + r0 + 10, :], LANES - off, 1),
        )
    return flat


def kernel_kernel(
    parity_ref, fwd_ref, adj_ref, first_ref, second_ref, flux_in_ref, cross_ref,
    kern_out_ref, elem_ref, flux_ref,
    own_ref, near_ref, plane_ref, win0_ref, win1_ref, kern_ref,
):
    lane = lax.broadcasted_iota(jnp.int32, (8, LANES), 1)
    even = parity_ref[0] == 0
    for f, ref in enumerate((fwd_ref, adj_ref)):
        for r in range(0, 136, 8):
            own_ref[ROWS * f + r : ROWS * f + r + 8, :] = ref[0:1, r * LANES : (r + 8) * LANES].reshape(8, LANES)
        own_ref[ROWS * f + 136 : ROWS * f + 144, :] = jnp.zeros((8, LANES), F32)
        own_ref[ROWS * f + 136 : ROWS * f + 137, 0:16] = ref[0:1, NPTS - 16 : NPTS]
    near_ref[0:144, :] = jnp.where(even, first_ref[...], second_ref[...])
    near_ref[144:224, :] = jnp.where(even, second_ref[0:80, :], first_ref[0:80, :])

    m = lax.broadcasted_iota(jnp.int32, (LANES, LANES), 0)
    n = lax.broadcasted_iota(jnp.int32, (LANES, LANES), 1) & 63
    layer = m >> 3
    base = jnp.where((layer == 0) | (layer == 5) | (layer == 10), n - (m & 7), -1)
    pick = jnp.concatenate([jnp.where(base == ez * 8, 1.0, 0.0).astype(BF16) for ez in range(EZ)], axis=0)
    low = lax.broadcasted_iota(jnp.int32, (64, LANES), 1) < 64
    packed = near_ref[80:144, :]
    packed = jnp.concatenate([jnp.where(low, packed, 0.0), jnp.where(low, 0.0, packed)], axis=0)
    extra = moved_by(split3(packed), pick)
    for ez in range(EZ):
        rows = pl.ds(ez, 125, stride=8)
        flux_ref[rows, :] = flux_in_ref[rows, :] + extra[0:125, ez * LANES : (ez + 1) * LANES]

    plane_ref[...] = jnp.zeros(plane_ref.shape, F32)
    for x in range(-4, PXU + 1):
        for f in range(2):
            if x < 0:
                flat = plane_of(near_ref, 12 + PYZ * (x + 4), 40 * f)
            elif x < PXU:
                flat = plane_of(own_ref, PYZ * x, ROWS * f)
            else:
                flat = plane_of(near_ref, 0, 144 + 40 * f)
            places = []
            if x < PXU:
                places.append((x % 4, x // 4 + 1))
            if x % 4 == 0 and x >= 0:
                places.append((4, x // 4))
            for i, layer in places:
                for r in (layer, 10 + layer) if f == 0 else (5 + layer,):
                    plane_ref[pl.ds(i * 144 + r, 9, stride=16), :] = flat
    for i in range(NGLL):
        for h in range(2):
            tiles = [plane_ref[i * 144 + t * 16 + 8 * h : i * 144 + t * 16 + 8 * h + 8, :] for t in range(9)]
            for ey in range(EY):
                near = [tiles[ey], tiles[ey + 1], tiles[min(ey + 2, 8)]]
                if ey:
                    near = [pltpu.roll(t, LANES - 4 * ey, 1) for t in near]
                    keep = lane < LANES - 4 * ey
                    near = [jnp.where(keep, near[0], near[1]), jnp.where(keep, near[1], near[2])]
                rows = pl.ds(i * LANES + h * 64 + ey, 8, stride=8)
                win0_ref[rows, :] = near[0]
                win1_ref[rows, :] = near[1]
    select = selector()
    hi, mid, low = split3(jnp.concatenate([win0_ref[...], win1_ref[...]], axis=1))
    elem_ref[...] = dot_nt(select, hi) + (dot_nt(select, mid) + dot_nt(select, low))

    for axis, line in lines():
        grads = derive([at(elem_ref, *c) for c in line])
        for n, c in enumerate(line):
            prod = grads[n] * pltpu.roll(grads[n], 40, 1)
            if axis > 0:
                prod = at(kern_ref, *c) + prod
            if axis == 2:
                prod = -prod * flux_at(flux_ref, *c)
            put(kern_ref, *c, prod)
    hi, mid, low = split3(kern_ref[...])
    back = dot_tn(hi, select) + (dot_tn(mid, select) + dot_tn(low, select))
    win0_ref[...] = back[:, :LANES]
    win1_ref[...] = back[:, LANES:]
    kern = [gathered(win0_ref, win1_ref, i, 1) for i in range(NGLL)]
    row = lax.broadcasted_iota(jnp.int32, (8, LANES), 0)
    inner = (row >= 3) & (row < 7)
    tiles = []
    for t in range(9):
        kern[0][t] = kern[0][t] + pltpu.roll(kern[4][t], 1, 0)
        tiles.append(
            jnp.concatenate([jnp.where(inner, kern[i][t], pltpu.roll(kern[i + 1][t], 4, 0)) for i in (0, 2)], axis=0)
        )
    lane16 = lax.broadcasted_iota(jnp.int32, (16, LANES), 1)
    for base, step in ((0, 1), (9, PZ)):
        total = None
        for tap in range(9):
            moved = shifted(tiles, step * (tap - 4), lane16) if tap != 4 else tiles
            scaled = [v * cross_ref[base + tap : base + tap + 1, t * LANES : (t + 1) * LANES] for t, v in enumerate(moved)]
            total = scaled if total is None else [a + b for a, b in zip(total, scaled)]
        tiles = total
    for t in range(9):
        kern_out_ref[:, t * LANES : (t + 1) * LANES] = tiles[t]


def gathered(win0_ref, win1_ref, i, h):
    lane = lax.broadcasted_iota(jnp.int32, (8, LANES), 1)
    tiles = [None] * 9
    for ey in range(EY):
        rows = pl.ds(i * LANES + h * 64 + ey, 8, stride=8)
        a, b = win0_ref[rows, :], win1_ref[rows, :]
        if ey:
            a, b = pltpu.roll(a, 4 * ey, 1), pltpu.roll(b, 4 * ey, 1)
            keep = lane >= 4 * ey
            a, b = jnp.where(keep, a, 0.0), jnp.where(keep, b, a)
        tiles[ey] = a if ey == 0 else tiles[ey] + a
        tiles[ey + 1] = b
    return tiles


def force_kernel(
    elem_ref, flux_ref, fwd_ref, fwd_speed_ref, adj_ref, adj_speed_ref, mass_ref, after_ref,
    fwd_out_ref, fwd_speed_out_ref, adj_out_ref, adj_speed_out_ref,
    term_ref, win0_ref, win1_ref, plane_ref, line_ref,
):
    for axis, line in lines():
        grads = derive([at(elem_ref, *c) for c in line])
        back = derive_back([g * flux_at(flux_ref, *c) for g, c in zip(grads, line)])
        for n, c in enumerate(line):
            put(term_ref, *c, back[n] if axis == 0 else at(term_ref, *c) + back[n])
    select = selector()
    hi, mid, low = split3(term_ref[...])
    back = dot_tn(hi, select) + (dot_tn(mid, select) + dot_tn(low, select))
    win0_ref[...] = back[:, :LANES]
    win1_ref[...] = back[:, LANES:]
    lane9 = lax.broadcasted_iota(jnp.int32, (9, LANES), 1)
    for i in range(NGLL):
        for h in range(2):
            for t, tile in enumerate(gathered(win0_ref, win1_ref, i, h)):
                plane_ref[i * 144 + t * 16 + 8 * h : i * 144 + t * 16 + 8 * h + 8, :] = tile
    line_ref[...] = jnp.zeros(line_ref.shape, F32)
    for f in range(2):
        for x in range(PXU):
            r0, off = divmod(PYZ * x, LANES)
            flat = plane_ref[pl.ds((x % 4) * 144 + 5 * f + x // 4 + 1, 9, stride=16), :]
            if x % 4 == 0:
                flat = flat + plane_ref[pl.ds(4 * 144 + 5 * f + x // 4, 9, stride=16), :]
            if off:
                flat = pltpu.roll(flat, off, 1)
                spill = jnp.where(lane9 < off, flat, 0.0)
                flat = jnp.where(lane9 < off, 0.0, flat)
            line_ref[f, r0 : r0 + 9, :] = line_ref[f, r0 : r0 + 9, :] + flat
            if off:
                line_ref[f, r0 + 1 : r0 + 10, :] = line_ref[f, r0 + 1 : r0 + 10, :] + spill

    def step(lo, hi, force):
        shape = (hi - lo) // force[0].shape[1], force[0].shape[1]
        take = lambda ref: ref[0:1, lo:hi].reshape(shape)
        scale = TIME_STEP * mass_ref[0:1, lo:hi].reshape(shape)
        speed = take(fwd_speed_ref) + scale * force[0]
        fwd_speed_out_ref[0:1, lo:hi] = speed.reshape(1, hi - lo)
        fwd_out_ref[0:1, lo:hi] = (take(fwd_ref) - TIME_STEP * speed).reshape(1, hi - lo)
        speed = take(adj_speed_ref) - scale * force[1]
        adj_speed_out_ref[0:1, lo:hi] = speed.reshape(1, hi - lo)
        adj_out_ref[0:1, lo:hi] = (take(adj_ref) + TIME_STEP * speed).reshape(1, hi - lo)

    for r in range(0, 136, 8):
        step(r * LANES, (r + 8) * LANES, [line_ref[f, r : r + 8, :] for f in range(2)])
    step(NPTS - 16, NPTS, [line_ref[f, 136:137, 0:16] for f in range(2)])


def band_kernel(parity_ref, own_ref, first_ref, second_ref, band_ref, out_ref):
    flat = jnp.concatenate([own_ref[...], first_ref[...], second_ref[...]], axis=0)
    k1 = flat.astype(BF16)
    rest = flat - k1.astype(F32)
    k2 = rest.astype(BF16)
    k3 = (rest - k2.astype(F32)).astype(BF16)
    stacked = jnp.concatenate([k1, k2, k3, k1, k2, k1], axis=0)
    band = band_ref[parity_ref[0]]
    out_ref[...] = jnp.dot(band, stacked, preferred_element_type=F32)[:, :PYZ]


def on_device(
    forward_displacement,
    forward_velocity,
    adjoint_displacement,
    adjoint_velocity,
    inverse_mass,
    shear_modulus,
    connectivity,
    face_points,
    element_count,
):
    events = lax.axis_size("event")
    cuts = lax.axis_size("cuts")
    parity = (lax.axis_index("cuts") % 2).astype(jnp.int32).reshape(1)
    pairs_first = [(i, (i - 1 if i % 2 == 0 else i + 1) % cuts) for i in range(cuts)]
    pairs_second = [(i, (i + 1 if i % 2 == 0 else i - 1) % cuts) for i in range(cuts)]

    vmem = pl.BlockSpec(memory_space=pltpu.VMEM)
    smem = pl.BlockSpec(memory_space=pltpu.SMEM)
    anywhere = pl.BlockSpec(memory_space=pl.ANY)
    message = jax.ShapeDtypeStruct((144, LANES), F32)
    conn = connectivity[0:8]
    first, second = pl.pallas_call(
        pack_kernel,
        out_shape=[message, message],
        in_specs=[smem, smem, vmem, vmem, vmem, vmem],
        scratch_shapes=[pltpu.VMEM((2, 80, LANES), F32)],
        cost_estimate=pl.CostEstimate(flops=100000000, bytes_accessed=1000000, transcendentals=0),
        name="pack",
    )(parity, element_count, conn, shear_modulus, forward_displacement, adjoint_displacement)
    first = lax.ppermute(first, "cuts", pairs_first)
    second = lax.ppermute(second, "cuts", pairs_second)

    flux = pl.pallas_call(
        flux_kernel,
        out_shape=jax.ShapeDtypeStruct((1000, LANES), F32),
        in_specs=[smem, vmem, vmem],
        cost_estimate=pl.CostEstimate(flops=200000000, bytes_accessed=2000000, transcendentals=0),
        name="flux",
    )(element_count, conn, shear_modulus)

    elem_shape = (200, 5 * LANES)
    kern, elem, flux = pl.pallas_call(
        kernel_kernel,
        out_shape=[
            jax.ShapeDtypeStruct((16, 9 * LANES), F32),
            jax.ShapeDtypeStruct(elem_shape, F32),
            jax.ShapeDtypeStruct((1000, LANES), F32),
        ],
        in_specs=[smem] + [vmem] * 6,
        scratch_shapes=[
            pltpu.VMEM((2 * ROWS, LANES), F32),
            pltpu.VMEM((224, LANES), F32),
            pltpu.VMEM((5 * 144, LANES), F32),
            pltpu.VMEM((5 * LANES, LANES), F32),
            pltpu.VMEM((5 * LANES, LANES), F32),
            pltpu.VMEM(elem_shape, F32),
        ],
        cost_estimate=pl.CostEstimate(flops=400000000, bytes_accessed=4000000, transcendentals=0),
        name="kernel_term",
    )(parity, forward_displacement, adjoint_displacement, first, second, flux, jnp.asarray(cross_table()))

    if events == 2:
        kern = kern + lax.ppermute(kern, "event", [(0, 1), (1, 0)])
    elif events > 2:
        kern = lax.psum(kern, "event")
    kern_first = lax.ppermute(kern, "cuts", pairs_first)
    kern_second = lax.ppermute(kern, "cuts", pairs_second)

    points = jax.ShapeDtypeStruct((1, NPTS), F32)
    outs = pl.pallas_call(
        force_kernel,
        out_shape=[points] * 4,
        in_specs=[vmem] * 7 + [anywhere],
        scratch_shapes=[
            pltpu.VMEM(elem_shape, F32),
            pltpu.VMEM((5 * LANES, LANES), F32),
            pltpu.VMEM((5 * LANES, LANES), F32),
            pltpu.VMEM((5 * 144, LANES), F32),
            pltpu.VMEM((2, ROWS, LANES), F32),
        ],
        cost_estimate=pl.CostEstimate(flops=400000000, bytes_accessed=4000000, transcendentals=0),
        name="forces",
    )(
        elem,
        flux,
        forward_displacement,
        forward_velocity,
        adjoint_displacement,
        adjoint_velocity,
        inverse_mass[None, :],
        kern,
    )
    shear_kernel = pl.pallas_call(
        band_kernel,
        out_shape=jax.ShapeDtypeStruct((PXU, PYZ), F32),
        in_specs=[smem] + [vmem] * 4,
        cost_estimate=pl.CostEstimate(flops=20000000, bytes_accessed=400000, transcendentals=0),
        name="band",
    )(parity, kern, kern_first, kern_second, jnp.asarray(band_table()))
    return (*outs, shear_kernel)


def solution(mesh):
    in_specs = (
        P("event", "cuts"),
        P("event", "cuts"),
        P("event", "cuts"),
        P("event", "cuts"),
        P("cuts"),
        P(None, "cuts"),
        P(None, "cuts"),
        P("cuts", None),
        P("cuts"),
    )
    out_specs = (
        P("event", "cuts"),
        P("event", "cuts"),
        P("event", "cuts"),
        P("event", "cuts"),
        P("cuts", None),
    )
    return jax.shard_map(on_device, mesh=mesh, in_specs=in_specs, out_specs=out_specs, check_vma=False)
```

time: 33.6 us -> 34.4 us (1.024)
  Pallas kernels: 7.27 us -> 14.1 us
  starting transfers between devices: 13 us -> 9.98 us
  other arithmetic: 2.63 us -> 0.9 us
  waiting for transfers between devices: 4.8 us -> 3.19 us
  local copies, waits for them, and re-layouts: 4.15 us -> 4.5 us
    pallas_call x1 -> x4, Pallas kernels: 4.83 us -> 11.7 us  [the longest x1 4.65 us: on_device(): pl.pallas_call(kernel_kernel, out_shape=[jax.ShapeDtypeStruct((16, 9 * LA...]
    ppermute x9 -> x5, starting transfers between devices: 13 us -> 9.98 us  [the longest x1 5.44 us: on_device(): first = lax.ppermute(first, 'cuts', pairs_first)]
    ppermute x9 -> x5, waiting for transfers between devices: 4.8 us -> 3.19 us  [the longest x1 3.18 us: on_device(): kern = kern + lax.ppermute(kern, 'event', [(0, 1), (1, 0)])]
    add x4 -> x1, other arithmetic: 1.76 us -> 0.9 us  [on_device(): kern = kern + lax.ppermute(kern, 'event', [(0, 1), (1, 0)])]
    unnamed x25 -> x12, local copies, waits for them, and re-layouts: 3.33 us -> 2.53 us
    unnamed x1 -> x0, other arithmetic: 0.74 us -> none
    broadcast_in_dim x0 -> x1, local copies, waits for them, and re-layouts: none -> 0.68 us  [on_device(): inverse_mass[None, :]]
    slice x2 -> x1, local copies, waits for them, and re-layouts: 0.81 us -> 1.3 us  [on_device(): conn = connectivity[0:8]]
  transfers between devices with their start and end apart: 9 -> 5, of which waited for: 4 -> 1; matrix products, arithmetic and copies ran while one was open for 6% -> 2% of each run, Pallas kernels for 7% -> 17%
where the time goes in v2:
time: 34.4 us; the launch traced here: 34 us
  Pallas kernels  14.1 us (41%)
  starting transfers between devices  9.98 us (29%)
  local copies, waits for them, and re-layouts  4.5 us (13%)
  waiting for transfers between devices  3.19 us (9%)
  between operations  1.33 us (4%)
  other arithmetic  0.9 us (3%)
    ppermute x1, starting transfers between devices, on_device(): first = lax.ppermute(first, 'cuts', pairs_first)  5.44 us
    pallas_call x1, Pallas kernels, on_device(): pl.pallas_call(kernel_kernel, out_shape=[jax.ShapeDtypeStruct((16, 9 * LA...  4.65 us
    pallas_call x1, Pallas kernels, on_device(): pl.pallas_call(force_kernel, out_shape=[points] * 4, in_specs=[vmem] * 7...  3.28 us
    ppermute x1, waiting for transfers between devices, on_device(): kern = kern + lax.ppermute(kern, 'event', [(0, 1), (1, 0)])  3.18 us
    ppermute x1, starting transfers between devices, on_device(): kern_first = lax.ppermute(kern, 'cuts', pairs_first)  2.81 us
    unnamed x12, local copies, waits for them, and re-layouts  2.53 us
    pallas_call x1, Pallas kernels, on_device(): pl.pallas_call(flux_kernel, out_shape=jax.ShapeDtypeStruct((1000, LANES),...  2.46 us
    pallas_call x1, Pallas kernels, on_device(): pl.pallas_call(pack_kernel, out_shape=[message, message], in_specs=[smem,...  1.97 us
  transfers between devices with their start and end apart: 5, of which 1 were waited for; matrix products, arithmetic and copies ran while one was open for 2% of the time, Pallas kernels for 17%

profile of v2, /device:TPU:0, one launch (start us, length us, event | category | flops | bytes accessed | tf_op | source)
XLA Modules:
  0.0 34.0 jit_solution(11185049520717416057)
XLA Ops:
  0.6 1.3 %slice.3.conn_ref = s32[8,256]{1,0:T(8,128)} slice(s32[125,256]{1,0:T(8,128)} %param.17), slice={[0:8], [0:256]} | slice | bytes 16384 | tf_op jit(solution)/shard_map/slice | solution.py:440
  2.6 2.0 %pack.1 = (f32[144,128]{1,0:T(8,128)}, f32[144,128]{1,0:T(8,128)}) custom-call(s32[1]{0:T(128)} %bitcast.parity_ref, s32[1]{0:T(128)S(6)} %copy.15.count_ref, s32[8,256]{1,0:T(8,128)} %slice.3.conn_ref, f32[125,256]{1,0:T(8,128)} %shear_ref.3, f32[1,17424]{1,0:T(1,128)} %fwd_ref.5, f32[1,17424]{1,0:T(1,128)} %adj_ref.5), custom_call_target="tpu_custom_call" | custom-call | flops 100000000 | bytes 1000000 | tf_op jit(solution)/shard_map/pack/pallas_call | solution.py:441
  4.6 5.4 %collective-permute-start = (f32[144,128]{1,0:T(8,128)}, f32[144,128]{1,0:T(8,128)S(1)}, u32[]{:S(2)}, u32[]{:S(2)}) collective-permute-start(f32[144,128]{1,0:T(8,128)} %get-tuple-element.14), channel_id=1, source_target_pairs={{0,15},{1,2},{2,1},{3,4},{4,3},{5,6},{6,5},{7,8},{8,7},{9,10},{10,... | collective-permute-start | bytes 221192 | tf_op jit(solution)/shard_map/ppermute | solution.py:449
  10.0 0.0 collective-permute-start.1
  10.0 2.5 %flux.1.flux_in_ref = f32[1000,128]{1,0:T(8,128)} custom-call(s32[1]{0:T(128)S(6)} %copy.15.count_ref, s32[8,256]{1,0:T(8,128)} %slice.3.conn_ref, f32[125,256]{1,0:T(8,128)} %shear_ref.3), custom_call_target="tpu_custom_call" | custom-call | flops 200000000 | bytes 2000000 | tf_op jit(solution)/shard_map/flux/pallas_call | solution.py:452
  12.5 0.0 collective-permute-done.first_ref
  12.5 0.0 collective-permute-done.1.second_ref
  12.5 0.6 %copy-done.4 = f32[144,128]{1,0:T(8,128)} copy-done((f32[144,128]{1,0:T(8,128)}, f32[144,128]{1,0:T(8,128)S(1)}, u32[]{:S(2)}) %copy-start.4) | copy-done | bytes 73752
  13.1 0.6 %copy-done.5 = f32[144,128]{1,0:T(8,128)} copy-done((f32[144,128]{1,0:T(8,128)}, f32[144,128]{1,0:T(8,128)S(1)}, u32[]{:S(2)}) %copy-start.5) | copy-done | bytes 73752
  13.7 4.6 %kernel_term.1 = (f32[16,1152]{1,0:T(8,128)}, f32[200,640]{1,0:T(8,128)}, f32[1000,128]{1,0:T(8,128)}) custom-call(s32[1]{0:T(128)} %bitcast.parity_ref, f32[1,17424]{1,0:T(1,128)} %fwd_ref.5, f32[1,17424]{1,0:T(1,128)} %adj_ref.5, f32[144,128]{1,0:T(8,128)} %copy-done.4, f32[144,128]{1,0:T(8,128)} %copy-done.5, f32[1000,128]{1,0:T(8,128)} %flux.1.flux_in_ref, ...), custom_call_target="tpu_custom_call" | custom-call | flops 400000000 | bytes 4000000 | tf_op jit(solution)/shard_map/kernel_term/pallas_call | solution.py:461
  18.4 1.7 %collective-permute-start.2 = (f32[16,1152]{1,0:T(8,128)}, f32[16,1152]{1,0:T(8,128)S(1)}, u32[]{:S(2)}, u32[]{:S(2)}) collective-permute-start(f32[16,1152]{1,0:T(8,128)} %get-tuple-element.18), channel_id=1, source_target_pairs={{0,16},{16,0},{1,17},{17,1},{2,18},{18,2},{3,19},{19,3},{4,20},{20... | collective-permute-start | bytes 221192 | tf_op jit(solution)/shard_map/ppermute | solution.py:482
  20.1 3.2 %collective-permute-done.2 = f32[16,1152]{1,0:T(8,128)S(1)} collective-permute-done((f32[16,1152]{1,0:T(8,128)}, f32[16,1152]{1,0:T(8,128)S(1)}, u32[]{:S(2)}, u32[]{:S(2)}) %collective-permute-start.2) | collective-permute-done | bytes 73760 | tf_op jit(solution)/shard_map/ppermute | solution.py:482
  23.3 0.9 %add.8.after_ref.own_ref = f32[16,1152]{1,0:T(8,128)S(1)} add(f32[16,1152]{1,0:T(8,128)} %get-tuple-element.18, f32[16,1152]{1,0:T(8,128)S(1)} %collective-permute-done.2) | non-fusion elementwise | flops 18432 | bytes 221184 | tf_op jit(solution)/shard_map/add | solution.py:482
  24.2 2.8 %collective-permute-start.3 = (f32[16,1152]{1,0:T(8,128)S(1)}, f32[16,1152]{1,0:T(8,128)S(1)}, u32[]{:S(2)}, u32[]{:S(2)}) collective-permute-start(f32[16,1152]{1,0:T(8,128)S(1)} %add.8.after_ref.own_ref), channel_id=1, source_target_pairs={{0,15},{1,2},{2,1},{3,4},{4,3},{5,6},{6,5},{7,8},{8,7},{9,10},{10,... | collective-permute-start | bytes 221192 | tf_op jit(solution)/shard_map/ppermute | solution.py:485
  27.0 0.0 collective-permute-start.4
  27.0 0.0 copy-done.3
  27.0 0.7 %broadcast_in_dim.3.mass_ref = f32[1,17424]{1,0:T(1,128)} reshape(f32[17424]{0:T(1024)S(1)} %copy-done.3) | data formatting | bytes 139392 | tf_op jit(solution)/shard_map/broadcast_in_dim | solution.py:509
  27.7 0.0 copy-done
  27.7 3.3 %forces.1 = (f32[1,17424]{1,0:T(1,128)}, f32[1,17424]{1,0:T(1,128)}, f32[1,17424]{1,0:T(1,128)}, f32[1,17424]{1,0:T(1,128)}) custom-call(f32[200,640]{1,0:T(8,128)} %get-tuple-element.16.elem_ref, f32[1000,128]{1,0:T(8,128)} %get-tuple-element.17.flux_ref, f32[1,17424]{1,0:T(1,128)} %fwd_ref.5, f32[1,17424]{1,0:T(1,128)} %fwd_speed_ref.1, ...), custom_call_target="tpu_custom_call" | custom-call | flops 400000000 | bytes 4000000 | tf_op jit(solution)/shard_map/forces/pallas_call | solution.py:489
  31.0 0.0 collective-permute-done.3.first_ref
  31.0 0.0 collective-permute-done.4.second_ref
  31.0 0.6 %copy-done.1 = f32[16,1152]{1,0:T(8,128)} copy-done((f32[16,1152]{1,0:T(8,128)}, f32[16,1152]{1,0:T(8,128)S(1)}, u32[]{:S(2)}) %copy-start.1) | copy-done | bytes 73752
  31.6 0.6 %copy-done.2 = f32[16,1152]{1,0:T(8,128)} copy-done((f32[16,1152]{1,0:T(8,128)}, f32[16,1152]{1,0:T(8,128)S(1)}, u32[]{:S(2)}) %copy-start.2) | copy-done | bytes 73752
  32.2 1.8 %band.1 = f32[16,1089]{1,0:T(8,128)} custom-call(s32[1]{0:T(128)} %bitcast.parity_ref, f32[16,1152]{1,0:T(8,128)} %copy-done, f32[16,1152]{1,0:T(8,128)} %copy-done.1, f32[16,1152]{1,0:T(8,128)} %copy-done.2, bf16[2,16,288]{2,1,0:T(8,128)(2,1)} %constant.22.clone.band_ref), custom_call_target="tpu_custom_call" | custom-call | flops 20000000 | bytes 400000 | tf_op jit(solution)/shard_map/band/pallas_call | solution.py:512
  (6 shorter events, 0.0 us)
Async XLA Ops:
  4.6 7.9 %collective-permute-start = (f32[144,128]{1,0:T(8,128)}, f32[144,128]{1,0:T(8,128)S(1)}, u32[]{:S(2)}, u32[]{:S(2)}) collective-permute-start(f32[144,128]{1,0:T(8,128)} %get-tuple-element.14), channel_id=1, source_target_pairs={{0,15},{1,2},{2,1},{3,4},{4,3},{5,6},{6,5},{7,8},{8,7},{9,10},{10,... | collective-permute-start | bytes 221192 | tf_op jit(solution)/shard_map/ppermute | solution.py:449
  10.0 2.5 %collective-permute-start.1 = (f32[144,128]{1,0:T(8,128)}, f32[144,128]{1,0:T(8,128)S(1)}, u32[]{:S(2)}, u32[]{:S(2)}) collective-permute-start(f32[144,128]{1,0:T(8,128)} %get-tuple-element.15), channel_id=1, source_target_pairs={{0,1},{1,0},{2,3},{3,2},{4,5},{5,4},{6,7},{7,6},{8,9},{9,8},{10,11... | collective-permute-start | bytes 221192 | tf_op jit(solution)/shard_map/ppermute | solution.py:450
  12.5 0.6 %copy-start.4 = (f32[144,128]{1,0:T(8,128)}, f32[144,128]{1,0:T(8,128)S(1)}, u32[]{:S(2)}) copy-start(f32[144,128]{1,0:T(8,128)S(1)} %collective-permute-done.first_ref) | copy-start | bytes 221188
  13.1 0.6 %copy-start.5 = (f32[144,128]{1,0:T(8,128)}, f32[144,128]{1,0:T(8,128)S(1)}, u32[]{:S(2)}) copy-start(f32[144,128]{1,0:T(8,128)S(1)} %collective-permute-done.1.second_ref) | copy-start | bytes 221188
  18.4 8.6 %copy-start.3 = (f32[17424]{0:T(1024)S(1)}, f32[17424]{0:T(1024)}, u32[]{:S(2)}) copy-start(f32[17424]{0:T(1024)} %param.15) | copy-start | bytes 209092
  18.4 4.9 %collective-permute-start.2 = (f32[16,1152]{1,0:T(8,128)}, f32[16,1152]{1,0:T(8,128)S(1)}, u32[]{:S(2)}, u32[]{:S(2)}) collective-permute-start(f32[16,1152]{1,0:T(8,128)} %get-tuple-element.18), channel_id=1, source_target_pairs={{0,16},{16,0},{1,17},{17,1},{2,18},{18,2},{3,19},{19,3},{4,20},{20... | collective-permute-start | bytes 221192 | tf_op jit(solution)/shard_map/ppermute | solution.py:482
  24.2 3.5 %copy-start = (f32[16,1152]{1,0:T(8,128)}, f32[16,1152]{1,0:T(8,128)S(1)}, u32[]{:S(2)}) copy-start(f32[16,1152]{1,0:T(8,128)S(1)} %add.8.after_ref.own_ref) | copy-start | bytes 221188
  24.2 6.8 %collective-permute-start.3 = (f32[16,1152]{1,0:T(8,128)S(1)}, f32[16,1152]{1,0:T(8,128)S(1)}, u32[]{:S(2)}, u32[]{:S(2)}) collective-permute-start(f32[16,1152]{1,0:T(8,128)S(1)} %add.8.after_ref.own_ref), channel_id=1, source_target_pairs={{0,15},{1,2},{2,1},{3,4},{4,3},{5,6},{6,5},{7,8},{8,7},{9,10},{10,... | collective-permute-start | bytes 221192 | tf_op jit(solution)/shard_map/ppermute | solution.py:485
  27.0 4.0 %collective-permute-start.4 = (f32[16,1152]{1,0:T(8,128)S(1)}, f32[16,1152]{1,0:T(8,128)S(1)}, u32[]{:S(2)}, u32[]{:S(2)}) collective-permute-start(f32[16,1152]{1,0:T(8,128)S(1)} %add.8.after_ref.own_ref), channel_id=1, source_target_pairs={{0,1},{1,0},{2,3},{3,2},{4,5},{5,4},{6,7},{7,6},{8,9},{9,8},{10,11... | collective-permute-start | bytes 221192 | tf_op jit(solution)/shard_map/ppermute | solution.py:486
  31.0 0.6 %copy-start.1 = (f32[16,1152]{1,0:T(8,128)}, f32[16,1152]{1,0:T(8,128)S(1)}, u32[]{:S(2)}) copy-start(f32[16,1152]{1,0:T(8,128)S(1)} %collective-permute-done.3.first_ref) | copy-start | bytes 221188
  31.6 0.6 %copy-start.2 = (f32[16,1152]{1,0:T(8,128)}, f32[16,1152]{1,0:T(8,128)S(1)}, u32[]{:S(2)}) copy-start(f32[16,1152]{1,0:T(8,128)S(1)} %collective-permute-done.4.second_ref) | copy-start | bytes 221188

commit v3 on v2

--- a/solution.py
+++ b/solution.py
@@ -125,15 +125,32 @@
     return dot_nt(hi, pick) + (dot_nt(mid, pick) + dot_nt(low, pick))
 
 
-def pack_kernel(parity_ref, count_ref, conn_ref, shear_ref, fwd_ref, adj_ref, first_ref, second_ref, line_ref):
+def fetch(sem, *pairs):
+    copies = [pltpu.make_async_copy(src, dst, sem.at[n]) for n, (src, dst) in enumerate(pairs)]
+    for c in copies:
+        c.start()
+    return copies
+
+
+def pack_kernel(
+    parity_ref, count_ref, conn_hbm, shear_hbm, fwd_hbm, adj_hbm,
+    first_ref, second_ref,
+    conn_ref, shear_ref, fwd_ref, adj_ref, line_ref, sem,
+):
+    copies = fetch(
+        sem, (conn_hbm.at[0:8], conn_ref), (shear_hbm, shear_ref), (fwd_hbm, fwd_ref), (adj_hbm, adj_ref)
+    )
+    copies[0].wait()
     code = slot_elements(conn_ref, count_ref)
     lane = lax.broadcasted_iota(jnp.int32, (LANES, 256), 0) & 63
     pick = jnp.where(code == (lane >> 3) * 32 + (lane & 7) * 4 + 3, 1.0, 0.0).astype(BF16)
+    copies[1].wait()
     flux = moved_by(weighted(shear_ref), pick)
     flux = jnp.concatenate([flux, jnp.zeros((3, LANES), F32)], axis=0)
     low = lax.broadcasted_iota(jnp.int32, (64, LANES), 1) < 64
     flux = jnp.where(low, flux[0:64], flux[64:128])
     for f, ref in enumerate((fwd_ref, adj_ref)):
+        copies[2 + f].wait()
         for r in (0, 8, 16, 24, 32):
             line_ref[f, r : r + 8, :] = ref[0:1, r * LANES : (r + 8) * LANES].reshape(8, LANES)
         base = 102 * LANES
@@ -151,7 +168,9 @@
         ref[80:144, :] = flux
 
 
-def flux_kernel(count_ref, conn_ref, shear_ref, flux_ref):
+def flux_kernel(count_ref, conn_hbm, shear_hbm, flux_ref, conn_ref, shear_ref, sem):
+    copies = fetch(sem, (conn_hbm.at[0:8], conn_ref), (shear_hbm, shear_ref))
+    copies[0].wait()
     code = slot_elements(conn_ref, count_ref)
     lane = lax.broadcasted_iota(jnp.int32, (LANES, 256), 0)
     layer = lane >> 3
@@ -159,6 +178,7 @@
     member = jnp.where((layer >= 0) & (layer < 4), (lane & 7) * 4 + layer, -1)
     member = jnp.where(member >= 0, member, 5000)
     pick = jnp.concatenate([jnp.where(code - member == ez * 32, 1.0, 0.0).astype(BF16) for ez in range(EZ)], axis=0)
+    copies[1].wait()
     moved = moved_by(weighted(shear_ref), pick)
     for ez in range(EZ):
         flux_ref[pl.ds(ez, 125, stride=8), :] = moved[:, ez * LANES : (ez + 1) * LANES]
@@ -245,13 +265,15 @@
 
 
 def kernel_kernel(
-    parity_ref, fwd_ref, adj_ref, first_ref, second_ref, flux_in_ref, cross_ref,
+    parity_ref, fwd_hbm, adj_hbm, first_ref, second_ref, flux_in_ref, cross_hbm,
     kern_out_ref, elem_ref, flux_ref,
-    own_ref, near_ref, plane_ref, win0_ref, win1_ref, kern_ref,
+    fwd_ref, adj_ref, cross_ref, own_ref, near_ref, plane_ref, win0_ref, win1_ref, kern_ref, sem,
 ):
+    copies = fetch(sem, (fwd_hbm, fwd_ref), (adj_hbm, adj_ref), (cross_hbm, cross_ref))
     lane = lax.broadcasted_iota(jnp.int32, (8, LANES), 1)
     even = parity_ref[0] == 0
     for f, ref in enumerate((fwd_ref, adj_ref)):
+        copies[f].wait()
         for r in range(0, 136, 8):
             own_ref[ROWS * f + r : ROWS * f + r + 8, :] = ref[0:1, r * LANES : (r + 8) * LANES].reshape(8, LANES)
         own_ref[ROWS * f + 136 : ROWS * f + 144, :] = jnp.zeros((8, LANES), F32)
@@ -328,6 +350,7 @@
             jnp.concatenate([jnp.where(inner, kern[i][t], pltpu.roll(kern[i + 1][t], 4, 0)) for i in (0, 2)], axis=0)
         )
     lane16 = lax.broadcasted_iota(jnp.int32, (16, LANES), 1)
+    copies[2].wait()
     for base, step in ((0, 1), (9, PZ)):
         total = None
         for tap in range(9):
@@ -354,11 +377,7 @@
     return tiles
 
 
-def force_kernel(
-    elem_ref, flux_ref, fwd_ref, fwd_speed_ref, adj_ref, adj_speed_ref, mass_ref, after_ref,
-    fwd_out_ref, fwd_speed_out_ref, adj_out_ref, adj_speed_out_ref,
-    term_ref, win0_ref, win1_ref, plane_ref, line_ref,
-):
+def force_kernel(elem_ref, flux_ref, win0_ref, win1_ref, term_ref):
     for axis, line in lines():
         grads = derive([at(elem_ref, *c) for c in line])
         back = derive_back([g * flux_at(flux_ref, *c) for g, c in zip(grads, line)])
@@ -369,6 +388,21 @@
     back = dot_tn(hi, select) + (dot_tn(mid, select) + dot_tn(low, select))
     win0_ref[...] = back[:, :LANES]
     win1_ref[...] = back[:, LANES:]
+
+
+def step_kernel(
+    win0_ref, win1_ref, fwd_hbm, fwd_speed_hbm, adj_hbm, adj_speed_hbm, mass_hbm, after_ref,
+    fwd_out_ref, fwd_speed_out_ref, adj_out_ref, adj_speed_out_ref,
+    fwd_ref, fwd_speed_ref, adj_ref, adj_speed_ref, mass_ref, plane_ref, line_ref, sem,
+):
+    copies = fetch(
+        sem,
+        (fwd_hbm, fwd_ref),
+        (fwd_speed_hbm, fwd_speed_ref),
+        (adj_hbm, adj_ref),
+        (adj_speed_hbm, adj_speed_ref),
+        (mass_hbm, mass_ref),
+    )
     lane9 = lax.broadcasted_iota(jnp.int32, (9, LANES), 1)
     for i in range(NGLL):
         for h in range(2):
@@ -392,7 +426,7 @@
     def step(lo, hi, force):
         shape = (hi - lo) // force[0].shape[1], force[0].shape[1]
         take = lambda ref: ref[0:1, lo:hi].reshape(shape)
-        scale = TIME_STEP * mass_ref[0:1, lo:hi].reshape(shape)
+        scale = TIME_STEP * mass_ref[lo:hi].reshape(shape)
         speed = take(fwd_speed_ref) + scale * force[0]
         fwd_speed_out_ref[0:1, lo:hi] = speed.reshape(1, hi - lo)
         fwd_out_ref[0:1, lo:hi] = (take(fwd_ref) - TIME_STEP * speed).reshape(1, hi - lo)
@@ -400,6 +434,8 @@
         adj_speed_out_ref[0:1, lo:hi] = speed.reshape(1, hi - lo)
         adj_out_ref[0:1, lo:hi] = (take(adj_ref) + TIME_STEP * speed).reshape(1, hi - lo)
 
+    for c in copies:
+        c.wait()
     for r in range(0, 136, 8):
         step(r * LANES, (r + 8) * LANES, [line_ref[f, r : r + 8, :] for f in range(2)])
     step(NPTS - 16, NPTS, [line_ref[f, 136:137, 0:16] for f in range(2)])
@@ -436,47 +472,74 @@
     vmem = pl.BlockSpec(memory_space=pltpu.VMEM)
     smem = pl.BlockSpec(memory_space=pltpu.SMEM)
     anywhere = pl.BlockSpec(memory_space=pl.ANY)
-    message = jax.ShapeDtypeStruct((144, LANES), F32)
-    conn = connectivity[0:8]
+
+    def held(block):
+        return pltpu.with_memory_space_constraint(block, pltpu.VMEM)
+
+    def in_hbm(block):
+        return pltpu.with_memory_space_constraint(block, pltpu.HBM)
+
+    def cost(flops):
+        return pl.CostEstimate(flops=flops, bytes_accessed=1000000, transcendentals=0)
+
+    dma = pltpu.SemaphoreType.DMA
+    point_row = pltpu.VMEM((1, NPTS), F32)
+    conn_rows = pltpu.VMEM((8, 256), jnp.int32)
+    shear_block = pltpu.VMEM((125, 256), F32)
+    elem_block = pltpu.VMEM((200, 5 * LANES), F32)
+    flux_block = pltpu.VMEM((1000, LANES), F32)
+    window = pltpu.VMEM((5 * LANES, LANES), F32)
+    message = pltpu.VMEM((144, LANES), F32)
+    fields = (in_hbm(forward_displacement), in_hbm(adjoint_displacement))
+    conn, shear = in_hbm(connectivity), in_hbm(shear_modulus)
     first, second = pl.pallas_call(
         pack_kernel,
         out_shape=[message, message],
-        in_specs=[smem, smem, vmem, vmem, vmem, vmem],
-        scratch_shapes=[pltpu.VMEM((2, 80, LANES), F32)],
-        cost_estimate=pl.CostEstimate(flops=100000000, bytes_accessed=1000000, transcendentals=0),
+        in_specs=[smem, smem] + [anywhere] * 4,
+        scratch_shapes=[conn_rows, shear_block, point_row, point_row, pltpu.VMEM((2, 80, LANES), F32), dma((4,))],
+        cost_estimate=cost(100000000),
         name="pack",
-    )(parity, element_count, conn, shear_modulus, forward_displacement, adjoint_displacement)
+    )(parity, element_count, conn, shear, *fields)
     first = lax.ppermute(first, "cuts", pairs_first)
     second = lax.ppermute(second, "cuts", pairs_second)
 
     flux = pl.pallas_call(
         flux_kernel,
-        out_shape=jax.ShapeDtypeStruct((1000, LANES), F32),
-        in_specs=[smem, vmem, vmem],
-        cost_estimate=pl.CostEstimate(flops=200000000, bytes_accessed=2000000, transcendentals=0),
+        out_shape=flux_block,
+        in_specs=[smem] + [anywhere] * 2,
+        scratch_shapes=[conn_rows, shear_block, dma((2,))],
+        cost_estimate=cost(200000000),
         name="flux",
-    )(element_count, conn, shear_modulus)
-
-    elem_shape = (200, 5 * LANES)
+    )(element_count, conn, shear)
+
     kern, elem, flux = pl.pallas_call(
         kernel_kernel,
-        out_shape=[
-            jax.ShapeDtypeStruct((16, 9 * LANES), F32),
-            jax.ShapeDtypeStruct(elem_shape, F32),
-            jax.ShapeDtypeStruct((1000, LANES), F32),
-        ],
-        in_specs=[smem] + [vmem] * 6,
+        out_shape=[pltpu.VMEM((16, 9 * LANES), F32), elem_block, flux_block],
+        in_specs=[smem, anywhere, anywhere, vmem, vmem, vmem, anywhere],
         scratch_shapes=[
+            point_row,
+            point_row,
+            pltpu.VMEM((24, 9 * LANES), F32),
             pltpu.VMEM((2 * ROWS, LANES), F32),
             pltpu.VMEM((224, LANES), F32),
             pltpu.VMEM((5 * 144, LANES), F32),
-            pltpu.VMEM((5 * LANES, LANES), F32),
-            pltpu.VMEM((5 * LANES, LANES), F32),
-            pltpu.VMEM(elem_shape, F32),
+            window,
+            window,
+            elem_block,
+            dma((3,)),
         ],
-        cost_estimate=pl.CostEstimate(flops=400000000, bytes_accessed=4000000, transcendentals=0),
+        cost_estimate=cost(400000000),
         name="kernel_term",
-    )(parity, forward_displacement, adjoint_displacement, first, second, flux, jnp.asarray(cross_table()))
+    )(parity, *fields, held(first), held(second), held(flux), in_hbm(jnp.asarray(cross_table())))
+
+    win0, win1 = pl.pallas_call(
+        force_kernel,
+        out_shape=[window, window],
+        in_specs=[vmem, vmem],
+        scratch_shapes=[elem_block],
+        cost_estimate=cost(200000000),
+        name="forces",
+    )(held(elem), held(flux))
 
     if events == 2:
         kern = kern + lax.ppermute(kern, "event", [(0, 1), (1, 0)])
@@ -487,35 +550,30 @@
 
     points = jax.ShapeDtypeStruct((1, NPTS), F32)
     outs = pl.pallas_call(
-        force_kernel,
+        step_kernel,
         out_shape=[points] * 4,
-        in_specs=[vmem] * 7 + [anywhere],
-        scratch_shapes=[
-            pltpu.VMEM(elem_shape, F32),
-            pltpu.VMEM((5 * LANES, LANES), F32),
-            pltpu.VMEM((5 * LANES, LANES), F32),
-            pltpu.VMEM((5 * 144, LANES), F32),
-            pltpu.VMEM((2, ROWS, LANES), F32),
-        ],
-        cost_estimate=pl.CostEstimate(flops=400000000, bytes_accessed=4000000, transcendentals=0),
-        name="forces",
+        in_specs=[vmem] * 2 + [anywhere] * 5 + [vmem],
+        scratch_shapes=[point_row] * 4
+        + [pltpu.VMEM((NPTS,), F32), pltpu.VMEM((5 * 144, LANES), F32), pltpu.VMEM((2, ROWS, LANES), F32), dma((5,))],
+        cost_estimate=cost(200000000),
+        name="step",
     )(
-        elem,
-        flux,
-        forward_displacement,
-        forward_velocity,
-        adjoint_displacement,
-        adjoint_velocity,
-        inverse_mass[None, :],
-        kern,
+        held(win0),
+        held(win1),
+        fields[0],
+        in_hbm(forward_velocity),
+        fields[1],
+        in_hbm(adjoint_velocity),
+        in_hbm(inverse_mass),
+        held(kern),
     )
     shear_kernel = pl.pallas_call(
         band_kernel,
         out_shape=jax.ShapeDtypeStruct((PXU, PYZ), F32),
         in_specs=[smem] + [vmem] * 4,
-        cost_estimate=pl.CostEstimate(flops=20000000, bytes_accessed=400000, transcendentals=0),
+        cost_estimate=cost(20000000),
         name="band",
-    )(parity, kern, kern_first, kern_second, jnp.asarray(band_table()))
+    )(parity, held(kern), held(kern_first), held(kern_second), held(jnp.asarray(band_table())))
     return (*outs, shear_kernel)
 
 

time: 34.4 us -> 25.9 us (0.75)
  local copies, waits for them, and re-layouts: 4.5 us -> 0.01 us
  Pallas kernels: 14.1 us -> 10.4 us
  starting transfers between devices: 9.98 us -> 10.9 us
  other arithmetic: 0.9 us -> 0.01 us
    unnamed x12 -> x2, local copies, waits for them, and re-layouts: 2.53 us -> 0.01 us
    pallas_call x3 -> x4, Pallas kernels: 10.4 us -> 8.28 us  [the longest x1 3.51 us: on_device(): pl.pallas_call(kernel_kernel, out_shape=[pltpu.VMEM((16, 9 * LANES), F32)...]
    slice x1 -> x0, local copies, waits for them, and re-layouts: 1.3 us -> none  [on_device(): conn = connectivity[0:8]]
    pallas_call x1, Pallas kernels: 1.8 us -> 0.85 us  [on_device(): pl.pallas_call(band_kernel, out_shape=jax.ShapeDtypeStruct((PXU, PYZ), F3...]
    add x1, other arithmetic: 0.9 us -> 0.01 us  [on_device(): kern = kern + lax.ppermute(kern, 'event', [(0, 1), (1, 0)])]
    ppermute x1, waiting for transfers between devices: 3.18 us -> 2.43 us  [on_device(): kern = kern + lax.ppermute(kern, 'event', [(0, 1), (1, 0)])]
    broadcast_in_dim x1 -> x0, local copies, waits for them, and re-layouts: 0.68 us -> none  [on_device(): inverse_mass[None, :]]
    pallas_call x1, Pallas kernels: 1.97 us -> 1.31 us  [on_device(): pl.pallas_call(pack_kernel, out_shape=[message, message], in_specs=[smem,...]
  transfers between devices with their start and end apart: 5 -> 5, of which waited for: 1 -> 2; matrix products, arithmetic and copies ran while one was open for 2% -> 0% of each run, Pallas kernels for 17% -> 19%
where the time goes in v3:
time: 25.9 us; the launch traced here: 25.6 us
  starting transfers between devices  10.9 us (42%)
  Pallas kernels  10.4 us (40%)
  waiting for transfers between devices  2.85 us (11%)
  between operations  1.37 us (5%)
    ppermute x1, starting transfers between devices, on_device(): first = lax.ppermute(first, 'cuts', pairs_first)  5.51 us
    pallas_call x1, Pallas kernels, on_device(): pl.pallas_call(kernel_kernel, out_shape=[pltpu.VMEM((16, 9 * LANES), F32)...  3.51 us
    ppermute x1, starting transfers between devices, on_device(): kern_first = lax.ppermute(kern, 'cuts', pairs_first)  3.35 us
    ppermute x1, waiting for transfers between devices, on_device(): kern = kern + lax.ppermute(kern, 'event', [(0, 1), (1, 0)])  2.43 us
    pallas_call x1, Pallas kernels, on_device(): pl.pallas_call(step_kernel, out_shape=[points] * 4, in_specs=[vmem] * 2 +...  2.07 us
    ppermute x1, starting transfers between devices, on_device(): kern = kern + lax.ppermute(kern, 'event', [(0, 1), (1, 0)])  1.99 us
    pallas_call x1, Pallas kernels, on_device(): pl.pallas_call(flux_kernel, out_shape=flux_block, in_specs=[smem] + [anyw...  1.61 us
    pallas_call x1, Pallas kernels, on_device(): pl.pallas_call(pack_kernel, out_shape=[message, message], in_specs=[smem,...  1.31 us
  transfers between devices with their start and end apart: 5, of which 2 were waited for; matrix products, arithmetic and copies ran while one was open for 0% of the time, Pallas kernels for 19%

profile of v3, /device:TPU:0, one launch (start us, length us, event | category | flops | bytes accessed | tf_op | source)
XLA Modules:
  0.0 25.6 jit_solution(5631884901578777585)
XLA Ops:
  1.3 1.3 %pack.1 = (f32[144,128]{1,0:T(8,128)S(1)}, f32[144,128]{1,0:T(8,128)S(1)}) custom-call(s32[1]{0:T(128)} %bitcast.parity_ref, s32[1]{0:T(128)S(6)} %copy.15.count_ref, s32[125,256]{1,0:T(8,128)} %conn_hbm.3, f32[125,256]{1,0:T(8,128)} %shear_hbm.3, f32[1,17424]{1,0:T(1,128)} %fwd_hbm.5, f32[1,17424]{1,0:T(1,128)} %adj_hbm.5), custom_call_target="tpu_custom_call" | custom-call | flops 100000000 | bytes 1000000 | tf_op jit(solution)/shard_map/pack/pallas_call | solution.py:495
  2.6 5.5 %collective-permute-start = (f32[144,128]{1,0:T(8,128)S(1)}, f32[144,128]{1,0:T(8,128)S(1)}, u32[]{:S(2)}, u32[]{:S(2)}) collective-permute-start(f32[144,128]{1,0:T(8,128)S(1)} %get-tuple-element.16), channel_id=1, source_target_pairs={{0,15},{1,2},{2,1},{3,4},{4,3},{5,6},{6,5},{7,8},{8,7},{9,10},{10,... | collective-permute-start | bytes 221192 | tf_op jit(solution)/shard_map/ppermute | solution.py:503
  8.1 0.0 collective-permute-start.1
  8.1 1.6 %flux.1.flux_in_ref = f32[1000,128]{1,0:T(8,128)S(1)} custom-call(s32[1]{0:T(128)S(6)} %copy.15.count_ref, s32[125,256]{1,0:T(8,128)} %conn_hbm.3, f32[125,256]{1,0:T(8,128)} %shear_hbm.3), custom_call_target="tpu_custom_call" | custom-call | flops 200000000 | bytes 1000000 | tf_op jit(solution)/shard_map/flux/pallas_call | solution.py:506
  9.7 0.4 %collective-permute-done.first_ref = f32[144,128]{1,0:T(8,128)S(1)} collective-permute-done((f32[144,128]{1,0:T(8,128)S(1)}, f32[144,128]{1,0:T(8,128)S(1)}, u32[]{:S(2)}, u32[]{:S(2)}) %collective-permute-start) | collective-permute-done | bytes 73760 | tf_op jit(solution)/shard_map/ppermute | solution.py:503
  10.2 0.0 collective-permute-done.1.second_ref
  10.2 3.5 %kernel_term.1 = (f32[16,1152]{1,0:T(8,128)S(1)}, f32[200,640]{1,0:T(8,128)S(1)}, f32[1000,128]{1,0:T(8,128)S(1)}) custom-call(s32[1]{0:T(128)} %bitcast.parity_ref, f32[1,17424]{1,0:T(1,128)} %fwd_hbm.5, f32[1,17424]{1,0:T(1,128)} %adj_hbm.5, f32[144,128]{1,0:T(8,128)S(1)} %collective-permute-done.first_ref, ...), custom_call_target="tpu_custom_call" | custom-call | flops 400000000 | bytes 1000000 | tf_op jit(solution)/shard_map/kernel_term/pallas_call | solution.py:515
  13.7 2.0 %collective-permute-start.2 = (f32[16,1152]{1,0:T(8,128)S(1)}, f32[16,1152]{1,0:T(8,128)S(1)}, u32[]{:S(2)}, u32[]{:S(2)}) collective-permute-start(f32[16,1152]{1,0:T(8,128)S(1)} %get-tuple-element.22), channel_id=1, source_target_pairs={{0,16},{16,0},{1,17},{17,1},{2,18},{18,2},{3,19},{19,3},{4,20},{20... | collective-permute-start | bytes 221192 | tf_op jit(solution)/shard_map/ppermute | solution.py:545
  15.7 2.4 %collective-permute-done.2 = f32[16,1152]{1,0:T(8,128)S(1)} collective-permute-done((f32[16,1152]{1,0:T(8,128)S(1)}, f32[16,1152]{1,0:T(8,128)S(1)}, u32[]{:S(2)}, u32[]{:S(2)}) %collective-permute-start.2) | collective-permute-done | bytes 73760 | tf_op jit(solution)/shard_map/ppermute | solution.py:545
  18.1 0.1 collective-permute-start.4
  18.2 3.4 %collective-permute-start.3 = (f32[16,1152]{1,0:T(8,128)S(1)}, f32[16,1152]{1,0:T(8,128)S(1)}, u32[]{:S(2)}, u32[]{:S(2)}) collective-permute-start(f32[16,1152]{1,0:T(8,128)S(1)} %add.8.after_ref.own_ref), channel_id=1, source_target_pairs={{0,15},{1,2},{2,1},{3,4},{4,3},{5,6},{6,5},{7,8},{8,7},{9,10},{10,... | collective-permute-start | bytes 221192 | tf_op jit(solution)/shard_map/ppermute | solution.py:548
  21.5 1.1 %forces.1 = (f32[640,128]{1,0:T(8,128)S(1)}, f32[640,128]{1,0:T(8,128)S(1)}) custom-call(f32[200,640]{1,0:T(8,128)S(1)} %get-tuple-element.18.elem_ref, f32[1000,128]{1,0:T(8,128)S(1)} %get-tuple-element.19.flux_ref), custom_call_target="tpu_custom_call" | custom-call | flops 200000000 | bytes 1000000 | tf_op jit(solution)/shard_map/forces/pallas_call | solution.py:535
  22.6 0.0 copy-start
  22.7 2.1 %step.1 = (f32[1,17424]{1,0:T(1,128)}, f32[1,17424]{1,0:T(1,128)}, f32[1,17424]{1,0:T(1,128)}, f32[1,17424]{1,0:T(1,128)}) custom-call(f32[640,128]{1,0:T(8,128)S(1)} %get-tuple-element.20.win0_ref, f32[640,128]{1,0:T(8,128)S(1)} %get-tuple-element.21.win1_ref, f32[1,17424]{1,0:T(1,128)} %fwd_hbm.5, f32[1,17424]{1,0:T(1,128)} %fwd_speed_hbm.1, ...), custom_call_target="tpu_custom_call" | custom-call | flops 200000000 | bytes 1000000 | tf_op jit(solution)/shard_map/step/pallas_call | solution.py:552
  24.7 0.0 collective-permute-done.4.second_ref
  24.7 0.0 collective-permute-done.3.first_ref
  24.8 0.0 copy-done
  24.8 0.8 %band.1 = f32[16,1089]{1,0:T(8,128)} custom-call(s32[1]{0:T(128)} %bitcast.parity_ref, f32[16,1152]{1,0:T(8,128)S(1)} %add.8.after_ref.own_ref, f32[16,1152]{1,0:T(8,128)S(1)} %collective-permute-done.3.first_ref, f32[16,1152]{1,0:T(8,128)S(1)} %collective-permute-done.4.second_ref, bf16[2,16,288]{2,1,0:T(8,128)(2,1)S(1)} %copy-done), custom_call_target="tpu_custom_call" | custom-call | flops 20000000 | bytes 1000000 | tf_op jit(solution)/shard_map/band/pallas_call | solution.py:570
  (1 shorter events, 0.0 us)
Async XLA Ops:
  2.6 7.6 %collective-permute-start = (f32[144,128]{1,0:T(8,128)S(1)}, f32[144,128]{1,0:T(8,128)S(1)}, u32[]{:S(2)}, u32[]{:S(2)}) collective-permute-start(f32[144,128]{1,0:T(8,128)S(1)} %get-tuple-element.16), channel_id=1, source_target_pairs={{0,15},{1,2},{2,1},{3,4},{4,3},{5,6},{6,5},{7,8},{8,7},{9,10},{10,... | collective-permute-start | bytes 221192 | tf_op jit(solution)/shard_map/ppermute | solution.py:503
  8.1 2.0 %collective-permute-start.1 = (f32[144,128]{1,0:T(8,128)S(1)}, f32[144,128]{1,0:T(8,128)S(1)}, u32[]{:S(2)}, u32[]{:S(2)}) collective-permute-start(f32[144,128]{1,0:T(8,128)S(1)} %get-tuple-element.17), channel_id=1, source_target_pairs={{0,1},{1,0},{2,3},{3,2},{4,5},{5,4},{6,7},{7,6},{8,9},{9,8},{10,11... | collective-permute-start | bytes 221192 | tf_op jit(solution)/shard_map/ppermute | solution.py:504
  13.7 4.4 %collective-permute-start.2 = (f32[16,1152]{1,0:T(8,128)S(1)}, f32[16,1152]{1,0:T(8,128)S(1)}, u32[]{:S(2)}, u32[]{:S(2)}) collective-permute-start(f32[16,1152]{1,0:T(8,128)S(1)} %get-tuple-element.22), channel_id=1, source_target_pairs={{0,16},{16,0},{1,17},{17,1},{2,18},{18,2},{3,19},{19,3},{4,20},{20... | collective-permute-start | bytes 221192 | tf_op jit(solution)/shard_map/ppermute | solution.py:545
  18.1 6.6 %collective-permute-start.4 = (f32[16,1152]{1,0:T(8,128)S(1)}, f32[16,1152]{1,0:T(8,128)S(1)}, u32[]{:S(2)}, u32[]{:S(2)}) collective-permute-start(f32[16,1152]{1,0:T(8,128)S(1)} %add.8.after_ref.own_ref), channel_id=1, source_target_pairs={{0,1},{1,0},{2,3},{3,2},{4,5},{5,4},{6,7},{7,6},{8,9},{9,8},{10,11... | collective-permute-start | bytes 221192 | tf_op jit(solution)/shard_map/ppermute | solution.py:549
  18.2 6.6 %collective-permute-start.3 = (f32[16,1152]{1,0:T(8,128)S(1)}, f32[16,1152]{1,0:T(8,128)S(1)}, u32[]{:S(2)}, u32[]{:S(2)}) collective-permute-start(f32[16,1152]{1,0:T(8,128)S(1)} %add.8.after_ref.own_ref), channel_id=1, source_target_pairs={{0,15},{1,2},{2,1},{3,4},{4,3},{5,6},{6,5},{7,8},{8,7},{9,10},{10,... | collective-permute-start | bytes 221192 | tf_op jit(solution)/shard_map/ppermute | solution.py:548
  22.6 2.1 %copy-start = (bf16[2,16,288]{2,1,0:T(8,128)(2,1)S(1)}, bf16[2,16,288]{2,1,0:T(8,128)(2,1)}, u32[]{:S(2)}) copy-start(bf16[2,16,288]{2,1,0:T(8,128)(2,1)} %constant.22.clone.band_ref) | copy-start | bytes 55300

commit v4 on v3

--- a/solution.py
+++ b/solution.py
@@ -133,9 +133,9 @@
 
 
 def pack_kernel(
-    parity_ref, count_ref, conn_hbm, shear_hbm, fwd_hbm, adj_hbm,
-    first_ref, second_ref,
-    conn_ref, shear_ref, fwd_ref, adj_ref, line_ref, sem,
+    count_ref, conn_hbm, shear_hbm, fwd_hbm, adj_hbm,
+    right_ref, left_ref,
+    conn_ref, shear_ref, fwd_ref, adj_ref, sem,
 ):
     copies = fetch(
         sem, (conn_hbm.at[0:8], conn_ref), (shear_hbm, shear_ref), (fwd_hbm, fwd_ref), (adj_hbm, adj_ref)
@@ -148,24 +148,18 @@
     flux = moved_by(weighted(shear_ref), pick)
     flux = jnp.concatenate([flux, jnp.zeros((3, LANES), F32)], axis=0)
     low = lax.broadcasted_iota(jnp.int32, (64, LANES), 1) < 64
-    flux = jnp.where(low, flux[0:64], flux[64:128])
+    right_ref[80:144, :] = jnp.where(low, flux[0:64], flux[64:128])
     for f, ref in enumerate((fwd_ref, adj_ref)):
         copies[2 + f].wait()
-        for r in (0, 8, 16, 24, 32):
-            line_ref[f, r : r + 8, :] = ref[0:1, r * LANES : (r + 8) * LANES].reshape(8, LANES)
-        base = 102 * LANES
+        left_ref[16 * f : 16 * f + 8, :] = ref[0:1, 0 : 8 * LANES].reshape(8, LANES)
+        left_ref[16 * f + 8 : 16 * f + 16, :] = ref[0:1, 8 * LANES : 16 * LANES].reshape(8, LANES)
         for r in (0, 8, 16, 24):
-            at = base + r * LANES
-            line_ref[f, 40 + r : 48 + r, :] = ref[0:1, at : at + 8 * LANES].reshape(8, LANES)
-        at = base + 32 * LANES
-        line_ref[f, 72:74, :] = ref[0:1, at : at + 2 * LANES].reshape(2, LANES)
-        line_ref[f, 74:80, :] = jnp.zeros((6, LANES), F32)
-        line_ref[f, 74:75, 0:16] = ref[0:1, at + 2 * LANES : at + 2 * LANES + 16]
-    odd = parity_ref[0] == 1
-    for ref, flip in ((first_ref, odd), (second_ref, jnp.logical_not(odd))):
-        for f in range(2):
-            ref[40 * f : 40 * f + 40, :] = jnp.where(flip, line_ref[f, 40:80, :], line_ref[f, 0:40, :])
-        ref[80:144, :] = flux
+            at = (102 + r) * LANES
+            right_ref[40 * f + r : 40 * f + r + 8, :] = ref[0:1, at : at + 8 * LANES].reshape(8, LANES)
+        at = 134 * LANES
+        right_ref[40 * f + 32 : 40 * f + 34, :] = ref[0:1, at : at + 2 * LANES].reshape(2, LANES)
+        right_ref[40 * f + 34 : 40 * f + 40, :] = jnp.zeros((6, LANES), F32)
+        right_ref[40 * f + 34 : 40 * f + 35, 0:16] = ref[0:1, NPTS - 16 : NPTS]
 
 
 def flux_kernel(count_ref, conn_hbm, shear_hbm, flux_ref, conn_ref, shear_ref, sem):
@@ -265,29 +259,25 @@
 
 
 def kernel_kernel(
-    parity_ref, fwd_hbm, adj_hbm, first_ref, second_ref, flux_in_ref, cross_hbm,
+    fwd_hbm, adj_hbm, prev_ref, next_ref, flux_in_ref, cross_hbm,
     kern_out_ref, elem_ref, flux_ref,
-    fwd_ref, adj_ref, cross_ref, own_ref, near_ref, plane_ref, win0_ref, win1_ref, kern_ref, sem,
+    fwd_ref, adj_ref, cross_ref, own_ref, plane_ref, win0_ref, win1_ref, kern_ref, sem,
 ):
     copies = fetch(sem, (fwd_hbm, fwd_ref), (adj_hbm, adj_ref), (cross_hbm, cross_ref))
     lane = lax.broadcasted_iota(jnp.int32, (8, LANES), 1)
-    even = parity_ref[0] == 0
     for f, ref in enumerate((fwd_ref, adj_ref)):
         copies[f].wait()
         for r in range(0, 136, 8):
             own_ref[ROWS * f + r : ROWS * f + r + 8, :] = ref[0:1, r * LANES : (r + 8) * LANES].reshape(8, LANES)
         own_ref[ROWS * f + 136 : ROWS * f + 144, :] = jnp.zeros((8, LANES), F32)
         own_ref[ROWS * f + 136 : ROWS * f + 137, 0:16] = ref[0:1, NPTS - 16 : NPTS]
-    near_ref[0:144, :] = jnp.where(even, first_ref[...], second_ref[...])
-    near_ref[144:224, :] = jnp.where(even, second_ref[0:80, :], first_ref[0:80, :])
-
     m = lax.broadcasted_iota(jnp.int32, (LANES, LANES), 0)
     n = lax.broadcasted_iota(jnp.int32, (LANES, LANES), 1) & 63
     layer = m >> 3
     base = jnp.where((layer == 0) | (layer == 5) | (layer == 10), n - (m & 7), -1)
     pick = jnp.concatenate([jnp.where(base == ez * 8, 1.0, 0.0).astype(BF16) for ez in range(EZ)], axis=0)
     low = lax.broadcasted_iota(jnp.int32, (64, LANES), 1) < 64
-    packed = near_ref[80:144, :]
+    packed = prev_ref[80:144, :]
     packed = jnp.concatenate([jnp.where(low, packed, 0.0), jnp.where(low, 0.0, packed)], axis=0)
     extra = moved_by(split3(packed), pick)
     for ez in range(EZ):
@@ -298,11 +288,11 @@
     for x in range(-4, PXU + 1):
         for f in range(2):
             if x < 0:
-                flat = plane_of(near_ref, 12 + PYZ * (x + 4), 40 * f)
+                flat = plane_of(prev_ref, 12 + PYZ * (x + 4), 40 * f)
             elif x < PXU:
                 flat = plane_of(own_ref, PYZ * x, ROWS * f)
             else:
-                flat = plane_of(near_ref, 0, 144 + 40 * f)
+                flat = plane_of(next_ref, 0, 16 * f)
             places = []
             if x < PXU:
                 places.append((x % 4, x // 4 + 1))
@@ -489,19 +479,19 @@
     elem_block = pltpu.VMEM((200, 5 * LANES), F32)
     flux_block = pltpu.VMEM((1000, LANES), F32)
     window = pltpu.VMEM((5 * LANES, LANES), F32)
-    message = pltpu.VMEM((144, LANES), F32)
     fields = (in_hbm(forward_displacement), in_hbm(adjoint_displacement))
     conn, shear = in_hbm(connectivity), in_hbm(shear_modulus)
-    first, second = pl.pallas_call(
+    right, left = pl.pallas_call(
         pack_kernel,
-        out_shape=[message, message],
-        in_specs=[smem, smem] + [anywhere] * 4,
-        scratch_shapes=[conn_rows, shear_block, point_row, point_row, pltpu.VMEM((2, 80, LANES), F32), dma((4,))],
+        out_shape=[pltpu.VMEM((144, LANES), F32), pltpu.VMEM((32, LANES), F32)],
+        in_specs=[smem] + [anywhere] * 4,
+        scratch_shapes=[conn_rows, shear_block, point_row, point_row, dma((4,))],
         cost_estimate=cost(100000000),
         name="pack",
-    )(parity, element_count, conn, shear, *fields)
-    first = lax.ppermute(first, "cuts", pairs_first)
-    second = lax.ppermute(second, "cuts", pairs_second)
+    )(element_count, conn, shear, *fields)
+    prev = lax.ppermute(right, "cuts", [(i, (i + 1) % cuts) for i in range(cuts)])
+    left, right = lax.optimization_barrier((left, right))
+    after = lax.ppermute(left, "cuts", [((i + 1) % cuts, i) for i in range(cuts)])
 
     flux = pl.pallas_call(
         flux_kernel,
@@ -515,13 +505,12 @@
     kern, elem, flux = pl.pallas_call(
         kernel_kernel,
         out_shape=[pltpu.VMEM((16, 9 * LANES), F32), elem_block, flux_block],
-        in_specs=[smem, anywhere, anywhere, vmem, vmem, vmem, anywhere],
+        in_specs=[anywhere, anywhere, vmem, vmem, vmem, anywhere],
         scratch_shapes=[
             point_row,
             point_row,
             pltpu.VMEM((24, 9 * LANES), F32),
             pltpu.VMEM((2 * ROWS, LANES), F32),
-            pltpu.VMEM((224, LANES), F32),
             pltpu.VMEM((5 * 144, LANES), F32),
             window,
             window,
@@ -530,7 +519,7 @@
         ],
         cost_estimate=cost(400000000),
         name="kernel_term",
-    )(parity, *fields, held(first), held(second), held(flux), in_hbm(jnp.asarray(cross_table())))
+    )(*fields, held(prev), held(after), held(flux), in_hbm(jnp.asarray(cross_table())))
 
     win0, win1 = pl.pallas_call(
         force_kernel,
@@ -542,7 +531,9 @@
     )(held(elem), held(flux))
 
     if events == 2:
-        kern = kern + lax.ppermute(kern, "event", [(0, 1), (1, 0)])
+        other = lax.ppermute(kern, "event", [(0, 1), (1, 0)])
+        other, win0, win1 = lax.optimization_barrier((other, win0, win1))
+        kern = kern + other
     elif events > 2:
         kern = lax.psum(kern, "event")
     kern_first = lax.ppermute(kern, "cuts", pairs_first)

time: 25.9 us -> 25.6 us (0.988)
  starting transfers between devices: 10.9 us -> 10.5 us
  waiting for transfers between devices: 2.85 us -> 3.22 us
    ppermute x1, waiting for transfers between devices: 0.01 us -> 1.52 us  [on_device(): kern_first = lax.ppermute(kern, 'cuts', pairs_first)]
    ppermute x3, waiting for transfers between devices: 2.85 us -> 1.69 us  [the longest x1 1.34 us: on_device(): other = lax.ppermute(kern, 'event', [(0, 1), (1, 0)])]
    ppermute x1, starting transfers between devices: 3.35 us -> 2.93 us  [on_device(): kern_first = lax.ppermute(kern, 'cuts', pairs_first)]
  transfers between devices with their start and end apart: 5 -> 5, of which waited for: 2 -> 3; matrix products, arithmetic and copies ran while one was open for 0% -> 0% of each run, Pallas kernels for 19% -> 19%
where the time goes in v4:
time: 25.6 us; the launch traced here: 25.4 us
  starting transfers between devices  10.5 us (41%)
  Pallas kernels  10.3 us (40%)
  waiting for transfers between devices  3.22 us (13%)
  between operations  1.33 us (5%)
    ppermute x1, starting transfers between devices, on_device(): lax.ppermute(left, 'cuts', [((i + 1) % cuts, i) for i in range(cuts)])  5.06 us
    pallas_call x1, Pallas kernels, on_device(): pl.pallas_call(kernel_kernel, out_shape=[pltpu.VMEM((16, 9 * LANES), F32)...  3.47 us
    ppermute x1, starting transfers between devices, on_device(): kern_first = lax.ppermute(kern, 'cuts', pairs_first)  2.93 us
    pallas_call x1, Pallas kernels, on_device(): pl.pallas_call(step_kernel, out_shape=[points] * 4, in_specs=[vmem] * 2 +...  2.07 us
    ppermute x1, starting transfers between devices, on_device(): other = lax.ppermute(kern, 'event', [(0, 1), (1, 0)])  1.99 us
    pallas_call x1, Pallas kernels, on_device(): pl.pallas_call(flux_kernel, out_shape=flux_block, in_specs=[smem] + [anyw...  1.6 us
    ppermute x1, waiting for transfers between devices, on_device(): kern_first = lax.ppermute(kern, 'cuts', pairs_first)  1.52 us
    ppermute x1, waiting for transfers between devices, on_device(): other = lax.ppermute(kern, 'event', [(0, 1), (1, 0)])  1.34 us
  transfers between devices with their start and end apart: 5, of which 3 were waited for; matrix products, arithmetic and copies ran while one was open for 0% of the time, Pallas kernels for 19%

profile of v4, /device:TPU:0, one launch (start us, length us, event | category | flops | bytes accessed | tf_op | source)
XLA Modules:
  0.0 25.4 jit_solution(8191203775092455927)
XLA Ops:
  1.3 1.3 %pack.1 = (f32[144,128]{1,0:T(8,128)S(1)}, f32[32,128]{1,0:T(8,128)S(1)}) custom-call(s32[1]{0:T(128)S(6)} %copy.15.count_ref, s32[125,256]{1,0:T(8,128)} %conn_hbm.3, f32[125,256]{1,0:T(8,128)} %shear_hbm.3, f32[1,17424]{1,0:T(1,128)} %fwd_hbm.5, f32[1,17424]{1,0:T(1,128)} %adj_hbm.5), custom_call_target="tpu_custom_call" | custom-call | flops 100000000 | bytes 1000000 | tf_op jit(solution)/shard_map/pack/pallas_call | solution.py:484
  2.5 0.5 %collective-permute-start = (f32[144,128]{1,0:T(8,128)S(1)}, f32[144,128]{1,0:T(8,128)S(1)}, u32[]{:S(2)}, u32[]{:S(2)}) collective-permute-start(f32[144,128]{1,0:T(8,128)S(1)} %get-tuple-element.20), channel_id=1, source_target_pairs={{0,1},{1,2},{2,3},{3,4},{4,5},{5,6},{6,7},{7,8},{8,9},{9,10},{10,1... | collective-permute-start | bytes 221192 | tf_op jit(solution)/shard_map/ppermute | solution.py:492
  3.0 5.1 %collective-permute-start.1 = (f32[32,128]{1,0:T(8,128)S(1)}, f32[32,128]{1,0:T(8,128)S(1)}, u32[]{:S(2)}, u32[]{:S(2)}) collective-permute-start(f32[32,128]{1,0:T(8,128)S(1)} %get-tuple-element.22), channel_id=1, source_target_pairs={{1,0},{2,1},{3,2},{4,3},{5,4},{6,5},{7,6},{8,7},{9,8},{10,9},{11,1... | collective-permute-start | bytes 49160 | tf_op jit(solution)/shard_map/ppermute | solution.py:494
  8.1 1.6 %flux.1.flux_in_ref = f32[1000,128]{1,0:T(8,128)S(1)} custom-call(s32[1]{0:T(128)S(6)} %copy.15.count_ref, s32[125,256]{1,0:T(8,128)} %conn_hbm.3, f32[125,256]{1,0:T(8,128)} %shear_hbm.3), custom_call_target="tpu_custom_call" | custom-call | flops 200000000 | bytes 1000000 | tf_op jit(solution)/shard_map/flux/pallas_call | solution.py:496
  9.7 0.0 collective-permute-done.1.next_ref
  9.7 0.3 %collective-permute-done.prev_ref = f32[144,128]{1,0:T(8,128)S(1)} collective-permute-done((f32[144,128]{1,0:T(8,128)S(1)}, f32[144,128]{1,0:T(8,128)S(1)}, u32[]{:S(2)}, u32[]{:S(2)}) %collective-permute-start) | collective-permute-done | bytes 73760 | tf_op jit(solution)/shard_map/ppermute | solution.py:492
  10.1 3.5 %kernel_term.1 = (f32[16,1152]{1,0:T(8,128)S(1)}, f32[200,640]{1,0:T(8,128)S(1)}, f32[1000,128]{1,0:T(8,128)S(1)}) custom-call(f32[1,17424]{1,0:T(1,128)} %fwd_hbm.5, f32[1,17424]{1,0:T(1,128)} %adj_hbm.5, f32[144,128]{1,0:T(8,128)S(1)} %collective-permute-done.prev_ref, f32[32,128]{1,0:T(8,128)S(1)} %collective-permute-done.1.next_ref, ...), custom_call_target="tpu_custom_call" | custom-call | flops 400000000 | bytes 1000000 | tf_op jit(solution)/shard_map/kernel_term/pallas_call | solution.py:505
  13.6 2.0 %collective-permute-start.2 = (f32[16,1152]{1,0:T(8,128)S(1)}, f32[16,1152]{1,0:T(8,128)S(1)}, u32[]{:S(2)}, u32[]{:S(2)}) collective-permute-start(f32[16,1152]{1,0:T(8,128)S(1)} %get-tuple-element.23), channel_id=1, source_target_pairs={{0,16},{16,0},{1,17},{17,1},{2,18},{18,2},{3,19},{19,3},{4,20},{20... | collective-permute-start | bytes 221192 | tf_op jit(solution)/shard_map/ppermute | solution.py:534
  15.5 1.1 %forces.1 = (f32[640,128]{1,0:T(8,128)S(1)}, f32[640,128]{1,0:T(8,128)S(1)}) custom-call(f32[200,640]{1,0:T(8,128)S(1)} %get-tuple-element.24.elem_ref, f32[1000,128]{1,0:T(8,128)S(1)} %get-tuple-element.25.flux_ref), custom_call_target="tpu_custom_call" | custom-call | flops 200000000 | bytes 1000000 | tf_op jit(solution)/shard_map/forces/pallas_call | solution.py:524
  16.6 1.3 %collective-permute-done.2 = f32[16,1152]{1,0:T(8,128)S(1)} collective-permute-done((f32[16,1152]{1,0:T(8,128)S(1)}, f32[16,1152]{1,0:T(8,128)S(1)}, u32[]{:S(2)}, u32[]{:S(2)}) %collective-permute-start.2) | collective-permute-done | bytes 73760 | tf_op jit(solution)/shard_map/ppermute | solution.py:534
  18.0 2.9 %collective-permute-start.3 = (f32[16,1152]{1,0:T(8,128)S(1)}, f32[16,1152]{1,0:T(8,128)S(1)}, u32[]{:S(2)}, u32[]{:S(2)}) collective-permute-start(f32[16,1152]{1,0:T(8,128)S(1)} %add.7.after_ref.own_ref), channel_id=1, source_target_pairs={{0,15},{1,2},{2,1},{3,4},{4,3},{5,6},{6,5},{7,8},{8,7},{9,10},{10,... | collective-permute-start | bytes 221192 | tf_op jit(solution)/shard_map/ppermute | solution.py:539
  20.9 0.0 collective-permute-start.4
  20.9 0.0 copy-start
  20.9 2.1 %step.1 = (f32[1,17424]{1,0:T(1,128)}, f32[1,17424]{1,0:T(1,128)}, f32[1,17424]{1,0:T(1,128)}, f32[1,17424]{1,0:T(1,128)}) custom-call(f32[640,128]{1,0:T(8,128)S(1)} %get-tuple-element.28.win0_ref, f32[640,128]{1,0:T(8,128)S(1)} %get-tuple-element.29.win1_ref, f32[1,17424]{1,0:T(1,128)} %fwd_hbm.5, f32[1,17424]{1,0:T(1,128)} %fwd_speed_hbm.1, ...), custom_call_target="tpu_custom_call" | custom-call | flops 200000000 | bytes 1000000 | tf_op jit(solution)/shard_map/step/pallas_call | solution.py:543
  23.0 1.5 %collective-permute-done.3.first_ref = f32[16,1152]{1,0:T(8,128)S(1)} collective-permute-done((f32[16,1152]{1,0:T(8,128)S(1)}, f32[16,1152]{1,0:T(8,128)S(1)}, u32[]{:S(2)}, u32[]{:S(2)}) %collective-permute-start.3) | collective-permute-done | bytes 73760 | tf_op jit(solution)/shard_map/ppermute | solution.py:539
  24.5 0.0 collective-permute-done.4.second_ref
  24.5 0.0 copy-done
  24.5 0.8 %band.1 = f32[16,1089]{1,0:T(8,128)} custom-call(s32[1]{0:T(128)} %bitcast.parity_ref, f32[16,1152]{1,0:T(8,128)S(1)} %add.7.after_ref.own_ref, f32[16,1152]{1,0:T(8,128)S(1)} %collective-permute-done.3.first_ref, f32[16,1152]{1,0:T(8,128)S(1)} %collective-permute-done.4.second_ref, bf16[2,16,288]{2,1,0:T(8,128)(2,1)S(1)} %copy-done), custom_call_target="tpu_custom_call" | custom-call | flops 20000000 | bytes 1000000 | tf_op jit(solution)/shard_map/band/pallas_call | solution.py:561
  (1 shorter events, 0.0 us)
Async XLA Ops:
  2.5 7.5 %collective-permute-start = (f32[144,128]{1,0:T(8,128)S(1)}, f32[144,128]{1,0:T(8,128)S(1)}, u32[]{:S(2)}, u32[]{:S(2)}) collective-permute-start(f32[144,128]{1,0:T(8,128)S(1)} %get-tuple-element.20), channel_id=1, source_target_pairs={{0,1},{1,2},{2,3},{3,4},{4,5},{5,6},{6,7},{7,8},{8,9},{9,10},{10,1... | collective-permute-start | bytes 221192 | tf_op jit(solution)/shard_map/ppermute | solution.py:492
  3.0 6.7 %collective-permute-start.1 = (f32[32,128]{1,0:T(8,128)S(1)}, f32[32,128]{1,0:T(8,128)S(1)}, u32[]{:S(2)}, u32[]{:S(2)}) collective-permute-start(f32[32,128]{1,0:T(8,128)S(1)} %get-tuple-element.22), channel_id=1, source_target_pairs={{1,0},{2,1},{3,2},{4,3},{5,4},{6,5},{7,6},{8,7},{9,8},{10,9},{11,1... | collective-permute-start | bytes 49160 | tf_op jit(solution)/shard_map/ppermute | solution.py:494
  13.6 4.4 %collective-permute-start.2 = (f32[16,1152]{1,0:T(8,128)S(1)}, f32[16,1152]{1,0:T(8,128)S(1)}, u32[]{:S(2)}, u32[]{:S(2)}) collective-permute-start(f32[16,1152]{1,0:T(8,128)S(1)} %get-tuple-element.23), channel_id=1, source_target_pairs={{0,16},{16,0},{1,17},{17,1},{2,18},{18,2},{3,19},{19,3},{4,20},{20... | collective-permute-start | bytes 221192 | tf_op jit(solution)/shard_map/ppermute | solution.py:534
  18.0 6.5 %collective-permute-start.3 = (f32[16,1152]{1,0:T(8,128)S(1)}, f32[16,1152]{1,0:T(8,128)S(1)}, u32[]{:S(2)}, u32[]{:S(2)}) collective-permute-start(f32[16,1152]{1,0:T(8,128)S(1)} %add.7.after_ref.own_ref), channel_id=1, source_target_pairs={{0,15},{1,2},{2,1},{3,4},{4,3},{5,6},{6,5},{7,8},{8,7},{9,10},{10,... | collective-permute-start | bytes 221192 | tf_op jit(solution)/shard_map/ppermute | solution.py:539
  20.9 3.6 %collective-permute-start.4 = (f32[16,1152]{1,0:T(8,128)S(1)}, f32[16,1152]{1,0:T(8,128)S(1)}, u32[]{:S(2)}, u32[]{:S(2)}) collective-permute-start(f32[16,1152]{1,0:T(8,128)S(1)} %add.7.after_ref.own_ref), channel_id=1, source_target_pairs={{0,1},{1,0},{2,3},{3,2},{4,5},{5,4},{6,7},{7,6},{8,9},{9,8},{10,11... | collective-permute-start | bytes 221192 | tf_op jit(solution)/shard_map/ppermute | solution.py:540
  20.9 3.6 %copy-start = (bf16[2,16,288]{2,1,0:T(8,128)(2,1)S(1)}, bf16[2,16,288]{2,1,0:T(8,128)(2,1)}, u32[]{:S(2)}) copy-start(bf16[2,16,288]{2,1,0:T(8,128)(2,1)} %constant.22.clone.band_ref) | copy-start | bytes 55300

commit v5 on v4

v5 whole, which is shorter than its diff:
```python
import numpy as np
import jax
import jax.numpy as jnp
import ml_dtypes
from jax import lax
from jax.experimental import pallas as pl
from jax.experimental.pallas import tpu as pltpu
from jax.sharding import PartitionSpec as P

NGLL = 5
EX, EY, EZ = 4, 8, 8
PXU = 16
PY = 33
PZ = 33
PYZ = 1089
NPTS = 17424
LANES = 128
ROWS = 144
TIME_STEP = 0.02
F32 = jnp.float32
BF16 = jnp.bfloat16


def gll():
    nodes = np.array([-1.0, -np.sqrt(3.0 / 7.0), 0.0, np.sqrt(3.0 / 7.0), 1.0])
    bary = np.array([1.0 / np.prod([nodes[r] - nodes[c] for c in range(5) if c != r]) for r in range(5)])
    d = np.zeros((5, 5))
    for r in range(5):
        for c in range(5):
            if c != r:
                d[r, c] = bary[c] / bary[r] / (nodes[r] - nodes[c])
        d[r, r] = -np.sum(d[r])
    return d


DERIV = gll()


def split_np(x):
    x = np.asarray(x, np.float32)
    parts = []
    for _ in range(3):
        p = x.astype(ml_dtypes.bfloat16)
        parts.append(p)
        x = x - p.astype(np.float32)
    return parts


ROW_PLANE = np.array([4 * (r % 3) + r // 3 for r in range(12)] + [12, 13, 14, 15])
OWN_AT = [[3 * i + m for i in range(5)] for m in range(3)]
NEAR_AT = [[1, 2, 3, 8, 0], [4, 5, 6, 7, 9]]


def band_table():
    offsets = np.arange(-PXU, PXU + 1)
    w = lambda d: np.exp(-d * d / (2.0 * (PXU / 4.0) ** 2))
    total = w(offsets.astype(np.float64)).sum()
    out = []
    for first in (-PXU, PXU):
        source = np.concatenate([ROW_PLANE, ROW_PLANE + first, ROW_PLANE - first])
        spread = np.arange(PXU)[:, None] - source[None, :]
        band = w(spread.astype(np.float64)) * (np.abs(spread) <= PXU) / total
        b1, b2, b3 = split_np(band)
        out.append(np.concatenate([b1, b1, b1, b2, b2, b3], axis=1))
    return np.stack(out)


def cross_table():
    off = np.arange(-4, 5)
    k = np.exp(-off * off / (2.0 * 1.5 * 1.5))
    point = np.arange(33)
    inside = ((point[None, :] + off[:, None]) >= 0) & ((point[None, :] + off[:, None]) < 33)
    taps = k[:, None] * inside
    taps = taps / taps.sum(axis=0, keepdims=True)
    out = np.zeros((24, 1152), np.float32)
    out[0:9, :PYZ] = np.tile(taps, (1, PY))
    out[9:18, :PYZ] = np.repeat(taps, PZ, axis=1)
    return out


def split3(x):
    hi = x.astype(BF16)
    rest = x - hi.astype(F32)
    mid = rest.astype(BF16)
    low = (rest - mid.astype(F32)).astype(BF16)
    return hi, mid, low


def dot_nt(a, b):
    return lax.dot_general(a, b, (((1,), (1,)), ((), ())), preferred_element_type=F32)


def dot_tn(a, b):
    return lax.dot_general(a, b, (((0,), (0,)), ((), ())), preferred_element_type=F32)


def selector():
    column = lax.broadcasted_iota(jnp.int32, (8, 256), 1)
    row = lax.broadcasted_iota(jnp.int32, (8, 256), 0)
    base = column - 4 * row
    blocks = [jnp.where(base == j * PZ + k, 1.0, 0.0) for j in range(5) for k in range(5)]
    return jnp.concatenate(blocks, axis=0).astype(BF16)


def fetch(sem, *pairs):
    copies = [pltpu.make_async_copy(src, dst, sem.at[n]) for n, (src, dst) in enumerate(pairs)]
    for c in copies:
        c.start()
    return copies


def add_parts(stacked):
    n = stacked.shape[0] // 3
    return stacked[0:n] + (stacked[n : 2 * n] + stacked[2 * n : 3 * n])


def pack_kernel(
    count_ref, conn_hbm, shear_hbm, fwd_hbm, adj_hbm,
    right_ref, left_ref, own_ref, code_ref, parts_ref,
    conn_ref, shear_ref, fwd_ref, adj_ref, block_ref, sem,
):
    copies = fetch(
        sem, (conn_hbm.at[0:8], conn_ref), (fwd_hbm, fwd_ref), (adj_hbm, adj_ref), (shear_hbm, shear_ref)
    )
    copies[0].wait()
    point = conn_ref[0:1, :].astype(F32)
    x = jnp.floor((point + 0.5) * (1.0 / PYZ))
    rest = point - x * PYZ
    y = jnp.floor((rest + 0.5) * (1.0 / PZ))
    z = rest - y * PZ
    code = (8.0 * z + 2.0 * x + 0.25 * y).astype(jnp.int32)
    slot = lax.broadcasted_iota(jnp.int32, (1, 256), 1)
    code = jnp.where(slot < count_ref[0], code, -1)
    code_ref[...] = jnp.broadcast_to(code, (8, 256))
    lane = lax.broadcasted_iota(jnp.int32, (LANES, 256), 0)
    pick = jnp.where(code == ((lane >> 3) & 7) * 32 + 24 + (lane & 7), 1.0, 0.0).astype(BF16)
    for f, ref in enumerate((fwd_ref, adj_ref)):
        copies[1 + f].wait()
        for r in range(0, 136, 8):
            own_ref[ROWS * f + r : ROWS * f + r + 8, :] = ref[0:1, r * LANES : (r + 8) * LANES].reshape(8, LANES)
        own_ref[ROWS * f + 136 : ROWS * f + 144, :] = jnp.zeros((8, LANES), F32)
        own_ref[ROWS * f + 136 : ROWS * f + 137, 0:16] = ref[0:1, NPTS - 16 : NPTS]
        right_ref[40 * f : 40 * f + 40, :] = own_ref[ROWS * f + 102 : ROWS * f + 142, :]
        left_ref[16 * f : 16 * f + 16, :] = own_ref[ROWS * f : ROWS * f + 16, :]
    copies[3].wait()
    block_ref[...] = jnp.zeros(block_ref.shape, F32)
    for i in range(NGLL):
        block_ref[32 * i : 32 * i + 25, :] = shear_ref[25 * i : 25 * i + 25, :]
    parts = jnp.concatenate(split3(block_ref[...]), axis=0)
    parts_ref[...] = parts
    flux = add_parts(dot_nt(parts, pick))
    low = lax.broadcasted_iota(jnp.int32, (80, LANES), 1) < 64
    right_ref[80:160, :] = jnp.where(low, flux[0:80], flux[80:160])


def gll_weight(i):
    return (0.1, 49.0 / 90.0, 32.0 / 45.0, 49.0 / 90.0, 0.1)[i]


def lane_weight(places):
    chunk = lax.broadcasted_iota(jnp.int32, (8, LANES), 1) >> 3
    weight = jnp.zeros((8, LANES), F32)
    for row in places:
        for i, place in enumerate(row):
            weight = jnp.where(chunk == place, gll_weight(i), weight)
    return weight


def scaled(ref, weight):
    for j in range(5):
        for k in range(5):
            r = (j * 5 + k) * 8
            ref[r : r + 8, :] = ref[r : r + 8, :] * (weight * (gll_weight(j) * gll_weight(k)))


def place_flux(ref, tile_of, moves):
    lane = lax.broadcasted_iota(jnp.int32, (32, LANES), 1)
    for ez in range(EZ):
        total = jnp.zeros((32, LANES), F32)
        for i in range(NGLL):
            tile, start = tile_of(i, ez)
            for source, target, width in moves(i):
                shift = (target - source - start) % LANES
                moved = pltpu.roll(tile, shift, 1) if shift else tile
                total = jnp.where((lane >= target) & (lane < target + width), moved, total)
        ref[pl.ds(ez, 25, stride=8), :] = total[0:25]


def derive(e):
    d = DERIV
    s0, s1 = e[0] + e[4], e[1] + e[3]
    d0, d1 = e[0] - e[4], e[1] - e[3]
    out = [None] * 5
    for i in (0, 1):
        even = float((d[i, 0] - d[i, 4]) / 2) * d0 + float((d[i, 1] - d[i, 3]) / 2) * d1
        odd = float((d[i, 0] + d[i, 4]) / 2) * s0 + float((d[i, 1] + d[i, 3]) / 2) * s1 + float(d[i, 2]) * e[2]
        out[i] = odd + even
        out[4 - i] = even - odd
    out[2] = float(d[2, 0]) * d0 + float(d[2, 1]) * d1
    return out


def derive_back(t):
    d = DERIV
    s0, s1 = t[0] + t[4], t[1] + t[3]
    d0, d1 = t[0] - t[4], t[1] - t[3]
    out = [None] * 5
    for i in (0, 1):
        even = float((d[0, i] - d[4, i]) / 2) * d0 + float((d[1, i] - d[3, i]) / 2) * d1
        odd = float((d[0, i] + d[4, i]) / 2) * s0 + float((d[1, i] + d[3, i]) / 2) * s1 + float(d[2, i]) * t[2]
        out[i] = odd + even
        out[4 - i] = even - odd
    out[2] = float(d[0, 2]) * d0 + float(d[1, 2]) * d1
    return out


def shifted(tiles, distance, lane):
    skip, part = divmod(distance, LANES)
    if part == 0:
        moved = tiles
        pick = None
    else:
        moved = [pltpu.roll(t, LANES - part, 1) for t in tiles]
        pick = lane < LANES - part
    n = len(tiles)
    out = []
    for i in range(n):
        a = moved[(i + skip) % n]
        b = moved[(i + skip + 1) % n]
        out.append(a if pick is None else jnp.where(pick, a, b))
    return out


def plane_of(ref, start, row):
    r0, off = divmod(start, LANES)
    lane9 = lax.broadcasted_iota(jnp.int32, (9, LANES), 1)
    flat = ref[row + r0 : row + r0 + 9, :]
    if off:
        flat = jnp.where(
            lane9 < LANES - off,
            pltpu.roll(flat, LANES - off, 1),
            pltpu.roll(ref[row + r0 + 1 : row + r0 + 10, :], LANES - off, 1),
        )
    return flat


def store_plane(ref, row, flat):
    ref[pl.ds(row, 9, stride=16), :] = flat


def make_windows(plane_ref, base, win_ref, row):
    lane = lax.broadcasted_iota(jnp.int32, (8, LANES), 1)
    for h in range(2):
        tiles = [plane_ref[base + t * 16 + 8 * h : base + t * 16 + 8 * h + 8, :] for t in range(9)]
        for ey in range(EY):
            near = [tiles[ey], tiles[ey + 1], tiles[min(ey + 2, 8)]]
            if ey:
                near = [pltpu.roll(t, LANES - 4 * ey, 1) for t in near]
                keep = lane < LANES - 4 * ey
                near = [jnp.where(keep, near[0], near[1]), jnp.where(keep, near[1], near[2])]
            for w in range(2):
                win_ref[w, pl.ds(row + 64 * h + ey, 8, stride=8), :] = near[w]


def along_x(win_ref, source, target, places, combine):
    for row in places:
        for w in range(2):
            values = combine([win_ref[w, source + 8 * c : source + 8 * c + 8, :] for c in row])
            for c, v in zip(row, values):
                yield w, target + 8 * c, v


def gather_elements(win_ref, elem_ref, places):
    win_ref[:, 256:512, :] = jnp.zeros((2, 256, LANES), F32)
    for f in range(2):
        for w, row, value in along_x(win_ref, 128 * f, 256 + 128 * f, places, derive):
            win_ref[w, row : row + 8, :] = value
    select = selector()
    hi, mid, low = split3(jnp.concatenate([win_ref[0], win_ref[1]], axis=1))
    elem_ref[...] = dot_nt(select, hi) + (dot_nt(select, mid) + dot_nt(select, low))


def part(ref, column, j, k):
    r = (j * 5 + k) * 8
    return ref[r : r + 8, column * LANES : (column + 1) * LANES]


def kernel_rows(elem_ref, flux_ref, win_ref, halves):
    kern = [[None] * 5 for _ in range(5)]
    for k in range(5):
        fwd = derive([part(elem_ref, 0, j, k) for j in range(5)])
        adj = derive([part(elem_ref, 1, j, k) for j in range(5)])
        for j in range(5):
            kern[j][k] = fwd[j] * adj[j] + part(elem_ref, 2, j, k) * part(elem_ref, 3, j, k)
    for j in range(5):
        fwd = derive([part(elem_ref, 0, j, k) for k in range(5)])
        adj = derive([part(elem_ref, 1, j, k) for k in range(5)])
        for k in range(5):
            kern[j][k] = -(kern[j][k] + fwd[k] * adj[k]) * part(flux_ref, 0, j, k)
    hi, mid, low = split3(jnp.concatenate([v for row in kern for v in row], axis=0))
    select = selector()
    back = dot_tn(hi, select) + (dot_tn(mid, select) + dot_tn(low, select))
    win_ref[0, 0:LANES, :] = back[:, :LANES]
    win_ref[1, 0:LANES, :] = back[:, LANES:]
    return [gathered(win_ref, 0, h) for h in range(halves)]


def cross_smoothed(tiles, cross_ref):
    lane = lax.broadcasted_iota(jnp.int32, tiles[0].shape, 1)
    for base, step in ((0, 1), (9, PZ)):
        total = None
        for tap in range(9):
            moved = shifted(tiles, step * (tap - 4), lane) if tap != 4 else tiles
            terms = [v * cross_ref[base + tap : base + tap + 1, t * LANES : (t + 1) * LANES] for t, v in enumerate(moved)]
            total = terms if total is None else [a + b for a, b in zip(total, terms)]
        tiles = total
    return tiles


def own_kernel(
    own_ref, code_ref, parts_ref, cross_hbm,
    elem_ref, flux_ref, near_flux_ref, kern_ref,
    cross_ref, plane_ref, win_ref, sem,
):
    copies = fetch(sem, (cross_hbm, cross_ref))
    element = lax.broadcasted_iota(jnp.int32, (256, 256), 0)
    pick = jnp.where(code_ref[0:1, :] == element, 1.0, 0.0).astype(BF16)
    moved = add_parts(dot_nt(parts_ref[...], pick))

    def tile_of(i, ez):
        t = ez // 4
        return moved[32 * i : 32 * i + 32, t * LANES : (t + 1) * LANES], 32 * (ez % 4)

    place_flux(flux_ref, tile_of, lambda i: [(0, 24 * i, 24)])
    place_flux(near_flux_ref, tile_of, lambda i: [(24, 8 * NEAR_AT[1][i], 8)])
    scaled(flux_ref, lane_weight(OWN_AT))
    scaled(near_flux_ref, lane_weight(NEAR_AT))
    plane_ref[...] = jnp.zeros(plane_ref.shape, F32)
    for f in range(2):
        for x in range(13):
            flat = plane_of(own_ref, PYZ * x, ROWS * f)
            if x < 12:
                store_plane(plane_ref, 144 * f + OWN_AT[x // 4][x % 4], flat)
            if x % 4 == 0 and x > 0:
                store_plane(plane_ref, 144 * f + OWN_AT[x // 4 - 1][4], flat)
        make_windows(plane_ref, 144 * f, win_ref, 128 * f)
    gather_elements(win_ref, elem_ref, OWN_AT)
    low, high = kernel_rows(elem_ref, flux_ref, win_ref, 2)
    row = lax.broadcasted_iota(jnp.int32, (8, LANES), 0)
    tiles = []
    for t in range(9):
        first = low[t] + jnp.where((row == 1) | (row == 2), pltpu.roll(high[t], 5, 0), 0.0)
        second = jnp.where(row < 4, high[t], jnp.where(row == 4, pltpu.roll(high[t], 6, 0), 0.0))
        tiles.append(jnp.concatenate([first, second], axis=0))
    copies[0].wait()
    for t, tile in enumerate(cross_smoothed(tiles, cross_ref)):
        kern_ref[:, t * LANES : (t + 1) * LANES] = tile


def near_kernel(
    own_ref, prev_ref, next_ref, flux_in_ref, kern_in_ref, cross_hbm,
    elem_ref, flux_ref, kern_ref,
    cross_ref, plane_ref, win_ref, sem,
):
    copies = fetch(sem, (cross_hbm, cross_ref))
    plane_ref[...] = jnp.zeros(plane_ref.shape, F32)
    for f in range(2):
        for i in range(5):
            flat = plane_of(prev_ref, 12 + PYZ * i, 40 * f) if i < 4 else plane_of(own_ref, 0, ROWS * f)
            store_plane(plane_ref, 144 * f + NEAR_AT[0][i], flat)
            flat = plane_of(own_ref, PYZ * (12 + i), ROWS * f) if i < 4 else plane_of(next_ref, 0, 16 * f)
            store_plane(plane_ref, 144 * f + NEAR_AT[1][i], flat)
        make_windows(plane_ref, 144 * f, win_ref, 128 * f)
    gather_elements(win_ref, elem_ref, NEAR_AT)

    def tile_of(i, ez):
        blocks = []
        for r in range(32 * i, 32 * i + 32, 16):
            at = 80 + r % 80
            blocks.append((prev_ref[at : at + 16, :], 64 * (r // 80)))
        (a, p), (b, q) = blocks
        if p != q:
            b = pltpu.roll(b, 64, 1)
        return jnp.concatenate([a, b], axis=0), 8 * ez + p

    place_flux(flux_ref, tile_of, lambda i: [(0, 8 * NEAR_AT[0][i], 8)])
    scaled(flux_ref, lane_weight(NEAR_AT))
    flux_ref[...] = flux_ref[...] + flux_in_ref[...]
    (tiles,) = kernel_rows(elem_ref, flux_ref, win_ref, 1)
    row = lax.broadcasted_iota(jnp.int32, (8, LANES), 0)
    tiles = [jnp.where((row == 0) | (row >= 4), v, 0.0) for v in tiles]
    copies[0].wait()
    for t, tile in enumerate(cross_smoothed(tiles, cross_ref)):
        columns = slice(t * LANES, (t + 1) * LANES)
        kern_ref[0:8, columns] = kern_in_ref[0:8, columns] + jnp.where(row == 0, tile, 0.0)
        kern_ref[8:16, columns] = kern_in_ref[8:16, columns] + jnp.where(row >= 4, tile, 0.0)


def gathered(win_ref, base, h):
    lane = lax.broadcasted_iota(jnp.int32, (8, LANES), 1)
    tiles = [None] * 9
    for ey in range(EY):
        rows = pl.ds(base + h * 64 + ey, 8, stride=8)
        a, b = win_ref[0, rows, :], win_ref[1, rows, :]
        if ey:
            a, b = pltpu.roll(a, 4 * ey, 1), pltpu.roll(b, 4 * ey, 1)
            keep = lane >= 4 * ey
            a, b = jnp.where(keep, a, 0.0), jnp.where(keep, b, a)
        tiles[ey] = a if ey == 0 else tiles[ey] + a
        tiles[ey + 1] = b
    return tiles


def force_kernel(elem_ref, flux_ref, near_elem_ref, near_flux_ref, out_ref, term_ref, win_ref):
    select = selector()
    for kind, (elem, flux, places) in enumerate(((elem_ref, flux_ref, OWN_AT), (near_elem_ref, near_flux_ref, NEAR_AT))):
        for f in range(2):
            term = [[None] * 5 for _ in range(5)]
            for k in range(5):
                grads = derive([part(elem, f, j, k) for j in range(5)])
                for j, v in enumerate(derive_back([g * part(flux, 0, j, k) for j, g in enumerate(grads)])):
                    term[j][k] = v
            for j in range(5):
                grads = derive([part(elem, f, j, k) for k in range(5)])
                for k, v in enumerate(derive_back([g * part(flux, 0, j, k) for k, g in enumerate(grads)])):
                    r = (j * 5 + k) * 8
                    term_ref[r : r + 8, f * LANES : (f + 1) * LANES] = term[j][k] + v
                    term_ref[r : r + 8, (2 + f) * LANES : (3 + f) * LANES] = part(elem, 2 + f, j, k) * part(flux, 0, j, k)
        hi, mid, low = split3(term_ref[...])
        back = dot_tn(hi, select) + (dot_tn(mid, select) + dot_tn(low, select))
        for w in range(2):
            win_ref[w] = back[:, w * LANES : (w + 1) * LANES]
        for f in range(2):
            to = 256 * kind + 128 * f
            for w, row, value in along_x(win_ref, 256 + 128 * f, 0, places, derive_back):
                out_ref[w, to + row : to + row + 8, :] = win_ref[w, 128 * f + row : 128 * f + row + 8, :] + value


def step_kernel(
    force_ref, fwd_hbm, fwd_speed_hbm, adj_hbm, adj_speed_hbm, mass_hbm, after_ref,
    fwd_out_ref, fwd_speed_out_ref, adj_out_ref, adj_speed_out_ref,
    fwd_ref, fwd_speed_ref, adj_ref, adj_speed_ref, mass_ref, plane_ref, line_ref, sem,
):
    copies = fetch(
        sem,
        (fwd_hbm, fwd_ref),
        (fwd_speed_hbm, fwd_speed_ref),
        (adj_hbm, adj_ref),
        (adj_speed_hbm, adj_speed_ref),
        (mass_hbm, mass_ref),
    )
    lane9 = lax.broadcasted_iota(jnp.int32, (9, LANES), 1)
    for n in range(4):
        for h in range(2):
            for t, tile in enumerate(gathered(force_ref, 128 * n, h)):
                plane_ref[n * 144 + t * 16 + 8 * h : n * 144 + t * 16 + 8 * h + 8, :] = tile
    line_ref[...] = jnp.zeros(line_ref.shape, F32)
    for f in range(2):
        for x in range(PXU):
            r0, off = divmod(PYZ * x, LANES)
            i, m = x % 4, x // 4
            rows = [144 * f + OWN_AT[m][i] if m < 3 else 288 + 144 * f + NEAR_AT[1][i]]
            if i == 0:
                rows.append(144 * f + OWN_AT[m - 1][4] if m > 0 else 288 + 144 * f + NEAR_AT[0][4])
            flat = plane_ref[pl.ds(rows[0], 9, stride=16), :]
            if i == 0:
                flat = flat + plane_ref[pl.ds(rows[1], 9, stride=16), :]
            if off:
                flat = pltpu.roll(flat, off, 1)
                spill = jnp.where(lane9 < off, flat, 0.0)
                flat = jnp.where(lane9 < off, 0.0, flat)
            line_ref[f, r0 : r0 + 9, :] = line_ref[f, r0 : r0 + 9, :] + flat
            if off:
                line_ref[f, r0 + 1 : r0 + 10, :] = line_ref[f, r0 + 1 : r0 + 10, :] + spill

    def step(lo, hi, force):
        shape = (hi - lo) // force[0].shape[1], force[0].shape[1]
        take = lambda ref: ref[0:1, lo:hi].reshape(shape)
        scale = TIME_STEP * mass_ref[lo:hi].reshape(shape)
        speed = take(fwd_speed_ref) + scale * force[0]
        fwd_speed_out_ref[0:1, lo:hi] = speed.reshape(1, hi - lo)
        fwd_out_ref[0:1, lo:hi] = (take(fwd_ref) - TIME_STEP * speed).reshape(1, hi - lo)
        speed = take(adj_speed_ref) - scale * force[1]
        adj_speed_out_ref[0:1, lo:hi] = speed.reshape(1, hi - lo)
        adj_out_ref[0:1, lo:hi] = (take(adj_ref) + TIME_STEP * speed).reshape(1, hi - lo)

    for c in copies:
        c.wait()
    for r in range(0, 136, 8):
        step(r * LANES, (r + 8) * LANES, [line_ref[f, r : r + 8, :] for f in range(2)])
    step(NPTS - 16, NPTS, [line_ref[f, 136:137, 0:16] for f in range(2)])


def band_kernel(parity_ref, own_ref, first_ref, second_ref, band_ref, out_ref):
    flat = jnp.concatenate([own_ref[...], first_ref[...], second_ref[...]], axis=0)
    k1 = flat.astype(BF16)
    rest = flat - k1.astype(F32)
    k2 = rest.astype(BF16)
    k3 = (rest - k2.astype(F32)).astype(BF16)
    stacked = jnp.concatenate([k1, k2, k3, k1, k2, k1], axis=0)
    band = band_ref[parity_ref[0]]
    out_ref[...] = jnp.dot(band, stacked, preferred_element_type=F32)[:, :PYZ]


def on_device(
    forward_displacement,
    forward_velocity,
    adjoint_displacement,
    adjoint_velocity,
    inverse_mass,
    shear_modulus,
    connectivity,
    face_points,
    element_count,
):
    events = lax.axis_size("event")
    cuts = lax.axis_size("cuts")
    parity = (lax.axis_index("cuts") % 2).astype(jnp.int32).reshape(1)
    pairs_first = [(i, (i - 1 if i % 2 == 0 else i + 1) % cuts) for i in range(cuts)]
    pairs_second = [(i, (i + 1 if i % 2 == 0 else i - 1) % cuts) for i in range(cuts)]

    vmem = pl.BlockSpec(memory_space=pltpu.VMEM)
    smem = pl.BlockSpec(memory_space=pltpu.SMEM)
    anywhere = pl.BlockSpec(memory_space=pl.ANY)

    def held(block):
        return pltpu.with_memory_space_constraint(block, pltpu.VMEM)

    def in_hbm(block):
        return pltpu.with_memory_space_constraint(block, pltpu.HBM)

    def cost(flops):
        return pl.CostEstimate(flops=flops, bytes_accessed=1000000, transcendentals=0)

    dma = pltpu.SemaphoreType.DMA
    point_row = pltpu.VMEM((1, NPTS), F32)
    elem_block = pltpu.VMEM((200, 4 * LANES), F32)
    flux_block = pltpu.VMEM((200, LANES), F32)
    kern_block = pltpu.VMEM((16, 9 * LANES), F32)
    cross_block = pltpu.VMEM((24, 9 * LANES), F32)
    plane_block = pltpu.VMEM((2 * 144, LANES), F32)
    window = pltpu.VMEM((2, 512, LANES), F32)
    fields = (in_hbm(forward_displacement), in_hbm(adjoint_displacement))
    cross = in_hbm(jnp.asarray(cross_table()))
    right, left, own, code, parts = pl.pallas_call(
        pack_kernel,
        out_shape=[
            pltpu.VMEM((160, LANES), F32),
            pltpu.VMEM((32, LANES), F32),
            pltpu.VMEM((2 * ROWS, LANES), F32),
            pltpu.VMEM((8, 256), jnp.int32),
            pltpu.VMEM((480, 256), BF16),
        ],
        in_specs=[smem] + [anywhere] * 4,
        scratch_shapes=[
            pltpu.VMEM((8, 256), jnp.int32),
            pltpu.VMEM((125, 256), F32),
            point_row,
            point_row,
            pltpu.VMEM((160, 256), F32),
            dma((4,)),
        ],
        cost_estimate=cost(100000000),
        name="pack",
    )(element_count, in_hbm(connectivity), in_hbm(shear_modulus), *fields)
    prev = lax.ppermute(right, "cuts", [(i, (i + 1) % cuts) for i in range(cuts)])
    left, right = lax.optimization_barrier((left, right))
    after = lax.ppermute(left, "cuts", [((i + 1) % cuts, i) for i in range(cuts)])

    elem, flux, near_flux, kern = pl.pallas_call(
        own_kernel,
        out_shape=[elem_block, flux_block, flux_block, kern_block],
        in_specs=[vmem] * 3 + [anywhere],
        scratch_shapes=[cross_block, plane_block, window, dma((1,))],
        cost_estimate=cost(300000000),
        name="own_layers",
    )(held(own), held(code), held(parts), cross)
    near_elem, near_flux, kern = pl.pallas_call(
        near_kernel,
        out_shape=[elem_block, flux_block, kern_block],
        in_specs=[vmem] * 5 + [anywhere],
        scratch_shapes=[cross_block, plane_block, window, dma((1,))],
        cost_estimate=cost(200000000),
        name="near_layers",
    )(held(own), held(prev), held(after), held(near_flux), held(kern), cross)

    (force,) = pl.pallas_call(
        force_kernel,
        out_shape=[window],
        in_specs=[vmem] * 4,
        scratch_shapes=[elem_block, window],
        cost_estimate=cost(200000000),
        name="forces",
    )(held(elem), held(flux), held(near_elem), held(near_flux))

    if events == 2:
        other = lax.ppermute(kern, "event", [(0, 1), (1, 0)])
        other, force = lax.optimization_barrier((other, force))
        kern = kern + other
    elif events > 2:
        kern = lax.psum(kern, "event")
    kern_first = lax.ppermute(kern, "cuts", pairs_first)
    kern_second = lax.ppermute(kern, "cuts", pairs_second)

    points = jax.ShapeDtypeStruct((1, NPTS), F32)
    outs = pl.pallas_call(
        step_kernel,
        out_shape=[points] * 4,
        in_specs=[vmem] + [anywhere] * 5 + [vmem],
        scratch_shapes=[point_row] * 4
        + [pltpu.VMEM((NPTS,), F32), pltpu.VMEM((4 * 144, LANES), F32), pltpu.VMEM((2, ROWS, LANES), F32), dma((5,))],
        cost_estimate=cost(200000000),
        name="step",
    )(
        held(force),
        fields[0],
        in_hbm(forward_velocity),
        fields[1],
        in_hbm(adjoint_velocity),
        in_hbm(inverse_mass),
        held(kern),
    )
    shear_kernel = pl.pallas_call(
        band_kernel,
        out_shape=jax.ShapeDtypeStruct((PXU, PYZ), F32),
        in_specs=[smem] + [vmem] * 4,
        cost_estimate=cost(20000000),
        name="band",
    )(parity, held(kern), held(kern_first), held(kern_second), held(jnp.asarray(band_table())))
    return (*outs, shear_kernel)


def solution(mesh):
    in_specs = (
        P("event", "cuts"),
        P("event", "cuts"),
        P("event", "cuts"),
        P("event", "cuts"),
        P("cuts"),
        P(None, "cuts"),
        P(None, "cuts"),
        P("cuts", None),
        P("cuts"),
    )
    out_specs = (
        P("event", "cuts"),
        P("event", "cuts"),
        P("event", "cuts"),
        P("event", "cuts"),
        P("cuts", None),
    )
    return jax.shard_map(on_device, mesh=mesh, in_specs=in_specs, out_specs=out_specs, check_vma=False)
```

time: 25.6 us -> 24.9 us (0.973)
  starting transfers between devices: 10.5 us -> 10 us
  Pallas kernels: 10.3 us -> 9.86 us
  waiting for transfers between devices: 3.22 us -> 3.48 us
    ppermute x1, waiting for transfers between devices: 1.52 us -> 2.02 us  [on_device(): kern_first = lax.ppermute(kern, 'cuts', pairs_first)]
    pallas_call x5, Pallas kernels: 9.48 us -> 9.01 us  [the longest x1 2.5 us: on_device(): pl.pallas_call(own_kernel, out_shape=[elem_block, flux_block, flux_block,...]
    ppermute x1, starting transfers between devices: 2.93 us -> 2.51 us  [on_device(): kern_first = lax.ppermute(kern, 'cuts', pairs_first)]
    ppermute x1, waiting for transfers between devices: 0.35 us -> 0.01 us  [on_device(): lax.ppermute(right, 'cuts', [(i, (i + 1) % cuts) for i in range(cuts)])]
  transfers between devices with their start and end apart: 5 -> 5, of which waited for: 3 -> 2; matrix products, arithmetic and copies ran while one was open for 0% -> 0% of each run, Pallas kernels for 19% -> 22%
where the time goes in v5:
time: 24.9 us; the launch traced here: 24.7 us
  starting transfers between devices  10 us (40%)
  Pallas kernels  9.86 us (40%)
  waiting for transfers between devices  3.48 us (14%)
  between operations  1.34 us (5%)
    ppermute x1, starting transfers between devices, on_device(): lax.ppermute(left, 'cuts', [((i + 1) % cuts, i) for i in range(cuts)])  5.06 us
    ppermute x1, starting transfers between devices, on_device(): kern_first = lax.ppermute(kern, 'cuts', pairs_first)  2.51 us
    pallas_call x1, Pallas kernels, on_device(): pl.pallas_call(own_kernel, out_shape=[elem_block, flux_block, flux_block,...  2.5 us
    pallas_call x1, Pallas kernels, on_device(): pl.pallas_call(near_kernel, out_shape=[elem_block, flux_block, kern_block...  2.23 us
    ppermute x1, waiting for transfers between devices, on_device(): kern_first = lax.ppermute(kern, 'cuts', pairs_first)  2.02 us
    pallas_call x1, Pallas kernels, on_device(): pl.pallas_call(step_kernel, out_shape=[points] * 4, in_specs=[vmem] + [an...  1.99 us
    ppermute x1, starting transfers between devices, on_device(): other = lax.ppermute(kern, 'event', [(0, 1), (1, 0)])  1.93 us
    ppermute x1, waiting for transfers between devices, on_device(): other = lax.ppermute(kern, 'event', [(0, 1), (1, 0)])  1.44 us
  transfers between devices with their start and end apart: 5, of which 2 were waited for; matrix products, arithmetic and copies ran while one was open for 0% of the time, Pallas kernels for 22%

profile of v5, /device:TPU:0, one launch (start us, length us, event | category | flops | bytes accessed | tf_op | source)
XLA Modules:
  0.0 24.7 jit_solution(3241277760861706205)
XLA Ops:
  1.3 1.3 %pack.1 = (f32[160,128]{1,0:T(8,128)S(1)}, f32[32,128]{1,0:T(8,128)S(1)}, f32[288,128]{1,0:T(8,128)S(1)}, s32[8,256]{1,0:T(8,128)S(1)}, bf16[480,256]{1,0:T(8,128)(2,1)S(1)}) custom-call(s32[1]{0:T(128)S(6)} %copy.15.count_ref, s32[125,256]{1,0:T(8,128)} %conn_hbm.1, f32[125,256]{1,0:T(8,128)} %shear_hbm.1, f32[1,17424]{1,0:T(1,128)} %fwd_hbm.3, ...), custom_call_target="tpu_custom_call" | custom-call | flops 100000000 | bytes 1000000 | tf_op jit(solution)/shard_map/pack/pallas_call | solution.py:545
  2.5 0.5 %collective-permute-start = (f32[160,128]{1,0:T(8,128)S(1)}, f32[160,128]{1,0:T(8,128)S(1)}, u32[]{:S(2)}, u32[]{:S(2)}) collective-permute-start(f32[160,128]{1,0:T(8,128)S(1)} %get-tuple-element.25), channel_id=1, source_target_pairs={{0,1},{1,2},{2,3},{3,4},{4,5},{5,6},{6,7},{7,8},{8,9},{9,10},{10,1... | collective-permute-start | bytes 245768 | tf_op jit(solution)/shard_map/ppermute | solution.py:566
  3.0 5.1 %collective-permute-start.1 = (f32[32,128]{1,0:T(8,128)S(1)}, f32[32,128]{1,0:T(8,128)S(1)}, u32[]{:S(2)}, u32[]{:S(2)}) collective-permute-start(f32[32,128]{1,0:T(8,128)S(1)} %get-tuple-element.27), channel_id=1, source_target_pairs={{1,0},{2,1},{3,2},{4,3},{5,4},{6,5},{7,6},{8,7},{9,8},{10,9},{11,1... | collective-permute-start | bytes 49160 | tf_op jit(solution)/shard_map/ppermute | solution.py:568
  8.1 2.5 %own_layers.1 = (f32[200,512]{1,0:T(8,128)S(1)}, f32[200,128]{1,0:T(8,128)S(1)}, f32[200,128]{1,0:T(8,128)S(1)}, f32[16,1152]{1,0:T(8,128)S(1)}) custom-call(f32[288,128]{1,0:T(8,128)S(1)} %get-tuple-element.24.own_ref, s32[8,256]{1,0:T(8,128)S(1)} %get-tuple-element.28.code_ref, bf16[480,256]{1,0:T(8,128)(2,1)S(1)} %get-tuple-element.29.parts_ref, ...), custom_call_target="tpu_custom_call" | custom-call | flops 300000000 | bytes 1000000 | tf_op jit(solution)/shard_map/own_layers/pallas_call | solution.py:570
  10.6 0.0 collective-permute-done.1.next_ref
  10.6 0.0 collective-permute-done.prev_ref
  10.6 2.2 %near_layers.1 = (f32[200,512]{1,0:T(8,128)S(1)}, f32[200,128]{1,0:T(8,128)S(1)}, f32[16,1152]{1,0:T(8,128)S(1)}) custom-call(f32[288,128]{1,0:T(8,128)S(1)} %get-tuple-element.24.own_ref, f32[160,128]{1,0:T(8,128)S(1)} %collective-permute-done.prev_ref, f32[32,128]{1,0:T(8,128)S(1)} %collective-permute-done.1.next_ref, ...), custom_call_target="tpu_custom_call" | custom-call | flops 200000000 | bytes 1000000 | tf_op jit(solution)/shard_map/near_layers/pallas_call | solution.py:578
  12.9 1.9 %collective-permute-start.2 = (f32[16,1152]{1,0:T(8,128)S(1)}, f32[16,1152]{1,0:T(8,128)S(1)}, u32[]{:S(2)}, u32[]{:S(2)}) collective-permute-start(f32[16,1152]{1,0:T(8,128)S(1)} %get-tuple-element.32), channel_id=1, source_target_pairs={{0,16},{16,0},{1,17},{17,1},{2,18},{18,2},{3,19},{19,3},{4,20},{20... | collective-permute-start | bytes 221192 | tf_op jit(solution)/shard_map/ppermute | solution.py:597
  14.8 1.0 %forces.1.force_ref = f32[2,512,128]{2,1,0:T(8,128)S(1)} custom-call(f32[200,512]{1,0:T(8,128)S(1)} %get-tuple-element.33.elem_ref, f32[200,128]{1,0:T(8,128)S(1)} %get-tuple-element.34.flux_ref, f32[200,512]{1,0:T(8,128)S(1)} %get-tuple-element.35.near_elem_ref, f32[200,128]{1,0:T(8,128)S(1)} %get-tuple-element.36.near_flux_ref), custom_call_target="tpu_custom_call" | custom-call | flops 200000000 | bytes 1000000 | tf_op jit(solution)/shard_map/forces/pallas_call | solution.py:587
  15.9 1.4 %collective-permute-done.2 = f32[16,1152]{1,0:T(8,128)S(1)} collective-permute-done((f32[16,1152]{1,0:T(8,128)S(1)}, f32[16,1152]{1,0:T(8,128)S(1)}, u32[]{:S(2)}, u32[]{:S(2)}) %collective-permute-start.2) | collective-permute-done | bytes 73760 | tf_op jit(solution)/shard_map/ppermute | solution.py:597
  17.3 2.5 %collective-permute-start.3 = (f32[16,1152]{1,0:T(8,128)S(1)}, f32[16,1152]{1,0:T(8,128)S(1)}, u32[]{:S(2)}, u32[]{:S(2)}) collective-permute-start(f32[16,1152]{1,0:T(8,128)S(1)} %add.7.after_ref.own_ref), channel_id=1, source_target_pairs={{0,15},{1,2},{2,1},{3,4},{4,3},{5,6},{6,5},{7,8},{8,7},{9,10},{10,... | collective-permute-start | bytes 221192 | tf_op jit(solution)/shard_map/ppermute | solution.py:602
  19.8 0.0 collective-permute-start.4
  19.8 0.0 copy-start
  19.8 2.0 %step.1 = (f32[1,17424]{1,0:T(1,128)}, f32[1,17424]{1,0:T(1,128)}, f32[1,17424]{1,0:T(1,128)}, f32[1,17424]{1,0:T(1,128)}) custom-call(f32[2,512,128]{2,1,0:T(8,128)S(1)} %forces.1.force_ref, f32[1,17424]{1,0:T(1,128)} %fwd_hbm.3, f32[1,17424]{1,0:T(1,128)} %fwd_speed_hbm.1, f32[1,17424]{1,0:T(1,128)} %adj_hbm.3, f32[1,17424]{1,0:T(1,128)} %adj_speed_hbm.1, ...), custom_call_target="tpu_custom_call" | custom-call | flops 200000000 | bytes 1000000 | tf_op jit(solution)/shard_map/step/pallas_call | solution.py:606
  21.8 2.0 %collective-permute-done.3.first_ref = f32[16,1152]{1,0:T(8,128)S(1)} collective-permute-done((f32[16,1152]{1,0:T(8,128)S(1)}, f32[16,1152]{1,0:T(8,128)S(1)}, u32[]{:S(2)}, u32[]{:S(2)}) %collective-permute-start.3) | collective-permute-done | bytes 73760 | tf_op jit(solution)/shard_map/ppermute | solution.py:602
  23.8 0.0 collective-permute-done.4.second_ref
  23.9 0.0 copy-done
  23.9 0.8 %band.1 = f32[16,1089]{1,0:T(8,128)} custom-call(s32[1]{0:T(128)} %bitcast.parity_ref, f32[16,1152]{1,0:T(8,128)S(1)} %add.7.after_ref.own_ref, f32[16,1152]{1,0:T(8,128)S(1)} %collective-permute-done.3.first_ref, f32[16,1152]{1,0:T(8,128)S(1)} %collective-permute-done.4.second_ref, bf16[2,16,288]{2,1,0:T(8,128)(2,1)S(1)} %copy-done), custom_call_target="tpu_custom_call" | custom-call | flops 20000000 | bytes 1000000 | tf_op jit(solution)/shard_map/band/pallas_call | solution.py:623
  (1 shorter events, 0.0 us)
Async XLA Ops:
  2.5 8.1 %collective-permute-start = (f32[160,128]{1,0:T(8,128)S(1)}, f32[160,128]{1,0:T(8,128)S(1)}, u32[]{:S(2)}, u32[]{:S(2)}) collective-permute-start(f32[160,128]{1,0:T(8,128)S(1)} %get-tuple-element.25), channel_id=1, source_target_pairs={{0,1},{1,2},{2,3},{3,4},{4,5},{5,6},{6,7},{7,8},{8,9},{9,10},{10,1... | collective-permute-start | bytes 245768 | tf_op jit(solution)/shard_map/ppermute | solution.py:566
  3.0 7.6 %collective-permute-start.1 = (f32[32,128]{1,0:T(8,128)S(1)}, f32[32,128]{1,0:T(8,128)S(1)}, u32[]{:S(2)}, u32[]{:S(2)}) collective-permute-start(f32[32,128]{1,0:T(8,128)S(1)} %get-tuple-element.27), channel_id=1, source_target_pairs={{1,0},{2,1},{3,2},{4,3},{5,4},{6,5},{7,6},{8,7},{9,8},{10,9},{11,1... | collective-permute-start | bytes 49160 | tf_op jit(solution)/shard_map/ppermute | solution.py:568
  12.9 4.4 %collective-permute-start.2 = (f32[16,1152]{1,0:T(8,128)S(1)}, f32[16,1152]{1,0:T(8,128)S(1)}, u32[]{:S(2)}, u32[]{:S(2)}) collective-permute-start(f32[16,1152]{1,0:T(8,128)S(1)} %get-tuple-element.32), channel_id=1, source_target_pairs={{0,16},{16,0},{1,17},{17,1},{2,18},{18,2},{3,19},{19,3},{4,20},{20... | collective-permute-start | bytes 221192 | tf_op jit(solution)/shard_map/ppermute | solution.py:597
  17.3 6.5 %collective-permute-start.3 = (f32[16,1152]{1,0:T(8,128)S(1)}, f32[16,1152]{1,0:T(8,128)S(1)}, u32[]{:S(2)}, u32[]{:S(2)}) collective-permute-start(f32[16,1152]{1,0:T(8,128)S(1)} %add.7.after_ref.own_ref), channel_id=1, source_target_pairs={{0,15},{1,2},{2,1},{3,4},{4,3},{5,6},{6,5},{7,8},{8,7},{9,10},{10,... | collective-permute-start | bytes 221192 | tf_op jit(solution)/shard_map/ppermute | solution.py:602
  19.8 4.0 %collective-permute-start.4 = (f32[16,1152]{1,0:T(8,128)S(1)}, f32[16,1152]{1,0:T(8,128)S(1)}, u32[]{:S(2)}, u32[]{:S(2)}) collective-permute-start(f32[16,1152]{1,0:T(8,128)S(1)} %add.7.after_ref.own_ref), channel_id=1, source_target_pairs={{0,1},{1,0},{2,3},{3,2},{4,5},{5,4},{6,7},{7,6},{8,9},{9,8},{10,11... | collective-permute-start | bytes 221192 | tf_op jit(solution)/shard_map/ppermute | solution.py:603
  19.8 4.0 %copy-start = (bf16[2,16,288]{2,1,0:T(8,128)(2,1)S(1)}, bf16[2,16,288]{2,1,0:T(8,128)(2,1)}, u32[]{:S(2)}) copy-start(bf16[2,16,288]{2,1,0:T(8,128)(2,1)} %constant.22.clone.band_ref) | copy-start | bytes 55300

commit v6 on v5

--- a/solution.py
+++ b/solution.py
@@ -48,7 +48,7 @@
 
 ROW_PLANE = np.array([4 * (r % 3) + r // 3 for r in range(12)] + [12, 13, 14, 15])
 OWN_AT = [[3 * i + m for i in range(5)] for m in range(3)]
-NEAR_AT = [[1, 2, 3, 8, 0], [4, 5, 6, 7, 9]]
+NEAR_AT = [[8, 9, 10, 11, 0], [4, 5, 6, 7, 12]]
 
 
 def band_table():
@@ -90,18 +90,6 @@
     return lax.dot_general(a, b, (((1,), (1,)), ((), ())), preferred_element_type=F32)
 
 
-def dot_tn(a, b):
-    return lax.dot_general(a, b, (((0,), (0,)), ((), ())), preferred_element_type=F32)
-
-
-def selector():
-    column = lax.broadcasted_iota(jnp.int32, (8, 256), 1)
-    row = lax.broadcasted_iota(jnp.int32, (8, 256), 0)
-    base = column - 4 * row
-    blocks = [jnp.where(base == j * PZ + k, 1.0, 0.0) for j in range(5) for k in range(5)]
-    return jnp.concatenate(blocks, axis=0).astype(BF16)
-
-
 def fetch(sem, *pairs):
     copies = [pltpu.make_async_copy(src, dst, sem.at[n]) for n, (src, dst) in enumerate(pairs)]
     for c in copies:
@@ -120,9 +108,9 @@
     conn_ref, shear_ref, fwd_ref, adj_ref, block_ref, sem,
 ):
     copies = fetch(
-        sem, (conn_hbm.at[0:8], conn_ref), (fwd_hbm, fwd_ref), (adj_hbm, adj_ref), (shear_hbm, shear_ref)
+        sem, (shear_hbm, shear_ref), (conn_hbm.at[0:8], conn_ref), (fwd_hbm, fwd_ref), (adj_hbm, adj_ref)
     )
-    copies[0].wait()
+    copies[1].wait()
     point = conn_ref[0:1, :].astype(F32)
     x = jnp.floor((point + 0.5) * (1.0 / PYZ))
     rest = point - x * PYZ
@@ -135,14 +123,14 @@
     lane = lax.broadcasted_iota(jnp.int32, (LANES, 256), 0)
     pick = jnp.where(code == ((lane >> 3) & 7) * 32 + 24 + (lane & 7), 1.0, 0.0).astype(BF16)
     for f, ref in enumerate((fwd_ref, adj_ref)):
-        copies[1 + f].wait()
+        copies[2 + f].wait()
         for r in range(0, 136, 8):
             own_ref[ROWS * f + r : ROWS * f + r + 8, :] = ref[0:1, r * LANES : (r + 8) * LANES].reshape(8, LANES)
         own_ref[ROWS * f + 136 : ROWS * f + 144, :] = jnp.zeros((8, LANES), F32)
         own_ref[ROWS * f + 136 : ROWS * f + 137, 0:16] = ref[0:1, NPTS - 16 : NPTS]
         right_ref[40 * f : 40 * f + 40, :] = own_ref[ROWS * f + 102 : ROWS * f + 142, :]
         left_ref[16 * f : 16 * f + 16, :] = own_ref[ROWS * f : ROWS * f + 16, :]
-    copies[3].wait()
+    copies[0].wait()
     block_ref[...] = jnp.zeros(block_ref.shape, F32)
     for i in range(NGLL):
         block_ref[32 * i : 32 * i + 25, :] = shear_ref[25 * i : 25 * i + 25, :]
@@ -173,11 +161,11 @@
             ref[r : r + 8, :] = ref[r : r + 8, :] * (weight * (gll_weight(j) * gll_weight(k)))
 
 
-def place_flux(ref, tile_of, moves):
+def place_flux(ref, tile_of, moves, layers=range(NGLL)):
     lane = lax.broadcasted_iota(jnp.int32, (32, LANES), 1)
     for ez in range(EZ):
         total = jnp.zeros((32, LANES), F32)
-        for i in range(NGLL):
+        for i in layers:
             tile, start = tile_of(i, ez)
             for source, target, width in moves(i):
                 shift = (target - source - start) % LANES
@@ -248,61 +236,66 @@
     ref[pl.ds(row, 9, stride=16), :] = flat
 
 
-def make_windows(plane_ref, base, win_ref, row):
+def make_windows(plane_ref, base, pitch, win_ref, row):
     lane = lax.broadcasted_iota(jnp.int32, (8, LANES), 1)
-    for h in range(2):
-        tiles = [plane_ref[base + t * 16 + 8 * h : base + t * 16 + 8 * h + 8, :] for t in range(9)]
-        for ey in range(EY):
-            near = [tiles[ey], tiles[ey + 1], tiles[min(ey + 2, 8)]]
-            if ey:
-                near = [pltpu.roll(t, LANES - 4 * ey, 1) for t in near]
-                keep = lane < LANES - 4 * ey
-                near = [jnp.where(keep, near[0], near[1]), jnp.where(keep, near[1], near[2])]
-            for w in range(2):
-                win_ref[w, pl.ds(row + 64 * h + ey, 8, stride=8), :] = near[w]
-
-
-def along_x(win_ref, source, target, places, combine):
-    for row in places:
+    tiles = [plane_ref[base + t * pitch : base + t * pitch + 8, :] for t in range(9)]
+    for ey in range(EY):
+        near = [tiles[ey], tiles[ey + 1], tiles[min(ey + 2, 8)]]
+        if ey:
+            near = [pltpu.roll(t, LANES - 4 * ey, 1) for t in near]
+            keep = lane < LANES - 4 * ey
+            near = [jnp.where(keep, near[0], near[1]), jnp.where(keep, near[1], near[2])]
         for w in range(2):
-            values = combine([win_ref[w, source + 8 * c : source + 8 * c + 8, :] for c in row])
-            for c, v in zip(row, values):
-                yield w, target + 8 * c, v
-
-
-def gather_elements(win_ref, elem_ref, places):
-    win_ref[:, 256:512, :] = jnp.zeros((2, 256, LANES), F32)
-    for f in range(2):
-        for w, row, value in along_x(win_ref, 128 * f, 256 + 128 * f, places, derive):
-            win_ref[w, row : row + 8, :] = value
-    select = selector()
-    hi, mid, low = split3(jnp.concatenate([win_ref[0], win_ref[1]], axis=1))
-    elem_ref[...] = dot_nt(select, hi) + (dot_nt(select, mid) + dot_nt(select, low))
+            win_ref[w, pl.ds(row + ey, 8, stride=8), :] = near[w]
+
+
+def along_x(win_ref, base, row, combine):
+    for w in range(2):
+        values = combine([win_ref[w, base + 8 * c : base + 8 * c + 8, :] for c in row])
+        for i, v in enumerate(values):
+            yield w, i, v
+
+
+def turned(win_ref, base, elem_ref, column):
+    elem_ref[column, 0:LANES, :] = win_ref[0, base : base + LANES, :].T
+    elem_ref[column, LANES:168, :] = win_ref[1, base : base + LANES, :].T[0:40, :]
 
 
 def part(ref, column, j, k):
+    return ref[column, pl.ds(j * PZ + k, 8, stride=4), :]
+
+
+def flux_part(ref, j, k):
     r = (j * 5 + k) * 8
-    return ref[r : r + 8, column * LANES : (column + 1) * LANES]
-
-
-def kernel_rows(elem_ref, flux_ref, win_ref, halves):
-    kern = [[None] * 5 for _ in range(5)]
+    return ref[r : r + 8, :]
+
+
+def folded(term, line_ref, win_ref, base):
+    row = lax.broadcasted_iota(jnp.int32, (8, LANES), 0)
+    line_ref[160:256, :] = jnp.zeros((96, LANES), F32)
+    for j in range(5):
+        for k in range(1, 4):
+            line_ref[pl.ds(j * PZ + k, 8, stride=4), :] = term[j][k]
+        last = term[j][4]
+        line_ref[pl.ds(j * PZ, 8, stride=4), :] = term[j][0] + jnp.where(row == 0, 0.0, pltpu.roll(last, 1, 0))
+        line_ref[j * PZ + 32 : j * PZ + 33, :] = last[7:8, :]
+    for w in range(2):
+        win_ref[w, base : base + LANES, :] = line_ref[w * LANES : (w + 1) * LANES, :].T
+
+
+def force_terms(elem_ref, value, slope, flux_ref, line_ref, win_ref, row):
+    term = [[None] * 5 for _ in range(5)]
     for k in range(5):
-        fwd = derive([part(elem_ref, 0, j, k) for j in range(5)])
-        adj = derive([part(elem_ref, 1, j, k) for j in range(5)])
-        for j in range(5):
-            kern[j][k] = fwd[j] * adj[j] + part(elem_ref, 2, j, k) * part(elem_ref, 3, j, k)
+        grads = derive([part(elem_ref, value, j, k) for j in range(5)])
+        for j, v in enumerate(derive_back([g * flux_part(flux_ref, j, k) for j, g in enumerate(grads)])):
+            term[j][k] = v
     for j in range(5):
-        fwd = derive([part(elem_ref, 0, j, k) for k in range(5)])
-        adj = derive([part(elem_ref, 1, j, k) for k in range(5)])
-        for k in range(5):
-            kern[j][k] = -(kern[j][k] + fwd[k] * adj[k]) * part(flux_ref, 0, j, k)
-    hi, mid, low = split3(jnp.concatenate([v for row in kern for v in row], axis=0))
-    select = selector()
-    back = dot_tn(hi, select) + (dot_tn(mid, select) + dot_tn(low, select))
-    win_ref[0, 0:LANES, :] = back[:, :LANES]
-    win_ref[1, 0:LANES, :] = back[:, LANES:]
-    return [gathered(win_ref, 0, h) for h in range(halves)]
+        grads = derive([part(elem_ref, value, j, k) for k in range(5)])
+        for k, v in enumerate(derive_back([g * flux_part(flux_ref, j, k) for k, g in enumerate(grads)])):
+            term[j][k] = term[j][k] + v
+    folded(term, line_ref, win_ref, row)
+    term = [[part(elem_ref, slope, j, k) * flux_part(flux_ref, j, k) for k in range(5)] for j in range(5)]
+    folded(term, line_ref, win_ref, row + LANES)
 
 
 def cross_smoothed(tiles, cross_ref):
@@ -319,10 +312,32 @@
 
 def own_kernel(
     own_ref, code_ref, parts_ref, cross_hbm,
-    elem_ref, flux_ref, near_flux_ref, kern_ref,
-    cross_ref, plane_ref, win_ref, sem,
+    elem_ref, flux_ref, near_flux_ref, near_win_ref, near_kern_ref, kern_ref,
+    cross_ref, plane_ref, win_ref, line_ref, near_elem_ref, sem,
 ):
     copies = fetch(sem, (cross_hbm, cross_ref))
+    plane_ref[...] = jnp.zeros(plane_ref.shape, F32)
+    for f in range(2):
+        base = 24 * 9 * f
+        for x in range(PXU):
+            flat = plane_of(own_ref, PYZ * x, ROWS * f)
+            rows = [OWN_AT[x // 4][x % 4]] if x < 12 else [16 + NEAR_AT[1][x - 12]]
+            if x % 4 == 0:
+                rows.append(OWN_AT[x // 4 - 1][4] if x else 16 + NEAR_AT[0][4])
+            for r in rows:
+                plane_ref[pl.ds(base + r, 9, stride=24), :] = flat
+        for h in range(2):
+            make_windows(plane_ref, base + 8 * h, 24, win_ref, 128 * f + 64 * h)
+        make_windows(plane_ref, base + 16, 24, near_win_ref, 64 * f)
+        win_ref[:, 256 + 128 * f : 384 + 128 * f, :] = jnp.zeros((2, LANES, LANES), F32)
+        for row in OWN_AT:
+            for w, i, v in along_x(win_ref, 128 * f, row, derive):
+                r = 256 + 128 * f + 8 * row[i]
+                win_ref[w, r : r + 8, :] = v
+    for column in range(4):
+        turned(win_ref, 128 * column, elem_ref, column)
+    turned(near_win_ref, 0, near_elem_ref, 0)
+
     element = lax.broadcasted_iota(jnp.int32, (256, 256), 0)
     pick = jnp.where(code_ref[0:1, :] == element, 1.0, 0.0).astype(BF16)
     moved = add_parts(dot_nt(parts_ref[...], pick))
@@ -335,17 +350,22 @@
     place_flux(near_flux_ref, tile_of, lambda i: [(24, 8 * NEAR_AT[1][i], 8)])
     scaled(flux_ref, lane_weight(OWN_AT))
     scaled(near_flux_ref, lane_weight(NEAR_AT))
-    plane_ref[...] = jnp.zeros(plane_ref.shape, F32)
-    for f in range(2):
-        for x in range(13):
-            flat = plane_of(own_ref, PYZ * x, ROWS * f)
-            if x < 12:
-                store_plane(plane_ref, 144 * f + OWN_AT[x // 4][x % 4], flat)
-            if x % 4 == 0 and x > 0:
-                store_plane(plane_ref, 144 * f + OWN_AT[x // 4 - 1][4], flat)
-        make_windows(plane_ref, 144 * f, win_ref, 128 * f)
-    gather_elements(win_ref, elem_ref, OWN_AT)
-    low, high = kernel_rows(elem_ref, flux_ref, win_ref, 2)
+
+    kern = [[None] * 5 for _ in range(5)]
+    near = [[None] * 5 for _ in range(5)]
+    for k in range(5):
+        fwd, adj, both = [derive([part(ref, c, j, k) for j in range(5)]) for ref, c in ((elem_ref, 0), (elem_ref, 1), (near_elem_ref, 0))]
+        for j in range(5):
+            kern[j][k] = fwd[j] * adj[j] + part(elem_ref, 2, j, k) * part(elem_ref, 3, j, k)
+            near[j][k] = both[j] * pltpu.roll(both[j], 64, 1)
+    for j in range(5):
+        fwd, adj, both = [derive([part(ref, c, j, k) for k in range(5)]) for ref, c in ((elem_ref, 0), (elem_ref, 1), (near_elem_ref, 0))]
+        for k in range(5):
+            kern[j][k] = -(kern[j][k] + fwd[k] * adj[k]) * flux_part(flux_ref, j, k)
+            r = (j * 5 + k) * 8
+            near_kern_ref[r : r + 8, :] = near[j][k] + both[k] * pltpu.roll(both[k], 64, 1)
+    folded(kern, line_ref, win_ref, 0)
+    low, high = [gathered(win_ref, 0, h) for h in range(2)]
     row = lax.broadcasted_iota(jnp.int32, (8, LANES), 0)
     tiles = []
     for t in range(9):
@@ -357,22 +377,7 @@
         kern_ref[:, t * LANES : (t + 1) * LANES] = tile
 
 
-def near_kernel(
-    own_ref, prev_ref, next_ref, flux_in_ref, kern_in_ref, cross_hbm,
-    elem_ref, flux_ref, kern_ref,
-    cross_ref, plane_ref, win_ref, sem,
-):
-    copies = fetch(sem, (cross_hbm, cross_ref))
-    plane_ref[...] = jnp.zeros(plane_ref.shape, F32)
-    for f in range(2):
-        for i in range(5):
-            flat = plane_of(prev_ref, 12 + PYZ * i, 40 * f) if i < 4 else plane_of(own_ref, 0, ROWS * f)
-            store_plane(plane_ref, 144 * f + NEAR_AT[0][i], flat)
-            flat = plane_of(own_ref, PYZ * (12 + i), ROWS * f) if i < 4 else plane_of(next_ref, 0, 16 * f)
-            store_plane(plane_ref, 144 * f + NEAR_AT[1][i], flat)
-        make_windows(plane_ref, 144 * f, win_ref, 128 * f)
-    gather_elements(win_ref, elem_ref, NEAR_AT)
-
+def message_flux(prev_ref):
     def tile_of(i, ez):
         blocks = []
         for r in range(32 * i, 32 * i + 32, 16):
@@ -383,12 +388,40 @@
             b = pltpu.roll(b, 64, 1)
         return jnp.concatenate([a, b], axis=0), 8 * ez + p
 
-    place_flux(flux_ref, tile_of, lambda i: [(0, 8 * NEAR_AT[0][i], 8)])
-    scaled(flux_ref, lane_weight(NEAR_AT))
-    flux_ref[...] = flux_ref[...] + flux_in_ref[...]
-    (tiles,) = kernel_rows(elem_ref, flux_ref, win_ref, 1)
+    return tile_of
+
+
+def near_kernel(
+    prev_ref, next_ref, flux_in_ref, near_in_ref, near_kern_ref, kern_in_ref, cross_hbm,
+    near_win_ref, kern_ref,
+    cross_ref, plane_ref, win_ref, elem_ref, flux_ref, line_ref, sem,
+):
+    copies = fetch(sem, (cross_hbm, cross_ref))
+    plane_ref[...] = jnp.zeros(plane_ref.shape, F32)
+    for f in range(2):
+        for i in range(5):
+            flat = plane_of(prev_ref, 12 + PYZ * i, 40 * f) if i < 4 else plane_of(next_ref, 0, 16 * f)
+            plane_ref[pl.ds(72 * f + i, 9, stride=8), :] = flat
+        near_win_ref[:, 128 * f : 128 * f + 64, :] = near_in_ref[:, 64 * f : 64 * f + 64, :]
+        make_windows(plane_ref, 72 * f, 8, near_win_ref, 128 * f + 64)
+        win_ref[:, 64 * f : 64 * f + 64, :] = jnp.zeros((2, 64, LANES), F32)
+        for layer, row in enumerate(NEAR_AT):
+            for w, i, v in along_x(near_win_ref, 128 * f, row, derive):
+                if (layer == 0) == (i == 4):
+                    r = 64 * f + 8 * row[i]
+                    win_ref[w, r : r + 8, :] = v
+    turned(win_ref, 0, elem_ref, 0)
+    place_flux(flux_ref, message_flux(prev_ref), lambda i: [(0, 8 * NEAR_AT[0][i], 8)], (4,))
+    scaled(flux_ref, lane_weight([NEAR_AT[0]]))
+    kern = [[None] * 5 for _ in range(5)]
+    for j in range(5):
+        for k in range(5):
+            slope = part(elem_ref, 0, j, k)
+            total = flux_part(near_kern_ref, j, k) + slope * pltpu.roll(slope, 64, 1)
+            kern[j][k] = -total * (flux_part(flux_ref, j, k) + flux_part(flux_in_ref, j, k))
+    folded(kern, line_ref, win_ref, 0)
     row = lax.broadcasted_iota(jnp.int32, (8, LANES), 0)
-    tiles = [jnp.where((row == 0) | (row >= 4), v, 0.0) for v in tiles]
+    tiles = [jnp.where((row == 0) | (row >= 4), v, 0.0) for v in gathered(win_ref, 0, 0)]
     copies[0].wait()
     for t, tile in enumerate(cross_smoothed(tiles, cross_ref)):
         columns = slice(t * LANES, (t + 1) * LANES)
@@ -411,35 +444,24 @@
     return tiles
 
 
-def force_kernel(elem_ref, flux_ref, near_elem_ref, near_flux_ref, out_ref, term_ref, win_ref):
-    select = selector()
-    for kind, (elem, flux, places) in enumerate(((elem_ref, flux_ref, OWN_AT), (near_elem_ref, near_flux_ref, NEAR_AT))):
-        for f in range(2):
-            term = [[None] * 5 for _ in range(5)]
-            for k in range(5):
-                grads = derive([part(elem, f, j, k) for j in range(5)])
-                for j, v in enumerate(derive_back([g * part(flux, 0, j, k) for j, g in enumerate(grads)])):
-                    term[j][k] = v
-            for j in range(5):
-                grads = derive([part(elem, f, j, k) for k in range(5)])
-                for k, v in enumerate(derive_back([g * part(flux, 0, j, k) for k, g in enumerate(grads)])):
-                    r = (j * 5 + k) * 8
-                    term_ref[r : r + 8, f * LANES : (f + 1) * LANES] = term[j][k] + v
-                    term_ref[r : r + 8, (2 + f) * LANES : (3 + f) * LANES] = part(elem, 2 + f, j, k) * part(flux, 0, j, k)
-        hi, mid, low = split3(term_ref[...])
-        back = dot_tn(hi, select) + (dot_tn(mid, select) + dot_tn(low, select))
-        for w in range(2):
-            win_ref[w] = back[:, w * LANES : (w + 1) * LANES]
-        for f in range(2):
-            to = 256 * kind + 128 * f
-            for w, row, value in along_x(win_ref, 256 + 128 * f, 0, places, derive_back):
-                out_ref[w, to + row : to + row + 8, :] = win_ref[w, 128 * f + row : 128 * f + row + 8, :] + value
+def summed_along_x(win_ref, places, out_ref, row):
+    for line in places:
+        for w, i, v in along_x(win_ref, LANES, line, derive_back):
+            r = 8 * line[i]
+            out_ref[w, row + r : row + r + 8, :] = win_ref[w, r : r + 8, :] + v
+
+
+def force_kernel(elem_ref, flux_ref, out_ref, win_ref, line_ref):
+    for f in range(2):
+        force_terms(elem_ref, f, 2 + f, flux_ref, line_ref, win_ref, 0)
+        summed_along_x(win_ref, OWN_AT, out_ref, LANES * f)
 
 
 def step_kernel(
-    force_ref, fwd_hbm, fwd_speed_hbm, adj_hbm, adj_speed_hbm, mass_hbm, after_ref,
+    force_ref, near_win_ref, near_flux_ref, prev_ref, fwd_hbm, fwd_speed_hbm, adj_hbm, adj_speed_hbm, mass_hbm, after_ref,
     fwd_out_ref, fwd_speed_out_ref, adj_out_ref, adj_speed_out_ref,
-    fwd_ref, fwd_speed_ref, adj_ref, adj_speed_ref, mass_ref, plane_ref, line_ref, sem,
+    fwd_ref, fwd_speed_ref, adj_ref, adj_speed_ref, mass_ref, plane_ref, line_ref,
+    flux_ref, win_ref, elem_ref, fold_ref, near_ref, sem,
 ):
     copies = fetch(
         sem,
@@ -450,9 +472,22 @@
         (mass_hbm, mass_ref),
     )
     lane9 = lax.broadcasted_iota(jnp.int32, (9, LANES), 1)
+    place_flux(flux_ref, message_flux(prev_ref), lambda i: [(0, 8 * NEAR_AT[0][i], 8)])
+    scaled(flux_ref, lane_weight([NEAR_AT[0]]))
+    flux_ref[...] = flux_ref[...] + near_flux_ref[...]
+    for f in range(2):
+        win_ref[...] = jnp.zeros(win_ref.shape, F32)
+        for row in NEAR_AT:
+            for w, i, v in along_x(near_win_ref, LANES * f, row, derive):
+                win_ref[w, 8 * row[i] : 8 * row[i] + 8, :] = v
+        turned(near_win_ref, LANES * f, elem_ref, 0)
+        turned(win_ref, 0, elem_ref, 1)
+        force_terms(elem_ref, 0, 1, flux_ref, fold_ref, win_ref, 0)
+        summed_along_x(win_ref, NEAR_AT, near_ref, LANES * f)
     for n in range(4):
         for h in range(2):
-            for t, tile in enumerate(gathered(force_ref, 128 * n, h)):
+            source = force_ref if n < 2 else near_ref
+            for t, tile in enumerate(gathered(source, 128 * (n % 2), h)):
                 plane_ref[n * 144 + t * 16 + 8 * h : n * 144 + t * 16 + 8 * h + 8, :] = tile
     line_ref[...] = jnp.zeros(line_ref.shape, F32)
     for f in range(2):
@@ -534,12 +569,17 @@
 
     dma = pltpu.SemaphoreType.DMA
     point_row = pltpu.VMEM((1, NPTS), F32)
-    elem_block = pltpu.VMEM((200, 4 * LANES), F32)
     flux_block = pltpu.VMEM((200, LANES), F32)
     kern_block = pltpu.VMEM((16, 9 * LANES), F32)
     cross_block = pltpu.VMEM((24, 9 * LANES), F32)
-    plane_block = pltpu.VMEM((2 * 144, LANES), F32)
-    window = pltpu.VMEM((2, 512, LANES), F32)
+    line_block = pltpu.VMEM((256, LANES), F32)
+
+    def elements(n):
+        return pltpu.VMEM((n, 168, LANES), F32)
+
+    def windows(n):
+        return pltpu.VMEM((2, n * LANES, LANES), F32)
+
     fields = (in_hbm(forward_displacement), in_hbm(adjoint_displacement))
     cross = in_hbm(jnp.asarray(cross_table()))
     right, left, own, code, parts = pl.pallas_call(
@@ -567,31 +607,35 @@
     left, right = lax.optimization_barrier((left, right))
     after = lax.ppermute(left, "cuts", [((i + 1) % cuts, i) for i in range(cuts)])
 
-    elem, flux, near_flux, kern = pl.pallas_call(
+    elem, flux, near_flux, near_win, near_kern, kern = pl.pallas_call(
         own_kernel,
-        out_shape=[elem_block, flux_block, flux_block, kern_block],
+        out_shape=[elements(4), flux_block, flux_block, windows(1), flux_block, kern_block],
         in_specs=[vmem] * 3 + [anywhere],
-        scratch_shapes=[cross_block, plane_block, window, dma((1,))],
+        scratch_shapes=[
+            cross_block, pltpu.VMEM((2 * 9 * 24, LANES), F32), windows(4), line_block, elements(1), dma((1,))
+        ],
         cost_estimate=cost(300000000),
         name="own_layers",
     )(held(own), held(code), held(parts), cross)
-    near_elem, near_flux, kern = pl.pallas_call(
+    near_win, kern = pl.pallas_call(
         near_kernel,
-        out_shape=[elem_block, flux_block, kern_block],
-        in_specs=[vmem] * 5 + [anywhere],
-        scratch_shapes=[cross_block, plane_block, window, dma((1,))],
+        out_shape=[windows(2), kern_block],
+        in_specs=[vmem] * 6 + [anywhere],
+        scratch_shapes=[
+            cross_block, pltpu.VMEM((2 * 72, LANES), F32), windows(1), elements(1), flux_block, line_block, dma((1,))
+        ],
         cost_estimate=cost(200000000),
         name="near_layers",
-    )(held(own), held(prev), held(after), held(near_flux), held(kern), cross)
+    )(held(prev), held(after), held(near_flux), held(near_win), held(near_kern), held(kern), cross)
 
     (force,) = pl.pallas_call(
         force_kernel,
-        out_shape=[window],
-        in_specs=[vmem] * 4,
-        scratch_shapes=[elem_block, window],
+        out_shape=[windows(2)],
+        in_specs=[vmem] * 2,
+        scratch_shapes=[windows(2), line_block],
         cost_estimate=cost(200000000),
         name="forces",
-    )(held(elem), held(flux), held(near_elem), held(near_flux))
+    )(held(elem), held(flux))
 
     if events == 2:
         other = lax.ppermute(kern, "event", [(0, 1), (1, 0)])
@@ -606,13 +650,17 @@
     outs = pl.pallas_call(
         step_kernel,
         out_shape=[points] * 4,
-        in_specs=[vmem] + [anywhere] * 5 + [vmem],
+        in_specs=[vmem] * 4 + [anywhere] * 5 + [vmem],
         scratch_shapes=[point_row] * 4
-        + [pltpu.VMEM((NPTS,), F32), pltpu.VMEM((4 * 144, LANES), F32), pltpu.VMEM((2, ROWS, LANES), F32), dma((5,))],
+        + [pltpu.VMEM((NPTS,), F32), pltpu.VMEM((4 * 144, LANES), F32), pltpu.VMEM((2, ROWS, LANES), F32)]
+        + [flux_block, windows(2), elements(2), line_block, windows(2), dma((5,))],
         cost_estimate=cost(200000000),
         name="step",
     )(
         held(force),
+        held(near_win),
+        held(near_flux),
+        held(prev),
         fields[0],
         in_hbm(forward_velocity),
         fields[1],

time: 24.9 us -> 24.4 us (0.980)
  waiting for transfers between devices: 3.48 us -> 3.05 us
    ppermute x1, waiting for transfers between devices: 2.02 us -> 0.92 us  [on_device(): kern_first = lax.ppermute(kern, 'cuts', pairs_first)]
    ppermute x1, waiting for transfers between devices: 1.44 us -> 2.12 us  [on_device(): other = lax.ppermute(kern, 'event', [(0, 1), (1, 0)])]
  transfers between devices with their start and end apart: 5 -> 5, of which waited for: 2 -> 2; matrix products, arithmetic and copies ran while one was open for 0% -> 0% of each run, Pallas kernels for 22% -> 24%
where the time goes in v6:
time: 24.4 us; the launch traced here: 24.1 us
  starting transfers between devices  10 us (41%)
  Pallas kernels  9.68 us (40%)
  waiting for transfers between devices  3.05 us (12%)
  between operations  1.34 us (5%)
    ppermute x1, starting transfers between devices, on_device(): lax.ppermute(left, 'cuts', [((i + 1) % cuts, i) for i in range(cuts)])  5.06 us
    pallas_call x1, Pallas kernels, on_device(): pl.pallas_call(step_kernel, out_shape=[points] * 4, in_specs=[vmem] * 4 +...  3.09 us
    ppermute x1, starting transfers between devices, on_device(): kern_first = lax.ppermute(kern, 'cuts', pairs_first)  2.52 us
    pallas_call x1, Pallas kernels, on_device(): pl.pallas_call(own_kernel, out_shape=[elements(4), flux_block, flux_block...  2.43 us
    ppermute x1, waiting for transfers between devices, on_device(): other = lax.ppermute(kern, 'event', [(0, 1), (1, 0)])  2.12 us
    ppermute x1, starting transfers between devices, on_device(): other = lax.ppermute(kern, 'event', [(0, 1), (1, 0)])  1.93 us
    pallas_call x1, Pallas kernels, on_device(): pl.pallas_call(near_kernel, out_shape=[windows(2), kern_block], in_specs=...  1.68 us
    pallas_call x1, Pallas kernels, on_device(): pl.pallas_call(pack_kernel, out_shape=[pltpu.VMEM((160, LANES), F32), plt...  1.28 us
  transfers between devices with their start and end apart: 5, of which 2 were waited for; matrix products, arithmetic and copies ran while one was open for 0% of the time, Pallas kernels for 24%

profile of v6, /device:TPU:0, one launch (start us, length us, event | category | flops | bytes accessed | tf_op | source)
XLA Modules:
  0.0 24.1 jit_solution(6708956887080083222)
XLA Ops:
  1.3 1.3 %pack.1 = (f32[160,128]{1,0:T(8,128)S(1)}, f32[32,128]{1,0:T(8,128)S(1)}, f32[288,128]{1,0:T(8,128)S(1)}, s32[8,256]{1,0:T(8,128)S(1)}, bf16[480,256]{1,0:T(8,128)(2,1)S(1)}) custom-call(s32[1]{0:T(128)S(6)} %copy.15.count_ref, s32[125,256]{1,0:T(8,128)} %conn_hbm.1, f32[125,256]{1,0:T(8,128)} %shear_hbm.1, f32[1,17424]{1,0:T(1,128)} %fwd_hbm.3, ...), custom_call_target="tpu_custom_call" | custom-call | flops 100000000 | bytes 1000000 | tf_op jit(solution)/shard_map/pack/pallas_call | solution.py:585
  2.6 0.5 %collective-permute-start = (f32[160,128]{1,0:T(8,128)S(1)}, f32[160,128]{1,0:T(8,128)S(1)}, u32[]{:S(2)}, u32[]{:S(2)}) collective-permute-start(f32[160,128]{1,0:T(8,128)S(1)} %get-tuple-element.25), channel_id=1, source_target_pairs={{0,1},{1,2},{2,3},{3,4},{4,5},{5,6},{6,7},{7,8},{8,9},{9,10},{10,1... | collective-permute-start | bytes 245768 | tf_op jit(solution)/shard_map/ppermute | solution.py:606
  3.1 5.1 %collective-permute-start.1 = (f32[32,128]{1,0:T(8,128)S(1)}, f32[32,128]{1,0:T(8,128)S(1)}, u32[]{:S(2)}, u32[]{:S(2)}) collective-permute-start(f32[32,128]{1,0:T(8,128)S(1)} %get-tuple-element.27), channel_id=1, source_target_pairs={{1,0},{2,1},{3,2},{4,3},{5,4},{6,5},{7,6},{8,7},{9,8},{10,9},{11,1... | collective-permute-start | bytes 49160 | tf_op jit(solution)/shard_map/ppermute | solution.py:608
  8.1 2.4 %own_layers.1 = (f32[4,168,128]{2,1,0:T(8,128)S(1)}, f32[200,128]{1,0:T(8,128)S(1)}, f32[200,128]{1,0:T(8,128)S(1)}, f32[2,128,128]{2,1,0:T(8,128)S(1)}, f32[200,128]{1,0:T(8,128)S(1)}, /*index=5*/f32[16,1152]{1,0:T(8,128)S(1)}) custom-call(f32[288,128]{1,0:T(8,128)S(1)} %get-tuple-element.28.own_ref, s32[8,256]{1,0:T(8,128)S(1)} %get-tuple-element.29.code_ref, ...), custom_call_target="tpu_custom_call" | custom-call | flops 300000000 | bytes 1000000 | tf_op jit(solution)/shard_map/own_layers/pallas_call | solution.py:610
  10.6 0.0 collective-permute-done.1.next_ref
  10.6 0.0 collective-permute-done.prev_ref
  10.6 1.7 %near_layers.1 = (f32[2,256,128]{2,1,0:T(8,128)S(1)}, f32[16,1152]{1,0:T(8,128)S(1)}) custom-call(f32[160,128]{1,0:T(8,128)S(1)} %collective-permute-done.prev_ref, f32[32,128]{1,0:T(8,128)S(1)} %collective-permute-done.1.next_ref, f32[200,128]{1,0:T(8,128)S(1)} %get-tuple-element.31.flux_in_ref.near_flux_ref, ...), custom_call_target="tpu_custom_call" | custom-call | flops 200000000 | bytes 1000000 | tf_op jit(solution)/shard_map/near_layers/pallas_call | solution.py:620
  12.3 1.9 %collective-permute-start.2 = (f32[16,1152]{1,0:T(8,128)S(1)}, f32[16,1152]{1,0:T(8,128)S(1)}, u32[]{:S(2)}, u32[]{:S(2)}) collective-permute-start(f32[16,1152]{1,0:T(8,128)S(1)} %get-tuple-element.35), channel_id=1, source_target_pairs={{0,16},{16,0},{1,17},{17,1},{2,18},{18,2},{3,19},{19,3},{4,20},{20... | collective-permute-start | bytes 221192 | tf_op jit(solution)/shard_map/ppermute | solution.py:641
  14.2 0.4 %forces.1.force_ref = f32[2,256,128]{2,1,0:T(8,128)S(1)} custom-call(f32[4,168,128]{2,1,0:T(8,128)S(1)} %get-tuple-element.36.elem_ref, f32[200,128]{1,0:T(8,128)S(1)} %get-tuple-element.37.flux_ref), custom_call_target="tpu_custom_call" | custom-call | flops 200000000 | bytes 1000000 | tf_op jit(solution)/shard_map/forces/pallas_call | solution.py:631
  14.6 2.1 %collective-permute-done.2 = f32[16,1152]{1,0:T(8,128)S(1)} collective-permute-done((f32[16,1152]{1,0:T(8,128)S(1)}, f32[16,1152]{1,0:T(8,128)S(1)}, u32[]{:S(2)}, u32[]{:S(2)}) %collective-permute-start.2) | collective-permute-done | bytes 73760 | tf_op jit(solution)/shard_map/ppermute | solution.py:641
  16.7 2.5 %collective-permute-start.3 = (f32[16,1152]{1,0:T(8,128)S(1)}, f32[16,1152]{1,0:T(8,128)S(1)}, u32[]{:S(2)}, u32[]{:S(2)}) collective-permute-start(f32[16,1152]{1,0:T(8,128)S(1)} %add.7.after_ref.own_ref), channel_id=1, source_target_pairs={{0,15},{1,2},{2,1},{3,4},{4,3},{5,6},{6,5},{7,8},{8,7},{9,10},{10,... | collective-permute-start | bytes 221192 | tf_op jit(solution)/shard_map/ppermute | solution.py:646
  19.2 0.0 collective-permute-start.4
  19.2 0.0 copy-start
  19.2 3.1 %step.1 = (f32[1,17424]{1,0:T(1,128)}, f32[1,17424]{1,0:T(1,128)}, f32[1,17424]{1,0:T(1,128)}, f32[1,17424]{1,0:T(1,128)}) custom-call(f32[2,256,128]{2,1,0:T(8,128)S(1)} %forces.1.force_ref, f32[2,256,128]{2,1,0:T(8,128)S(1)} %get-tuple-element.39.near_win_ref, f32[200,128]{1,0:T(8,128)S(1)} %get-tuple-element.31.flux_in_ref.near_flux_ref, ...), custom_call_target="tpu_custom_call" | custom-call | flops 200000000 | bytes 1000000 | tf_op jit(solution)/shard_map/step/pallas_call | solution.py:650
  22.3 0.9 %collective-permute-done.3.first_ref = f32[16,1152]{1,0:T(8,128)S(1)} collective-permute-done((f32[16,1152]{1,0:T(8,128)S(1)}, f32[16,1152]{1,0:T(8,128)S(1)}, u32[]{:S(2)}, u32[]{:S(2)}) %collective-permute-start.3) | collective-permute-done | bytes 73760 | tf_op jit(solution)/shard_map/ppermute | solution.py:646
  23.3 0.0 collective-permute-done.4.second_ref
  23.3 0.0 copy-done
  23.3 0.8 %band.1 = f32[16,1089]{1,0:T(8,128)} custom-call(s32[1]{0:T(128)} %bitcast.parity_ref, f32[16,1152]{1,0:T(8,128)S(1)} %add.7.after_ref.own_ref, f32[16,1152]{1,0:T(8,128)S(1)} %collective-permute-done.3.first_ref, f32[16,1152]{1,0:T(8,128)S(1)} %collective-permute-done.4.second_ref, bf16[2,16,288]{2,1,0:T(8,128)(2,1)S(1)} %copy-done), custom_call_target="tpu_custom_call" | custom-call | flops 20000000 | bytes 1000000 | tf_op jit(solution)/shard_map/band/pallas_call | solution.py:671
  (1 shorter events, 0.0 us)
Async XLA Ops:
  2.6 8.0 %collective-permute-start = (f32[160,128]{1,0:T(8,128)S(1)}, f32[160,128]{1,0:T(8,128)S(1)}, u32[]{:S(2)}, u32[]{:S(2)}) collective-permute-start(f32[160,128]{1,0:T(8,128)S(1)} %get-tuple-element.25), channel_id=1, source_target_pairs={{0,1},{1,2},{2,3},{3,4},{4,5},{5,6},{6,7},{7,8},{8,9},{9,10},{10,1... | collective-permute-start | bytes 245768 | tf_op jit(solution)/shard_map/ppermute | solution.py:606
  3.1 7.5 %collective-permute-start.1 = (f32[32,128]{1,0:T(8,128)S(1)}, f32[32,128]{1,0:T(8,128)S(1)}, u32[]{:S(2)}, u32[]{:S(2)}) collective-permute-start(f32[32,128]{1,0:T(8,128)S(1)} %get-tuple-element.27), channel_id=1, source_target_pairs={{1,0},{2,1},{3,2},{4,3},{5,4},{6,5},{7,6},{8,7},{9,8},{10,9},{11,1... | collective-permute-start | bytes 49160 | tf_op jit(solution)/shard_map/ppermute | solution.py:608
  12.3 4.4 %collective-permute-start.2 = (f32[16,1152]{1,0:T(8,128)S(1)}, f32[16,1152]{1,0:T(8,128)S(1)}, u32[]{:S(2)}, u32[]{:S(2)}) collective-permute-start(f32[16,1152]{1,0:T(8,128)S(1)} %get-tuple-element.35), channel_id=1, source_target_pairs={{0,16},{16,0},{1,17},{17,1},{2,18},{18,2},{3,19},{19,3},{4,20},{20... | collective-permute-start | bytes 221192 | tf_op jit(solution)/shard_map/ppermute | solution.py:641
  16.7 6.5 %collective-permute-start.3 = (f32[16,1152]{1,0:T(8,128)S(1)}, f32[16,1152]{1,0:T(8,128)S(1)}, u32[]{:S(2)}, u32[]{:S(2)}) collective-permute-start(f32[16,1152]{1,0:T(8,128)S(1)} %add.7.after_ref.own_ref), channel_id=1, source_target_pairs={{0,15},{1,2},{2,1},{3,4},{4,3},{5,6},{6,5},{7,8},{8,7},{9,10},{10,... | collective-permute-start | bytes 221192 | tf_op jit(solution)/shard_map/ppermute | solution.py:646
  19.2 4.0 %collective-permute-start.4 = (f32[16,1152]{1,0:T(8,128)S(1)}, f32[16,1152]{1,0:T(8,128)S(1)}, u32[]{:S(2)}, u32[]{:S(2)}) collective-permute-start(f32[16,1152]{1,0:T(8,128)S(1)} %add.7.after_ref.own_ref), channel_id=1, source_target_pairs={{0,1},{1,0},{2,3},{3,2},{4,5},{5,4},{6,7},{7,6},{8,9},{9,8},{10,11... | collective-permute-start | bytes 221192 | tf_op jit(solution)/shard_map/ppermute | solution.py:647
  19.2 4.0 %copy-start = (bf16[2,16,288]{2,1,0:T(8,128)(2,1)S(1)}, bf16[2,16,288]{2,1,0:T(8,128)(2,1)}, u32[]{:S(2)}) copy-start(bf16[2,16,288]{2,1,0:T(8,128)(2,1)} %constant.22.clone.band_ref) | copy-start | bytes 55300

commit v7 on v6

--- a/solution.py
+++ b/solution.py
@@ -458,7 +458,7 @@
 
 
 def step_kernel(
-    force_ref, near_win_ref, near_flux_ref, prev_ref, fwd_hbm, fwd_speed_hbm, adj_hbm, adj_speed_hbm, mass_hbm, after_ref,
+    force_ref, near_win_ref, near_flux_ref, prev_ref, fwd_hbm, fwd_speed_hbm, adj_hbm, adj_speed_hbm, mass_hbm,
     fwd_out_ref, fwd_speed_out_ref, adj_out_ref, adj_speed_out_ref,
     fwd_ref, fwd_speed_ref, adj_ref, adj_speed_ref, mass_ref, plane_ref, line_ref,
     flux_ref, win_ref, elem_ref, fold_ref, near_ref, sem,
@@ -637,12 +637,6 @@
         name="forces",
     )(held(elem), held(flux))
 
-    if events == 2:
-        other = lax.ppermute(kern, "event", [(0, 1), (1, 0)])
-        other, force = lax.optimization_barrier((other, force))
-        kern = kern + other
-    elif events > 2:
-        kern = lax.psum(kern, "event")
     kern_first = lax.ppermute(kern, "cuts", pairs_first)
     kern_second = lax.ppermute(kern, "cuts", pairs_second)
 
@@ -650,7 +644,7 @@
     outs = pl.pallas_call(
         step_kernel,
         out_shape=[points] * 4,
-        in_specs=[vmem] * 4 + [anywhere] * 5 + [vmem],
+        in_specs=[vmem] * 4 + [anywhere] * 5,
         scratch_shapes=[point_row] * 4
         + [pltpu.VMEM((NPTS,), F32), pltpu.VMEM((4 * 144, LANES), F32), pltpu.VMEM((2, ROWS, LANES), F32)]
         + [flux_block, windows(2), elements(2), line_block, windows(2), dma((5,))],
@@ -666,15 +660,19 @@
         fields[1],
         in_hbm(adjoint_velocity),
         in_hbm(inverse_mass),
-        held(kern),
     )
-    shear_kernel = pl.pallas_call(
+    kern_first, kern_second, *outs = lax.optimization_barrier((kern_first, kern_second, *outs))
+    share = pl.pallas_call(
         band_kernel,
-        out_shape=jax.ShapeDtypeStruct((PXU, PYZ), F32),
+        out_shape=pltpu.VMEM((PXU, PYZ), F32),
         in_specs=[smem] + [vmem] * 4,
         cost_estimate=cost(20000000),
         name="band",
     )(parity, held(kern), held(kern_first), held(kern_second), held(jnp.asarray(band_table())))
+    if events == 2:
+        shear_kernel = share + lax.ppermute(share, "event", [(0, 1), (1, 0)])
+    else:
+        shear_kernel = lax.psum(share, "event")
     return (*outs, shear_kernel)
 
 

time: 24.4 us -> 25.2 us (1.033)
  starting transfers between devices: 10 us -> 11 us
  Pallas kernels: 9.68 us -> 9.04 us
  other arithmetic: 0.01 us -> 0.64 us
    ppermute x1, starting transfers between devices: 2.52 us -> 3.47 us  [on_device(): kern_first = lax.ppermute(kern, 'cuts', pairs_first)]
    ppermute x1, waiting for transfers between devices: 0.92 us -> 0.01 us  [on_device(): kern_first = lax.ppermute(kern, 'cuts', pairs_first)]
    ppermute x1, waiting for transfers between devices: 2.12 us -> 2.94 us  [on_device(): shear_kernel = share + lax.ppermute(share, 'event', [(0, 1), (1, 0)])]
    pallas_call x1, Pallas kernels: 0.85 us -> 0.2 us  [on_device(): pl.pallas_call(band_kernel, out_shape=pltpu.VMEM((PXU, PYZ), F32), in_spe...]
    add x1, other arithmetic: 0.01 us -> 0.64 us  [on_device(): shear_kernel = share + lax.ppermute(share, 'event', [(0, 1), (1, 0)])]
  transfers between devices with their start and end apart: 5 -> 5, of which waited for: 2 -> 1; matrix products, arithmetic and copies ran while one was open for 0% -> 0% of each run, Pallas kernels for 24% -> 24%
where the time goes in v7:
time: 25.2 us; the launch traced here: 25 us
  starting transfers between devices  11 us (44%)
  Pallas kernels  9.04 us (36%)
  waiting for transfers between devices  2.95 us (12%)
  between operations  1.38 us (5%)
  other arithmetic  0.64 us (3%)
    ppermute x1, starting transfers between devices, on_device(): lax.ppermute(left, 'cuts', [((i + 1) % cuts, i) for i in range(cuts)])  5.06 us
    ppermute x1, starting transfers between devices, on_device(): kern_first = lax.ppermute(kern, 'cuts', pairs_first)  3.47 us
    pallas_call x1, Pallas kernels, on_device(): pl.pallas_call(step_kernel, out_shape=[points] * 4, in_specs=[vmem] * 4 +...  3.09 us
    ppermute x1, waiting for transfers between devices, on_device(): shear_kernel = share + lax.ppermute(share, 'event', [(0, 1), (1, 0)])  2.94 us
    pallas_call x1, Pallas kernels, on_device(): pl.pallas_call(own_kernel, out_shape=[elements(4), flux_block, flux_block...  2.43 us
    ppermute x1, starting transfers between devices, on_device(): shear_kernel = share + lax.ppermute(share, 'event', [(0, 1), (1, 0)])  1.93 us
    pallas_call x1, Pallas kernels, on_device(): pl.pallas_call(near_kernel, out_shape=[windows(2), kern_block], in_specs=...  1.68 us
    pallas_call x1, Pallas kernels, on_device(): pl.pallas_call(pack_kernel, out_shape=[pltpu.VMEM((160, LANES), F32), plt...  1.28 us
  transfers between devices with their start and end apart: 5, of which 1 were waited for; matrix products, arithmetic and copies ran while one was open for 0% of the time, Pallas kernels for 24%

profile of v7, /device:TPU:0, one launch (start us, length us, event | category | flops | bytes accessed | tf_op | source)
XLA Modules:
  0.0 25.0 jit_solution(16718031186947229260)
XLA Ops:
  1.3 1.3 %pack.1 = (f32[160,128]{1,0:T(8,128)S(1)}, f32[32,128]{1,0:T(8,128)S(1)}, f32[288,128]{1,0:T(8,128)S(1)}, s32[8,256]{1,0:T(8,128)S(1)}, bf16[480,256]{1,0:T(8,128)(2,1)S(1)}) custom-call(s32[1]{0:T(128)S(6)} %copy.15.count_ref, s32[125,256]{1,0:T(8,128)} %conn_hbm.1, f32[125,256]{1,0:T(8,128)} %shear_hbm.1, f32[1,17424]{1,0:T(1,128)} %fwd_hbm.3, ...), custom_call_target="tpu_custom_call" | custom-call | flops 100000000 | bytes 1000000 | tf_op jit(solution)/shard_map/pack/pallas_call | solution.py:585
  2.6 0.5 %collective-permute-start = (f32[160,128]{1,0:T(8,128)S(1)}, f32[160,128]{1,0:T(8,128)S(1)}, u32[]{:S(2)}, u32[]{:S(2)}) collective-permute-start(f32[160,128]{1,0:T(8,128)S(1)} %get-tuple-element.29), channel_id=1, source_target_pairs={{0,1},{1,2},{2,3},{3,4},{4,5},{5,6},{6,7},{7,8},{8,9},{9,10},{10,1... | collective-permute-start | bytes 245768 | tf_op jit(solution)/shard_map/ppermute | solution.py:606
  3.1 5.1 %collective-permute-start.1 = (f32[32,128]{1,0:T(8,128)S(1)}, f32[32,128]{1,0:T(8,128)S(1)}, u32[]{:S(2)}, u32[]{:S(2)}) collective-permute-start(f32[32,128]{1,0:T(8,128)S(1)} %get-tuple-element.31), channel_id=1, source_target_pairs={{1,0},{2,1},{3,2},{4,3},{5,4},{6,5},{7,6},{8,7},{9,8},{10,9},{11,1... | collective-permute-start | bytes 49160 | tf_op jit(solution)/shard_map/ppermute | solution.py:608
  8.1 2.4 %own_layers.1 = (f32[4,168,128]{2,1,0:T(8,128)S(1)}, f32[200,128]{1,0:T(8,128)S(1)}, f32[200,128]{1,0:T(8,128)S(1)}, f32[2,128,128]{2,1,0:T(8,128)S(1)}, f32[200,128]{1,0:T(8,128)S(1)}, /*index=5*/f32[16,1152]{1,0:T(8,128)S(1)}) custom-call(f32[288,128]{1,0:T(8,128)S(1)} %get-tuple-element.32.own_ref, s32[8,256]{1,0:T(8,128)S(1)} %get-tuple-element.33.code_ref, ...), custom_call_target="tpu_custom_call" | custom-call | flops 300000000 | bytes 1000000 | tf_op jit(solution)/shard_map/own_layers/pallas_call | solution.py:610
  10.6 0.0 collective-permute-done.1.next_ref
  10.6 0.0 collective-permute-done.prev_ref
  10.6 1.7 %near_layers.1 = (f32[2,256,128]{2,1,0:T(8,128)S(1)}, f32[16,1152]{1,0:T(8,128)S(1)}) custom-call(f32[160,128]{1,0:T(8,128)S(1)} %collective-permute-done.prev_ref, f32[32,128]{1,0:T(8,128)S(1)} %collective-permute-done.1.next_ref, f32[200,128]{1,0:T(8,128)S(1)} %get-tuple-element.35.flux_in_ref.near_flux_ref, ...), custom_call_target="tpu_custom_call" | custom-call | flops 200000000 | bytes 1000000 | tf_op jit(solution)/shard_map/near_layers/pallas_call | solution.py:620
  12.3 3.5 %collective-permute-start.2 = (f32[16,1152]{1,0:T(8,128)S(1)}, f32[16,1152]{1,0:T(8,128)S(1)}, u32[]{:S(2)}, u32[]{:S(2)}) collective-permute-start(f32[16,1152]{1,0:T(8,128)S(1)} %get-tuple-element.39.own_ref), channel_id=1, source_target_pairs={{0,15},{1,2},{2,1},{3,4},{4,3},{5,6},{6,5},{7,8},{8,7},{9,10},{10,... | collective-permute-start | bytes 221192 | tf_op jit(solution)/shard_map/ppermute | solution.py:640
  15.8 0.0 collective-permute-start.3
  15.8 0.4 %forces.1.force_ref = f32[2,256,128]{2,1,0:T(8,128)S(1)} custom-call(f32[4,168,128]{2,1,0:T(8,128)S(1)} %get-tuple-element.40.elem_ref, f32[200,128]{1,0:T(8,128)S(1)} %get-tuple-element.41.flux_ref), custom_call_target="tpu_custom_call" | custom-call | flops 200000000 | bytes 1000000 | tf_op jit(solution)/shard_map/forces/pallas_call | solution.py:631
  16.1 0.0 copy-start
  16.1 3.1 %step.1 = (f32[1,17424]{1,0:T(1,128)}, f32[1,17424]{1,0:T(1,128)}, f32[1,17424]{1,0:T(1,128)}, f32[1,17424]{1,0:T(1,128)}) custom-call(f32[2,256,128]{2,1,0:T(8,128)S(1)} %forces.1.force_ref, f32[2,256,128]{2,1,0:T(8,128)S(1)} %get-tuple-element.42.near_win_ref, f32[200,128]{1,0:T(8,128)S(1)} %get-tuple-element.35.flux_in_ref.near_flux_ref, ...), custom_call_target="tpu_custom_call" | custom-call | flops 200000000 | bytes 1000000 | tf_op jit(solution)/shard_map/step/pallas_call | solution.py:644
  19.2 0.0 collective-permute-done.2.first_ref
  19.2 0.0 collective-permute-done.3.second_ref
  19.3 0.0 copy-done
  19.3 0.2 band.1
  19.5 1.9 %collective-permute-start.4 = (f32[16,1089]{1,0:T(8,128)S(1)}, f32[16,1089]{1,0:T(8,128)S(1)}, u32[]{:S(2)}, u32[]{:S(2)}) collective-permute-start(f32[16,1089]{1,0:T(8,128)S(1)} %band.1), channel_id=1, source_target_pairs={{0,16},{16,0},{1,17},{17,1},{2,18},{18,2},{3,19},{19,3},{4,20},{20... | collective-permute-start | bytes 209096 | tf_op jit(solution)/shard_map/ppermute | solution.py:673
  21.4 2.9 %collective-permute-done.4 = f32[16,1089]{1,0:T(8,128)S(1)} collective-permute-done((f32[16,1089]{1,0:T(8,128)S(1)}, f32[16,1089]{1,0:T(8,128)S(1)}, u32[]{:S(2)}, u32[]{:S(2)}) %collective-permute-start.4) | collective-permute-done | bytes 69728 | tf_op jit(solution)/shard_map/ppermute | solution.py:673
  24.3 0.6 %add.8 = f32[16,1089]{1,0:T(8,128)} add(f32[16,1089]{1,0:T(8,128)S(1)} %band.1, f32[16,1089]{1,0:T(8,128)S(1)} %collective-permute-done.4) | non-fusion elementwise | flops 17424 | bytes 209088 | tf_op jit(solution)/shard_map/add | solution.py:673
Async XLA Ops:
  2.6 8.0 %collective-permute-start = (f32[160,128]{1,0:T(8,128)S(1)}, f32[160,128]{1,0:T(8,128)S(1)}, u32[]{:S(2)}, u32[]{:S(2)}) collective-permute-start(f32[160,128]{1,0:T(8,128)S(1)} %get-tuple-element.29), channel_id=1, source_target_pairs={{0,1},{1,2},{2,3},{3,4},{4,5},{5,6},{6,7},{7,8},{8,9},{9,10},{10,1... | collective-permute-start | bytes 245768 | tf_op jit(solution)/shard_map/ppermute | solution.py:606
  3.1 7.5 %collective-permute-start.1 = (f32[32,128]{1,0:T(8,128)S(1)}, f32[32,128]{1,0:T(8,128)S(1)}, u32[]{:S(2)}, u32[]{:S(2)}) collective-permute-start(f32[32,128]{1,0:T(8,128)S(1)} %get-tuple-element.31), channel_id=1, source_target_pairs={{1,0},{2,1},{3,2},{4,3},{5,4},{6,5},{7,6},{8,7},{9,8},{10,9},{11,1... | collective-permute-start | bytes 49160 | tf_op jit(solution)/shard_map/ppermute | solution.py:608
  12.3 7.0 %collective-permute-start.2 = (f32[16,1152]{1,0:T(8,128)S(1)}, f32[16,1152]{1,0:T(8,128)S(1)}, u32[]{:S(2)}, u32[]{:S(2)}) collective-permute-start(f32[16,1152]{1,0:T(8,128)S(1)} %get-tuple-element.39.own_ref), channel_id=1, source_target_pairs={{0,15},{1,2},{2,1},{3,4},{4,3},{5,6},{6,5},{7,8},{8,7},{9,10},{10,... | collective-permute-start | bytes 221192 | tf_op jit(solution)/shard_map/ppermute | solution.py:640
  15.8 3.5 %collective-permute-start.3 = (f32[16,1152]{1,0:T(8,128)S(1)}, f32[16,1152]{1,0:T(8,128)S(1)}, u32[]{:S(2)}, u32[]{:S(2)}) collective-permute-start(f32[16,1152]{1,0:T(8,128)S(1)} %get-tuple-element.39.own_ref), channel_id=1, source_target_pairs={{0,1},{1,0},{2,3},{3,2},{4,5},{5,4},{6,7},{7,6},{8,9},{9,8},{10,11... | collective-permute-start | bytes 221192 | tf_op jit(solution)/shard_map/ppermute | solution.py:641
  16.1 3.1 %copy-start = (bf16[2,16,288]{2,1,0:T(8,128)(2,1)S(1)}, bf16[2,16,288]{2,1,0:T(8,128)(2,1)}, u32[]{:S(2)}) copy-start(bf16[2,16,288]{2,1,0:T(8,128)(2,1)} %constant.22.clone.band_ref) | copy-start | bytes 55300
  19.5 4.9 %collective-permute-start.4 = (f32[16,1089]{1,0:T(8,128)S(1)}, f32[16,1089]{1,0:T(8,128)S(1)}, u32[]{:S(2)}, u32[]{:S(2)}) collective-permute-start(f32[16,1089]{1,0:T(8,128)S(1)} %band.1), channel_id=1, source_target_pairs={{0,16},{16,0},{1,17},{17,1},{2,18},{18,2},{3,19},{19,3},{4,20},{20... | collective-permute-start | bytes 209096 | tf_op jit(solution)/shard_map/ppermute | solution.py:673

commit v8 on v6

--- a/solution.py
+++ b/solution.py
@@ -1,3 +1,5 @@
+import functools
+
 import numpy as np
 import jax
 import jax.numpy as jnp
@@ -17,6 +19,7 @@
 LANES = 128
 ROWS = 144
 TIME_STEP = 0.02
+OWN_OUTS, OWN_SCRATCH = 7, 5
 F32 = jnp.float32
 BF16 = jnp.bfloat16
 
@@ -103,14 +106,20 @@
 
 
 def pack_kernel(
-    count_ref, conn_hbm, shear_hbm, fwd_hbm, adj_hbm,
+    count_hbm, conn_hbm, shear_hbm, fwd_hbm, adj_hbm,
     right_ref, left_ref, own_ref, code_ref, parts_ref,
-    conn_ref, shear_ref, fwd_ref, adj_ref, block_ref, sem,
+    count_ref, conn_ref, shear_ref, fwd_ref, adj_ref, block_ref, sem,
 ):
     copies = fetch(
-        sem, (shear_hbm, shear_ref), (conn_hbm.at[0:8], conn_ref), (fwd_hbm, fwd_ref), (adj_hbm, adj_ref)
+        sem,
+        (shear_hbm, shear_ref),
+        (conn_hbm.at[0:8], conn_ref),
+        (fwd_hbm, fwd_ref),
+        (adj_hbm, adj_ref),
+        (count_hbm, count_ref),
     )
     copies[1].wait()
+    copies[4].wait()
     point = conn_ref[0:1, :].astype(F32)
     x = jnp.floor((point + 0.5) * (1.0 / PYZ))
     rest = point - x * PYZ
@@ -131,14 +140,13 @@
         right_ref[40 * f : 40 * f + 40, :] = own_ref[ROWS * f + 102 : ROWS * f + 142, :]
         left_ref[16 * f : 16 * f + 16, :] = own_ref[ROWS * f : ROWS * f + 16, :]
     copies[0].wait()
-    block_ref[...] = jnp.zeros(block_ref.shape, F32)
-    for i in range(NGLL):
-        block_ref[32 * i : 32 * i + 25, :] = shear_ref[25 * i : 25 * i + 25, :]
+    block_ref[0:125, :] = shear_ref[...]
+    block_ref[125:128, :] = jnp.zeros((3, 256), F32)
     parts = jnp.concatenate(split3(block_ref[...]), axis=0)
     parts_ref[...] = parts
     flux = add_parts(dot_nt(parts, pick))
-    low = lax.broadcasted_iota(jnp.int32, (80, LANES), 1) < 64
-    right_ref[80:160, :] = jnp.where(low, flux[0:80], flux[80:160])
+    low = lax.broadcasted_iota(jnp.int32, (64, LANES), 1) < 64
+    right_ref[80:144, :] = jnp.where(low, flux[0:64], flux[64:128])
 
 
 def gll_weight(i):
@@ -310,12 +318,20 @@
     return tiles
 
 
-def own_kernel(
-    own_ref, code_ref, parts_ref, cross_hbm,
-    elem_ref, flux_ref, near_flux_ref, near_win_ref, near_kern_ref, kern_ref,
-    cross_ref, plane_ref, win_ref, line_ref, near_elem_ref, sem,
+def own_kernel(turn, cut_ref, own_ref, code_ref, parts_ref, cross_ref, *refs):
+    refs = refs[-OWN_OUTS - OWN_SCRATCH :]
+    mine = (cut_ref[0] == 0) if turn == 0 else (cut_ref[0] != 0)
+
+    @pl.when(mine)
+    def _():
+        own_layers(own_ref, code_ref, parts_ref, cross_ref, *refs)
+
+
+def own_layers(
+    own_ref, code_ref, parts_ref, cross_ref,
+    elem_ref, flux_ref, near_flux_ref, near_win_ref, near_slope_ref, near_kern_ref, kern_ref,
+    plane_ref, win_ref, line_ref, near_elem_ref, moved_ref,
 ):
-    copies = fetch(sem, (cross_hbm, cross_ref))
     plane_ref[...] = jnp.zeros(plane_ref.shape, F32)
     for f in range(2):
         base = 24 * 9 * f
@@ -337,14 +353,23 @@
     for column in range(4):
         turned(win_ref, 128 * column, elem_ref, column)
     turned(near_win_ref, 0, near_elem_ref, 0)
+    near_slope_ref[...] = jnp.zeros(near_slope_ref.shape, F32)
+    for f in range(2):
+        for w in range(2):
+            value = [near_win_ref[w, 64 * f + 8 * c : 64 * f + 8 * c + 8, :] for c in (0, 4, 5, 6, 7)]
+            near_slope_ref[w, 64 * f : 64 * f + 8, :] = float(DERIV[4, 4]) * value[0]
+            for i, v in enumerate(derive(value[1:] + [jnp.zeros((8, LANES), F32)])[:4]):
+                r = 64 * f + 8 * NEAR_AT[1][i]
+                near_slope_ref[w, r : r + 8, :] = v
 
     element = lax.broadcasted_iota(jnp.int32, (256, 256), 0)
     pick = jnp.where(code_ref[0:1, :] == element, 1.0, 0.0).astype(BF16)
-    moved = add_parts(dot_nt(parts_ref[...], pick))
+    moved_ref[0:128, :] = add_parts(dot_nt(parts_ref[...], pick))
+    moved_ref[128:136, :] = jnp.zeros((8, 256), F32)
 
     def tile_of(i, ez):
         t = ez // 4
-        return moved[32 * i : 32 * i + 32, t * LANES : (t + 1) * LANES], 32 * (ez % 4)
+        return moved_ref[25 * i : 25 * i + 32, t * LANES : (t + 1) * LANES], 32 * (ez % 4)
 
     place_flux(flux_ref, tile_of, lambda i: [(0, 24 * i, 24)])
     place_flux(near_flux_ref, tile_of, lambda i: [(24, 8 * NEAR_AT[1][i], 8)])
@@ -372,46 +397,42 @@
         first = low[t] + jnp.where((row == 1) | (row == 2), pltpu.roll(high[t], 5, 0), 0.0)
         second = jnp.where(row < 4, high[t], jnp.where(row == 4, pltpu.roll(high[t], 6, 0), 0.0))
         tiles.append(jnp.concatenate([first, second], axis=0))
-    copies[0].wait()
     for t, tile in enumerate(cross_smoothed(tiles, cross_ref)):
         kern_ref[:, t * LANES : (t + 1) * LANES] = tile
 
 
-def message_flux(prev_ref):
-    def tile_of(i, ez):
-        blocks = []
-        for r in range(32 * i, 32 * i + 32, 16):
-            at = 80 + r % 80
-            blocks.append((prev_ref[at : at + 16, :], 64 * (r // 80)))
-        (a, p), (b, q) = blocks
-        if p != q:
-            b = pltpu.roll(b, 64, 1)
-        return jnp.concatenate([a, b], axis=0), 8 * ez + p
-
-    return tile_of
+def message_flux(prev_ref, spread_ref):
+    spread_ref[0:64, :] = prev_ref[80:144, :]
+    spread_ref[64:128, :] = pltpu.roll(prev_ref[80:144, :], 64, 1)
+    spread_ref[128:136, :] = jnp.zeros((8, LANES), F32)
+    return lambda i, ez: (spread_ref[25 * i : 25 * i + 32, :], 8 * ez)
 
 
 def near_kernel(
-    prev_ref, next_ref, flux_in_ref, near_in_ref, near_kern_ref, kern_in_ref, cross_hbm,
-    near_win_ref, kern_ref,
-    cross_ref, plane_ref, win_ref, elem_ref, flux_ref, line_ref, sem,
+    prev_ref, next_ref, flux_in_ref, slope_ref, near_kern_ref, kern_in_ref, cross_ref,
+    kern_ref,
+    plane_ref, new_ref, win_ref, elem_ref, flux_ref, line_ref, spread_ref,
 ):
-    copies = fetch(sem, (cross_hbm, cross_ref))
     plane_ref[...] = jnp.zeros(plane_ref.shape, F32)
     for f in range(2):
-        for i in range(5):
-            flat = plane_of(prev_ref, 12 + PYZ * i, 40 * f) if i < 4 else plane_of(next_ref, 0, 16 * f)
-            plane_ref[pl.ds(72 * f + i, 9, stride=8), :] = flat
-        near_win_ref[:, 128 * f : 128 * f + 64, :] = near_in_ref[:, 64 * f : 64 * f + 64, :]
-        make_windows(plane_ref, 72 * f, 8, near_win_ref, 128 * f + 64)
-        win_ref[:, 64 * f : 64 * f + 64, :] = jnp.zeros((2, 64, LANES), F32)
-        for layer, row in enumerate(NEAR_AT):
-            for w, i, v in along_x(near_win_ref, 128 * f, row, derive):
-                if (layer == 0) == (i == 4):
-                    r = 64 * f + 8 * row[i]
-                    win_ref[w, r : r + 8, :] = v
+        share = None
+        for l in range(4):
+            term = float(DERIV[4, l]) * plane_of(prev_ref, 12 + PYZ * l, 40 * f)
+            share = term if share is None else share + term
+        plane_ref[pl.ds(f, 9, stride=8), :] = share
+        plane_ref[pl.ds(2 + f, 9, stride=8), :] = plane_of(next_ref, 0, 16 * f)
+    make_windows(plane_ref, 0, 8, new_ref, 0)
+    win_ref[...] = slope_ref[...]
+    for f in range(2):
+        for w in range(2):
+            r = 64 * f
+            win_ref[w, r : r + 8, :] = win_ref[w, r : r + 8, :] + new_ref[w, 8 * f : 8 * f + 8, :]
+            for i in range(4):
+                r = 64 * f + 8 * NEAR_AT[1][i]
+                new = float(DERIV[i, 4]) * new_ref[w, 16 + 8 * f : 24 + 8 * f, :]
+                win_ref[w, r : r + 8, :] = win_ref[w, r : r + 8, :] + new
     turned(win_ref, 0, elem_ref, 0)
-    place_flux(flux_ref, message_flux(prev_ref), lambda i: [(0, 8 * NEAR_AT[0][i], 8)], (4,))
+    place_flux(flux_ref, message_flux(prev_ref, spread_ref), lambda i: [(0, 8 * NEAR_AT[0][i], 8)], (4,))
     scaled(flux_ref, lane_weight([NEAR_AT[0]]))
     kern = [[None] * 5 for _ in range(5)]
     for j in range(5):
@@ -422,7 +443,6 @@
     folded(kern, line_ref, win_ref, 0)
     row = lax.broadcasted_iota(jnp.int32, (8, LANES), 0)
     tiles = [jnp.where((row == 0) | (row >= 4), v, 0.0) for v in gathered(win_ref, 0, 0)]
-    copies[0].wait()
     for t, tile in enumerate(cross_smoothed(tiles, cross_ref)):
         columns = slice(t * LANES, (t + 1) * LANES)
         kern_ref[0:8, columns] = kern_in_ref[0:8, columns] + jnp.where(row == 0, tile, 0.0)
@@ -458,10 +478,10 @@
 
 
 def step_kernel(
-    force_ref, near_win_ref, near_flux_ref, prev_ref, fwd_hbm, fwd_speed_hbm, adj_hbm, adj_speed_hbm, mass_hbm, after_ref,
+    force_ref, near_half_ref, near_flux_ref, prev_ref, next_ref, fwd_hbm, fwd_speed_hbm, adj_hbm, adj_speed_hbm, mass_hbm, after_ref,
     fwd_out_ref, fwd_speed_out_ref, adj_out_ref, adj_speed_out_ref,
     fwd_ref, fwd_speed_ref, adj_ref, adj_speed_ref, mass_ref, plane_ref, line_ref,
-    flux_ref, win_ref, elem_ref, fold_ref, near_ref, sem,
+    flux_ref, win_ref, elem_ref, fold_ref, near_ref, near_win_ref, near_plane_ref, spread_ref, sem,
 ):
     copies = fetch(
         sem,
@@ -472,7 +492,14 @@
         (mass_hbm, mass_ref),
     )
     lane9 = lax.broadcasted_iota(jnp.int32, (9, LANES), 1)
-    place_flux(flux_ref, message_flux(prev_ref), lambda i: [(0, 8 * NEAR_AT[0][i], 8)])
+    near_plane_ref[...] = jnp.zeros(near_plane_ref.shape, F32)
+    for f in range(2):
+        for i in range(5):
+            flat = plane_of(prev_ref, 12 + PYZ * i, 40 * f) if i < 4 else plane_of(next_ref, 0, 16 * f)
+            near_plane_ref[pl.ds(72 * f + i, 9, stride=8), :] = flat
+        near_win_ref[:, 128 * f : 128 * f + 64, :] = near_half_ref[:, 64 * f : 64 * f + 64, :]
+        make_windows(near_plane_ref, 72 * f, 8, near_win_ref, 128 * f + 64)
+    place_flux(flux_ref, message_flux(prev_ref, spread_ref), lambda i: [(0, 8 * NEAR_AT[0][i], 8)])
     scaled(flux_ref, lane_weight([NEAR_AT[0]]))
     flux_ref[...] = flux_ref[...] + near_flux_ref[...]
     for f in range(2):
@@ -526,14 +553,14 @@
     step(NPTS - 16, NPTS, [line_ref[f, 136:137, 0:16] for f in range(2)])
 
 
-def band_kernel(parity_ref, own_ref, first_ref, second_ref, band_ref, out_ref):
+def band_kernel(cut_ref, own_ref, first_ref, second_ref, band_ref, out_ref):
     flat = jnp.concatenate([own_ref[...], first_ref[...], second_ref[...]], axis=0)
     k1 = flat.astype(BF16)
     rest = flat - k1.astype(F32)
     k2 = rest.astype(BF16)
     k3 = (rest - k2.astype(F32)).astype(BF16)
     stacked = jnp.concatenate([k1, k2, k3, k1, k2, k1], axis=0)
-    band = band_ref[parity_ref[0]]
+    band = band_ref[cut_ref[0] & 1]
     out_ref[...] = jnp.dot(band, stacked, preferred_element_type=F32)[:, :PYZ]
 
 
@@ -550,7 +577,7 @@
 ):
     events = lax.axis_size("event")
     cuts = lax.axis_size("cuts")
-    parity = (lax.axis_index("cuts") % 2).astype(jnp.int32).reshape(1)
+    cut = lax.axis_index("cuts").astype(jnp.int32).reshape(1)
     pairs_first = [(i, (i - 1 if i % 2 == 0 else i + 1) % cuts) for i in range(cuts)]
     pairs_second = [(i, (i + 1 if i % 2 == 0 else i - 1) % cuts) for i in range(cuts)]
 
@@ -571,7 +598,6 @@
     point_row = pltpu.VMEM((1, NPTS), F32)
     flux_block = pltpu.VMEM((200, LANES), F32)
     kern_block = pltpu.VMEM((16, 9 * LANES), F32)
-    cross_block = pltpu.VMEM((24, 9 * LANES), F32)
     line_block = pltpu.VMEM((256, LANES), F32)
 
     def elements(n):
@@ -581,52 +607,70 @@
         return pltpu.VMEM((2, n * LANES, LANES), F32)
 
     fields = (in_hbm(forward_displacement), in_hbm(adjoint_displacement))
-    cross = in_hbm(jnp.asarray(cross_table()))
+    cross = held(jnp.asarray(cross_table()))
     right, left, own, code, parts = pl.pallas_call(
         pack_kernel,
         out_shape=[
-            pltpu.VMEM((160, LANES), F32),
+            pltpu.VMEM((144, LANES), F32),
             pltpu.VMEM((32, LANES), F32),
             pltpu.VMEM((2 * ROWS, LANES), F32),
             pltpu.VMEM((8, 256), jnp.int32),
-            pltpu.VMEM((480, 256), BF16),
+            pltpu.VMEM((384, 256), BF16),
         ],
-        in_specs=[smem] + [anywhere] * 4,
+        in_specs=[anywhere] * 5,
         scratch_shapes=[
+            pltpu.SMEM((1,), jnp.int32),
             pltpu.VMEM((8, 256), jnp.int32),
             pltpu.VMEM((125, 256), F32),
             point_row,
             point_row,
-            pltpu.VMEM((160, 256), F32),
-            dma((4,)),
+            pltpu.VMEM((128, 256), F32),
+            dma((5,)),
         ],
         cost_estimate=cost(100000000),
         name="pack",
     )(element_count, in_hbm(connectivity), in_hbm(shear_modulus), *fields)
     prev = lax.ppermute(right, "cuts", [(i, (i + 1) % cuts) for i in range(cuts)])
-    left, right = lax.optimization_barrier((left, right))
+
+    own_blocks = [elements(4), flux_block, flux_block, windows(1), windows(1), flux_block, kern_block]
+
+    def own_part(turn, before):
+        given = (cut, held(own), held(code), held(parts), cross)
+        return pl.pallas_call(
+            functools.partial(own_kernel, turn),
+            out_shape=own_blocks,
+            in_specs=[smem] + [vmem] * (4 + len(before)),
+            scratch_shapes=[
+                pltpu.VMEM((2 * 9 * 24, LANES), F32),
+                windows(4),
+                line_block,
+                elements(1),
+                pltpu.VMEM((136, 256), F32),
+            ],
+            input_output_aliases={len(given) + n: n for n in range(len(before))},
+            cost_estimate=cost(300000000),
+            name="own_layers",
+        )(*given, *[held(block) for block in before])
+
+    left, *blocks = lax.optimization_barrier((left, *own_part(0, [])))
     after = lax.ppermute(left, "cuts", [((i + 1) % cuts, i) for i in range(cuts)])
-
-    elem, flux, near_flux, near_win, near_kern, kern = pl.pallas_call(
-        own_kernel,
-        out_shape=[elements(4), flux_block, flux_block, windows(1), flux_block, kern_block],
-        in_specs=[vmem] * 3 + [anywhere],
+    elem, flux, near_flux, near_win, near_slope, near_kern, kern = own_part(1, blocks)
+    kern = pl.pallas_call(
+        near_kernel,
+        out_shape=kern_block,
+        in_specs=[vmem] * 7,
         scratch_shapes=[
-            cross_block, pltpu.VMEM((2 * 9 * 24, LANES), F32), windows(4), line_block, elements(1), dma((1,))
-        ],
-        cost_estimate=cost(300000000),
-        name="own_layers",
-    )(held(own), held(code), held(parts), cross)
-    near_win, kern = pl.pallas_call(
-        near_kernel,
-        out_shape=[windows(2), kern_block],
-        in_specs=[vmem] * 6 + [anywhere],
-        scratch_shapes=[
-            cross_block, pltpu.VMEM((2 * 72, LANES), F32), windows(1), elements(1), flux_block, line_block, dma((1,))
+            pltpu.VMEM((72, LANES), F32),
+            pltpu.VMEM((2, 64, LANES), F32),
+            windows(1),
+            elements(1),
+            flux_block,
+            line_block,
+            pltpu.VMEM((136, LANES), F32),
         ],
         cost_estimate=cost(200000000),
         name="near_layers",
-    )(held(prev), held(after), held(near_flux), held(near_win), held(near_kern), held(kern), cross)
+    )(held(prev), held(after), held(near_flux), held(near_slope), held(near_kern), held(kern), cross)
 
     (force,) = pl.pallas_call(
         force_kernel,
@@ -650,10 +694,11 @@
     outs = pl.pallas_call(
         step_kernel,
         out_shape=[points] * 4,
-        in_specs=[vmem] * 4 + [anywhere] * 5 + [vmem],
+        in_specs=[vmem] * 5 + [anywhere] * 5 + [vmem],
         scratch_shapes=[point_row] * 4
         + [pltpu.VMEM((NPTS,), F32), pltpu.VMEM((4 * 144, LANES), F32), pltpu.VMEM((2, ROWS, LANES), F32)]
-        + [flux_block, windows(2), elements(2), line_block, windows(2), dma((5,))],
+        + [flux_block, windows(2), elements(2), line_block, windows(2), windows(2)]
+        + [pltpu.VMEM((2 * 72, LANES), F32), pltpu.VMEM((136, LANES), F32), dma((5,))],
         cost_estimate=cost(200000000),
         name="step",
     )(
@@ -661,6 +706,7 @@
         held(near_win),
         held(near_flux),
         held(prev),
+        held(after),
         fields[0],
         in_hbm(forward_velocity),
         fields[1],
@@ -674,7 +720,7 @@
         in_specs=[smem] + [vmem] * 4,
         cost_estimate=cost(20000000),
         name="band",
-    )(parity, held(kern), held(kern_first), held(kern_second), held(jnp.asarray(band_table())))
+    )(cut, held(kern), held(kern_first), held(kern_second), held(jnp.asarray(band_table())))
     return (*outs, shear_kernel)
 
 

time: 24.4 us -> 23.2 us (0.951)
  Pallas kernels: 9.68 us -> 7.95 us
  waiting for transfers between devices: 3.05 us -> 4.66 us
  starting transfers between devices: 10 us -> 8.99 us
    pallas_call x4 -> x5, Pallas kernels: 8.48 us -> 6.74 us  [the longest x1 2.91 us: on_device(): pl.pallas_call(step_kernel, out_shape=[points] * 4, in_specs=[vmem] * 5 +...]
    ppermute x1, starting transfers between devices: 5.06 us -> 3.48 us  [on_device(): lax.ppermute(left, 'cuts', [((i + 1) % cuts, i) for i in range(cuts)])]
    ppermute x1, waiting for transfers between devices: 0.01 us -> 1.44 us  [on_device(): lax.ppermute(left, 'cuts', [((i + 1) % cuts, i) for i in range(cuts)])]
    ppermute x1, waiting for transfers between devices: 0.01 us -> 0.49 us  [on_device(): lax.ppermute(right, 'cuts', [(i, (i + 1) % cuts) for i in range(cuts)])]
    ppermute x1, starting transfers between devices: 2.52 us -> 2.94 us  [on_device(): kern_first = lax.ppermute(kern, 'cuts', pairs_first)]
    ppermute x1, waiting for transfers between devices: 0.92 us -> 0.66 us  [on_device(): kern_first = lax.ppermute(kern, 'cuts', pairs_first)]
  transfers between devices with their start and end apart: 5 -> 5, of which waited for: 2 -> 4; matrix products, arithmetic and copies ran while one was open for 0% -> 0% of each run, Pallas kernels for 24% -> 21%
where the time goes in v8:
time: 23.2 us; the launch traced here: 23 us
  starting transfers between devices  8.99 us (39%)
  Pallas kernels  7.95 us (34%)
  waiting for transfers between devices  4.66 us (20%)
  between operations  1.35 us (6%)
    ppermute x1, starting transfers between devices, on_device(): lax.ppermute(left, 'cuts', [((i + 1) % cuts, i) for i in range(cuts)])  3.48 us
    ppermute x1, starting transfers between devices, on_device(): kern_first = lax.ppermute(kern, 'cuts', pairs_first)  2.94 us
    pallas_call x1, Pallas kernels, on_device(): pl.pallas_call(step_kernel, out_shape=[points] * 4, in_specs=[vmem] * 5 +...  2.91 us
    ppermute x1, waiting for transfers between devices, on_device(): other = lax.ppermute(kern, 'event', [(0, 1), (1, 0)])  2.05 us
    ppermute x1, starting transfers between devices, on_device(): other = lax.ppermute(kern, 'event', [(0, 1), (1, 0)])  2 us
    pallas_call x2, Pallas kernels, own_part(): pl.pallas_call(functools.partial(own_kernel, turn), out_shape=own_blocks,...  1.6 us
    ppermute x1, waiting for transfers between devices, on_device(): lax.ppermute(left, 'cuts', [((i + 1) % cuts, i) for i in range(cuts)])  1.44 us
    pallas_call x1, Pallas kernels, on_device(): pl.pallas_call(pack_kernel, out_shape=[pltpu.VMEM((144, LANES), F32), plt...  1.3 us
  transfers between devices with their start and end apart: 5, of which 4 were waited for; matrix products, arithmetic and copies ran while one was open for 0% of the time, Pallas kernels for 21%

profile of v8, /device:TPU:0, one launch (start us, length us, event | category | flops | bytes accessed | tf_op | source)
XLA Modules:
  0.0 23.0 jit_solution(337193449159621277)
XLA Ops:
  1.3 0.0 copy-start
  1.3 1.3 %pack.1 = (f32[144,128]{1,0:T(8,128)S(1)}, f32[32,128]{1,0:T(8,128)S(1)}, f32[288,128]{1,0:T(8,128)S(1)}, s32[8,256]{1,0:T(8,128)S(1)}, bf16[384,256]{1,0:T(8,128)(2,1)S(1)}) custom-call(s32[1]{0:T(128)S(6)} %copy.29.count_hbm, s32[125,256]{1,0:T(8,128)} %conn_hbm.1, f32[125,256]{1,0:T(8,128)} %shear_hbm.1, f32[1,17424]{1,0:T(1,128)} %fwd_hbm.3, ...), custom_call_target="tpu_custom_call" | custom-call | flops 100000000 | bytes 1000000 | tf_op jit(solution)/shard_map/pack/pallas_call | solution.py:611
  2.6 0.5 %collective-permute-start = (f32[144,128]{1,0:T(8,128)S(1)}, f32[144,128]{1,0:T(8,128)S(1)}, u32[]{:S(2)}, u32[]{:S(2)}) collective-permute-start(f32[144,128]{1,0:T(8,128)S(1)} %get-tuple-element.38), channel_id=1, source_target_pairs={{0,1},{1,2},{2,3},{3,4},{4,5},{5,6},{6,7},{7,8},{8,9},{9,10},{10,1... | collective-permute-start | bytes 221192 | tf_op jit(solution)/shard_map/ppermute | solution.py:633
  3.1 0.0 copy-done
  3.1 1.6 %own_layers.2 = (f32[4,168,128]{2,1,0:T(8,128)S(1)}, f32[200,128]{1,0:T(8,128)S(1)}, f32[200,128]{1,0:T(8,128)S(1)}, f32[2,128,128]{2,1,0:T(8,128)S(1)}, f32[2,1...) custom-call(s32[1]{0:T(128)} %bitcast.cut_ref, f32[288,128]{1,0:T(8,128)S(1)} %get-tuple-element.40.own_ref, ...), custom_call_target="tpu_custom_call" | custom-call | flops 300000000 | bytes 1000000 | tf_op jit(solution)/shard_map/own_layers/pallas_call | solution.py:639
  4.7 3.5 %collective-permute-start.1 = (f32[32,128]{1,0:T(8,128)S(1)}, f32[32,128]{1,0:T(8,128)S(1)}, u32[]{:S(2)}, u32[]{:S(2)}) collective-permute-start(f32[32,128]{1,0:T(8,128)S(1)} %get-tuple-element.50), channel_id=1, source_target_pairs={{1,0},{2,1},{3,2},{4,3},{5,4},{6,5},{7,6},{8,7},{9,8},{10,9},{11,1... | collective-permute-start | bytes 49160 | tf_op jit(solution)/shard_map/ppermute | solution.py:656
  8.2 1.4 %collective-permute-done.1.next_ref = f32[32,128]{1,0:T(8,128)S(1)} collective-permute-done((f32[32,128]{1,0:T(8,128)S(1)}, f32[32,128]{1,0:T(8,128)S(1)}, u32[]{:S(2)}, u32[]{:S(2)}) %collective-permute-start.1) | collective-permute-done | bytes 16416 | tf_op jit(solution)/shard_map/ppermute | solution.py:656
  9.6 0.5 %collective-permute-done.prev_ref = f32[144,128]{1,0:T(8,128)S(1)} collective-permute-done((f32[144,128]{1,0:T(8,128)S(1)}, f32[144,128]{1,0:T(8,128)S(1)}, u32[]{:S(2)}, u32[]{:S(2)}) %collective-permute-start) | collective-permute-done | bytes 73760 | tf_op jit(solution)/shard_map/ppermute | solution.py:633
  10.1 0.9 %near_layers.1 = f32[16,1152]{1,0:T(8,128)S(1)} custom-call(f32[144,128]{1,0:T(8,128)S(1)} %collective-permute-done.prev_ref, f32[32,128]{1,0:T(8,128)S(1)} %collective-permute-done.1.next_ref, f32[200,128]{1,0:T(8,128)S(1)} %get-tuple-element.58.flux_in_ref.near_flux_ref, f32[2,128,128]{2,1,0:T(8,128)S(1)} %get-tuple-element.59.slope_ref, ...), custom_call_target="tpu_custom_call" | custom-call | flops 200000000 | bytes 1000000 | tf_op jit(solution)/shard_map/near_layers/pallas_call | solution.py:658
  11.1 2.0 %collective-permute-start.2 = (f32[16,1152]{1,0:T(8,128)S(1)}, f32[16,1152]{1,0:T(8,128)S(1)}, u32[]{:S(2)}, u32[]{:S(2)}) collective-permute-start(f32[16,1152]{1,0:T(8,128)S(1)} %near_layers.1), channel_id=1, source_target_pairs={{0,16},{16,0},{1,17},{17,1},{2,18},{18,2},{3,19},{19,3},{4,20},{20... | collective-permute-start | bytes 221192 | tf_op jit(solution)/shard_map/ppermute | solution.py:685
  13.1 0.4 %forces.1.force_ref = f32[2,256,128]{2,1,0:T(8,128)S(1)} custom-call(f32[4,168,128]{2,1,0:T(8,128)S(1)} %get-tuple-element.62.elem_ref, f32[200,128]{1,0:T(8,128)S(1)} %get-tuple-element.63.flux_ref), custom_call_target="tpu_custom_call" | custom-call | flops 200000000 | bytes 1000000 | tf_op jit(solution)/shard_map/forces/pallas_call | solution.py:675
  13.4 2.1 %collective-permute-done.2 = f32[16,1152]{1,0:T(8,128)S(1)} collective-permute-done((f32[16,1152]{1,0:T(8,128)S(1)}, f32[16,1152]{1,0:T(8,128)S(1)}, u32[]{:S(2)}, u32[]{:S(2)}) %collective-permute-start.2) | collective-permute-done | bytes 73760 | tf_op jit(solution)/shard_map/ppermute | solution.py:685
  15.5 0.1 collective-permute-start.4
  15.6 2.9 %collective-permute-start.3 = (f32[16,1152]{1,0:T(8,128)S(1)}, f32[16,1152]{1,0:T(8,128)S(1)}, u32[]{:S(2)}, u32[]{:S(2)}) collective-permute-start(f32[16,1152]{1,0:T(8,128)S(1)} %add.3.after_ref.own_ref), channel_id=1, source_target_pairs={{0,15},{1,2},{2,1},{3,4},{4,3},{5,6},{6,5},{7,8},{8,7},{9,10},{10,... | collective-permute-start | bytes 221192 | tf_op jit(solution)/shard_map/ppermute | solution.py:690
  18.5 0.0 copy-start.1
  18.5 2.9 %step.1 = (f32[1,17424]{1,0:T(1,128)}, f32[1,17424]{1,0:T(1,128)}, f32[1,17424]{1,0:T(1,128)}, f32[1,17424]{1,0:T(1,128)}) custom-call(f32[2,256,128]{2,1,0:T(8,128)S(1)} %forces.1.force_ref, f32[2,128,128]{2,1,0:T(8,128)S(1)} %get-tuple-element.65.near_half_ref, f32[200,128]{1,0:T(8,128)S(1)} %get-tuple-element.58.flux_in_ref.near_flux_ref, ...), custom_call_target="tpu_custom_call" | custom-call | flops 200000000 | bytes 1000000 | tf_op jit(solution)/shard_map/step/pallas_call | solution.py:694
  21.4 0.0 collective-permute-done.4.second_ref
  21.4 0.7 %collective-permute-done.3.first_ref = f32[16,1152]{1,0:T(8,128)S(1)} collective-permute-done((f32[16,1152]{1,0:T(8,128)S(1)}, f32[16,1152]{1,0:T(8,128)S(1)}, u32[]{:S(2)}, u32[]{:S(2)}) %collective-permute-start.3) | collective-permute-done | bytes 73760 | tf_op jit(solution)/shard_map/ppermute | solution.py:690
  22.1 0.0 copy-done.1
  22.1 0.8 %band.1 = f32[16,1089]{1,0:T(8,128)} custom-call(s32[1]{0:T(128)} %bitcast.cut_ref, f32[16,1152]{1,0:T(8,128)S(1)} %add.3.after_ref.own_ref, f32[16,1152]{1,0:T(8,128)S(1)} %collective-permute-done.3.first_ref, f32[16,1152]{1,0:T(8,128)S(1)} %collective-permute-done.4.second_ref, bf16[2,16,288]{2,1,0:T(8,128)(2,1)S(1)} %copy-done.1), custom_call_target="tpu_custom_call" | custom-call | flops 20000000 | bytes 1000000 | tf_op jit(solution)/shard_map/band/pallas_call | solution.py:717
  (2 shorter events, 0.0 us)
Async XLA Ops:
  1.3 1.8 %copy-start = (f32[24,1152]{1,0:T(8,128)S(1)}, f32[24,1152]{1,0:T(8,128)}, u32[]{:S(2)}) copy-start(f32[24,1152]{1,0:T(8,128)} %constant.8.clone.cross_ref) | copy-start | bytes 331780
  2.6 7.5 %collective-permute-start = (f32[144,128]{1,0:T(8,128)S(1)}, f32[144,128]{1,0:T(8,128)S(1)}, u32[]{:S(2)}, u32[]{:S(2)}) collective-permute-start(f32[144,128]{1,0:T(8,128)S(1)} %get-tuple-element.38), channel_id=1, source_target_pairs={{0,1},{1,2},{2,3},{3,4},{4,5},{5,6},{6,7},{7,8},{8,9},{9,10},{10,1... | collective-permute-start | bytes 221192 | tf_op jit(solution)/shard_map/ppermute | solution.py:633
  4.7 4.9 %collective-permute-start.1 = (f32[32,128]{1,0:T(8,128)S(1)}, f32[32,128]{1,0:T(8,128)S(1)}, u32[]{:S(2)}, u32[]{:S(2)}) collective-permute-start(f32[32,128]{1,0:T(8,128)S(1)} %get-tuple-element.50), channel_id=1, source_target_pairs={{1,0},{2,1},{3,2},{4,3},{5,4},{6,5},{7,6},{8,7},{9,8},{10,9},{11,1... | collective-permute-start | bytes 49160 | tf_op jit(solution)/shard_map/ppermute | solution.py:656
  11.1 4.4 %collective-permute-start.2 = (f32[16,1152]{1,0:T(8,128)S(1)}, f32[16,1152]{1,0:T(8,128)S(1)}, u32[]{:S(2)}, u32[]{:S(2)}) collective-permute-start(f32[16,1152]{1,0:T(8,128)S(1)} %near_layers.1), channel_id=1, source_target_pairs={{0,16},{16,0},{1,17},{17,1},{2,18},{18,2},{3,19},{19,3},{4,20},{20... | collective-permute-start | bytes 221192 | tf_op jit(solution)/shard_map/ppermute | solution.py:685
  15.5 5.9 %collective-permute-start.4 = (f32[16,1152]{1,0:T(8,128)S(1)}, f32[16,1152]{1,0:T(8,128)S(1)}, u32[]{:S(2)}, u32[]{:S(2)}) collective-permute-start(f32[16,1152]{1,0:T(8,128)S(1)} %add.3.after_ref.own_ref), channel_id=1, source_target_pairs={{0,1},{1,0},{2,3},{3,2},{4,5},{5,4},{6,7},{7,6},{8,9},{9,8},{10,11... | collective-permute-start | bytes 221192 | tf_op jit(solution)/shard_map/ppermute | solution.py:691
  15.6 6.5 %collective-permute-start.3 = (f32[16,1152]{1,0:T(8,128)S(1)}, f32[16,1152]{1,0:T(8,128)S(1)}, u32[]{:S(2)}, u32[]{:S(2)}) collective-permute-start(f32[16,1152]{1,0:T(8,128)S(1)} %add.3.after_ref.own_ref), channel_id=1, source_target_pairs={{0,15},{1,2},{2,1},{3,4},{4,3},{5,6},{6,5},{7,8},{8,7},{9,10},{10,... | collective-permute-start | bytes 221192 | tf_op jit(solution)/shard_map/ppermute | solution.py:690
  18.5 3.6 %copy-start.1 = (bf16[2,16,288]{2,1,0:T(8,128)(2,1)S(1)}, bf16[2,16,288]{2,1,0:T(8,128)(2,1)}, u32[]{:S(2)}) copy-start(bf16[2,16,288]{2,1,0:T(8,128)(2,1)} %constant.9.clone.band_ref) | copy-start | bytes 55300

commit v9 on v8

--- a/solution.py
+++ b/solution.py
@@ -106,9 +106,9 @@
 
 
 def pack_kernel(
-    count_hbm, conn_hbm, shear_hbm, fwd_hbm, adj_hbm,
+    conn_hbm, shear_hbm, fwd_hbm, adj_hbm,
     right_ref, left_ref, own_ref, code_ref, parts_ref,
-    count_ref, conn_ref, shear_ref, fwd_ref, adj_ref, block_ref, sem,
+    conn_ref, shear_ref, fwd_ref, adj_ref, block_ref, sem,
 ):
     copies = fetch(
         sem,
@@ -116,10 +116,8 @@
         (conn_hbm.at[0:8], conn_ref),
         (fwd_hbm, fwd_ref),
         (adj_hbm, adj_ref),
-        (count_hbm, count_ref),
     )
     copies[1].wait()
-    copies[4].wait()
     point = conn_ref[0:1, :].astype(F32)
     x = jnp.floor((point + 0.5) * (1.0 / PYZ))
     rest = point - x * PYZ
@@ -127,7 +125,6 @@
     z = rest - y * PZ
     code = (8.0 * z + 2.0 * x + 0.25 * y).astype(jnp.int32)
     slot = lax.broadcasted_iota(jnp.int32, (1, 256), 1)
-    code = jnp.where(slot < count_ref[0], code, -1)
     code_ref[...] = jnp.broadcast_to(code, (8, 256))
     lane = lax.broadcasted_iota(jnp.int32, (LANES, 256), 0)
     pick = jnp.where(code == ((lane >> 3) & 7) * 32 + 24 + (lane & 7), 1.0, 0.0).astype(BF16)
@@ -141,7 +138,8 @@
         left_ref[16 * f : 16 * f + 16, :] = own_ref[ROWS * f : ROWS * f + 16, :]
     copies[0].wait()
     block_ref[0:125, :] = shear_ref[...]
-    block_ref[125:128, :] = jnp.zeros((3, 256), F32)
+    block_ref[125:126, :] = slot.astype(F32)
+    block_ref[126:128, :] = jnp.zeros((2, 256), F32)
     parts = jnp.concatenate(split3(block_ref[...]), axis=0)
     parts_ref[...] = parts
     flux = add_parts(dot_nt(parts, pick))
@@ -318,17 +316,17 @@
     return tiles
 
 
-def own_kernel(turn, cut_ref, own_ref, code_ref, parts_ref, cross_ref, *refs):
+def own_kernel(turn, cut_ref, count_ref, own_ref, code_ref, parts_ref, cross_ref, *refs):
     refs = refs[-OWN_OUTS - OWN_SCRATCH :]
     mine = (cut_ref[0] == 0) if turn == 0 else (cut_ref[0] != 0)
 
     @pl.when(mine)
     def _():
-        own_layers(own_ref, code_ref, parts_ref, cross_ref, *refs)
+        own_layers(count_ref, own_ref, code_ref, parts_ref, cross_ref, *refs)
 
 
 def own_layers(
-    own_ref, code_ref, parts_ref, cross_ref,
+    count_ref, own_ref, code_ref, parts_ref, cross_ref,
     elem_ref, flux_ref, near_flux_ref, near_win_ref, near_slope_ref, near_kern_ref, kern_ref,
     plane_ref, win_ref, line_ref, near_elem_ref, moved_ref,
 ):
@@ -363,7 +361,10 @@
                 near_slope_ref[w, r : r + 8, :] = v
 
     element = lax.broadcasted_iota(jnp.int32, (256, 256), 0)
-    pick = jnp.where(code_ref[0:1, :] == element, 1.0, 0.0).astype(BF16)
+    slot = lax.broadcasted_iota(jnp.int32, (1, 256), 1)
+    live = jnp.concatenate([count_ref[0:1, :], count_ref[0:1, :]], axis=1)
+    code = jnp.where(slot < live, code_ref[0:1, :], -1)
+    pick = jnp.where(code == element, 1.0, 0.0).astype(BF16)
     moved_ref[0:128, :] = add_parts(dot_nt(parts_ref[...], pick))
     moved_ref[128:136, :] = jnp.zeros((8, 256), F32)
 
@@ -401,15 +402,17 @@
         kern_ref[:, t * LANES : (t + 1) * LANES] = tile
 
 
-def message_flux(prev_ref, spread_ref):
-    spread_ref[0:64, :] = prev_ref[80:144, :]
-    spread_ref[64:128, :] = pltpu.roll(prev_ref[80:144, :], 64, 1)
+def message_flux(prev_ref, count_ref, spread_ref):
+    upper = pltpu.roll(prev_ref[80:144, :], 64, 1)
+    live = upper[61:62, :] < count_ref[0:1, :].astype(F32)
+    spread_ref[0:64, :] = jnp.where(live, prev_ref[80:144, :], 0.0)
+    spread_ref[64:128, :] = jnp.where(live, upper, 0.0)
     spread_ref[128:136, :] = jnp.zeros((8, LANES), F32)
     return lambda i, ez: (spread_ref[25 * i : 25 * i + 32, :], 8 * ez)
 
 
 def near_kernel(
-    prev_ref, next_ref, flux_in_ref, slope_ref, near_kern_ref, kern_in_ref, cross_ref,
+    prev_ref, next_ref, count_ref, flux_in_ref, slope_ref, near_kern_ref, kern_in_ref, cross_ref,
     kern_ref,
     plane_ref, new_ref, win_ref, elem_ref, flux_ref, line_ref, spread_ref,
 ):
@@ -432,7 +435,7 @@
                 new = float(DERIV[i, 4]) * new_ref[w, 16 + 8 * f : 24 + 8 * f, :]
                 win_ref[w, r : r + 8, :] = win_ref[w, r : r + 8, :] + new
     turned(win_ref, 0, elem_ref, 0)
-    place_flux(flux_ref, message_flux(prev_ref, spread_ref), lambda i: [(0, 8 * NEAR_AT[0][i], 8)], (4,))
+    place_flux(flux_ref, message_flux(prev_ref, count_ref, spread_ref), lambda i: [(0, 8 * NEAR_AT[0][i], 8)], (4,))
     scaled(flux_ref, lane_weight([NEAR_AT[0]]))
     kern = [[None] * 5 for _ in range(5)]
     for j in range(5):
@@ -478,7 +481,7 @@
 
 
 def step_kernel(
-    force_ref, near_half_ref, near_flux_ref, prev_ref, next_ref, fwd_hbm, fwd_speed_hbm, adj_hbm, adj_speed_hbm, mass_hbm, after_ref,
+    force_ref, near_half_ref, near_flux_ref, prev_ref, next_ref, count_ref, fwd_hbm, fwd_speed_hbm, adj_hbm, adj_speed_hbm, mass_hbm, after_ref,
     fwd_out_ref, fwd_speed_out_ref, adj_out_ref, adj_speed_out_ref,
     fwd_ref, fwd_speed_ref, adj_ref, adj_speed_ref, mass_ref, plane_ref, line_ref,
     flux_ref, win_ref, elem_ref, fold_ref, near_ref, near_win_ref, near_plane_ref, spread_ref, sem,
@@ -499,7 +502,7 @@
             near_plane_ref[pl.ds(72 * f + i, 9, stride=8), :] = flat
         near_win_ref[:, 128 * f : 128 * f + 64, :] = near_half_ref[:, 64 * f : 64 * f + 64, :]
         make_windows(near_plane_ref, 72 * f, 8, near_win_ref, 128 * f + 64)
-    place_flux(flux_ref, message_flux(prev_ref, spread_ref), lambda i: [(0, 8 * NEAR_AT[0][i], 8)])
+    place_flux(flux_ref, message_flux(prev_ref, count_ref, spread_ref), lambda i: [(0, 8 * NEAR_AT[0][i], 8)])
     scaled(flux_ref, lane_weight([NEAR_AT[0]]))
     flux_ref[...] = flux_ref[...] + near_flux_ref[...]
     for f in range(2):
@@ -617,29 +620,33 @@
             pltpu.VMEM((8, 256), jnp.int32),
             pltpu.VMEM((384, 256), BF16),
         ],
-        in_specs=[anywhere] * 5,
+        in_specs=[anywhere] * 4,
         scratch_shapes=[
-            pltpu.SMEM((1,), jnp.int32),
             pltpu.VMEM((8, 256), jnp.int32),
             pltpu.VMEM((125, 256), F32),
             point_row,
             point_row,
             pltpu.VMEM((128, 256), F32),
-            dma((5,)),
+            dma((4,)),
         ],
         cost_estimate=cost(100000000),
         name="pack",
-    )(element_count, in_hbm(connectivity), in_hbm(shear_modulus), *fields)
-    prev = lax.ppermute(right, "cuts", [(i, (i + 1) % cuts) for i in range(cuts)])
+    )(in_hbm(connectivity), in_hbm(shear_modulus), *fields)
+    to_next = [(i, (i + 1) % cuts) for i in range(cuts)]
+    prev = lax.ppermute(right, "cuts", to_next)
+    count, left = lax.optimization_barrier((element_count, left))
+    count = jnp.broadcast_to(count.reshape(1, 1), (8, LANES))
+    prev_count = lax.ppermute(count, "cuts", to_next)
+    count, left = lax.optimization_barrier((count, left))
 
     own_blocks = [elements(4), flux_block, flux_block, windows(1), windows(1), flux_block, kern_block]
 
     def own_part(turn, before):
-        given = (cut, held(own), held(code), held(parts), cross)
+        given = (cut, held(count), held(own), held(code), held(parts), cross)
         return pl.pallas_call(
             functools.partial(own_kernel, turn),
             out_shape=own_blocks,
-            in_specs=[smem] + [vmem] * (4 + len(before)),
+            in_specs=[smem] + [vmem] * (5 + len(before)),
             scratch_shapes=[
                 pltpu.VMEM((2 * 9 * 24, LANES), F32),
                 windows(4),
@@ -658,7 +665,7 @@
     kern = pl.pallas_call(
         near_kernel,
         out_shape=kern_block,
-        in_specs=[vmem] * 7,
+        in_specs=[vmem] * 8,
         scratch_shapes=[
             pltpu.VMEM((72, LANES), F32),
             pltpu.VMEM((2, 64, LANES), F32),
@@ -670,7 +677,7 @@
         ],
         cost_estimate=cost(200000000),
         name="near_layers",
-    )(held(prev), held(after), held(near_flux), held(near_slope), held(near_kern), held(kern), cross)
+    )(held(prev), held(after), held(prev_count), held(near_flux), held(near_slope), held(near_kern), held(kern), cross)
 
     (force,) = pl.pallas_call(
         force_kernel,
@@ -694,7 +701,7 @@
     outs = pl.pallas_call(
         step_kernel,
         out_shape=[points] * 4,
-        in_specs=[vmem] * 5 + [anywhere] * 5 + [vmem],
+        in_specs=[vmem] * 6 + [anywhere] * 5 + [vmem],
         scratch_shapes=[point_row] * 4
         + [pltpu.VMEM((NPTS,), F32), pltpu.VMEM((4 * 144, LANES), F32), pltpu.VMEM((2, ROWS, LANES), F32)]
         + [flux_block, windows(2), elements(2), line_block, windows(2), windows(2)]
@@ -707,6 +714,7 @@
         held(near_flux),
         held(prev),
         held(after),
+        held(prev_count),
         fields[0],
         in_hbm(forward_velocity),
         fields[1],

time: 23.2 us -> 22.7 us (0.978)
  waiting for transfers between devices: 4.66 us -> 3.59 us
  starting transfers between devices: 8.99 us -> 9.56 us
    ppermute x1 -> x2, starting transfers between devices: 0.5 us -> 3.19 us  [the longest x1 2.68 us: on_device(): prev_count = lax.ppermute(count, 'cuts', to_next)]
    ppermute x1, starting transfers between devices: 3.48 us -> 0.87 us  [on_device(): lax.ppermute(left, 'cuts', [((i + 1) % cuts, i) for i in range(cuts)])]
    ppermute x1, waiting for transfers between devices: 1.44 us -> 0.14 us  [on_device(): lax.ppermute(left, 'cuts', [((i + 1) % cuts, i) for i in range(cuts)])]
    ppermute x1 -> x2, waiting for transfers between devices: 0.49 us -> 1.31 us  [the longest x1 1.31 us: on_device(): prev_count = lax.ppermute(count, 'cuts', to_next)]
    ppermute x1, waiting for transfers between devices: 0.66 us -> 0.08 us  [on_device(): kern_first = lax.ppermute(kern, 'cuts', pairs_first)]
    ppermute x1, starting transfers between devices: 2.94 us -> 3.52 us  [on_device(): kern_first = lax.ppermute(kern, 'cuts', pairs_first)]
  transfers between devices with their start and end apart: 5 -> 6, of which waited for: 4 -> 4; matrix products, arithmetic and copies ran while one was open for 0% -> 0% of each run, Pallas kernels for 21% -> 22%
where the time goes in v9:
time: 22.7 us; the launch traced here: 22.5 us
  starting transfers between devices  9.56 us (42%)
  Pallas kernels  7.94 us (35%)
  waiting for transfers between devices  3.59 us (16%)
  between operations  1.35 us (6%)
    ppermute x1, starting transfers between devices, on_device(): kern_first = lax.ppermute(kern, 'cuts', pairs_first)  3.52 us
    pallas_call x1, Pallas kernels, on_device(): pl.pallas_call(step_kernel, out_shape=[points] * 4, in_specs=[vmem] * 6 +...  2.93 us
    ppermute x1, starting transfers between devices, on_device(): prev_count = lax.ppermute(count, 'cuts', to_next)  2.68 us
    ppermute x1, waiting for transfers between devices, on_device(): other = lax.ppermute(kern, 'event', [(0, 1), (1, 0)])  2.06 us
    ppermute x1, starting transfers between devices, on_device(): other = lax.ppermute(kern, 'event', [(0, 1), (1, 0)])  1.99 us
    pallas_call x2, Pallas kernels, own_part(): pl.pallas_call(functools.partial(own_kernel, turn), out_shape=own_blocks,...  1.6 us
    ppermute x1, waiting for transfers between devices, on_device(): prev_count = lax.ppermute(count, 'cuts', to_next)  1.31 us
    pallas_call x1, Pallas kernels, on_device(): pl.pallas_call(pack_kernel, out_shape=[pltpu.VMEM((144, LANES), F32), plt...  1.28 us
  transfers between devices with their start and end apart: 6, of which 4 were waited for; matrix products, arithmetic and copies ran while one was open for 0% of the time, Pallas kernels for 22%

profile of v9, /device:TPU:0, one launch (start us, length us, event | category | flops | bytes accessed | tf_op | source)
XLA Modules:
  0.0 22.5 jit_solution(11160634041196599834)
XLA Ops:
  0.6 0.0 copy-start
  0.6 1.3 %pack.1 = (f32[144,128]{1,0:T(8,128)S(1)}, f32[32,128]{1,0:T(8,128)S(1)}, f32[288,128]{1,0:T(8,128)S(1)}, s32[8,256]{1,0:T(8,128)S(1)}, bf16[384,256]{1,0:T(8,128)(2,1)S(1)}) custom-call(s32[125,256]{1,0:T(8,128)} %conn_hbm.1, f32[125,256]{1,0:T(8,128)} %shear_hbm.1, f32[1,17424]{1,0:T(1,128)} %fwd_hbm.3, f32[1,17424]{1,0:T(1,128)} %adj_hbm.3), custom_call_target="tpu_custom_call" | custom-call | flops 100000000 | bytes 1000000 | tf_op jit(solution)/shard_map/pack/pallas_call | solution.py:614
  1.9 0.5 %collective-permute-start = (f32[144,128]{1,0:T(8,128)S(1)}, f32[144,128]{1,0:T(8,128)S(1)}, u32[]{:S(2)}, u32[]{:S(2)}) collective-permute-start(f32[144,128]{1,0:T(8,128)S(1)} %get-tuple-element.42), channel_id=1, source_target_pairs={{0,1},{1,2},{2,3},{3,4},{4,5},{5,6},{6,7},{7,8},{8,9},{9,10},{10,1... | collective-permute-start | bytes 221192 | tf_op jit(solution)/shard_map/ppermute | solution.py:636
  3.1 2.7 %collective-permute-start.2 = (s32[8,128]{1,0:T(8,128)S(1)}, s32[8,128]{1,0:T(8,128)S(1)}, u32[]{:S(2)}, u32[]{:S(2)}) collective-permute-start(s32[8,128]{1,0:T(8,128)S(1)} %broadcast_in_dim.8.count_ref), channel_id=1, source_target_pairs={{0,1},{1,2},{2,3},{3,4},{4,5},{5,6},{6,7},{7,8},{8,9},{9,10},{10,1... | collective-permute-start | bytes 12296 | tf_op jit(solution)/shard_map/ppermute | solution.py:639
  5.8 0.0 copy-done
  5.8 1.6 %own_layers.2 = (f32[4,168,128]{2,1,0:T(8,128)S(1)}, f32[200,128]{1,0:T(8,128)S(1)}, f32[200,128]{1,0:T(8,128)S(1)}, f32[2,128,128]{2,1,0:T(8,128)S(1)}, f32[2,1...) custom-call(s32[1]{0:T(128)} %bitcast.1.cut_ref, s32[8,128]{1,0:T(8,128)S(1)} %broadcast_in_dim.8.count_ref, ...), custom_call_target="tpu_custom_call" | custom-call | flops 300000000 | bytes 1000000 | tf_op jit(solution)/shard_map/own_layers/pallas_call | solution.py:646
  7.4 0.9 %collective-permute-start.1 = (f32[32,128]{1,0:T(8,128)S(1)}, f32[32,128]{1,0:T(8,128)S(1)}, u32[]{:S(2)}, u32[]{:S(2)}) collective-permute-start(f32[32,128]{1,0:T(8,128)S(1)} %get-tuple-element.58), channel_id=1, source_target_pairs={{1,0},{2,1},{3,2},{4,3},{5,4},{6,5},{7,6},{8,7},{9,8},{10,9},{11,1... | collective-permute-start | bytes 49160 | tf_op jit(solution)/shard_map/ppermute | solution.py:663
  8.3 1.3 %collective-permute-done.2.count_ref = s32[8,128]{1,0:T(8,128)S(1)} collective-permute-done((s32[8,128]{1,0:T(8,128)S(1)}, s32[8,128]{1,0:T(8,128)S(1)}, u32[]{:S(2)}, u32[]{:S(2)}) %collective-permute-start.2) | collective-permute-done | bytes 4128 | tf_op jit(solution)/shard_map/ppermute | solution.py:639
  9.6 0.1 collective-permute-done.1.next_ref
  9.7 0.0 collective-permute-done.prev_ref
  9.7 0.9 %near_layers.1 = f32[16,1152]{1,0:T(8,128)S(1)} custom-call(f32[144,128]{1,0:T(8,128)S(1)} %collective-permute-done.prev_ref, f32[32,128]{1,0:T(8,128)S(1)} %collective-permute-done.1.next_ref, s32[8,128]{1,0:T(8,128)S(1)} %collective-permute-done.2.count_ref, f32[200,128]{1,0:T(8,128)S(1)} %get-tuple-element.66.flux_in_ref.near_flux_ref, ...), custom_call_target="tpu_custom_call" | custom-call | flops 200000000 | bytes 1000000 | tf_op jit(solution)/shard_map/near_layers/pallas_call | solution.py:665
  10.6 2.0 %collective-permute-start.3 = (f32[16,1152]{1,0:T(8,128)S(1)}, f32[16,1152]{1,0:T(8,128)S(1)}, u32[]{:S(2)}, u32[]{:S(2)}) collective-permute-start(f32[16,1152]{1,0:T(8,128)S(1)} %near_layers.1), channel_id=1, source_target_pairs={{0,16},{16,0},{1,17},{17,1},{2,18},{18,2},{3,19},{19,3},{4,20},{20... | collective-permute-start | bytes 221192 | tf_op jit(solution)/shard_map/ppermute | solution.py:692
  12.6 0.4 %forces.1.force_ref = f32[2,256,128]{2,1,0:T(8,128)S(1)} custom-call(f32[4,168,128]{2,1,0:T(8,128)S(1)} %get-tuple-element.70.elem_ref, f32[200,128]{1,0:T(8,128)S(1)} %get-tuple-element.71.flux_ref), custom_call_target="tpu_custom_call" | custom-call | flops 200000000 | bytes 1000000 | tf_op jit(solution)/shard_map/forces/pallas_call | solution.py:682
  13.0 2.1 %collective-permute-done.3 = f32[16,1152]{1,0:T(8,128)S(1)} collective-permute-done((f32[16,1152]{1,0:T(8,128)S(1)}, f32[16,1152]{1,0:T(8,128)S(1)}, u32[]{:S(2)}, u32[]{:S(2)}) %collective-permute-start.3) | collective-permute-done | bytes 73760 | tf_op jit(solution)/shard_map/ppermute | solution.py:692
  15.1 3.5 %collective-permute-start.4 = (f32[16,1152]{1,0:T(8,128)S(1)}, f32[16,1152]{1,0:T(8,128)S(1)}, u32[]{:S(2)}, u32[]{:S(2)}) collective-permute-start(f32[16,1152]{1,0:T(8,128)S(1)} %add.3.after_ref.own_ref), channel_id=1, source_target_pairs={{0,15},{1,2},{2,1},{3,4},{4,3},{5,6},{6,5},{7,8},{8,7},{9,10},{10,... | collective-permute-start | bytes 221192 | tf_op jit(solution)/shard_map/ppermute | solution.py:697
  18.6 0.0 collective-permute-start.5
  18.6 0.0 copy-start.1
  18.6 2.9 %step.1 = (f32[1,17424]{1,0:T(1,128)}, f32[1,17424]{1,0:T(1,128)}, f32[1,17424]{1,0:T(1,128)}, f32[1,17424]{1,0:T(1,128)}) custom-call(f32[2,256,128]{2,1,0:T(8,128)S(1)} %forces.1.force_ref, f32[2,128,128]{2,1,0:T(8,128)S(1)} %get-tuple-element.73.near_half_ref, f32[200,128]{1,0:T(8,128)S(1)} %get-tuple-element.66.flux_in_ref.near_flux_ref, ...), custom_call_target="tpu_custom_call" | custom-call | flops 200000000 | bytes 1000000 | tf_op jit(solution)/shard_map/step/pallas_call | solution.py:701
  21.5 0.1 collective-permute-done.4.first_ref
  21.6 0.0 collective-permute-done.5.second_ref
  21.6 0.0 copy-done.1
  21.6 0.8 %band.1 = f32[16,1089]{1,0:T(8,128)} custom-call(s32[1]{0:T(128)} %bitcast.1.cut_ref, f32[16,1152]{1,0:T(8,128)S(1)} %add.3.after_ref.own_ref, f32[16,1152]{1,0:T(8,128)S(1)} %collective-permute-done.4.first_ref, f32[16,1152]{1,0:T(8,128)S(1)} %collective-permute-done.5.second_ref, bf16[2,16,288]{2,1,0:T(8,128)(2,1)S(1)} %copy-done.1), custom_call_target="tpu_custom_call" | custom-call | flops 20000000 | bytes 1000000 | tf_op jit(solution)/shard_map/band/pallas_call | solution.py:725
  (3 shorter events, 0.0 us)
Async XLA Ops:
  0.6 5.2 %copy-start = (f32[24,1152]{1,0:T(8,128)S(1)}, f32[24,1152]{1,0:T(8,128)}, u32[]{:S(2)}) copy-start(f32[24,1152]{1,0:T(8,128)} %constant.8.clone.cross_ref) | copy-start | bytes 331780
  1.9 7.8 %collective-permute-start = (f32[144,128]{1,0:T(8,128)S(1)}, f32[144,128]{1,0:T(8,128)S(1)}, u32[]{:S(2)}, u32[]{:S(2)}) collective-permute-start(f32[144,128]{1,0:T(8,128)S(1)} %get-tuple-element.42), channel_id=1, source_target_pairs={{0,1},{1,2},{2,3},{3,4},{4,5},{5,6},{6,7},{7,8},{8,9},{9,10},{10,1... | collective-permute-start | bytes 221192 | tf_op jit(solution)/shard_map/ppermute | solution.py:636
  3.1 6.5 %collective-permute-start.2 = (s32[8,128]{1,0:T(8,128)S(1)}, s32[8,128]{1,0:T(8,128)S(1)}, u32[]{:S(2)}, u32[]{:S(2)}) collective-permute-start(s32[8,128]{1,0:T(8,128)S(1)} %broadcast_in_dim.8.count_ref), channel_id=1, source_target_pairs={{0,1},{1,2},{2,3},{3,4},{4,5},{5,6},{6,7},{7,8},{8,9},{9,10},{10,1... | collective-permute-start | bytes 12296 | tf_op jit(solution)/shard_map/ppermute | solution.py:639
  7.4 2.3 %collective-permute-start.1 = (f32[32,128]{1,0:T(8,128)S(1)}, f32[32,128]{1,0:T(8,128)S(1)}, u32[]{:S(2)}, u32[]{:S(2)}) collective-permute-start(f32[32,128]{1,0:T(8,128)S(1)} %get-tuple-element.58), channel_id=1, source_target_pairs={{1,0},{2,1},{3,2},{4,3},{5,4},{6,5},{7,6},{8,7},{9,8},{10,9},{11,1... | collective-permute-start | bytes 49160 | tf_op jit(solution)/shard_map/ppermute | solution.py:663
  10.6 4.4 %collective-permute-start.3 = (f32[16,1152]{1,0:T(8,128)S(1)}, f32[16,1152]{1,0:T(8,128)S(1)}, u32[]{:S(2)}, u32[]{:S(2)}) collective-permute-start(f32[16,1152]{1,0:T(8,128)S(1)} %near_layers.1), channel_id=1, source_target_pairs={{0,16},{16,0},{1,17},{17,1},{2,18},{18,2},{3,19},{19,3},{4,20},{20... | collective-permute-start | bytes 221192 | tf_op jit(solution)/shard_map/ppermute | solution.py:692
  15.1 6.5 %collective-permute-start.4 = (f32[16,1152]{1,0:T(8,128)S(1)}, f32[16,1152]{1,0:T(8,128)S(1)}, u32[]{:S(2)}, u32[]{:S(2)}) collective-permute-start(f32[16,1152]{1,0:T(8,128)S(1)} %add.3.after_ref.own_ref), channel_id=1, source_target_pairs={{0,15},{1,2},{2,1},{3,4},{4,3},{5,6},{6,5},{7,8},{8,7},{9,10},{10,... | collective-permute-start | bytes 221192 | tf_op jit(solution)/shard_map/ppermute | solution.py:697
  18.6 3.0 %collective-permute-start.5 = (f32[16,1152]{1,0:T(8,128)S(1)}, f32[16,1152]{1,0:T(8,128)S(1)}, u32[]{:S(2)}, u32[]{:S(2)}) collective-permute-start(f32[16,1152]{1,0:T(8,128)S(1)} %add.3.after_ref.own_ref), channel_id=1, source_target_pairs={{0,1},{1,0},{2,3},{3,2},{4,5},{5,4},{6,7},{7,6},{8,9},{9,8},{10,11... | collective-permute-start | bytes 221192 | tf_op jit(solution)/shard_map/ppermute | solution.py:698
  18.6 3.0 %copy-start.1 = (bf16[2,16,288]{2,1,0:T(8,128)(2,1)S(1)}, bf16[2,16,288]{2,1,0:T(8,128)(2,1)}, u32[]{:S(2)}) copy-start(bf16[2,16,288]{2,1,0:T(8,128)(2,1)} %constant.9.clone.band_ref) | copy-start | bytes 55300

commit v10 on v9

--- a/solution.py
+++ b/solution.py
@@ -362,8 +362,7 @@
 
     element = lax.broadcasted_iota(jnp.int32, (256, 256), 0)
     slot = lax.broadcasted_iota(jnp.int32, (1, 256), 1)
-    live = jnp.concatenate([count_ref[0:1, :], count_ref[0:1, :]], axis=1)
-    code = jnp.where(slot < live, code_ref[0:1, :], -1)
+    code = jnp.where(slot < count_ref[0:1, 0:1], code_ref[0:1, :], -1)
     pick = jnp.where(code == element, 1.0, 0.0).astype(BF16)
     moved_ref[0:128, :] = add_parts(dot_nt(parts_ref[...], pick))
     moved_ref[128:136, :] = jnp.zeros((8, 256), F32)
@@ -404,7 +403,7 @@
 
 def message_flux(prev_ref, count_ref, spread_ref):
     upper = pltpu.roll(prev_ref[80:144, :], 64, 1)
-    live = upper[61:62, :] < count_ref[0:1, :].astype(F32)
+    live = upper[61:62, :] < count_ref[0:1, 0:1].astype(F32)
     spread_ref[0:64, :] = jnp.where(live, prev_ref[80:144, :], 0.0)
     spread_ref[64:128, :] = jnp.where(live, upper, 0.0)
     spread_ref[128:136, :] = jnp.zeros((8, LANES), F32)
@@ -412,7 +411,7 @@
 
 
 def near_kernel(
-    prev_ref, next_ref, count_ref, flux_in_ref, slope_ref, near_kern_ref, kern_in_ref, cross_ref,
+    prev_ref, next_ref, count_ref, flux_in_ref, slope_ref, near_kern_ref, cross_ref,
     kern_ref,
     plane_ref, new_ref, win_ref, elem_ref, flux_ref, line_ref, spread_ref,
 ):
@@ -447,9 +446,7 @@
     row = lax.broadcasted_iota(jnp.int32, (8, LANES), 0)
     tiles = [jnp.where((row == 0) | (row >= 4), v, 0.0) for v in gathered(win_ref, 0, 0)]
     for t, tile in enumerate(cross_smoothed(tiles, cross_ref)):
-        columns = slice(t * LANES, (t + 1) * LANES)
-        kern_ref[0:8, columns] = kern_in_ref[0:8, columns] + jnp.where(row == 0, tile, 0.0)
-        kern_ref[8:16, columns] = kern_in_ref[8:16, columns] + jnp.where(row >= 4, tile, 0.0)
+        kern_ref[:, t * LANES : (t + 1) * LANES] = tile
 
 
 def gathered(win_ref, base, h):
@@ -474,10 +471,37 @@
             out_ref[w, row + r : row + r + 8, :] = win_ref[w, r : r + 8, :] + v
 
 
-def force_kernel(elem_ref, flux_ref, out_ref, win_ref, line_ref):
+def to_planes(win_ref, base, plane_ref):
+    for h in range(2):
+        for t, tile in enumerate(gathered(win_ref, base, h)):
+            plane_ref[t * 16 + 8 * h : t * 16 + 8 * h + 8, :] = tile
+
+
+def add_plane(line_ref, f, x, flat):
+    lane9 = lax.broadcasted_iota(jnp.int32, (9, LANES), 1)
+    r0, off = divmod(PYZ * x, LANES)
+    if off:
+        flat = pltpu.roll(flat, off, 1)
+        spill = jnp.where(lane9 < off, flat, 0.0)
+        flat = jnp.where(lane9 < off, 0.0, flat)
+    line_ref[f, r0 : r0 + 9, :] = line_ref[f, r0 : r0 + 9, :] + flat
+    if off:
+        line_ref[f, r0 + 1 : r0 + 10, :] = line_ref[f, r0 + 1 : r0 + 10, :] + spill
+
+
+def force_kernel(elem_ref, flux_ref, out_ref, win_ref, line_ref, force_ref, plane_ref):
+    out_ref[...] = jnp.zeros(out_ref.shape, F32)
     for f in range(2):
         force_terms(elem_ref, f, 2 + f, flux_ref, line_ref, win_ref, 0)
-        summed_along_x(win_ref, OWN_AT, out_ref, LANES * f)
+        summed_along_x(win_ref, OWN_AT, force_ref, 0)
+        to_planes(force_ref, 0, plane_ref)
+        for x in range(13):
+            i, m = x % 4, x // 4
+            rows = [OWN_AT[m][i]] if m < 3 else []
+            if i == 0 and m > 0:
+                rows.append(OWN_AT[m - 1][4])
+            flat = [plane_ref[pl.ds(r, 9, stride=16), :] for r in rows]
+            add_plane(out_ref, f, x, sum(flat[1:], flat[0]))
 
 
 def step_kernel(
@@ -494,7 +518,7 @@
         (adj_speed_hbm, adj_speed_ref),
         (mass_hbm, mass_ref),
     )
-    lane9 = lax.broadcasted_iota(jnp.int32, (9, LANES), 1)
+    line_ref[...] = force_ref[...]
     near_plane_ref[...] = jnp.zeros(near_plane_ref.shape, F32)
     for f in range(2):
         for i in range(5):
@@ -513,30 +537,10 @@
         turned(near_win_ref, LANES * f, elem_ref, 0)
         turned(win_ref, 0, elem_ref, 1)
         force_terms(elem_ref, 0, 1, flux_ref, fold_ref, win_ref, 0)
-        summed_along_x(win_ref, NEAR_AT, near_ref, LANES * f)
-    for n in range(4):
-        for h in range(2):
-            source = force_ref if n < 2 else near_ref
-            for t, tile in enumerate(gathered(source, 128 * (n % 2), h)):
-                plane_ref[n * 144 + t * 16 + 8 * h : n * 144 + t * 16 + 8 * h + 8, :] = tile
-    line_ref[...] = jnp.zeros(line_ref.shape, F32)
-    for f in range(2):
-        for x in range(PXU):
-            r0, off = divmod(PYZ * x, LANES)
-            i, m = x % 4, x // 4
-            rows = [144 * f + OWN_AT[m][i] if m < 3 else 288 + 144 * f + NEAR_AT[1][i]]
-            if i == 0:
-                rows.append(144 * f + OWN_AT[m - 1][4] if m > 0 else 288 + 144 * f + NEAR_AT[0][4])
-            flat = plane_ref[pl.ds(rows[0], 9, stride=16), :]
-            if i == 0:
-                flat = flat + plane_ref[pl.ds(rows[1], 9, stride=16), :]
-            if off:
-                flat = pltpu.roll(flat, off, 1)
-                spill = jnp.where(lane9 < off, flat, 0.0)
-                flat = jnp.where(lane9 < off, 0.0, flat)
-            line_ref[f, r0 : r0 + 9, :] = line_ref[f, r0 : r0 + 9, :] + flat
-            if off:
-                line_ref[f, r0 + 1 : r0 + 10, :] = line_ref[f, r0 + 1 : r0 + 10, :] + spill
+        summed_along_x(win_ref, NEAR_AT, near_ref, 0)
+        to_planes(near_ref, 0, plane_ref)
+        for x, r in [(0, NEAR_AT[0][4])] + [(12 + i, NEAR_AT[1][i]) for i in range(4)]:
+            add_plane(line_ref, f, x, plane_ref[pl.ds(r, 9, stride=16), :])
 
     def step(lo, hi, force):
         shape = (hi - lo) // force[0].shape[1], force[0].shape[1]
@@ -594,8 +598,8 @@
     def in_hbm(block):
         return pltpu.with_memory_space_constraint(block, pltpu.HBM)
 
-    def cost(flops):
-        return pl.CostEstimate(flops=flops, bytes_accessed=1000000, transcendentals=0)
+    def cost(flops, moved=1000000):
+        return pl.CostEstimate(flops=flops, bytes_accessed=moved, transcendentals=0)
 
     dma = pltpu.SemaphoreType.DMA
     point_row = pltpu.VMEM((1, NPTS), F32)
@@ -641,12 +645,12 @@
 
     own_blocks = [elements(4), flux_block, flux_block, windows(1), windows(1), flux_block, kern_block]
 
-    def own_part(turn, before):
+    def own_part(turn, before, waits=()):
         given = (cut, held(count), held(own), held(code), held(parts), cross)
         return pl.pallas_call(
             functools.partial(own_kernel, turn),
             out_shape=own_blocks,
-            in_specs=[smem] + [vmem] * (5 + len(before)),
+            in_specs=[smem] + [vmem] * (5 + len(before)) + [anywhere] * len(waits),
             scratch_shapes=[
                 pltpu.VMEM((2 * 9 * 24, LANES), F32),
                 windows(4),
@@ -657,15 +661,15 @@
             input_output_aliases={len(given) + n: n for n in range(len(before))},
             cost_estimate=cost(300000000),
             name="own_layers",
-        )(*given, *[held(block) for block in before])
+        )(*given, *[held(block) for block in before], *[held(block) for block in waits])
 
     left, *blocks = lax.optimization_barrier((left, *own_part(0, [])))
     after = lax.ppermute(left, "cuts", [((i + 1) % cuts, i) for i in range(cuts)])
-    elem, flux, near_flux, near_win, near_slope, near_kern, kern = own_part(1, blocks)
-    kern = pl.pallas_call(
+    elem, flux, near_flux, near_win, near_slope, near_kern, kern = own_part(1, blocks, [prev])
+    near = pl.pallas_call(
         near_kernel,
-        out_shape=kern_block,
-        in_specs=[vmem] * 8,
+        out_shape=pltpu.VMEM((8, 9 * LANES), F32),
+        in_specs=[vmem] * 7,
         scratch_shapes=[
             pltpu.VMEM((72, LANES), F32),
             pltpu.VMEM((2, 64, LANES), F32),
@@ -675,25 +679,31 @@
             line_block,
             pltpu.VMEM((136, LANES), F32),
         ],
-        cost_estimate=cost(200000000),
+        cost_estimate=cost(200000000, 40000000),
         name="near_layers",
-    )(held(prev), held(after), held(prev_count), held(near_flux), held(near_slope), held(near_kern), held(kern), cross)
-
-    (force,) = pl.pallas_call(
+    )(held(prev), held(after), held(prev_count), held(near_flux), held(near_slope), held(near_kern), cross)
+
+    force = pl.pallas_call(
         force_kernel,
-        out_shape=[windows(2)],
+        out_shape=pltpu.VMEM((2, ROWS, LANES), F32),
         in_specs=[vmem] * 2,
-        scratch_shapes=[windows(2), line_block],
-        cost_estimate=cost(200000000),
+        scratch_shapes=[windows(2), line_block, windows(1), pltpu.VMEM((144, LANES), F32)],
+        cost_estimate=cost(200000000, 40000000),
         name="forces",
     )(held(elem), held(flux))
 
+    def joined(rows, near):
+        low = (lax.broadcasted_iota(jnp.int32, (8, 1), 0) < 4).astype(F32)
+        return rows + jnp.concatenate([near * low, near * (1.0 - low)], axis=0)
+
     if events == 2:
-        other = lax.ppermute(kern, "event", [(0, 1), (1, 0)])
-        other, force = lax.optimization_barrier((other, force))
-        kern = kern + other
-    elif events > 2:
-        kern = lax.psum(kern, "event")
+        swap = [(0, 1), (1, 0)]
+        both = kern + lax.ppermute(kern, "event", swap)
+        other = lax.ppermute(near, "event", swap)
+        other, both, force = lax.optimization_barrier((other, both, force))
+        kern = joined(both, near + other)
+    else:
+        kern = lax.psum(joined(kern, near), "event")
     kern_first = lax.ppermute(kern, "cuts", pairs_first)
     kern_second = lax.ppermute(kern, "cuts", pairs_second)
 
@@ -703,8 +713,8 @@
         out_shape=[points] * 4,
         in_specs=[vmem] * 6 + [anywhere] * 5 + [vmem],
         scratch_shapes=[point_row] * 4
-        + [pltpu.VMEM((NPTS,), F32), pltpu.VMEM((4 * 144, LANES), F32), pltpu.VMEM((2, ROWS, LANES), F32)]
-        + [flux_block, windows(2), elements(2), line_block, windows(2), windows(2)]
+        + [pltpu.VMEM((NPTS,), F32), pltpu.VMEM((144, LANES), F32), pltpu.VMEM((2, ROWS, LANES), F32)]
+        + [flux_block, windows(2), elements(2), line_block, windows(1), windows(2)]
         + [pltpu.VMEM((2 * 72, LANES), F32), pltpu.VMEM((136, LANES), F32), dma((5,))],
         cost_estimate=cost(200000000),
         name="step",

time: 22.7 us -> 24.1 us (1.062)
  waiting for transfers between devices: 3.59 us -> 6.28 us
  starting transfers between devices: 9.56 us -> 7.63 us
  Pallas kernels: 7.94 us -> 8.54 us
    ppermute x1, waiting for transfers between devices: 0.08 us -> 1.91 us  [on_device(): kern_first = lax.ppermute(kern, 'cuts', pairs_first)]
    ppermute x1, starting transfers between devices: 3.52 us -> 1.71 us  [on_device(): kern_first = lax.ppermute(kern, 'cuts', pairs_first)]
    ppermute x1, waiting for transfers between devices: 1.31 us -> 0.01 us  [on_device(): prev_count = lax.ppermute(count, 'cuts', to_next)]
    ppermute x1, waiting for transfers between devices: 0.01 us -> 1.25 us  [on_device(): prev = lax.ppermute(right, 'cuts', to_next)]
    ppermute x1 -> x2, waiting for transfers between devices: 2.06 us -> 3.11 us  [the longest x1 2.03 us: on_device(): other = lax.ppermute(near, 'event', swap)]
    pallas_call x2, Pallas kernels: 1.29 us -> 1.6 us  [the longest x1 0.9 us: on_device(): pl.pallas_call(near_kernel, out_shape=pltpu.VMEM((8, 9 * LANES), F32), in...]
    pallas_call x2, Pallas kernels: 1.6 us -> 1.89 us  [own_part(): pl.pallas_call(functools.partial(own_kernel, turn), out_shape=own_blocks,...]
    ppermute x1, starting transfers between devices: 0.87 us -> 0.57 us  [on_device(): lax.ppermute(left, 'cuts', [((i + 1) % cuts, i) for i in range(cuts)])]
  transfers between devices with their start and end apart: 6 -> 7, of which waited for: 4 -> 4; matrix products, arithmetic and copies ran while one was open for 0% -> 0% of each run, Pallas kernels for 22% -> 27%
where the time goes in v10:
time: 24.1 us; the launch traced here: 23.9 us
  Pallas kernels  8.54 us (35%)
  starting transfers between devices  7.63 us (32%)
  waiting for transfers between devices  6.28 us (26%)
  between operations  1.35 us (6%)
    pallas_call x1, Pallas kernels, on_device(): pl.pallas_call(step_kernel, out_shape=[points] * 4, in_specs=[vmem] * 6 +...  2.91 us
    ppermute x1, starting transfers between devices, on_device(): prev_count = lax.ppermute(count, 'cuts', to_next)  2.68 us
    ppermute x1, waiting for transfers between devices, on_device(): other = lax.ppermute(near, 'event', swap)  2.03 us
    ppermute x1, starting transfers between devices, on_device(): both = kern + lax.ppermute(kern, 'event', swap)  1.98 us
    ppermute x1, waiting for transfers between devices, on_device(): kern_first = lax.ppermute(kern, 'cuts', pairs_first)  1.91 us
    pallas_call x2, Pallas kernels, own_part(): pl.pallas_call(functools.partial(own_kernel, turn), out_shape=own_blocks,...  1.89 us
    ppermute x1, starting transfers between devices, on_device(): kern_first = lax.ppermute(kern, 'cuts', pairs_first)  1.71 us
    pallas_call x1, Pallas kernels, on_device(): pl.pallas_call(pack_kernel, out_shape=[pltpu.VMEM((144, LANES), F32), plt...  1.28 us
  transfers between devices with their start and end apart: 7, of which 4 were waited for; matrix products, arithmetic and copies ran while one was open for 0% of the time, Pallas kernels for 27%

profile of v10, /device:TPU:0, one launch (start us, length us, event | category | flops | bytes accessed | tf_op | source)
XLA Modules:
  0.0 23.9 jit_solution(14833857320091468517)
XLA Ops:
  0.6 0.0 copy-start
  0.6 1.3 %pack.1 = (f32[144,128]{1,0:T(8,128)S(1)}, f32[32,128]{1,0:T(8,128)S(1)}, f32[288,128]{1,0:T(8,128)S(1)}, s32[8,256]{1,0:T(8,128)S(1)}, bf16[384,256]{1,0:T(8,128)(2,1)S(1)}) custom-call(s32[125,256]{1,0:T(8,128)} %conn_hbm.1, f32[125,256]{1,0:T(8,128)} %shear_hbm.1, f32[1,17424]{1,0:T(1,128)} %fwd_hbm.3, f32[1,17424]{1,0:T(1,128)} %adj_hbm.3), custom_call_target="tpu_custom_call" | custom-call | flops 100000000 | bytes 1000000 | tf_op jit(solution)/shard_map/pack/pallas_call | solution.py:618
  1.9 0.5 %collective-permute-start = (f32[144,128]{1,0:T(8,128)S(1)}, f32[144,128]{1,0:T(8,128)S(1)}, u32[]{:S(2)}, u32[]{:S(2)}) collective-permute-start(f32[144,128]{1,0:T(8,128)S(1)} %get-tuple-element.43), channel_id=1, source_target_pairs={{0,1},{1,2},{2,3},{3,4},{4,5},{5,6},{6,7},{7,8},{8,9},{9,10},{10,1... | collective-permute-start | bytes 221192 | tf_op jit(solution)/shard_map/ppermute | solution.py:640
  3.1 2.7 %collective-permute-start.2 = (s32[8,128]{1,0:T(8,128)S(1)}, s32[8,128]{1,0:T(8,128)S(1)}, u32[]{:S(2)}, u32[]{:S(2)}) collective-permute-start(s32[8,128]{1,0:T(8,128)S(1)} %broadcast_in_dim.8.count_ref), channel_id=1, source_target_pairs={{0,1},{1,2},{2,3},{3,4},{4,5},{5,6},{6,7},{7,8},{8,9},{9,10},{10,1... | collective-permute-start | bytes 12296 | tf_op jit(solution)/shard_map/ppermute | solution.py:643
  5.8 0.0 copy-done
  5.8 1.9 %own_layers.2 = (f32[4,168,128]{2,1,0:T(8,128)S(1)}, f32[200,128]{1,0:T(8,128)S(1)}, f32[200,128]{1,0:T(8,128)S(1)}, f32[2,128,128]{2,1,0:T(8,128)S(1)}, f32[2,1...) custom-call(s32[1]{0:T(128)} %bitcast.1.cut_ref, s32[8,128]{1,0:T(8,128)S(1)} %broadcast_in_dim.8.count_ref, ...), custom_call_target="tpu_custom_call" | custom-call | flops 300000000 | bytes 1000000 | tf_op jit(solution)/shard_map/own_layers/pallas_call | solution.py:650
  7.7 0.6 %collective-permute-start.1 = (f32[32,128]{1,0:T(8,128)S(1)}, f32[32,128]{1,0:T(8,128)S(1)}, u32[]{:S(2)}, u32[]{:S(2)}) collective-permute-start(f32[32,128]{1,0:T(8,128)S(1)} %get-tuple-element.59), channel_id=1, source_target_pairs={{1,0},{2,1},{3,2},{4,3},{5,4},{6,5},{7,6},{8,7},{9,8},{10,9},{11,1... | collective-permute-start | bytes 49160 | tf_op jit(solution)/shard_map/ppermute | solution.py:667
  8.3 1.3 %collective-permute-done.refs_7_.prev_ref = f32[144,128]{1,0:T(8,128)S(1)} collective-permute-done((f32[144,128]{1,0:T(8,128)S(1)}, f32[144,128]{1,0:T(8,128)S(1)}, u32[]{:S(2)}, u32[]{:S(2)}) %collective-permute-start) | collective-permute-done | bytes 73760 | tf_op jit(solution)/shard_map/ppermute | solution.py:640
  9.5 2.0 %collective-permute-start.4 = (f32[16,1152]{1,0:T(8,128)S(1)}, f32[16,1152]{1,0:T(8,128)S(1)}, u32[]{:S(2)}, u32[]{:S(2)}) collective-permute-start(f32[16,1152]{1,0:T(8,128)S(1)} %get-tuple-element.70), channel_id=1, source_target_pairs={{0,16},{16,0},{1,17},{17,1},{2,18},{18,2},{3,19},{19,3},{4,20},{20... | collective-permute-start | bytes 221192 | tf_op jit(solution)/shard_map/ppermute | solution.py:701
  11.5 0.0 collective-permute-done.2.count_ref
  11.5 0.0 collective-permute-done.1.next_ref
  11.5 0.9 %near_layers.1 = f32[8,1152]{1,0:T(8,128)S(1)} custom-call(f32[144,128]{1,0:T(8,128)S(1)} %collective-permute-done.refs_7_.prev_ref, f32[32,128]{1,0:T(8,128)S(1)} %collective-permute-done.1.next_ref, s32[8,128]{1,0:T(8,128)S(1)} %collective-permute-done.2.count_ref, f32[200,128]{1,0:T(8,128)S(1)} %get-tuple-element.67.flux_in_ref.near_flux_ref, ...), custom_call_target="tpu_custom_call" | custom-call | flops 200000000 | bytes 40000000 | tf_op jit(solution)/shard_map/near_layers/pallas_call | solution.py:669
  12.4 0.2 collective-permute-start.3
  12.6 0.7 %forces.1.force_ref = f32[2,144,128]{2,1,0:T(8,128)S(1)} custom-call(f32[4,168,128]{2,1,0:T(8,128)S(1)} %get-tuple-element.71.elem_ref, f32[200,128]{1,0:T(8,128)S(1)} %get-tuple-element.72.flux_ref), custom_call_target="tpu_custom_call" | custom-call | flops 200000000 | bytes 40000000 | tf_op jit(solution)/shard_map/forces/pallas_call | solution.py:686
  13.3 1.1 %collective-permute-done.4 = f32[16,1152]{1,0:T(8,128)S(1)} collective-permute-done((f32[16,1152]{1,0:T(8,128)S(1)}, f32[16,1152]{1,0:T(8,128)S(1)}, u32[]{:S(2)}, u32[]{:S(2)}) %collective-permute-start.4) | collective-permute-done | bytes 73760 | tf_op jit(solution)/shard_map/ppermute | solution.py:701
  14.4 2.0 %collective-permute-done.3 = f32[8,1152]{1,0:T(8,128)S(1)} collective-permute-done((f32[8,1152]{1,0:T(8,128)S(1)}, f32[8,1152]{1,0:T(8,128)S(1)}, u32[]{:S(2)}, u32[]{:S(2)}) %collective-permute-start.3) | collective-permute-done | bytes 36896 | tf_op jit(solution)/shard_map/ppermute | solution.py:702
  16.4 0.1 broadcast_multiply_fusion.1
  16.5 1.7 %collective-permute-start.5 = (f32[16,1152]{1,0:T(8,128)S(1)}, f32[16,1152]{1,0:T(8,128)S(1)}, u32[]{:S(2)}, u32[]{:S(2)}) collective-permute-start(f32[16,1152]{1,0:T(8,128)S(1)} %maximum_add_fusion.after_ref.own_ref), channel_id=1, source_target_pairs={{0,15},{1,2},{2,1},{3,4},{4,3},{5,6},{6,5},{7,8},{8,7},{9,10},{10,... | collective-permute-start | bytes 221192 | tf_op jit(solution)/shard_map/ppermute | solution.py:707
  18.2 0.0 collective-permute-start.6
  18.2 2.9 %step.1 = (f32[1,17424]{1,0:T(1,128)}, f32[1,17424]{1,0:T(1,128)}, f32[1,17424]{1,0:T(1,128)}, f32[1,17424]{1,0:T(1,128)}) custom-call(f32[2,144,128]{2,1,0:T(8,128)S(1)} %forces.1.force_ref, f32[2,128,128]{2,1,0:T(8,128)S(1)} %get-tuple-element.74.near_half_ref, f32[200,128]{1,0:T(8,128)S(1)} %get-tuple-element.67.flux_in_ref.near_flux_ref, ...), custom_call_target="tpu_custom_call" | custom-call | flops 200000000 | bytes 1000000 | tf_op jit(solution)/shard_map/step/pallas_call | solution.py:711
  21.2 1.9 %collective-permute-done.5.first_ref = f32[16,1152]{1,0:T(8,128)S(1)} collective-permute-done((f32[16,1152]{1,0:T(8,128)S(1)}, f32[16,1152]{1,0:T(8,128)S(1)}, u32[]{:S(2)}, u32[]{:S(2)}) %collective-permute-start.5) | collective-permute-done | bytes 73760 | tf_op jit(solution)/shard_map/ppermute | solution.py:707
  23.1 0.0 collective-permute-done.6.second_ref
  23.1 0.0 copy-done.1
  23.1 0.8 %band.1 = f32[16,1089]{1,0:T(8,128)} custom-call(s32[1]{0:T(128)} %bitcast.1.cut_ref, f32[16,1152]{1,0:T(8,128)S(1)} %maximum_add_fusion.after_ref.own_ref, f32[16,1152]{1,0:T(8,128)S(1)} %collective-permute-done.5.first_ref, f32[16,1152]{1,0:T(8,128)S(1)} %collective-permute-done.6.second_ref, bf16[2,16,288]{2,1,0:T(8,128)(2,1)S(1)} %copy-done.1), custom_call_target="tpu_custom_call" | custom-call | flops 20000000 | bytes 1000000 | tf_op jit(solution)/shard_map/band/pallas_call | solution.py:735
  (7 shorter events, 0.0 us)
Async XLA Ops:
  0.6 5.2 %copy-start = (f32[24,1152]{1,0:T(8,128)S(1)}, f32[24,1152]{1,0:T(8,128)}, u32[]{:S(2)}) copy-start(f32[24,1152]{1,0:T(8,128)} %constant.12.clone.cross_ref) | copy-start | bytes 331780
  1.9 7.6 %collective-permute-start = (f32[144,128]{1,0:T(8,128)S(1)}, f32[144,128]{1,0:T(8,128)S(1)}, u32[]{:S(2)}, u32[]{:S(2)}) collective-permute-start(f32[144,128]{1,0:T(8,128)S(1)} %get-tuple-element.43), channel_id=1, source_target_pairs={{0,1},{1,2},{2,3},{3,4},{4,5},{5,6},{6,7},{7,8},{8,9},{9,10},{10,1... | collective-permute-start | bytes 221192 | tf_op jit(solution)/shard_map/ppermute | solution.py:640
  3.1 8.4 %collective-permute-start.2 = (s32[8,128]{1,0:T(8,128)S(1)}, s32[8,128]{1,0:T(8,128)S(1)}, u32[]{:S(2)}, u32[]{:S(2)}) collective-permute-start(s32[8,128]{1,0:T(8,128)S(1)} %broadcast_in_dim.8.count_ref), channel_id=1, source_target_pairs={{0,1},{1,2},{2,3},{3,4},{4,5},{5,6},{6,7},{7,8},{8,9},{9,10},{10,1... | collective-permute-start | bytes 12296 | tf_op jit(solution)/shard_map/ppermute | solution.py:643
  7.7 3.8 %collective-permute-start.1 = (f32[32,128]{1,0:T(8,128)S(1)}, f32[32,128]{1,0:T(8,128)S(1)}, u32[]{:S(2)}, u32[]{:S(2)}) collective-permute-start(f32[32,128]{1,0:T(8,128)S(1)} %get-tuple-element.59), channel_id=1, source_target_pairs={{1,0},{2,1},{3,2},{4,3},{5,4},{6,5},{7,6},{8,7},{9,8},{10,9},{11,1... | collective-permute-start | bytes 49160 | tf_op jit(solution)/shard_map/ppermute | solution.py:667
  9.5 4.9 %collective-permute-start.4 = (f32[16,1152]{1,0:T(8,128)S(1)}, f32[16,1152]{1,0:T(8,128)S(1)}, u32[]{:S(2)}, u32[]{:S(2)}) collective-permute-start(f32[16,1152]{1,0:T(8,128)S(1)} %get-tuple-element.70), channel_id=1, source_target_pairs={{0,16},{16,0},{1,17},{17,1},{2,18},{18,2},{3,19},{19,3},{4,20},{20... | collective-permute-start | bytes 221192 | tf_op jit(solution)/shard_map/ppermute | solution.py:701
  12.4 4.0 %collective-permute-start.3 = (f32[8,1152]{1,0:T(8,128)S(1)}, f32[8,1152]{1,0:T(8,128)S(1)}, u32[]{:S(2)}, u32[]{:S(2)}) collective-permute-start(f32[8,1152]{1,0:T(8,128)S(1)} %near_layers.1), channel_id=1, source_target_pairs={{0,16},{16,0},{1,17},{17,1},{2,18},{18,2},{3,19},{19,3},{4,20},{20... | collective-permute-start | bytes 110600 | tf_op jit(solution)/shard_map/ppermute | solution.py:702
  16.5 6.5 %collective-permute-start.5 = (f32[16,1152]{1,0:T(8,128)S(1)}, f32[16,1152]{1,0:T(8,128)S(1)}, u32[]{:S(2)}, u32[]{:S(2)}) collective-permute-start(f32[16,1152]{1,0:T(8,128)S(1)} %maximum_add_fusion.after_ref.own_ref), channel_id=1, source_target_pairs={{0,15},{1,2},{2,1},{3,4},{4,3},{5,6},{6,5},{7,8},{8,7},{9,10},{10,... | collective-permute-start | bytes 221192 | tf_op jit(solution)/shard_map/ppermute | solution.py:707
  18.2 4.8 %collective-permute-start.6 = (f32[16,1152]{1,0:T(8,128)S(1)}, f32[16,1152]{1,0:T(8,128)S(1)}, u32[]{:S(2)}, u32[]{:S(2)}) collective-permute-start(f32[16,1152]{1,0:T(8,128)S(1)} %maximum_add_fusion.after_ref.own_ref), channel_id=1, source_target_pairs={{0,1},{1,0},{2,3},{3,2},{4,5},{5,4},{6,7},{7,6},{8,9},{9,8},{10,11... | collective-permute-start | bytes 221192 | tf_op jit(solution)/shard_map/ppermute | solution.py:708
  18.2 4.8 %copy-start.1 = (bf16[2,16,288]{2,1,0:T(8,128)(2,1)S(1)}, bf16[2,16,288]{2,1,0:T(8,128)(2,1)}, u32[]{:S(2)}) copy-start(bf16[2,16,288]{2,1,0:T(8,128)(2,1)} %constant.13.clone.band_ref) | copy-start | bytes 55300

commit v11 on v10

--- a/solution.py
+++ b/solution.py
@@ -107,7 +107,7 @@
 
 def pack_kernel(
     conn_hbm, shear_hbm, fwd_hbm, adj_hbm,
-    right_ref, left_ref, own_ref, code_ref, parts_ref,
+    small_ref, right_ref, left_ref, own_ref, code_ref, parts_ref,
     conn_ref, shear_ref, fwd_ref, adj_ref, block_ref, sem,
 ):
     copies = fetch(
@@ -136,6 +136,9 @@
         own_ref[ROWS * f + 136 : ROWS * f + 137, 0:16] = ref[0:1, NPTS - 16 : NPTS]
         right_ref[40 * f : 40 * f + 40, :] = own_ref[ROWS * f + 102 : ROWS * f + 142, :]
         left_ref[16 * f : 16 * f + 16, :] = own_ref[ROWS * f : ROWS * f + 16, :]
+        share = [float(DERIV[4, l]) * plane_of(own_ref, PYZ * (12 + l), ROWS * f) for l in range(4)]
+        small_ref[16 * f : 16 * f + 9, :] = (share[0] + share[1]) + (share[2] + share[3])
+        small_ref[16 * f + 9 : 16 * f + 16, :] = jnp.zeros((7, LANES), F32)
     copies[0].wait()
     block_ref[0:125, :] = shear_ref[...]
     block_ref[125:126, :] = slot.astype(F32)
@@ -145,6 +148,7 @@
     flux = add_parts(dot_nt(parts, pick))
     low = lax.broadcasted_iota(jnp.int32, (64, LANES), 1) < 64
     right_ref[80:144, :] = jnp.where(low, flux[0:64], flux[64:128])
+    small_ref[32:48, :] = jnp.where(low[0:16], flux[96:112], flux[112:128])
 
 
 def gll_weight(i):
@@ -317,7 +321,8 @@
 
 
 def own_kernel(turn, cut_ref, count_ref, own_ref, code_ref, parts_ref, cross_ref, *refs):
-    refs = refs[-OWN_OUTS - OWN_SCRATCH :]
+    outs = refs[len(refs) - OWN_SCRATCH - OWN_OUTS - turn : len(refs) - OWN_SCRATCH - turn]
+    refs = outs + refs[len(refs) - OWN_SCRATCH :]
     mine = (cut_ref[0] == 0) if turn == 0 else (cut_ref[0] != 0)
 
     @pl.when(mine)
@@ -362,7 +367,8 @@
 
     element = lax.broadcasted_iota(jnp.int32, (256, 256), 0)
     slot = lax.broadcasted_iota(jnp.int32, (1, 256), 1)
-    code = jnp.where(slot < count_ref[0:1, 0:1], code_ref[0:1, :], -1)
+    live = jnp.concatenate([count_ref[0:1, :], count_ref[0:1, :]], axis=1)
+    code = jnp.where(slot < live, code_ref[0:1, :], -1)
     pick = jnp.where(code == element, 1.0, 0.0).astype(BF16)
     moved_ref[0:128, :] = add_parts(dot_nt(parts_ref[...], pick))
     moved_ref[128:136, :] = jnp.zeros((8, 256), F32)
@@ -403,7 +409,7 @@
 
 def message_flux(prev_ref, count_ref, spread_ref):
     upper = pltpu.roll(prev_ref[80:144, :], 64, 1)
-    live = upper[61:62, :] < count_ref[0:1, 0:1].astype(F32)
+    live = upper[61:62, :] < count_ref[0:1, :].astype(F32)
     spread_ref[0:64, :] = jnp.where(live, prev_ref[80:144, :], 0.0)
     spread_ref[64:128, :] = jnp.where(live, upper, 0.0)
     spread_ref[128:136, :] = jnp.zeros((8, LANES), F32)
@@ -411,16 +417,13 @@
 
 
 def near_kernel(
-    prev_ref, next_ref, count_ref, flux_in_ref, slope_ref, near_kern_ref, cross_ref,
+    small_ref, next_ref, count_ref, flux_in_ref, slope_ref, near_kern_ref, kern_in_ref, cross_ref,
     kern_ref,
     plane_ref, new_ref, win_ref, elem_ref, flux_ref, line_ref, spread_ref,
 ):
     plane_ref[...] = jnp.zeros(plane_ref.shape, F32)
     for f in range(2):
-        share = None
-        for l in range(4):
-            term = float(DERIV[4, l]) * plane_of(prev_ref, 12 + PYZ * l, 40 * f)
-            share = term if share is None else share + term
+        share = small_ref[16 * f : 16 * f + 9, :]
         plane_ref[pl.ds(f, 9, stride=8), :] = share
         plane_ref[pl.ds(2 + f, 9, stride=8), :] = plane_of(next_ref, 0, 16 * f)
     make_windows(plane_ref, 0, 8, new_ref, 0)
@@ -434,7 +437,12 @@
                 new = float(DERIV[i, 4]) * new_ref[w, 16 + 8 * f : 24 + 8 * f, :]
                 win_ref[w, r : r + 8, :] = win_ref[w, r : r + 8, :] + new
     turned(win_ref, 0, elem_ref, 0)
-    place_flux(flux_ref, message_flux(prev_ref, count_ref, spread_ref), lambda i: [(0, 8 * NEAR_AT[0][i], 8)], (4,))
+    lower, upper = small_ref[32:48, :], pltpu.roll(small_ref[32:48, :], 64, 1)
+    live = upper[13:14, :] < count_ref[0:1, 0:1].astype(F32)
+    spread_ref[0:16, :] = jnp.where(live, lower, 0.0)
+    spread_ref[16:32, :] = jnp.where(live, upper, 0.0)
+    spread_ref[32:40, :] = jnp.zeros((8, LANES), F32)
+    place_flux(flux_ref, lambda i, ez: (spread_ref[4:36, :], 8 * ez), lambda i: [(0, 8 * NEAR_AT[0][i], 8)], (4,))
     scaled(flux_ref, lane_weight([NEAR_AT[0]]))
     kern = [[None] * 5 for _ in range(5)]
     for j in range(5):
@@ -446,7 +454,9 @@
     row = lax.broadcasted_iota(jnp.int32, (8, LANES), 0)
     tiles = [jnp.where((row == 0) | (row >= 4), v, 0.0) for v in gathered(win_ref, 0, 0)]
     for t, tile in enumerate(cross_smoothed(tiles, cross_ref)):
-        kern_ref[:, t * LANES : (t + 1) * LANES] = tile
+        columns = slice(t * LANES, (t + 1) * LANES)
+        kern_ref[0:8, columns] = kern_in_ref[0:8, columns] + jnp.where(row == 0, tile, 0.0)
+        kern_ref[8:16, columns] = kern_in_ref[8:16, columns] + jnp.where(row >= 4, tile, 0.0)
 
 
 def gathered(win_ref, base, h):
@@ -489,10 +499,10 @@
         line_ref[f, r0 + 1 : r0 + 10, :] = line_ref[f, r0 + 1 : r0 + 10, :] + spill
 
 
-def force_kernel(elem_ref, flux_ref, out_ref, win_ref, line_ref, force_ref, plane_ref):
+def force_kernel(elem_ref, flux_ref, out_ref, win_ref, fold_ref, force_ref, plane_ref):
     out_ref[...] = jnp.zeros(out_ref.shape, F32)
     for f in range(2):
-        force_terms(elem_ref, f, 2 + f, flux_ref, line_ref, win_ref, 0)
+        force_terms(elem_ref, f, 2 + f, flux_ref, fold_ref, win_ref, 0)
         summed_along_x(win_ref, OWN_AT, force_ref, 0)
         to_planes(force_ref, 0, plane_ref)
         for x in range(13):
@@ -504,21 +514,12 @@
             add_plane(out_ref, f, x, sum(flat[1:], flat[0]))
 
 
-def step_kernel(
-    force_ref, near_half_ref, near_flux_ref, prev_ref, next_ref, count_ref, fwd_hbm, fwd_speed_hbm, adj_hbm, adj_speed_hbm, mass_hbm, after_ref,
-    fwd_out_ref, fwd_speed_out_ref, adj_out_ref, adj_speed_out_ref,
-    fwd_ref, fwd_speed_ref, adj_ref, adj_speed_ref, mass_ref, plane_ref, line_ref,
-    flux_ref, win_ref, elem_ref, fold_ref, near_ref, near_win_ref, near_plane_ref, spread_ref, sem,
+def near_force_kernel(
+    force_ref, near_half_ref, near_flux_ref, prev_ref, next_ref, count_ref, after_ref,
+    out_ref,
+    win_ref, fold_ref, near_force_ref, plane_ref, flux_ref, elem_ref, near_win_ref, near_plane_ref, spread_ref,
 ):
-    copies = fetch(
-        sem,
-        (fwd_hbm, fwd_ref),
-        (fwd_speed_hbm, fwd_speed_ref),
-        (adj_hbm, adj_ref),
-        (adj_speed_hbm, adj_speed_ref),
-        (mass_hbm, mass_ref),
-    )
-    line_ref[...] = force_ref[...]
+    out_ref[...] = force_ref[...]
     near_plane_ref[...] = jnp.zeros(near_plane_ref.shape, F32)
     for f in range(2):
         for i in range(5):
@@ -537,11 +538,16 @@
         turned(near_win_ref, LANES * f, elem_ref, 0)
         turned(win_ref, 0, elem_ref, 1)
         force_terms(elem_ref, 0, 1, flux_ref, fold_ref, win_ref, 0)
-        summed_along_x(win_ref, NEAR_AT, near_ref, 0)
-        to_planes(near_ref, 0, plane_ref)
+        summed_along_x(win_ref, NEAR_AT, near_force_ref, 0)
+        to_planes(near_force_ref, 0, plane_ref)
         for x, r in [(0, NEAR_AT[0][4])] + [(12 + i, NEAR_AT[1][i]) for i in range(4)]:
-            add_plane(line_ref, f, x, plane_ref[pl.ds(r, 9, stride=16), :])
-
+            add_plane(out_ref, f, x, plane_ref[pl.ds(r, 9, stride=16), :])
+
+
+def step_kernel(
+    line_ref, fwd_ref, fwd_speed_ref, adj_ref, adj_speed_ref, mass_ref,
+    fwd_out_ref, fwd_speed_out_ref, adj_out_ref, adj_speed_out_ref,
+):
     def step(lo, hi, force):
         shape = (hi - lo) // force[0].shape[1], force[0].shape[1]
         take = lambda ref: ref[0:1, lo:hi].reshape(shape)
@@ -553,8 +559,6 @@
         adj_speed_out_ref[0:1, lo:hi] = speed.reshape(1, hi - lo)
         adj_out_ref[0:1, lo:hi] = (take(adj_ref) + TIME_STEP * speed).reshape(1, hi - lo)
 
-    for c in copies:
-        c.wait()
     for r in range(0, 136, 8):
         step(r * LANES, (r + 8) * LANES, [line_ref[f, r : r + 8, :] for f in range(2)])
     step(NPTS - 16, NPTS, [line_ref[f, 136:137, 0:16] for f in range(2)])
@@ -598,8 +602,8 @@
     def in_hbm(block):
         return pltpu.with_memory_space_constraint(block, pltpu.HBM)
 
-    def cost(flops, moved=1000000):
-        return pl.CostEstimate(flops=flops, bytes_accessed=moved, transcendentals=0)
+    def cost(flops):
+        return pl.CostEstimate(flops=flops, bytes_accessed=1000000, transcendentals=0)
 
     dma = pltpu.SemaphoreType.DMA
     point_row = pltpu.VMEM((1, NPTS), F32)
@@ -615,9 +619,10 @@
 
     fields = (in_hbm(forward_displacement), in_hbm(adjoint_displacement))
     cross = held(jnp.asarray(cross_table()))
-    right, left, own, code, parts = pl.pallas_call(
+    small, right, left, own, code, parts = pl.pallas_call(
         pack_kernel,
         out_shape=[
+            pltpu.VMEM((48, LANES), F32),
             pltpu.VMEM((144, LANES), F32),
             pltpu.VMEM((32, LANES), F32),
             pltpu.VMEM((2 * ROWS, LANES), F32),
@@ -637,7 +642,7 @@
         name="pack",
     )(in_hbm(connectivity), in_hbm(shear_modulus), *fields)
     to_next = [(i, (i + 1) % cuts) for i in range(cuts)]
-    prev = lax.ppermute(right, "cuts", to_next)
+    small = lax.ppermute(small, "cuts", to_next)
     count, left = lax.optimization_barrier((element_count, left))
     count = jnp.broadcast_to(count.reshape(1, 1), (8, LANES))
     prev_count = lax.ppermute(count, "cuts", to_next)
@@ -649,7 +654,7 @@
         given = (cut, held(count), held(own), held(code), held(parts), cross)
         return pl.pallas_call(
             functools.partial(own_kernel, turn),
-            out_shape=own_blocks,
+            out_shape=own_blocks + [pltpu.VMEM((144, LANES), F32)] * turn,
             in_specs=[smem] + [vmem] * (5 + len(before)) + [anywhere] * len(waits),
             scratch_shapes=[
                 pltpu.VMEM((2 * 9 * 24, LANES), F32),
@@ -665,11 +670,12 @@
 
     left, *blocks = lax.optimization_barrier((left, *own_part(0, [])))
     after = lax.ppermute(left, "cuts", [((i + 1) % cuts, i) for i in range(cuts)])
-    elem, flux, near_flux, near_win, near_slope, near_kern, kern = own_part(1, blocks, [prev])
-    near = pl.pallas_call(
+    elem, flux, near_flux, near_win, near_slope, near_kern, kern, right = own_part(1, blocks + [right], [small])
+    prev = lax.ppermute(right, "cuts", to_next)
+    kern = pl.pallas_call(
         near_kernel,
-        out_shape=pltpu.VMEM((8, 9 * LANES), F32),
-        in_specs=[vmem] * 7,
+        out_shape=kern_block,
+        in_specs=[vmem] * 8,
         scratch_shapes=[
             pltpu.VMEM((72, LANES), F32),
             pltpu.VMEM((2, 64, LANES), F32),
@@ -679,58 +685,60 @@
             line_block,
             pltpu.VMEM((136, LANES), F32),
         ],
-        cost_estimate=cost(200000000, 40000000),
+        cost_estimate=cost(200000000),
         name="near_layers",
-    )(held(prev), held(after), held(prev_count), held(near_flux), held(near_slope), held(near_kern), cross)
+    )(held(small), held(after), held(prev_count), held(near_flux), held(near_slope), held(near_kern), held(kern), cross)
 
     force = pl.pallas_call(
         force_kernel,
         out_shape=pltpu.VMEM((2, ROWS, LANES), F32),
         in_specs=[vmem] * 2,
         scratch_shapes=[windows(2), line_block, windows(1), pltpu.VMEM((144, LANES), F32)],
-        cost_estimate=cost(200000000, 40000000),
+        cost_estimate=cost(200000000),
         name="forces",
     )(held(elem), held(flux))
 
-    def joined(rows, near):
-        low = (lax.broadcasted_iota(jnp.int32, (8, 1), 0) < 4).astype(F32)
-        return rows + jnp.concatenate([near * low, near * (1.0 - low)], axis=0)
-
     if events == 2:
-        swap = [(0, 1), (1, 0)]
-        both = kern + lax.ppermute(kern, "event", swap)
-        other = lax.ppermute(near, "event", swap)
-        other, both, force = lax.optimization_barrier((other, both, force))
-        kern = joined(both, near + other)
-    else:
-        kern = lax.psum(joined(kern, near), "event")
+        other = lax.ppermute(kern, "event", [(0, 1), (1, 0)])
+        other, force = lax.optimization_barrier((other, force))
+        kern = kern + other
+    elif events > 2:
+        kern = lax.psum(kern, "event")
     kern_first = lax.ppermute(kern, "cuts", pairs_first)
     kern_second = lax.ppermute(kern, "cuts", pairs_second)
 
+    force = pl.pallas_call(
+        near_force_kernel,
+        out_shape=pltpu.VMEM((2, ROWS, LANES), F32),
+        in_specs=[vmem] * 7,
+        scratch_shapes=[
+            windows(2),
+            line_block,
+            windows(1),
+            pltpu.VMEM((144, LANES), F32),
+            flux_block,
+            elements(2),
+            windows(2),
+            pltpu.VMEM((2 * 72, LANES), F32),
+            pltpu.VMEM((136, LANES), F32),
+        ],
+        cost_estimate=cost(200000000),
+        name="near_forces",
+    )(held(force), held(near_win), held(near_flux), held(prev), held(after), held(prev_count), held(kern))
     points = jax.ShapeDtypeStruct((1, NPTS), F32)
     outs = pl.pallas_call(
         step_kernel,
         out_shape=[points] * 4,
-        in_specs=[vmem] * 6 + [anywhere] * 5 + [vmem],
-        scratch_shapes=[point_row] * 4
-        + [pltpu.VMEM((NPTS,), F32), pltpu.VMEM((144, LANES), F32), pltpu.VMEM((2, ROWS, LANES), F32)]
-        + [flux_block, windows(2), elements(2), line_block, windows(1), windows(2)]
-        + [pltpu.VMEM((2 * 72, LANES), F32), pltpu.VMEM((136, LANES), F32), dma((5,))],
+        in_specs=[vmem] * 6,
         cost_estimate=cost(200000000),
         name="step",
     )(
         held(force),
-        held(near_win),
-        held(near_flux),
-        held(prev),
-        held(after),
-        held(prev_count),
-        fields[0],
-        in_hbm(forward_velocity),
-        fields[1],
-        in_hbm(adjoint_velocity),
-        in_hbm(inverse_mass),
-        held(kern),
+        held(forward_displacement),
+        held(forward_velocity),
+        held(adjoint_displacement),
+        held(adjoint_velocity),
+        held(inverse_mass),
     )
     shear_kernel = pl.pallas_call(
         band_kernel,

time: 24.1 us -> 22.6 us (0.938)
  waiting for transfers between devices: 6.28 us -> 3.84 us
  starting transfers between devices: 7.63 us -> 9.87 us
  Pallas kernels: 8.54 us -> 7.3 us
    ppermute x1, starting transfers between devices: 1.71 us -> 3.82 us  [on_device(): kern_first = lax.ppermute(kern, 'cuts', pairs_first)]
    ppermute x1, waiting for transfers between devices: 1.91 us -> 0.48 us  [on_device(): kern_first = lax.ppermute(kern, 'cuts', pairs_first)]
    pallas_call x5 -> x6, Pallas kernels: 6.98 us -> 5.74 us  [the longest x2 1.6 us: own_part(): pl.pallas_call(functools.partial(own_kernel, turn), out_shape=own_blocks...]
    ppermute x1, waiting for transfers between devices: 1.25 us -> 0.22 us  [on_device(): prev = lax.ppermute(right, 'cuts', to_next)]
    ppermute x2, waiting for transfers between devices: 3.11 us -> 2.39 us  [the longest x1 1.7 us: on_device(): other = lax.ppermute(kern, 'event', [(0, 1), (1, 0)])]
    ppermute x1, starting transfers between devices: 0.5 us -> 0.01 us  [on_device(): prev = lax.ppermute(right, 'cuts', to_next)]
    ppermute x1, waiting for transfers between devices: 0.01 us -> 0.5 us  [on_device(): prev_count = lax.ppermute(count, 'cuts', to_next)]
    ppermute x2, starting transfers between devices: 2.16 us -> 2.5 us  [the longest x1 2 us: on_device(): other = lax.ppermute(kern, 'event', [(0, 1), (1, 0)])]
  transfers between devices with their start and end apart: 7 -> 7, of which waited for: 4 -> 6; matrix products, arithmetic and copies ran while one was open for 0% -> 0% of each run, Pallas kernels for 27% -> 19%
where the time goes in v11:
time: 22.6 us; the launch traced here: 22.5 us
  starting transfers between devices  9.87 us (44%)
  Pallas kernels  7.3 us (32%)
  waiting for transfers between devices  3.84 us (17%)
  between operations  1.41 us (6%)
    ppermute x1, starting transfers between devices, on_device(): kern_first = lax.ppermute(kern, 'cuts', pairs_first)  3.82 us
    ppermute x1, starting transfers between devices, on_device(): prev_count = lax.ppermute(count, 'cuts', to_next)  2.69 us
    ppermute x1, starting transfers between devices, on_device(): other = lax.ppermute(kern, 'event', [(0, 1), (1, 0)])  2 us
    ppermute x1, waiting for transfers between devices, on_device(): other = lax.ppermute(kern, 'event', [(0, 1), (1, 0)])  1.7 us
    pallas_call x2, Pallas kernels, own_part(): pl.pallas_call(functools.partial(own_kernel, turn), out_shape=own_blocks...  1.6 us
    pallas_call x1, Pallas kernels, on_device(): pl.pallas_call(pack_kernel, out_shape=[pltpu.VMEM((48, LANES), F32), pltp...  1.44 us
    pallas_call x1, Pallas kernels, on_device(): pl.pallas_call(near_force_kernel, out_shape=pltpu.VMEM((2, ROWS, LANES),...  1.19 us
    ppermute x1, starting transfers between devices, on_device(): lax.ppermute(left, 'cuts', [((i + 1) % cuts, i) for i in range(cuts)])  0.86 us
  transfers between devices with their start and end apart: 7, of which 6 were waited for; matrix products, arithmetic and copies ran while one was open for 0% of the time, Pallas kernels for 19%

profile of v11, /device:TPU:0, one launch (start us, length us, event | category | flops | bytes accessed | tf_op | source)
XLA Modules:
  0.0 22.5 jit_solution(2668776451590357742)
XLA Ops:
  0.6 0.0 copy-start
  0.6 1.4 %pack.1 = (f32[48,128]{1,0:T(8,128)S(1)}, f32[144,128]{1,0:T(8,128)S(1)}, f32[32,128]{1,0:T(8,128)S(1)}, f32[288,128]{1,0:T(8,128)S(1)}, s32[8,256]{1,0:T(8,128)S(1)}, /*index=5*/bf16[384,256]{1,0:T(8,128)(2,1)S(1)}) custom-call(s32[125,256]{1,0:T(8,128)} %conn_hbm.1, f32[125,256]{1,0:T(8,128)} %shear_hbm.1, f32[1,17424]{1,0:T(1,128)} %fwd_ref.1, ...), custom_call_target="tpu_custom_call" | custom-call | flops 100000000 | bytes 1000000 | tf_op jit(solution)/shard_map/pack/pallas_call | solution.py:622
  2.1 0.5 %collective-permute-start = (f32[48,128]{1,0:T(8,128)S(1)}, f32[48,128]{1,0:T(8,128)S(1)}, u32[]{:S(2)}, u32[]{:S(2)}) collective-permute-start(f32[48,128]{1,0:T(8,128)S(1)} %get-tuple-element.44), channel_id=1, source_target_pairs={{0,1},{1,2},{2,3},{3,4},{4,5},{5,6},{6,7},{7,8},{8,9},{9,10},{10,1... | collective-permute-start | bytes 73736 | tf_op jit(solution)/shard_map/ppermute | solution.py:645
  3.2 2.7 %collective-permute-start.2 = (s32[8,128]{1,0:T(8,128)S(1)}, s32[8,128]{1,0:T(8,128)S(1)}, u32[]{:S(2)}, u32[]{:S(2)}) collective-permute-start(s32[8,128]{1,0:T(8,128)S(1)} %broadcast_in_dim.8.count_ref), channel_id=1, source_target_pairs={{0,1},{1,2},{2,3},{3,4},{4,5},{5,6},{6,7},{7,8},{8,9},{9,10},{10,1... | collective-permute-start | bytes 12296 | tf_op jit(solution)/shard_map/ppermute | solution.py:648
  5.9 1.6 %own_layers.2 = (f32[4,168,128]{2,1,0:T(8,128)S(1)}, f32[200,128]{1,0:T(8,128)S(1)}, f32[200,128]{1,0:T(8,128)S(1)}, f32[2,128,128]{2,1,0:T(8,128)S(1)}, f32[2,1...) custom-call(s32[1]{0:T(128)} %bitcast.1.cut_ref, s32[8,128]{1,0:T(8,128)S(1)} %broadcast_in_dim.8.count_ref, ...), custom_call_target="tpu_custom_call" | custom-call | flops 300000000 | bytes 1000000 | tf_op jit(solution)/shard_map/own_layers/pallas_call | solution.py:655
  7.5 0.9 %collective-permute-start.1 = (f32[32,128]{1,0:T(8,128)S(1)}, f32[32,128]{1,0:T(8,128)S(1)}, u32[]{:S(2)}, u32[]{:S(2)}) collective-permute-start(f32[32,128]{1,0:T(8,128)S(1)} %get-tuple-element.60), channel_id=1, source_target_pairs={{1,0},{2,1},{3,2},{4,3},{5,4},{6,5},{7,6},{8,7},{9,8},{10,9},{11,1... | collective-permute-start | bytes 49160 | tf_op jit(solution)/shard_map/ppermute | solution.py:672
  8.4 0.7 %collective-permute-done.refs_8_.small_ref = f32[48,128]{1,0:T(8,128)S(1)} collective-permute-done((f32[48,128]{1,0:T(8,128)S(1)}, f32[48,128]{1,0:T(8,128)S(1)}, u32[]{:S(2)}, u32[]{:S(2)}) %collective-permute-start) | collective-permute-done | bytes 24608 | tf_op jit(solution)/shard_map/ppermute | solution.py:645
  9.1 0.5 %collective-permute-done.2.count_ref = s32[8,128]{1,0:T(8,128)S(1)} collective-permute-done((s32[8,128]{1,0:T(8,128)S(1)}, s32[8,128]{1,0:T(8,128)S(1)}, u32[]{:S(2)}, u32[]{:S(2)}) %collective-permute-start.2) | collective-permute-done | bytes 4128 | tf_op jit(solution)/shard_map/ppermute | solution.py:648
  9.6 0.3 %collective-permute-done.1.next_ref = f32[32,128]{1,0:T(8,128)S(1)} collective-permute-done((f32[32,128]{1,0:T(8,128)S(1)}, f32[32,128]{1,0:T(8,128)S(1)}, u32[]{:S(2)}, u32[]{:S(2)}) %collective-permute-start.1) | collective-permute-done | bytes 16416 | tf_op jit(solution)/shard_map/ppermute | solution.py:672
  9.8 0.8 %near_layers.1 = f32[16,1152]{1,0:T(8,128)S(1)} custom-call(f32[48,128]{1,0:T(8,128)S(1)} %collective-permute-done.refs_8_.small_ref, f32[32,128]{1,0:T(8,128)S(1)} %collective-permute-done.1.next_ref, s32[8,128]{1,0:T(8,128)S(1)} %collective-permute-done.2.count_ref, f32[200,128]{1,0:T(8,128)S(1)} %get-tuple-element.69.flux_in_ref.near_flux_ref, ...), custom_call_target="tpu_custom_call" | custom-call | flops 200000000 | bytes 1000000 | tf_op jit(solution)/shard_map/near_layers/pallas_call | solution.py:675
  10.6 2.0 %collective-permute-start.3 = (f32[16,1152]{1,0:T(8,128)S(1)}, f32[16,1152]{1,0:T(8,128)S(1)}, u32[]{:S(2)}, u32[]{:S(2)}) collective-permute-start(f32[16,1152]{1,0:T(8,128)S(1)} %near_layers.1), channel_id=1, source_target_pairs={{0,16},{16,0},{1,17},{17,1},{2,18},{18,2},{3,19},{19,3},{4,20},{20... | collective-permute-start | bytes 221192 | tf_op jit(solution)/shard_map/ppermute | solution.py:702
  12.6 0.0 collective-permute-start.4
  12.6 0.7 %forces.1.force_ref = f32[2,144,128]{2,1,0:T(8,128)S(1)} custom-call(f32[4,168,128]{2,1,0:T(8,128)S(1)} %get-tuple-element.73.elem_ref, f32[200,128]{1,0:T(8,128)S(1)} %get-tuple-element.74.flux_ref), custom_call_target="tpu_custom_call" | custom-call | flops 200000000 | bytes 1000000 | tf_op jit(solution)/shard_map/forces/pallas_call | solution.py:692
  13.4 1.7 %collective-permute-done.3 = f32[16,1152]{1,0:T(8,128)S(1)} collective-permute-done((f32[16,1152]{1,0:T(8,128)S(1)}, f32[16,1152]{1,0:T(8,128)S(1)}, u32[]{:S(2)}, u32[]{:S(2)}) %collective-permute-start.3) | collective-permute-done | bytes 73760 | tf_op jit(solution)/shard_map/ppermute | solution.py:702
  15.1 3.8 %collective-permute-start.5 = (f32[16,1152]{1,0:T(8,128)S(1)}, f32[16,1152]{1,0:T(8,128)S(1)}, u32[]{:S(2)}, u32[]{:S(2)}) collective-permute-start(f32[16,1152]{1,0:T(8,128)S(1)} %add.3.after_ref.own_ref), channel_id=1, source_target_pairs={{0,15},{1,2},{2,1},{3,4},{4,3},{5,6},{6,5},{7,8},{8,7},{9,10},{10,... | collective-permute-start | bytes 221192 | tf_op jit(solution)/shard_map/ppermute | solution.py:707
  18.9 0.0 collective-permute-start.6
  18.9 0.2 collective-permute-done.4.prev_ref
  19.1 0.0 copy-start.6
  19.1 1.2 %near_forces.1.line_ref = f32[2,144,128]{2,1,0:T(8,128)S(1)} custom-call(f32[2,144,128]{2,1,0:T(8,128)S(1)} %forces.1.force_ref, f32[2,128,128]{2,1,0:T(8,128)S(1)} %get-tuple-element.76.near_half_ref, f32[200,128]{1,0:T(8,128)S(1)} %get-tuple-element.69.flux_in_ref.near_flux_ref, f32[144,128]{1,0:T(8,128)S(1)} %collective-permute-done.4.prev_ref, ...), custom_call_target="tpu_custom_call" | custom-call | flops 200000000 | bytes 1000000 | tf_op jit(solution)/shard_map/near_forces/pallas_call | solution.py:710
  20.4 0.0 copy-start.3
  20.4 0.7 %step.1 = (f32[1,17424]{1,0:T(1,128)}, f32[1,17424]{1,0:T(1,128)}, f32[1,17424]{1,0:T(1,128)}, f32[1,17424]{1,0:T(1,128)}) custom-call(f32[2,144,128]{2,1,0:T(8,128)S(1)} %near_forces.1.line_ref, f32[1,17424]{1,0:T(1,128)S(1)} %copy-done.1, f32[1,17424]{1,0:T(1,128)S(1)} %copy-done.5, f32[1,17424]{1,0:T(1,128)S(1)} %copy-done.2, f32[1,17424]{1,0:T(1,128)S(1)} %copy-done.6, ...), custom_call_target="tpu_custom_call" | custom-call | flops 200000000 | bytes 1000000 | tf_op jit(solution)/shard_map/step/pallas_call | solution.py:729
  21.1 0.5 %collective-permute-done.5.first_ref = f32[16,1152]{1,0:T(8,128)S(1)} collective-permute-done((f32[16,1152]{1,0:T(8,128)S(1)}, f32[16,1152]{1,0:T(8,128)S(1)}, u32[]{:S(2)}, u32[]{:S(2)}) %collective-permute-start.5) | collective-permute-done | bytes 73760 | tf_op jit(solution)/shard_map/ppermute | solution.py:707
  21.6 0.0 collective-permute-done.6.second_ref
  21.6 0.8 %band.1 = f32[16,1089]{1,0:T(8,128)} custom-call(s32[1]{0:T(128)} %bitcast.1.cut_ref, f32[16,1152]{1,0:T(8,128)S(1)} %add.3.after_ref.own_ref, f32[16,1152]{1,0:T(8,128)S(1)} %collective-permute-done.5.first_ref, f32[16,1152]{1,0:T(8,128)S(1)} %collective-permute-done.6.second_ref, bf16[2,16,288]{2,1,0:T(8,128)(2,1)S(1)} %copy-done.3), custom_call_target="tpu_custom_call" | custom-call | flops 20000000 | bytes 1000000 | tf_op jit(solution)/shard_map/band/pallas_call | solution.py:743
  (14 shorter events, 0.0 us)
Async XLA Ops:
  0.6 5.3 %copy-start = (f32[24,1152]{1,0:T(8,128)S(1)}, f32[24,1152]{1,0:T(8,128)}, u32[]{:S(2)}) copy-start(f32[24,1152]{1,0:T(8,128)} %constant.8.clone.cross_ref) | copy-start | bytes 331780
  2.1 7.0 %collective-permute-start = (f32[48,128]{1,0:T(8,128)S(1)}, f32[48,128]{1,0:T(8,128)S(1)}, u32[]{:S(2)}, u32[]{:S(2)}) collective-permute-start(f32[48,128]{1,0:T(8,128)S(1)} %get-tuple-element.44), channel_id=1, source_target_pairs={{0,1},{1,2},{2,3},{3,4},{4,5},{5,6},{6,7},{7,8},{8,9},{9,10},{10,1... | collective-permute-start | bytes 73736 | tf_op jit(solution)/shard_map/ppermute | solution.py:645
  3.2 6.3 %collective-permute-start.2 = (s32[8,128]{1,0:T(8,128)S(1)}, s32[8,128]{1,0:T(8,128)S(1)}, u32[]{:S(2)}, u32[]{:S(2)}) collective-permute-start(s32[8,128]{1,0:T(8,128)S(1)} %broadcast_in_dim.8.count_ref), channel_id=1, source_target_pairs={{0,1},{1,2},{2,3},{3,4},{4,5},{5,6},{6,7},{7,8},{8,9},{9,10},{10,1... | collective-permute-start | bytes 12296 | tf_op jit(solution)/shard_map/ppermute | solution.py:648
  7.5 2.3 %collective-permute-start.1 = (f32[32,128]{1,0:T(8,128)S(1)}, f32[32,128]{1,0:T(8,128)S(1)}, u32[]{:S(2)}, u32[]{:S(2)}) collective-permute-start(f32[32,128]{1,0:T(8,128)S(1)} %get-tuple-element.60), channel_id=1, source_target_pairs={{1,0},{2,1},{3,2},{4,3},{5,4},{6,5},{7,6},{8,7},{9,8},{10,9},{11,1... | collective-permute-start | bytes 49160 | tf_op jit(solution)/shard_map/ppermute | solution.py:672
  10.6 4.4 %collective-permute-start.3 = (f32[16,1152]{1,0:T(8,128)S(1)}, f32[16,1152]{1,0:T(8,128)S(1)}, u32[]{:S(2)}, u32[]{:S(2)}) collective-permute-start(f32[16,1152]{1,0:T(8,128)S(1)} %near_layers.1), channel_id=1, source_target_pairs={{0,16},{16,0},{1,17},{17,1},{2,18},{18,2},{3,19},{19,3},{4,20},{20... | collective-permute-start | bytes 221192 | tf_op jit(solution)/shard_map/ppermute | solution.py:702
  12.6 6.5 %collective-permute-start.4 = (f32[144,128]{1,0:T(8,128)S(1)}, f32[144,128]{1,0:T(8,128)S(1)}, u32[]{:S(2)}, u32[]{:S(2)}) collective-permute-start(f32[144,128]{1,0:T(8,128)S(1)} %get-tuple-element.77), channel_id=1, source_target_pairs={{0,1},{1,2},{2,3},{3,4},{4,5},{5,6},{6,7},{7,8},{8,9},{9,10},{10,1... | collective-permute-start | bytes 221192 | tf_op jit(solution)/shard_map/ppermute | solution.py:674
  15.1 6.5 %collective-permute-start.5 = (f32[16,1152]{1,0:T(8,128)S(1)}, f32[16,1152]{1,0:T(8,128)S(1)}, u32[]{:S(2)}, u32[]{:S(2)}) collective-permute-start(f32[16,1152]{1,0:T(8,128)S(1)} %add.3.after_ref.own_ref), channel_id=1, source_target_pairs={{0,15},{1,2},{2,1},{3,4},{4,3},{5,6},{6,5},{7,8},{8,7},{9,10},{10,... | collective-permute-start | bytes 221192 | tf_op jit(solution)/shard_map/ppermute | solution.py:707
  18.9 2.7 %collective-permute-start.6 = (f32[16,1152]{1,0:T(8,128)S(1)}, f32[16,1152]{1,0:T(8,128)S(1)}, u32[]{:S(2)}, u32[]{:S(2)}) collective-permute-start(f32[16,1152]{1,0:T(8,128)S(1)} %add.3.after_ref.own_ref), channel_id=1, source_target_pairs={{0,1},{1,0},{2,3},{3,2},{4,5},{5,4},{6,7},{7,6},{8,9},{9,8},{10,11... | collective-permute-start | bytes 221192 | tf_op jit(solution)/shard_map/ppermute | solution.py:708
  19.1 1.2 %copy-start.1 = (f32[1,17424]{1,0:T(1,128)S(1)}, f32[1,17424]{1,0:T(1,128)}, u32[]{:S(2)}) copy-start(f32[1,17424]{1,0:T(1,128)} %fwd_ref.1) | copy-start | bytes 209092
  19.1 1.2 %copy-start.2 = (f32[1,17424]{1,0:T(1,128)S(1)}, f32[1,17424]{1,0:T(1,128)}, u32[]{:S(2)}) copy-start(f32[1,17424]{1,0:T(1,128)} %adj_ref.1) | copy-start | bytes 209092
  19.1 1.2 %copy-start.4 = (f32[17424]{0:T(1024)S(1)}, f32[17424]{0:T(1024)}, u32[]{:S(2)}) copy-start(f32[17424]{0:T(1024)} %mass_ref.1) | copy-start | bytes 209092
  19.1 1.2 %copy-start.5 = (f32[1,17424]{1,0:T(1,128)S(1)}, f32[1,17424]{1,0:T(1,128)}, u32[]{:S(2)}) copy-start(f32[1,17424]{1,0:T(1,128)} %fwd_speed_ref.1) | copy-start | bytes 209092
  19.1 1.3 %copy-start.6 = (f32[1,17424]{1,0:T(1,128)S(1)}, f32[1,17424]{1,0:T(1,128)}, u32[]{:S(2)}) copy-start(f32[1,17424]{1,0:T(1,128)} %adj_speed_ref.1) | copy-start | bytes 209092
  20.4 1.2 %copy-start.3 = (bf16[2,16,288]{2,1,0:T(8,128)(2,1)S(1)}, bf16[2,16,288]{2,1,0:T(8,128)(2,1)}, u32[]{:S(2)}) copy-start(bf16[2,16,288]{2,1,0:T(8,128)(2,1)} %constant.9.clone.band_ref) | copy-start | bytes 55300

commit v12 on v11

--- a/solution.py
+++ b/solution.py
@@ -19,7 +19,7 @@
 LANES = 128
 ROWS = 144
 TIME_STEP = 0.02
-OWN_OUTS, OWN_SCRATCH = 7, 5
+OWN_OUTS, OWN_SCRATCH = 8, 12
 F32 = jnp.float32
 BF16 = jnp.bfloat16
 
@@ -105,10 +105,40 @@
     return stacked[0:n] + (stacked[n : 2 * n] + stacked[2 * n : 3 * n])
 
 
+def slot_elements(conn_ref):
+    point = conn_ref[0:1, :].astype(F32)
+    x = jnp.floor((point + 0.5) * (1.0 / PYZ))
+    rest = point - x * PYZ
+    y = jnp.floor((rest + 0.5) * (1.0 / PZ))
+    z = rest - y * PZ
+    return (8.0 * z + 2.0 * x + 0.25 * y).astype(jnp.int32)
+
+
+def last_layer(code):
+    lane = lax.broadcasted_iota(jnp.int32, (LANES, 256), 0)
+    return jnp.where(code == ((lane >> 3) & 7) * 32 + 24 + (lane & 7), 1.0, 0.0).astype(BF16)
+
+
+def halves(flux):
+    n = flux.shape[0] // 2
+    low = lax.broadcasted_iota(jnp.int32, (n, LANES), 1) < 64
+    return jnp.where(low, flux[0:n], flux[n : 2 * n])
+
+
+def lay_rows(ref, target, first, last):
+    for r in range(first, last, 8):
+        full = min(r + 8, last, NPTS // LANES)
+        if full > r:
+            target[r - first : full - first, :] = ref[0:1, r * LANES : full * LANES].reshape(full - r, LANES)
+        if full < min(r + 8, last):
+            target[full - first : min(r + 8, last) - first, :] = jnp.zeros((min(r + 8, last) - full, LANES), F32)
+            target[full - first : full - first + 1, 0 : NPTS % LANES] = ref[0:1, full * LANES : NPTS]
+
+
 def pack_kernel(
     conn_hbm, shear_hbm, fwd_hbm, adj_hbm,
-    small_ref, right_ref, left_ref, own_ref, code_ref, parts_ref,
-    conn_ref, shear_ref, fwd_ref, adj_ref, block_ref, sem,
+    small_ref, left_ref,
+    conn_ref, shear_ref, fwd_ref, adj_ref, block_ref, line_ref, sem,
 ):
     copies = fetch(
         sem,
@@ -118,37 +148,20 @@
         (adj_hbm, adj_ref),
     )
     copies[1].wait()
-    point = conn_ref[0:1, :].astype(F32)
-    x = jnp.floor((point + 0.5) * (1.0 / PYZ))
-    rest = point - x * PYZ
-    y = jnp.floor((rest + 0.5) * (1.0 / PZ))
-    z = rest - y * PZ
-    code = (8.0 * z + 2.0 * x + 0.25 * y).astype(jnp.int32)
-    slot = lax.broadcasted_iota(jnp.int32, (1, 256), 1)
-    code_ref[...] = jnp.broadcast_to(code, (8, 256))
-    lane = lax.broadcasted_iota(jnp.int32, (LANES, 256), 0)
-    pick = jnp.where(code == ((lane >> 3) & 7) * 32 + 24 + (lane & 7), 1.0, 0.0).astype(BF16)
+    pick = last_layer(slot_elements(conn_ref))
+    copies[0].wait()
+    block_ref[0:29, :] = shear_ref[96:125, :]
+    block_ref[29:30, :] = lax.broadcasted_iota(jnp.int32, (1, 256), 1).astype(F32)
+    block_ref[30:32, :] = jnp.zeros((2, 256), F32)
+    flux = add_parts(dot_nt(jnp.concatenate(split3(block_ref[...]), axis=0), pick))
+    small_ref[32:48, :] = halves(flux)
     for f, ref in enumerate((fwd_ref, adj_ref)):
         copies[2 + f].wait()
-        for r in range(0, 136, 8):
-            own_ref[ROWS * f + r : ROWS * f + r + 8, :] = ref[0:1, r * LANES : (r + 8) * LANES].reshape(8, LANES)
-        own_ref[ROWS * f + 136 : ROWS * f + 144, :] = jnp.zeros((8, LANES), F32)
-        own_ref[ROWS * f + 136 : ROWS * f + 137, 0:16] = ref[0:1, NPTS - 16 : NPTS]
-        right_ref[40 * f : 40 * f + 40, :] = own_ref[ROWS * f + 102 : ROWS * f + 142, :]
-        left_ref[16 * f : 16 * f + 16, :] = own_ref[ROWS * f : ROWS * f + 16, :]
-        share = [float(DERIV[4, l]) * plane_of(own_ref, PYZ * (12 + l), ROWS * f) for l in range(4)]
+        lay_rows(ref, left_ref.at[16 * f : 16 * f + 16], 0, 16)
+        lay_rows(ref, line_ref, 102, 142)
+        share = [float(DERIV[4, l]) * plane_of(line_ref, 12 + PYZ * l, 0) for l in range(4)]
         small_ref[16 * f : 16 * f + 9, :] = (share[0] + share[1]) + (share[2] + share[3])
         small_ref[16 * f + 9 : 16 * f + 16, :] = jnp.zeros((7, LANES), F32)
-    copies[0].wait()
-    block_ref[0:125, :] = shear_ref[...]
-    block_ref[125:126, :] = slot.astype(F32)
-    block_ref[126:128, :] = jnp.zeros((2, 256), F32)
-    parts = jnp.concatenate(split3(block_ref[...]), axis=0)
-    parts_ref[...] = parts
-    flux = add_parts(dot_nt(parts, pick))
-    low = lax.broadcasted_iota(jnp.int32, (64, LANES), 1) < 64
-    right_ref[80:144, :] = jnp.where(low, flux[0:64], flux[64:128])
-    small_ref[32:48, :] = jnp.where(low[0:16], flux[96:112], flux[112:128])
 
 
 def gll_weight(i):
@@ -320,21 +333,32 @@
     return tiles
 
 
-def own_kernel(turn, cut_ref, count_ref, own_ref, code_ref, parts_ref, cross_ref, *refs):
-    outs = refs[len(refs) - OWN_SCRATCH - OWN_OUTS - turn : len(refs) - OWN_SCRATCH - turn]
-    refs = outs + refs[len(refs) - OWN_SCRATCH :]
+def own_kernel(turn, cut_ref, count_ref, conn_hbm, shear_hbm, fwd_hbm, adj_hbm, cross_ref, *refs):
+    refs = refs[len(refs) - OWN_OUTS - OWN_SCRATCH :]
     mine = (cut_ref[0] == 0) if turn == 0 else (cut_ref[0] != 0)
 
     @pl.when(mine)
     def _():
-        own_layers(count_ref, own_ref, code_ref, parts_ref, cross_ref, *refs)
+        own_layers(count_ref, conn_hbm, shear_hbm, fwd_hbm, adj_hbm, cross_ref, *refs)
 
 
 def own_layers(
-    count_ref, own_ref, code_ref, parts_ref, cross_ref,
-    elem_ref, flux_ref, near_flux_ref, near_win_ref, near_slope_ref, near_kern_ref, kern_ref,
+    count_ref, conn_hbm, shear_hbm, fwd_hbm, adj_hbm, cross_ref,
+    elem_ref, flux_ref, near_flux_ref, near_win_ref, near_slope_ref, near_kern_ref, kern_ref, right_ref,
     plane_ref, win_ref, line_ref, near_elem_ref, moved_ref,
+    conn_ref, shear_ref, fwd_ref, adj_ref, block_ref, own_ref, sem,
 ):
+    copies = fetch(
+        sem,
+        (fwd_hbm, fwd_ref),
+        (adj_hbm, adj_ref),
+        (conn_hbm.at[0:8], conn_ref),
+        (shear_hbm, shear_ref),
+    )
+    for f, ref in enumerate((fwd_ref, adj_ref)):
+        copies[f].wait()
+        lay_rows(ref, own_ref.at[ROWS * f : ROWS * f + ROWS], 0, ROWS)
+        right_ref[40 * f : 40 * f + 40, :] = own_ref[ROWS * f + 102 : ROWS * f + 142, :]
     plane_ref[...] = jnp.zeros(plane_ref.shape, F32)
     for f in range(2):
         base = 24 * 9 * f
@@ -365,12 +389,17 @@
                 r = 64 * f + 8 * NEAR_AT[1][i]
                 near_slope_ref[w, r : r + 8, :] = v
 
+    copies[2].wait()
+    copies[3].wait()
+    slot = lax.broadcasted_iota(jnp.int32, (1, 256), 1)
+    code = jnp.where(slot < count_ref[0:1, 0:1], slot_elements(conn_ref), -1)
     element = lax.broadcasted_iota(jnp.int32, (256, 256), 0)
-    slot = lax.broadcasted_iota(jnp.int32, (1, 256), 1)
-    live = jnp.concatenate([count_ref[0:1, :], count_ref[0:1, :]], axis=1)
-    code = jnp.where(slot < live, code_ref[0:1, :], -1)
-    pick = jnp.where(code == element, 1.0, 0.0).astype(BF16)
-    moved_ref[0:128, :] = add_parts(dot_nt(parts_ref[...], pick))
+    pick = jnp.concatenate([jnp.where(code == element, 1.0, 0.0).astype(BF16), last_layer(code)], axis=0)
+    block_ref[0:125, :] = shear_ref[...]
+    block_ref[125:128, :] = jnp.zeros((3, 256), F32)
+    moved = add_parts(dot_nt(jnp.concatenate(split3(block_ref[...]), axis=0), pick))
+    right_ref[80:144, :] = halves(moved[:, 256:])
+    moved_ref[0:128, :] = moved[:, 0:256]
     moved_ref[128:136, :] = jnp.zeros((8, 256), F32)
 
     def tile_of(i, ez):
@@ -407,11 +436,9 @@
         kern_ref[:, t * LANES : (t + 1) * LANES] = tile
 
 
-def message_flux(prev_ref, count_ref, spread_ref):
-    upper = pltpu.roll(prev_ref[80:144, :], 64, 1)
-    live = upper[61:62, :] < count_ref[0:1, :].astype(F32)
-    spread_ref[0:64, :] = jnp.where(live, prev_ref[80:144, :], 0.0)
-    spread_ref[64:128, :] = jnp.where(live, upper, 0.0)
+def message_flux(prev_ref, spread_ref):
+    spread_ref[0:64, :] = prev_ref[80:144, :]
+    spread_ref[64:128, :] = pltpu.roll(prev_ref[80:144, :], 64, 1)
     spread_ref[128:136, :] = jnp.zeros((8, LANES), F32)
     return lambda i, ez: (spread_ref[25 * i : 25 * i + 32, :], 8 * ez)
 
@@ -515,7 +542,7 @@
 
 
 def near_force_kernel(
-    force_ref, near_half_ref, near_flux_ref, prev_ref, next_ref, count_ref, after_ref,
+    force_ref, near_half_ref, near_flux_ref, prev_ref, next_ref, after_ref,
     out_ref,
     win_ref, fold_ref, near_force_ref, plane_ref, flux_ref, elem_ref, near_win_ref, near_plane_ref, spread_ref,
 ):
@@ -527,7 +554,7 @@
             near_plane_ref[pl.ds(72 * f + i, 9, stride=8), :] = flat
         near_win_ref[:, 128 * f : 128 * f + 64, :] = near_half_ref[:, 64 * f : 64 * f + 64, :]
         make_windows(near_plane_ref, 72 * f, 8, near_win_ref, 128 * f + 64)
-    place_flux(flux_ref, message_flux(prev_ref, count_ref, spread_ref), lambda i: [(0, 8 * NEAR_AT[0][i], 8)])
+    place_flux(flux_ref, message_flux(prev_ref, spread_ref), lambda i: [(0, 8 * NEAR_AT[0][i], 8)])
     scaled(flux_ref, lane_weight([NEAR_AT[0]]))
     flux_ref[...] = flux_ref[...] + near_flux_ref[...]
     for f in range(2):
@@ -619,28 +646,16 @@
 
     fields = (in_hbm(forward_displacement), in_hbm(adjoint_displacement))
     cross = held(jnp.asarray(cross_table()))
-    small, right, left, own, code, parts = pl.pallas_call(
+    conn, shear = in_hbm(connectivity), in_hbm(shear_modulus)
+    inputs = [pltpu.VMEM((8, 256), jnp.int32), pltpu.VMEM((125, 256), F32), point_row, point_row]
+    small, left = pl.pallas_call(
         pack_kernel,
-        out_shape=[
-            pltpu.VMEM((48, LANES), F32),
-            pltpu.VMEM((144, LANES), F32),
-            pltpu.VMEM((32, LANES), F32),
-            pltpu.VMEM((2 * ROWS, LANES), F32),
-            pltpu.VMEM((8, 256), jnp.int32),
-            pltpu.VMEM((384, 256), BF16),
-        ],
+        out_shape=[pltpu.VMEM((48, LANES), F32), pltpu.VMEM((32, LANES), F32)],
         in_specs=[anywhere] * 4,
-        scratch_shapes=[
-            pltpu.VMEM((8, 256), jnp.int32),
-            pltpu.VMEM((125, 256), F32),
-            point_row,
-            point_row,
-            pltpu.VMEM((128, 256), F32),
-            dma((4,)),
-        ],
+        scratch_shapes=inputs + [pltpu.VMEM((32, 256), F32), pltpu.VMEM((40, LANES), F32), dma((4,))],
         cost_estimate=cost(100000000),
         name="pack",
-    )(in_hbm(connectivity), in_hbm(shear_modulus), *fields)
+    )(conn, shear, *fields)
     to_next = [(i, (i + 1) % cuts) for i in range(cuts)]
     small = lax.ppermute(small, "cuts", to_next)
     count, left = lax.optimization_barrier((element_count, left))
@@ -648,20 +663,25 @@
     prev_count = lax.ppermute(count, "cuts", to_next)
     count, left = lax.optimization_barrier((count, left))
 
-    own_blocks = [elements(4), flux_block, flux_block, windows(1), windows(1), flux_block, kern_block]
+    message = pltpu.VMEM((144, LANES), F32)
+    own_blocks = [elements(4), flux_block, flux_block, windows(1), windows(1), flux_block, kern_block, message]
 
     def own_part(turn, before, waits=()):
-        given = (cut, held(count), held(own), held(code), held(parts), cross)
+        given = (cut, held(count), conn, shear, *fields, cross)
         return pl.pallas_call(
             functools.partial(own_kernel, turn),
-            out_shape=own_blocks + [pltpu.VMEM((144, LANES), F32)] * turn,
-            in_specs=[smem] + [vmem] * (5 + len(before)) + [anywhere] * len(waits),
+            out_shape=own_blocks,
+            in_specs=[smem, vmem] + [anywhere] * 4 + [vmem] * (1 + len(before)) + [anywhere] * len(waits),
             scratch_shapes=[
                 pltpu.VMEM((2 * 9 * 24, LANES), F32),
                 windows(4),
                 line_block,
                 elements(1),
                 pltpu.VMEM((136, 256), F32),
+                *inputs,
+                pltpu.VMEM((128, 256), F32),
+                pltpu.VMEM((2 * ROWS, LANES), F32),
+                dma((4,)),
             ],
             input_output_aliases={len(given) + n: n for n in range(len(before))},
             cost_estimate=cost(300000000),
@@ -670,7 +690,7 @@
 
     left, *blocks = lax.optimization_barrier((left, *own_part(0, [])))
     after = lax.ppermute(left, "cuts", [((i + 1) % cuts, i) for i in range(cuts)])
-    elem, flux, near_flux, near_win, near_slope, near_kern, kern, right = own_part(1, blocks + [right], [small])
+    elem, flux, near_flux, near_win, near_slope, near_kern, kern, right = own_part(1, blocks, [small])
     prev = lax.ppermute(right, "cuts", to_next)
     kern = pl.pallas_call(
         near_kernel,
@@ -710,7 +730,7 @@
     force = pl.pallas_call(
         near_force_kernel,
         out_shape=pltpu.VMEM((2, ROWS, LANES), F32),
-        in_specs=[vmem] * 7,
+        in_specs=[vmem] * 6,
         scratch_shapes=[
             windows(2),
             line_block,
@@ -724,7 +744,7 @@
         ],
         cost_estimate=cost(200000000),
         name="near_forces",
-    )(held(force), held(near_win), held(near_flux), held(prev), held(after), held(prev_count), held(kern))
+    )(held(force), held(near_win), held(near_flux), held(prev), held(after), held(kern))
     points = jax.ShapeDtypeStruct((1, NPTS), F32)
     outs = pl.pallas_call(
         step_kernel,

time: 22.6 us -> 23.1 us (1.022)
  waiting for transfers between devices: 3.84 us -> 1.96 us
  Pallas kernels: 7.3 us -> 8.61 us
  starting transfers between devices: 9.87 us -> 10.9 us
    ppermute x1, starting transfers between devices: 0.01 us -> 1.82 us  [on_device(): prev = lax.ppermute(right, 'cuts', to_next)]
    pallas_call x2, Pallas kernels: 1.6 us -> 3.04 us  [own_part(): pl.pallas_call(functools.partial(own_kernel, turn), out_shape=own_blocks,...]
    ppermute x1, waiting for transfers between devices: 1.7 us -> 0.33 us  [on_device(): other = lax.ppermute(kern, 'event', [(0, 1), (1, 0)])]
    ppermute x1, starting transfers between devices: 0.86 us -> 0.06 us  [on_device(): lax.ppermute(left, 'cuts', [((i + 1) % cuts, i) for i in range(cuts)])]
    ppermute x1, waiting for transfers between devices: 0.69 us -> 0.08 us  [on_device(): small = lax.ppermute(small, 'cuts', to_next)]
    ppermute x1, waiting for transfers between devices: 0.25 us -> 0.85 us  [on_device(): lax.ppermute(left, 'cuts', [((i + 1) % cuts, i) for i in range(cuts)])]
    ppermute x1, starting transfers between devices: 3.82 us -> 4.28 us  [on_device(): kern_first = lax.ppermute(kern, 'cuts', pairs_first)]
    ppermute x1, starting transfers between devices: 2 us -> 1.55 us  [on_device(): other = lax.ppermute(kern, 'event', [(0, 1), (1, 0)])]
  transfers between devices with their start and end apart: 7 -> 7, of which waited for: 6 -> 5; matrix products, arithmetic and copies ran while one was open for 0% -> 0% of each run, Pallas kernels for 19% -> 25%
where the time goes in v12:
time: 23.1 us; the launch traced here: 23 us
  starting transfers between devices  10.9 us (47%)
  Pallas kernels  8.61 us (37%)
  waiting for transfers between devices  1.96 us (8%)
  between operations  1.44 us (6%)
    ppermute x1, starting transfers between devices, on_device(): kern_first = lax.ppermute(kern, 'cuts', pairs_first)  4.28 us
    pallas_call x2, Pallas kernels, own_part(): pl.pallas_call(functools.partial(own_kernel, turn), out_shape=own_blocks,...  3.04 us
    ppermute x1, starting transfers between devices, on_device(): prev_count = lax.ppermute(count, 'cuts', to_next)  2.68 us
    ppermute x1, starting transfers between devices, on_device(): prev = lax.ppermute(right, 'cuts', to_next)  1.82 us
    ppermute x1, starting transfers between devices, on_device(): other = lax.ppermute(kern, 'event', [(0, 1), (1, 0)])  1.55 us
    pallas_call x1, Pallas kernels, on_device(): pl.pallas_call(pack_kernel, out_shape=[pltpu.VMEM((48, LANES), F32), pltp...  1.32 us
    pallas_call x1, Pallas kernels, on_device(): pl.pallas_call(near_force_kernel, out_shape=pltpu.VMEM((2, ROWS, LANES),...  1.18 us
    ppermute x1, waiting for transfers between devices, on_device(): lax.ppermute(left, 'cuts', [((i + 1) % cuts, i) for i in range(cuts)])  0.85 us
  transfers between devices with their start and end apart: 7, of which 5 were waited for; matrix products, arithmetic and copies ran while one was open for 0% of the time, Pallas kernels for 25%

profile of v12, /device:TPU:0, one launch (start us, length us, event | category | flops | bytes accessed | tf_op | source)
XLA Modules:
  0.0 23.0 jit_solution(11680927086008588278)
XLA Ops:
  0.6 0.0 copy-start.2
  0.6 1.3 %pack.1 = (f32[48,128]{1,0:T(8,128)S(1)}, f32[32,128]{1,0:T(8,128)S(1)}) custom-call(s32[125,256]{1,0:T(8,128)} %conn_hbm.5, f32[125,256]{1,0:T(8,128)} %shear_hbm.5, f32[1,17424]{1,0:T(1,128)} %fwd_ref.1, f32[1,17424]{1,0:T(1,128)} %adj_ref.1), custom_call_target="tpu_custom_call" | custom-call | flops 100000000 | bytes 1000000 | tf_op jit(solution)/shard_map/pack/pallas_call | solution.py:651
  2.0 0.5 %collective-permute-start = (f32[48,128]{1,0:T(8,128)S(1)}, f32[48,128]{1,0:T(8,128)S(1)}, u32[]{:S(2)}, u32[]{:S(2)}) collective-permute-start(f32[48,128]{1,0:T(8,128)S(1)} %get-tuple-element.42), channel_id=1, source_target_pairs={{0,1},{1,2},{2,3},{3,4},{4,5},{5,6},{6,7},{7,8},{8,9},{9,10},{10,1... | collective-permute-start | bytes 73736 | tf_op jit(solution)/shard_map/ppermute | solution.py:660
  3.1 2.7 %collective-permute-start.2 = (s32[8,128]{1,0:T(8,128)S(1)}, s32[8,128]{1,0:T(8,128)S(1)}, u32[]{:S(2)}, u32[]{:S(2)}) collective-permute-start(s32[8,128]{1,0:T(8,128)S(1)} %broadcast_in_dim.8.count_ref), channel_id=1, source_target_pairs={{0,1},{1,2},{2,3},{3,4},{4,5},{5,6},{6,7},{7,8},{8,9},{9,10},{10,1... | collective-permute-start | bytes 12296 | tf_op jit(solution)/shard_map/ppermute | solution.py:663
  5.8 3.0 %own_layers.2 = (f32[4,168,128]{2,1,0:T(8,128)S(1)}, f32[200,128]{1,0:T(8,128)S(1)}, f32[200,128]{1,0:T(8,128)S(1)}, f32[2,128,128]{2,1,0:T(8,128)S(1)}, f32[2,1...) custom-call(s32[1]{0:T(128)} %bitcast.1.cut_ref, ...), custom_call_target="tpu_custom_call" | custom-call | flops 300000000 | bytes 1000000 | tf_op jit(solution)/shard_map/own_layers/pallas_call | solution.py:671
  8.8 0.1 collective-permute-start.1
  8.9 0.1 collective-permute-done.refs_8_.small_ref
  9.0 0.5 %collective-permute-done.2.count_ref = s32[8,128]{1,0:T(8,128)S(1)} collective-permute-done((s32[8,128]{1,0:T(8,128)S(1)}, s32[8,128]{1,0:T(8,128)S(1)}, u32[]{:S(2)}, u32[]{:S(2)}) %collective-permute-start.2) | collective-permute-done | bytes 4128 | tf_op jit(solution)/shard_map/ppermute | solution.py:663
  9.5 0.9 %collective-permute-done.1.next_ref = f32[32,128]{1,0:T(8,128)S(1)} collective-permute-done((f32[32,128]{1,0:T(8,128)S(1)}, f32[32,128]{1,0:T(8,128)S(1)}, u32[]{:S(2)}, u32[]{:S(2)}) %collective-permute-start.1) | collective-permute-done | bytes 16416 | tf_op jit(solution)/shard_map/ppermute | solution.py:692
  10.3 0.8 %near_layers.1 = f32[16,1152]{1,0:T(8,128)S(1)} custom-call(f32[48,128]{1,0:T(8,128)S(1)} %collective-permute-done.refs_8_.small_ref, f32[32,128]{1,0:T(8,128)S(1)} %collective-permute-done.1.next_ref, s32[8,128]{1,0:T(8,128)S(1)} %collective-permute-done.2.count_ref, f32[200,128]{1,0:T(8,128)S(1)} %get-tuple-element.65.flux_in_ref.near_flux_ref, ...), custom_call_target="tpu_custom_call" | custom-call | flops 200000000 | bytes 1000000 | tf_op jit(solution)/shard_map/near_layers/pallas_call | solution.py:695
  11.1 1.6 %collective-permute-start.3 = (f32[16,1152]{1,0:T(8,128)S(1)}, f32[16,1152]{1,0:T(8,128)S(1)}, u32[]{:S(2)}, u32[]{:S(2)}) collective-permute-start(f32[16,1152]{1,0:T(8,128)S(1)} %near_layers.1), channel_id=1, source_target_pairs={{0,16},{16,0},{1,17},{17,1},{2,18},{18,2},{3,19},{19,3},{4,20},{20... | collective-permute-start | bytes 221192 | tf_op jit(solution)/shard_map/ppermute | solution.py:722
  12.7 1.8 %collective-permute-start.4 = (f32[144,128]{1,0:T(8,128)S(1)}, f32[144,128]{1,0:T(8,128)S(1)}, u32[]{:S(2)}, u32[]{:S(2)}) collective-permute-start(f32[144,128]{1,0:T(8,128)S(1)} %get-tuple-element.73), channel_id=1, source_target_pairs={{0,1},{1,2},{2,3},{3,4},{4,5},{5,6},{6,7},{7,8},{8,9},{9,10},{10,1... | collective-permute-start | bytes 221192 | tf_op jit(solution)/shard_map/ppermute | solution.py:694
  14.5 0.7 %forces.1.force_ref = f32[2,144,128]{2,1,0:T(8,128)S(1)} custom-call(f32[4,168,128]{2,1,0:T(8,128)S(1)} %get-tuple-element.69.elem_ref, f32[200,128]{1,0:T(8,128)S(1)} %get-tuple-element.70.flux_ref), custom_call_target="tpu_custom_call" | custom-call | flops 200000000 | bytes 1000000 | tf_op jit(solution)/shard_map/forces/pallas_call | solution.py:712
  15.2 0.3 %collective-permute-done.3 = f32[16,1152]{1,0:T(8,128)S(1)} collective-permute-done((f32[16,1152]{1,0:T(8,128)S(1)}, f32[16,1152]{1,0:T(8,128)S(1)}, u32[]{:S(2)}, u32[]{:S(2)}) %collective-permute-start.3) | collective-permute-done | bytes 73760 | tf_op jit(solution)/shard_map/ppermute | solution.py:722
  15.6 4.3 %collective-permute-start.5 = (f32[16,1152]{1,0:T(8,128)S(1)}, f32[16,1152]{1,0:T(8,128)S(1)}, u32[]{:S(2)}, u32[]{:S(2)}) collective-permute-start(f32[16,1152]{1,0:T(8,128)S(1)} %add.3.after_ref.own_ref), channel_id=1, source_target_pairs={{0,15},{1,2},{2,1},{3,4},{4,3},{5,6},{6,5},{7,8},{8,7},{9,10},{10,... | collective-permute-start | bytes 221192 | tf_op jit(solution)/shard_map/ppermute | solution.py:727
  19.9 0.0 copy-start.1
  19.9 0.0 copy-start.4
  19.9 0.0 copy-start.5
  19.9 0.0 copy-start.6
  19.9 1.2 %near_forces.1.line_ref = f32[2,144,128]{2,1,0:T(8,128)S(1)} custom-call(f32[2,144,128]{2,1,0:T(8,128)S(1)} %forces.1.force_ref, f32[2,128,128]{2,1,0:T(8,128)S(1)} %get-tuple-element.72.near_half_ref, f32[200,128]{1,0:T(8,128)S(1)} %get-tuple-element.65.flux_in_ref.near_flux_ref, f32[144,128]{1,0:T(8,128)S(1)} %collective-permute-done.4.prev_ref, ...), custom_call_target="tpu_custom_call" | custom-call | flops 200000000 | bytes 1000000 | tf_op jit(solution)/shard_map/near_forces/pallas_call | solution.py:730
  21.1 0.0 copy-start.3
  21.2 0.7 %step.1 = (f32[1,17424]{1,0:T(1,128)}, f32[1,17424]{1,0:T(1,128)}, f32[1,17424]{1,0:T(1,128)}, f32[1,17424]{1,0:T(1,128)}) custom-call(f32[2,144,128]{2,1,0:T(8,128)S(1)} %near_forces.1.line_ref, f32[1,17424]{1,0:T(1,128)S(1)} %copy-done, f32[1,17424]{1,0:T(1,128)S(1)} %copy-done.5, f32[1,17424]{1,0:T(1,128)S(1)} %copy-done.1, f32[1,17424]{1,0:T(1,128)S(1)} %copy-done.6, ...), custom_call_target="tpu_custom_call" | custom-call | flops 200000000 | bytes 1000000 | tf_op jit(solution)/shard_map/step/pallas_call | solution.py:749
  21.9 0.2 %collective-permute-done.5.first_ref = f32[16,1152]{1,0:T(8,128)S(1)} collective-permute-done((f32[16,1152]{1,0:T(8,128)S(1)}, f32[16,1152]{1,0:T(8,128)S(1)}, u32[]{:S(2)}, u32[]{:S(2)}) %collective-permute-start.5) | collective-permute-done | bytes 73760 | tf_op jit(solution)/shard_map/ppermute | solution.py:727
  22.1 0.8 %band.1 = f32[16,1089]{1,0:T(8,128)} custom-call(s32[1]{0:T(128)} %bitcast.1.cut_ref, f32[16,1152]{1,0:T(8,128)S(1)} %add.3.after_ref.own_ref, f32[16,1152]{1,0:T(8,128)S(1)} %collective-permute-done.5.first_ref, f32[16,1152]{1,0:T(8,128)S(1)} %collective-permute-done.6.second_ref, bf16[2,16,288]{2,1,0:T(8,128)(2,1)S(1)} %copy-done.3), custom_call_target="tpu_custom_call" | custom-call | flops 20000000 | bytes 1000000 | tf_op jit(solution)/shard_map/band/pallas_call | solution.py:763
  (14 shorter events, 0.1 us)
Async XLA Ops:
  0.6 5.2 %copy-start.2 = (f32[24,1152]{1,0:T(8,128)S(1)}, f32[24,1152]{1,0:T(8,128)}, u32[]{:S(2)}) copy-start(f32[24,1152]{1,0:T(8,128)} %constant.8.clone.cross_ref) | copy-start | bytes 331780
  2.0 7.0 %collective-permute-start = (f32[48,128]{1,0:T(8,128)S(1)}, f32[48,128]{1,0:T(8,128)S(1)}, u32[]{:S(2)}, u32[]{:S(2)}) collective-permute-start(f32[48,128]{1,0:T(8,128)S(1)} %get-tuple-element.42), channel_id=1, source_target_pairs={{0,1},{1,2},{2,3},{3,4},{4,5},{5,6},{6,7},{7,8},{8,9},{9,10},{10,1... | collective-permute-start | bytes 73736 | tf_op jit(solution)/shard_map/ppermute | solution.py:660
  3.1 6.3 %collective-permute-start.2 = (s32[8,128]{1,0:T(8,128)S(1)}, s32[8,128]{1,0:T(8,128)S(1)}, u32[]{:S(2)}, u32[]{:S(2)}) collective-permute-start(s32[8,128]{1,0:T(8,128)S(1)} %broadcast_in_dim.8.count_ref), channel_id=1, source_target_pairs={{0,1},{1,2},{2,3},{3,4},{4,5},{5,6},{6,7},{7,8},{8,9},{9,10},{10,1... | collective-permute-start | bytes 12296 | tf_op jit(solution)/shard_map/ppermute | solution.py:663
  8.8 1.5 %collective-permute-start.1 = (f32[32,128]{1,0:T(8,128)S(1)}, f32[32,128]{1,0:T(8,128)S(1)}, u32[]{:S(2)}, u32[]{:S(2)}) collective-permute-start(f32[32,128]{1,0:T(8,128)S(1)} %get-tuple-element.56), channel_id=1, source_target_pairs={{1,0},{2,1},{3,2},{4,3},{5,4},{6,5},{7,6},{8,7},{9,8},{10,9},{11,1... | collective-permute-start | bytes 49160 | tf_op jit(solution)/shard_map/ppermute | solution.py:692
  11.1 4.4 %collective-permute-start.3 = (f32[16,1152]{1,0:T(8,128)S(1)}, f32[16,1152]{1,0:T(8,128)S(1)}, u32[]{:S(2)}, u32[]{:S(2)}) collective-permute-start(f32[16,1152]{1,0:T(8,128)S(1)} %near_layers.1), channel_id=1, source_target_pairs={{0,16},{16,0},{1,17},{17,1},{2,18},{18,2},{3,19},{19,3},{4,20},{20... | collective-permute-start | bytes 221192 | tf_op jit(solution)/shard_map/ppermute | solution.py:722
  12.7 7.2 %collective-permute-start.4 = (f32[144,128]{1,0:T(8,128)S(1)}, f32[144,128]{1,0:T(8,128)S(1)}, u32[]{:S(2)}, u32[]{:S(2)}) collective-permute-start(f32[144,128]{1,0:T(8,128)S(1)} %get-tuple-element.73), channel_id=1, source_target_pairs={{0,1},{1,2},{2,3},{3,4},{4,5},{5,6},{6,7},{7,8},{8,9},{9,10},{10,1... | collective-permute-start | bytes 221192 | tf_op jit(solution)/shard_map/ppermute | solution.py:694
  15.6 6.5 %collective-permute-start.5 = (f32[16,1152]{1,0:T(8,128)S(1)}, f32[16,1152]{1,0:T(8,128)S(1)}, u32[]{:S(2)}, u32[]{:S(2)}) collective-permute-start(f32[16,1152]{1,0:T(8,128)S(1)} %add.3.after_ref.own_ref), channel_id=1, source_target_pairs={{0,15},{1,2},{2,1},{3,4},{4,3},{5,6},{6,5},{7,8},{8,7},{9,10},{10,... | collective-permute-start | bytes 221192 | tf_op jit(solution)/shard_map/ppermute | solution.py:727
  19.8 2.3 %collective-permute-start.6 = (f32[16,1152]{1,0:T(8,128)S(1)}, f32[16,1152]{1,0:T(8,128)S(1)}, u32[]{:S(2)}, u32[]{:S(2)}) collective-permute-start(f32[16,1152]{1,0:T(8,128)S(1)} %add.3.after_ref.own_ref), channel_id=1, source_target_pairs={{0,1},{1,0},{2,3},{3,2},{4,5},{5,4},{6,7},{7,6},{8,9},{9,8},{10,11... | collective-permute-start | bytes 221192 | tf_op jit(solution)/shard_map/ppermute | solution.py:728
  19.8 1.2 %copy-start = (f32[1,17424]{1,0:T(1,128)S(1)}, f32[1,17424]{1,0:T(1,128)}, u32[]{:S(2)}) copy-start(f32[1,17424]{1,0:T(1,128)} %fwd_ref.1) | copy-start | bytes 209092
  19.9 1.2 %copy-start.1 = (f32[1,17424]{1,0:T(1,128)S(1)}, f32[1,17424]{1,0:T(1,128)}, u32[]{:S(2)}) copy-start(f32[1,17424]{1,0:T(1,128)} %adj_ref.1) | copy-start | bytes 209092
  19.9 1.2 %copy-start.4 = (f32[17424]{0:T(1024)S(1)}, f32[17424]{0:T(1024)}, u32[]{:S(2)}) copy-start(f32[17424]{0:T(1024)} %mass_ref.1) | copy-start | bytes 209092
  19.9 1.2 %copy-start.5 = (f32[1,17424]{1,0:T(1,128)S(1)}, f32[1,17424]{1,0:T(1,128)}, u32[]{:S(2)}) copy-start(f32[1,17424]{1,0:T(1,128)} %fwd_speed_ref.1) | copy-start | bytes 209092
  19.9 1.2 %copy-start.6 = (f32[1,17424]{1,0:T(1,128)S(1)}, f32[1,17424]{1,0:T(1,128)}, u32[]{:S(2)}) copy-start(f32[1,17424]{1,0:T(1,128)} %adj_speed_ref.1) | copy-start | bytes 209092
  21.1 1.0 %copy-start.3 = (bf16[2,16,288]{2,1,0:T(8,128)(2,1)S(1)}, bf16[2,16,288]{2,1,0:T(8,128)(2,1)}, u32[]{:S(2)}) copy-start(bf16[2,16,288]{2,1,0:T(8,128)(2,1)} %constant.9.clone.band_ref) | copy-start | bytes 55300

commit v13 on v11

--- a/solution.py
+++ b/solution.py
@@ -107,7 +107,7 @@
 
 def pack_kernel(
     conn_hbm, shear_hbm, fwd_hbm, adj_hbm,
-    small_ref, right_ref, left_ref, own_ref, code_ref, parts_ref,
+    right_ref, left_ref, own_ref, code_ref, parts_ref,
     conn_ref, shear_ref, fwd_ref, adj_ref, block_ref, sem,
 ):
     copies = fetch(
@@ -136,9 +136,6 @@
         own_ref[ROWS * f + 136 : ROWS * f + 137, 0:16] = ref[0:1, NPTS - 16 : NPTS]
         right_ref[40 * f : 40 * f + 40, :] = own_ref[ROWS * f + 102 : ROWS * f + 142, :]
         left_ref[16 * f : 16 * f + 16, :] = own_ref[ROWS * f : ROWS * f + 16, :]
-        share = [float(DERIV[4, l]) * plane_of(own_ref, PYZ * (12 + l), ROWS * f) for l in range(4)]
-        small_ref[16 * f : 16 * f + 9, :] = (share[0] + share[1]) + (share[2] + share[3])
-        small_ref[16 * f + 9 : 16 * f + 16, :] = jnp.zeros((7, LANES), F32)
     copies[0].wait()
     block_ref[0:125, :] = shear_ref[...]
     block_ref[125:126, :] = slot.astype(F32)
@@ -148,7 +145,6 @@
     flux = add_parts(dot_nt(parts, pick))
     low = lax.broadcasted_iota(jnp.int32, (64, LANES), 1) < 64
     right_ref[80:144, :] = jnp.where(low, flux[0:64], flux[64:128])
-    small_ref[32:48, :] = jnp.where(low[0:16], flux[96:112], flux[112:128])
 
 
 def gll_weight(i):
@@ -321,8 +317,7 @@
 
 
 def own_kernel(turn, cut_ref, count_ref, own_ref, code_ref, parts_ref, cross_ref, *refs):
-    outs = refs[len(refs) - OWN_SCRATCH - OWN_OUTS - turn : len(refs) - OWN_SCRATCH - turn]
-    refs = outs + refs[len(refs) - OWN_SCRATCH :]
+    refs = refs[-OWN_OUTS - OWN_SCRATCH :]
     mine = (cut_ref[0] == 0) if turn == 0 else (cut_ref[0] != 0)
 
     @pl.when(mine)
@@ -417,13 +412,16 @@
 
 
 def near_kernel(
-    small_ref, next_ref, count_ref, flux_in_ref, slope_ref, near_kern_ref, kern_in_ref, cross_ref,
+    prev_ref, next_ref, count_ref, flux_in_ref, slope_ref, near_kern_ref, kern_in_ref, cross_ref,
     kern_ref,
     plane_ref, new_ref, win_ref, elem_ref, flux_ref, line_ref, spread_ref,
 ):
     plane_ref[...] = jnp.zeros(plane_ref.shape, F32)
     for f in range(2):
-        share = small_ref[16 * f : 16 * f + 9, :]
+        share = None
+        for l in range(4):
+            term = float(DERIV[4, l]) * plane_of(prev_ref, 12 + PYZ * l, 40 * f)
+            share = term if share is None else share + term
         plane_ref[pl.ds(f, 9, stride=8), :] = share
         plane_ref[pl.ds(2 + f, 9, stride=8), :] = plane_of(next_ref, 0, 16 * f)
     make_windows(plane_ref, 0, 8, new_ref, 0)
@@ -437,12 +435,7 @@
                 new = float(DERIV[i, 4]) * new_ref[w, 16 + 8 * f : 24 + 8 * f, :]
                 win_ref[w, r : r + 8, :] = win_ref[w, r : r + 8, :] + new
     turned(win_ref, 0, elem_ref, 0)
-    lower, upper = small_ref[32:48, :], pltpu.roll(small_ref[32:48, :], 64, 1)
-    live = upper[13:14, :] < count_ref[0:1, 0:1].astype(F32)
-    spread_ref[0:16, :] = jnp.where(live, lower, 0.0)
-    spread_ref[16:32, :] = jnp.where(live, upper, 0.0)
-    spread_ref[32:40, :] = jnp.zeros((8, LANES), F32)
-    place_flux(flux_ref, lambda i, ez: (spread_ref[4:36, :], 8 * ez), lambda i: [(0, 8 * NEAR_AT[0][i], 8)], (4,))
+    place_flux(flux_ref, message_flux(prev_ref, count_ref, spread_ref), lambda i: [(0, 8 * NEAR_AT[0][i], 8)], (4,))
     scaled(flux_ref, lane_weight([NEAR_AT[0]]))
     kern = [[None] * 5 for _ in range(5)]
     for j in range(5):
@@ -545,7 +538,7 @@
 
 
 def step_kernel(
-    line_ref, fwd_ref, fwd_speed_ref, adj_ref, adj_speed_ref, mass_ref,
+    line_ref, fwd_ref, fwd_speed_ref, adj_ref, adj_speed_ref, mass_ref, after_ref,
     fwd_out_ref, fwd_speed_out_ref, adj_out_ref, adj_speed_out_ref,
 ):
     def step(lo, hi, force):
@@ -564,7 +557,7 @@
     step(NPTS - 16, NPTS, [line_ref[f, 136:137, 0:16] for f in range(2)])
 
 
-def band_kernel(cut_ref, own_ref, first_ref, second_ref, band_ref, out_ref):
+def band_kernel(cut_ref, own_ref, first_ref, second_ref, band_ref, before_ref, out_ref):
     flat = jnp.concatenate([own_ref[...], first_ref[...], second_ref[...]], axis=0)
     k1 = flat.astype(BF16)
     rest = flat - k1.astype(F32)
@@ -619,10 +612,9 @@
 
     fields = (in_hbm(forward_displacement), in_hbm(adjoint_displacement))
     cross = held(jnp.asarray(cross_table()))
-    small, right, left, own, code, parts = pl.pallas_call(
+    right, left, own, code, parts = pl.pallas_call(
         pack_kernel,
         out_shape=[
-            pltpu.VMEM((48, LANES), F32),
             pltpu.VMEM((144, LANES), F32),
             pltpu.VMEM((32, LANES), F32),
             pltpu.VMEM((2 * ROWS, LANES), F32),
@@ -642,7 +634,7 @@
         name="pack",
     )(in_hbm(connectivity), in_hbm(shear_modulus), *fields)
     to_next = [(i, (i + 1) % cuts) for i in range(cuts)]
-    small = lax.ppermute(small, "cuts", to_next)
+    prev = lax.ppermute(right, "cuts", to_next)
     count, left = lax.optimization_barrier((element_count, left))
     count = jnp.broadcast_to(count.reshape(1, 1), (8, LANES))
     prev_count = lax.ppermute(count, "cuts", to_next)
@@ -650,12 +642,12 @@
 
     own_blocks = [elements(4), flux_block, flux_block, windows(1), windows(1), flux_block, kern_block]
 
-    def own_part(turn, before, waits=()):
+    def own_part(turn, before):
         given = (cut, held(count), held(own), held(code), held(parts), cross)
         return pl.pallas_call(
             functools.partial(own_kernel, turn),
-            out_shape=own_blocks + [pltpu.VMEM((144, LANES), F32)] * turn,
-            in_specs=[smem] + [vmem] * (5 + len(before)) + [anywhere] * len(waits),
+            out_shape=own_blocks,
+            in_specs=[smem] + [vmem] * (5 + len(before)),
             scratch_shapes=[
                 pltpu.VMEM((2 * 9 * 24, LANES), F32),
                 windows(4),
@@ -666,12 +658,11 @@
             input_output_aliases={len(given) + n: n for n in range(len(before))},
             cost_estimate=cost(300000000),
             name="own_layers",
-        )(*given, *[held(block) for block in before], *[held(block) for block in waits])
+        )(*given, *[held(block) for block in before])
 
     left, *blocks = lax.optimization_barrier((left, *own_part(0, [])))
     after = lax.ppermute(left, "cuts", [((i + 1) % cuts, i) for i in range(cuts)])
-    elem, flux, near_flux, near_win, near_slope, near_kern, kern, right = own_part(1, blocks + [right], [small])
-    prev = lax.ppermute(right, "cuts", to_next)
+    elem, flux, near_flux, near_win, near_slope, near_kern, kern = own_part(1, blocks)
     kern = pl.pallas_call(
         near_kernel,
         out_shape=kern_block,
@@ -687,7 +678,7 @@
         ],
         cost_estimate=cost(200000000),
         name="near_layers",
-    )(held(small), held(after), held(prev_count), held(near_flux), held(near_slope), held(near_kern), held(kern), cross)
+    )(held(prev), held(after), held(prev_count), held(near_flux), held(near_slope), held(near_kern), held(kern), cross)
 
     force = pl.pallas_call(
         force_kernel,
@@ -698,12 +689,6 @@
         name="forces",
     )(held(elem), held(flux))
 
-    if events == 2:
-        other = lax.ppermute(kern, "event", [(0, 1), (1, 0)])
-        other, force = lax.optimization_barrier((other, force))
-        kern = kern + other
-    elif events > 2:
-        kern = lax.psum(kern, "event")
     kern_first = lax.ppermute(kern, "cuts", pairs_first)
     kern_second = lax.ppermute(kern, "cuts", pairs_second)
 
@@ -725,11 +710,22 @@
         cost_estimate=cost(200000000),
         name="near_forces",
     )(held(force), held(near_win), held(near_flux), held(prev), held(after), held(prev_count), held(kern))
+    share = pl.pallas_call(
+        band_kernel,
+        out_shape=pltpu.VMEM((PXU, PYZ), F32),
+        in_specs=[smem] + [vmem] * 5,
+        cost_estimate=cost(20000000),
+        name="band",
+    )(cut, held(kern), held(kern_first), held(kern_second), held(jnp.asarray(band_table())), held(force))
+    if events == 2:
+        shear_kernel = share + lax.ppermute(share, "event", [(0, 1), (1, 0)])
+    else:
+        shear_kernel = lax.psum(share, "event")
     points = jax.ShapeDtypeStruct((1, NPTS), F32)
     outs = pl.pallas_call(
         step_kernel,
         out_shape=[points] * 4,
-        in_specs=[vmem] * 6,
+        in_specs=[vmem] * 7,
         cost_estimate=cost(200000000),
         name="step",
     )(
@@ -739,14 +735,8 @@
         held(adjoint_displacement),
         held(adjoint_velocity),
         held(inverse_mass),
+        held(share),
     )
-    shear_kernel = pl.pallas_call(
-        band_kernel,
-        out_shape=jax.ShapeDtypeStruct((PXU, PYZ), F32),
-        in_specs=[smem] + [vmem] * 4,
-        cost_estimate=cost(20000000),
-        name="band",
-    )(cut, held(kern), held(kern_first), held(kern_second), held(jnp.asarray(band_table())))
     return (*outs, shear_kernel)
 
 

time: 22.6 us -> 23.1 us (1.022)
  Pallas kernels: 7.3 us -> 6.64 us
  starting transfers between devices: 9.87 us -> 10.5 us
  other arithmetic: 0.01 us -> 0.64 us
    ppermute x1, waiting for transfers between devices: 0.5 us -> 1.31 us  [on_device(): prev_count = lax.ppermute(count, 'cuts', to_next)]
    pallas_call x5, Pallas kernels: 4.61 us -> 3.81 us  [the longest x2 1.6 us: own_part(): pl.pallas_call(functools.partial(own_kernel, turn), out_shape=own_blocks,...]
    ppermute x1, starting transfers between devices: 3.82 us -> 4.48 us  [on_device(): kern_first = lax.ppermute(kern, 'cuts', pairs_first)]
    add x1, other arithmetic: 0.01 us -> 0.64 us  [on_device(): shear_kernel = share + lax.ppermute(share, 'event', [(0, 1), (1, 0)])]
    ppermute x2 -> x1, starting transfers between devices: 2.5 us -> 1.99 us  [on_device(): shear_kernel = share + lax.ppermute(share, 'event', [(0, 1), (1, 0)])]
    ppermute x1, starting transfers between devices: 0.01 us -> 0.5 us  [on_device(): prev = lax.ppermute(right, 'cuts', to_next)]
    ppermute x1, waiting for transfers between devices: 0.48 us -> 0.06 us  [on_device(): kern_first = lax.ppermute(kern, 'cuts', pairs_first)]
    ppermute x2 -> x1, waiting for transfers between devices: 2.39 us -> 2.15 us  [on_device(): shear_kernel = share + lax.ppermute(share, 'event', [(0, 1), (1, 0)])]
  transfers between devices with their start and end apart: 7 -> 6, of which waited for: 6 -> 4; matrix products, arithmetic and copies ran while one was open for 0% -> 0% of each run, Pallas kernels for 19% -> 18%
where the time goes in v13:
time: 23.1 us; the launch traced here: 22.9 us
  starting transfers between devices  10.5 us (45%)
  Pallas kernels  6.64 us (29%)
  waiting for transfers between devices  3.66 us (16%)
  between operations  1.41 us (6%)
  other arithmetic  0.64 us (3%)
    ppermute x1, starting transfers between devices, on_device(): kern_first = lax.ppermute(kern, 'cuts', pairs_first)  4.48 us
    ppermute x1, starting transfers between devices, on_device(): prev_count = lax.ppermute(count, 'cuts', to_next)  2.68 us
    ppermute x1, waiting for transfers between devices, on_device(): shear_kernel = share + lax.ppermute(share, 'event', [(0, 1), (1, 0)])  2.15 us
    ppermute x1, starting transfers between devices, on_device(): shear_kernel = share + lax.ppermute(share, 'event', [(0, 1), (1, 0)])  1.99 us
    pallas_call x2, Pallas kernels, own_part(): pl.pallas_call(functools.partial(own_kernel, turn), out_shape=own_blocks,...  1.6 us
    ppermute x1, waiting for transfers between devices, on_device(): prev_count = lax.ppermute(count, 'cuts', to_next)  1.31 us
    pallas_call x1, Pallas kernels, on_device(): pl.pallas_call(pack_kernel, out_shape=[pltpu.VMEM((144, LANES), F32), plt...  1.28 us
    pallas_call x1, Pallas kernels, on_device(): pl.pallas_call(near_force_kernel, out_shape=pltpu.VMEM((2, ROWS, LANES),...  1.19 us
  transfers between devices with their start and end apart: 6, of which 4 were waited for; matrix products, arithmetic and copies ran while one was open for 0% of the time, Pallas kernels for 18%

profile of v13, /device:TPU:0, one launch (start us, length us, event | category | flops | bytes accessed | tf_op | source)
XLA Modules:
  0.0 22.9 jit_solution(13543562753294504603)
XLA Ops:
  0.6 0.0 copy-start
  0.6 1.3 %pack.1 = (f32[144,128]{1,0:T(8,128)S(1)}, f32[32,128]{1,0:T(8,128)S(1)}, f32[288,128]{1,0:T(8,128)S(1)}, s32[8,256]{1,0:T(8,128)S(1)}, bf16[384,256]{1,0:T(8,128)(2,1)S(1)}) custom-call(s32[125,256]{1,0:T(8,128)} %conn_hbm.1, f32[125,256]{1,0:T(8,128)} %shear_hbm.1, f32[1,17424]{1,0:T(1,128)} %fwd_ref.1, f32[1,17424]{1,0:T(1,128)} %adj_ref.1), custom_call_target="tpu_custom_call" | custom-call | flops 100000000 | bytes 1000000 | tf_op jit(solution)/shard_map/pack/pallas_call | solution.py:615
  1.9 0.5 %collective-permute-start = (f32[144,128]{1,0:T(8,128)S(1)}, f32[144,128]{1,0:T(8,128)S(1)}, u32[]{:S(2)}, u32[]{:S(2)}) collective-permute-start(f32[144,128]{1,0:T(8,128)S(1)} %get-tuple-element.66), channel_id=1, source_target_pairs={{0,1},{1,2},{2,3},{3,4},{4,5},{5,6},{6,7},{7,8},{8,9},{9,10},{10,1... | collective-permute-start | bytes 221192 | tf_op jit(solution)/shard_map/ppermute | solution.py:637
  3.1 2.7 %collective-permute-start.2 = (s32[8,128]{1,0:T(8,128)S(1)}, s32[8,128]{1,0:T(8,128)S(1)}, u32[]{:S(2)}, u32[]{:S(2)}) collective-permute-start(s32[8,128]{1,0:T(8,128)S(1)} %broadcast_in_dim.8.count_ref), channel_id=1, source_target_pairs={{0,1},{1,2},{2,3},{3,4},{4,5},{5,6},{6,7},{7,8},{8,9},{9,10},{10,1... | collective-permute-start | bytes 12296 | tf_op jit(solution)/shard_map/ppermute | solution.py:640
  5.8 1.6 %own_layers.2 = (f32[4,168,128]{2,1,0:T(8,128)S(1)}, f32[200,128]{1,0:T(8,128)S(1)}, f32[200,128]{1,0:T(8,128)S(1)}, f32[2,128,128]{2,1,0:T(8,128)S(1)}, f32[2,1...) custom-call(s32[1]{0:T(128)} %bitcast.cut_ref, s32[8,128]{1,0:T(8,128)S(1)} %broadcast_in_dim.8.count_ref, ...), custom_call_target="tpu_custom_call" | custom-call | flops 300000000 | bytes 1000000 | tf_op jit(solution)/shard_map/own_layers/pallas_call | solution.py:647
  7.4 0.9 %collective-permute-start.1 = (f32[32,128]{1,0:T(8,128)S(1)}, f32[32,128]{1,0:T(8,128)S(1)}, u32[]{:S(2)}, u32[]{:S(2)}) collective-permute-start(f32[32,128]{1,0:T(8,128)S(1)} %get-tuple-element.67), channel_id=1, source_target_pairs={{1,0},{2,1},{3,2},{4,3},{5,4},{6,5},{7,6},{8,7},{9,8},{10,9},{11,1... | collective-permute-start | bytes 49160 | tf_op jit(solution)/shard_map/ppermute | solution.py:664
  8.3 1.3 %collective-permute-done.2.count_ref = s32[8,128]{1,0:T(8,128)S(1)} collective-permute-done((s32[8,128]{1,0:T(8,128)S(1)}, s32[8,128]{1,0:T(8,128)S(1)}, u32[]{:S(2)}, u32[]{:S(2)}) %collective-permute-start.2) | collective-permute-done | bytes 4128 | tf_op jit(solution)/shard_map/ppermute | solution.py:640
  9.6 0.1 collective-permute-done.1.next_ref
  9.7 0.9 %near_layers.1.after_ref.own_ref = f32[16,1152]{1,0:T(8,128)S(1)} custom-call(f32[144,128]{1,0:T(8,128)S(1)} %collective-permute-done.prev_ref, f32[32,128]{1,0:T(8,128)S(1)} %collective-permute-done.1.next_ref, s32[8,128]{1,0:T(8,128)S(1)} %collective-permute-done.2.count_ref, f32[200,128]{1,0:T(8,128)S(1)} %get-tuple-element.65.flux_in_ref.near_flux_ref, ...), custom_call_target="tpu_custom_call" | custom-call | flops 200000000 | bytes 1000000 | tf_op jit(solution)/shard_map/near_layers/pallas_call | solution.py:666
  10.6 4.5 %collective-permute-start.3 = (f32[16,1152]{1,0:T(8,128)S(1)}, f32[16,1152]{1,0:T(8,128)S(1)}, u32[]{:S(2)}, u32[]{:S(2)}) collective-permute-start(f32[16,1152]{1,0:T(8,128)S(1)} %near_layers.1.after_ref.own_ref), channel_id=1, source_target_pairs={{0,15},{1,2},{2,1},{3,4},{4,3},{5,6},{6,5},{7,8},{8,7},{9,10},{10,... | collective-permute-start | bytes 221192 | tf_op jit(solution)/shard_map/ppermute | solution.py:692
  15.1 0.7 %forces.1.force_ref = f32[2,144,128]{2,1,0:T(8,128)S(1)} custom-call(f32[4,168,128]{2,1,0:T(8,128)S(1)} %get-tuple-element.62.elem_ref, f32[200,128]{1,0:T(8,128)S(1)} %get-tuple-element.63.flux_ref), custom_call_target="tpu_custom_call" | custom-call | flops 200000000 | bytes 1000000 | tf_op jit(solution)/shard_map/forces/pallas_call | solution.py:683
  15.8 0.0 copy-start.3
  15.9 1.2 %near_forces.1.before_ref.line_ref = f32[2,144,128]{2,1,0:T(8,128)S(1)} custom-call(f32[2,144,128]{2,1,0:T(8,128)S(1)} %forces.1.force_ref, f32[2,128,128]{2,1,0:T(8,128)S(1)} %get-tuple-element.64.near_half_ref, f32[200,128]{1,0:T(8,128)S(1)} %get-tuple-element.65.flux_in_ref.near_flux_ref, f32[144,128]{1,0:T(8,128)S(1)} %collective-permute-done.prev_ref, ...), custom_call_target="tpu_custom_call" | custom-call | flops 200000000 | bytes 1000000 | tf_op jit(solution)/shard_map/near_forces/pallas_call | solution.py:695
  17.1 0.0 copy-start.1
  17.1 0.0 copy-start.2
  17.1 0.0 copy-start.4
  17.1 0.0 copy-start.5
  17.1 0.0 copy-start.6
  17.1 0.1 collective-permute-done.3.first_ref
  17.2 0.2 band.1.after_ref
  17.4 2.0 %collective-permute-start.5 = (f32[16,1089]{1,0:T(8,128)S(1)}, f32[16,1089]{1,0:T(8,128)S(1)}, u32[]{:S(2)}, u32[]{:S(2)}) collective-permute-start(f32[16,1089]{1,0:T(8,128)S(1)} %band.1.after_ref), channel_id=1, source_target_pairs={{0,16},{16,0},{1,17},{17,1},{2,18},{18,2},{3,19},{19,3},{4,20},{20... | collective-permute-start | bytes 209096 | tf_op jit(solution)/shard_map/ppermute | solution.py:721
  19.4 0.7 %step.1 = (f32[1,17424]{1,0:T(1,128)}, f32[1,17424]{1,0:T(1,128)}, f32[1,17424]{1,0:T(1,128)}, f32[1,17424]{1,0:T(1,128)}) custom-call(f32[2,144,128]{2,1,0:T(8,128)S(1)} %near_forces.1.before_ref.line_ref, f32[1,17424]{1,0:T(1,128)S(1)} %copy-done.1, f32[1,17424]{1,0:T(1,128)S(1)} %copy-done.5, f32[1,17424]{1,0:T(1,128)S(1)} %copy-done.2, ...), custom_call_target="tpu_custom_call" | custom-call | flops 200000000 | bytes 1000000 | tf_op jit(solution)/shard_map/step/pallas_call | solution.py:725
  20.1 2.2 %collective-permute-done.5 = f32[16,1089]{1,0:T(8,128)S(1)} collective-permute-done((f32[16,1089]{1,0:T(8,128)S(1)}, f32[16,1089]{1,0:T(8,128)S(1)}, u32[]{:S(2)}, u32[]{:S(2)}) %collective-permute-start.5) | collective-permute-done | bytes 69728 | tf_op jit(solution)/shard_map/ppermute | solution.py:721
  22.3 0.6 %add.3 = f32[16,1089]{1,0:T(8,128)} add(f32[16,1089]{1,0:T(8,128)S(1)} %band.1.after_ref, f32[16,1089]{1,0:T(8,128)S(1)} %collective-permute-done.5) | non-fusion elementwise | flops 17424 | bytes 209088 | tf_op jit(solution)/shard_map/add | solution.py:721
  (12 shorter events, 0.0 us)
Async XLA Ops:
  0.6 5.2 %copy-start = (f32[24,1152]{1,0:T(8,128)S(1)}, f32[24,1152]{1,0:T(8,128)}, u32[]{:S(2)}) copy-start(f32[24,1152]{1,0:T(8,128)} %constant.8.clone.cross_ref) | copy-start | bytes 331780
  1.9 7.8 %collective-permute-start = (f32[144,128]{1,0:T(8,128)S(1)}, f32[144,128]{1,0:T(8,128)S(1)}, u32[]{:S(2)}, u32[]{:S(2)}) collective-permute-start(f32[144,128]{1,0:T(8,128)S(1)} %get-tuple-element.66), channel_id=1, source_target_pairs={{0,1},{1,2},{2,3},{3,4},{4,5},{5,6},{6,7},{7,8},{8,9},{9,10},{10,1... | collective-permute-start | bytes 221192 | tf_op jit(solution)/shard_map/ppermute | solution.py:637
  3.1 6.5 %collective-permute-start.2 = (s32[8,128]{1,0:T(8,128)S(1)}, s32[8,128]{1,0:T(8,128)S(1)}, u32[]{:S(2)}, u32[]{:S(2)}) collective-permute-start(s32[8,128]{1,0:T(8,128)S(1)} %broadcast_in_dim.8.count_ref), channel_id=1, source_target_pairs={{0,1},{1,2},{2,3},{3,4},{4,5},{5,6},{6,7},{7,8},{8,9},{9,10},{10,1... | collective-permute-start | bytes 12296 | tf_op jit(solution)/shard_map/ppermute | solution.py:640
  7.4 2.3 %collective-permute-start.1 = (f32[32,128]{1,0:T(8,128)S(1)}, f32[32,128]{1,0:T(8,128)S(1)}, u32[]{:S(2)}, u32[]{:S(2)}) collective-permute-start(f32[32,128]{1,0:T(8,128)S(1)} %get-tuple-element.67), channel_id=1, source_target_pairs={{1,0},{2,1},{3,2},{4,3},{5,4},{6,5},{7,6},{8,7},{9,8},{10,9},{11,1... | collective-permute-start | bytes 49160 | tf_op jit(solution)/shard_map/ppermute | solution.py:664
  10.6 6.5 %collective-permute-start.3 = (f32[16,1152]{1,0:T(8,128)S(1)}, f32[16,1152]{1,0:T(8,128)S(1)}, u32[]{:S(2)}, u32[]{:S(2)}) collective-permute-start(f32[16,1152]{1,0:T(8,128)S(1)} %near_layers.1.after_ref.own_ref), channel_id=1, source_target_pairs={{0,15},{1,2},{2,1},{3,4},{4,3},{5,6},{6,5},{7,8},{8,7},{9,10},{10,... | collective-permute-start | bytes 221192 | tf_op jit(solution)/shard_map/ppermute | solution.py:692
  15.1 2.1 %collective-permute-start.4 = (f32[16,1152]{1,0:T(8,128)S(1)}, f32[16,1152]{1,0:T(8,128)S(1)}, u32[]{:S(2)}, u32[]{:S(2)}) collective-permute-start(f32[16,1152]{1,0:T(8,128)S(1)} %near_layers.1.after_ref.own_ref), channel_id=1, source_target_pairs={{0,1},{1,0},{2,3},{3,2},{4,5},{5,4},{6,7},{7,6},{8,9},{9,8},{10,11... | collective-permute-start | bytes 221192 | tf_op jit(solution)/shard_map/ppermute | solution.py:693
  15.8 1.3 %copy-start.3 = (bf16[2,16,288]{2,1,0:T(8,128)(2,1)S(1)}, bf16[2,16,288]{2,1,0:T(8,128)(2,1)}, u32[]{:S(2)}) copy-start(bf16[2,16,288]{2,1,0:T(8,128)(2,1)} %constant.9.clone.band_ref) | copy-start | bytes 55300
  17.1 2.3 %copy-start.1 = (f32[1,17424]{1,0:T(1,128)S(1)}, f32[1,17424]{1,0:T(1,128)}, u32[]{:S(2)}) copy-start(f32[1,17424]{1,0:T(1,128)} %fwd_ref.1) | copy-start | bytes 209092
  17.1 2.3 %copy-start.2 = (f32[1,17424]{1,0:T(1,128)S(1)}, f32[1,17424]{1,0:T(1,128)}, u32[]{:S(2)}) copy-start(f32[1,17424]{1,0:T(1,128)} %adj_ref.1) | copy-start | bytes 209092
  17.1 2.3 %copy-start.4 = (f32[17424]{0:T(1024)S(1)}, f32[17424]{0:T(1024)}, u32[]{:S(2)}) copy-start(f32[17424]{0:T(1024)} %mass_ref.1) | copy-start | bytes 209092
  17.1 2.3 %copy-start.5 = (f32[1,17424]{1,0:T(1,128)S(1)}, f32[1,17424]{1,0:T(1,128)}, u32[]{:S(2)}) copy-start(f32[1,17424]{1,0:T(1,128)} %fwd_speed_ref.1) | copy-start | bytes 209092
  17.1 2.3 %copy-start.6 = (f32[1,17424]{1,0:T(1,128)S(1)}, f32[1,17424]{1,0:T(1,128)}, u32[]{:S(2)}) copy-start(f32[1,17424]{1,0:T(1,128)} %adj_speed_ref.1) | copy-start | bytes 209092
  17.4 4.9 %collective-permute-start.5 = (f32[16,1089]{1,0:T(8,128)S(1)}, f32[16,1089]{1,0:T(8,128)S(1)}, u32[]{:S(2)}, u32[]{:S(2)}) collective-permute-start(f32[16,1089]{1,0:T(8,128)S(1)} %band.1.after_ref), channel_id=1, source_target_pairs={{0,16},{16,0},{1,17},{17,1},{2,18},{18,2},{3,19},{19,3},{4,20},{20... | collective-permute-start | bytes 209096 | tf_op jit(solution)/shard_map/ppermute | solution.py:721

commit v14 on v13

--- a/solution.py
+++ b/solution.py
@@ -538,7 +538,7 @@
 
 
 def step_kernel(
-    line_ref, fwd_ref, fwd_speed_ref, adj_ref, adj_speed_ref, mass_ref, after_ref,
+    line_ref, fwd_ref, fwd_speed_ref, adj_ref, adj_speed_ref, mass_ref,
     fwd_out_ref, fwd_speed_out_ref, adj_out_ref, adj_speed_out_ref,
 ):
     def step(lo, hi, force):
@@ -557,7 +557,7 @@
     step(NPTS - 16, NPTS, [line_ref[f, 136:137, 0:16] for f in range(2)])
 
 
-def band_kernel(cut_ref, own_ref, first_ref, second_ref, band_ref, before_ref, out_ref):
+def band_kernel(cut_ref, own_ref, first_ref, second_ref, band_ref, out_ref):
     flat = jnp.concatenate([own_ref[...], first_ref[...], second_ref[...]], axis=0)
     k1 = flat.astype(BF16)
     rest = flat - k1.astype(F32)
@@ -689,6 +689,12 @@
         name="forces",
     )(held(elem), held(flux))
 
+    if events == 2:
+        other = lax.ppermute(kern, "event", [(0, 1), (1, 0)])
+        other, force = lax.optimization_barrier((other, force))
+        kern = kern + other
+    elif events > 2:
+        kern = lax.psum(kern, "event")
     kern_first = lax.ppermute(kern, "cuts", pairs_first)
     kern_second = lax.ppermute(kern, "cuts", pairs_second)
 
@@ -710,22 +716,11 @@
         cost_estimate=cost(200000000),
         name="near_forces",
     )(held(force), held(near_win), held(near_flux), held(prev), held(after), held(prev_count), held(kern))
-    share = pl.pallas_call(
-        band_kernel,
-        out_shape=pltpu.VMEM((PXU, PYZ), F32),
-        in_specs=[smem] + [vmem] * 5,
-        cost_estimate=cost(20000000),
-        name="band",
-    )(cut, held(kern), held(kern_first), held(kern_second), held(jnp.asarray(band_table())), held(force))
-    if events == 2:
-        shear_kernel = share + lax.ppermute(share, "event", [(0, 1), (1, 0)])
-    else:
-        shear_kernel = lax.psum(share, "event")
     points = jax.ShapeDtypeStruct((1, NPTS), F32)
     outs = pl.pallas_call(
         step_kernel,
         out_shape=[points] * 4,
-        in_specs=[vmem] * 7,
+        in_specs=[vmem] * 6,
         cost_estimate=cost(200000000),
         name="step",
     )(
@@ -735,8 +730,14 @@
         held(adjoint_displacement),
         held(adjoint_velocity),
         held(inverse_mass),
-        held(share),
     )
+    shear_kernel = pl.pallas_call(
+        band_kernel,
+        out_shape=jax.ShapeDtypeStruct((PXU, PYZ), F32),
+        in_specs=[smem] + [vmem] * 4,
+        cost_estimate=cost(20000000),
+        name="band",
+    )(cut, held(kern), held(kern_first), held(kern_second), held(jnp.asarray(band_table())))
     return (*outs, shear_kernel)
 
 

time: 23.1 us -> 22.6 us (0.978)
  starting transfers between devices: 10.5 us -> 9.56 us
  Pallas kernels: 6.64 us -> 7.28 us
  other arithmetic: 0.64 us -> 0.01 us
  waiting for transfers between devices: 3.66 us -> 4.15 us
    ppermute x1, starting transfers between devices: 4.48 us -> 3.52 us  [on_device(): kern_first = lax.ppermute(kern, 'cuts', pairs_first)]
    ppermute x1, waiting for transfers between devices: 0.06 us -> 1 us  [on_device(): kern_first = lax.ppermute(kern, 'cuts', pairs_first)]
    pallas_call x2, Pallas kernels: 0.93 us -> 1.57 us  [the longest x1 0.85 us: on_device(): pl.pallas_call(band_kernel, out_shape=jax.ShapeDtypeStruct((PXU, PYZ), F3...]
    add x1, other arithmetic: 0.64 us -> 0.01 us  [on_device(): kern = kern + other]
    ppermute x1, waiting for transfers between devices: 2.15 us -> 1.71 us  [on_device(): other = lax.ppermute(kern, 'event', [(0, 1), (1, 0)])]
  transfers between devices with their start and end apart: 6 -> 6, of which waited for: 4 -> 4; matrix products, arithmetic and copies ran while one was open for 0% -> 0% of each run, Pallas kernels for 18% -> 19%
where the time goes in v14:
time: 22.6 us; the launch traced here: 22.5 us
  starting transfers between devices  9.56 us (42%)
  Pallas kernels  7.28 us (32%)
  waiting for transfers between devices  4.15 us (18%)
  between operations  1.42 us (6%)
    ppermute x1, starting transfers between devices, on_device(): kern_first = lax.ppermute(kern, 'cuts', pairs_first)  3.52 us
    ppermute x1, starting transfers between devices, on_device(): prev_count = lax.ppermute(count, 'cuts', to_next)  2.68 us
    ppermute x1, starting transfers between devices, on_device(): other = lax.ppermute(kern, 'event', [(0, 1), (1, 0)])  1.99 us
    ppermute x1, waiting for transfers between devices, on_device(): other = lax.ppermute(kern, 'event', [(0, 1), (1, 0)])  1.71 us
    pallas_call x2, Pallas kernels, own_part(): pl.pallas_call(functools.partial(own_kernel, turn), out_shape=own_blocks,...  1.6 us
    ppermute x1, waiting for transfers between devices, on_device(): prev_count = lax.ppermute(count, 'cuts', to_next)  1.31 us
    pallas_call x1, Pallas kernels, on_device(): pl.pallas_call(pack_kernel, out_shape=[pltpu.VMEM((144, LANES), F32), plt...  1.28 us
    pallas_call x1, Pallas kernels, on_device(): pl.pallas_call(near_force_kernel, out_shape=pltpu.VMEM((2, ROWS, LANES),...  1.19 us
  transfers between devices with their start and end apart: 6, of which 4 were waited for; matrix products, arithmetic and copies ran while one was open for 0% of the time, Pallas kernels for 19%

profile of v14, /device:TPU:0, one launch (start us, length us, event | category | flops | bytes accessed | tf_op | source)
XLA Modules:
  0.0 22.5 jit_solution(803985453564333124)
XLA Ops:
  0.6 0.0 copy-start
  0.6 1.3 %pack.1 = (f32[144,128]{1,0:T(8,128)S(1)}, f32[32,128]{1,0:T(8,128)S(1)}, f32[288,128]{1,0:T(8,128)S(1)}, s32[8,256]{1,0:T(8,128)S(1)}, bf16[384,256]{1,0:T(8,128)(2,1)S(1)}) custom-call(s32[125,256]{1,0:T(8,128)} %conn_hbm.1, f32[125,256]{1,0:T(8,128)} %shear_hbm.1, f32[1,17424]{1,0:T(1,128)} %fwd_ref.1, f32[1,17424]{1,0:T(1,128)} %adj_ref.1), custom_call_target="tpu_custom_call" | custom-call | flops 100000000 | bytes 1000000 | tf_op jit(solution)/shard_map/pack/pallas_call | solution.py:615
  1.9 0.5 %collective-permute-start = (f32[144,128]{1,0:T(8,128)S(1)}, f32[144,128]{1,0:T(8,128)S(1)}, u32[]{:S(2)}, u32[]{:S(2)}) collective-permute-start(f32[144,128]{1,0:T(8,128)S(1)} %get-tuple-element.42), channel_id=1, source_target_pairs={{0,1},{1,2},{2,3},{3,4},{4,5},{5,6},{6,7},{7,8},{8,9},{9,10},{10,1... | collective-permute-start | bytes 221192 | tf_op jit(solution)/shard_map/ppermute | solution.py:637
  3.1 2.7 %collective-permute-start.2 = (s32[8,128]{1,0:T(8,128)S(1)}, s32[8,128]{1,0:T(8,128)S(1)}, u32[]{:S(2)}, u32[]{:S(2)}) collective-permute-start(s32[8,128]{1,0:T(8,128)S(1)} %broadcast_in_dim.8.count_ref), channel_id=1, source_target_pairs={{0,1},{1,2},{2,3},{3,4},{4,5},{5,6},{6,7},{7,8},{8,9},{9,10},{10,1... | collective-permute-start | bytes 12296 | tf_op jit(solution)/shard_map/ppermute | solution.py:640
  5.8 0.0 copy-done
  5.8 1.6 %own_layers.2 = (f32[4,168,128]{2,1,0:T(8,128)S(1)}, f32[200,128]{1,0:T(8,128)S(1)}, f32[200,128]{1,0:T(8,128)S(1)}, f32[2,128,128]{2,1,0:T(8,128)S(1)}, f32[2,1...) custom-call(s32[1]{0:T(128)} %bitcast.1.cut_ref, s32[8,128]{1,0:T(8,128)S(1)} %broadcast_in_dim.8.count_ref, ...), custom_call_target="tpu_custom_call" | custom-call | flops 300000000 | bytes 1000000 | tf_op jit(solution)/shard_map/own_layers/pallas_call | solution.py:647
  7.4 0.9 %collective-permute-start.1 = (f32[32,128]{1,0:T(8,128)S(1)}, f32[32,128]{1,0:T(8,128)S(1)}, u32[]{:S(2)}, u32[]{:S(2)}) collective-permute-start(f32[32,128]{1,0:T(8,128)S(1)} %get-tuple-element.58), channel_id=1, source_target_pairs={{1,0},{2,1},{3,2},{4,3},{5,4},{6,5},{7,6},{8,7},{9,8},{10,9},{11,1... | collective-permute-start | bytes 49160 | tf_op jit(solution)/shard_map/ppermute | solution.py:664
  8.3 1.3 %collective-permute-done.2.count_ref = s32[8,128]{1,0:T(8,128)S(1)} collective-permute-done((s32[8,128]{1,0:T(8,128)S(1)}, s32[8,128]{1,0:T(8,128)S(1)}, u32[]{:S(2)}, u32[]{:S(2)}) %collective-permute-start.2) | collective-permute-done | bytes 4128 | tf_op jit(solution)/shard_map/ppermute | solution.py:640
  9.6 0.1 collective-permute-done.1.next_ref
  9.7 0.0 collective-permute-done.prev_ref
  9.7 0.9 %near_layers.1 = f32[16,1152]{1,0:T(8,128)S(1)} custom-call(f32[144,128]{1,0:T(8,128)S(1)} %collective-permute-done.prev_ref, f32[32,128]{1,0:T(8,128)S(1)} %collective-permute-done.1.next_ref, s32[8,128]{1,0:T(8,128)S(1)} %collective-permute-done.2.count_ref, f32[200,128]{1,0:T(8,128)S(1)} %get-tuple-element.66.flux_in_ref.near_flux_ref, ...), custom_call_target="tpu_custom_call" | custom-call | flops 200000000 | bytes 1000000 | tf_op jit(solution)/shard_map/near_layers/pallas_call | solution.py:666
  10.6 2.0 %collective-permute-start.3 = (f32[16,1152]{1,0:T(8,128)S(1)}, f32[16,1152]{1,0:T(8,128)S(1)}, u32[]{:S(2)}, u32[]{:S(2)}) collective-permute-start(f32[16,1152]{1,0:T(8,128)S(1)} %near_layers.1), channel_id=1, source_target_pairs={{0,16},{16,0},{1,17},{17,1},{2,18},{18,2},{3,19},{19,3},{4,20},{20... | collective-permute-start | bytes 221192 | tf_op jit(solution)/shard_map/ppermute | solution.py:693
  12.6 0.7 %forces.1.force_ref = f32[2,144,128]{2,1,0:T(8,128)S(1)} custom-call(f32[4,168,128]{2,1,0:T(8,128)S(1)} %get-tuple-element.70.elem_ref, f32[200,128]{1,0:T(8,128)S(1)} %get-tuple-element.71.flux_ref), custom_call_target="tpu_custom_call" | custom-call | flops 200000000 | bytes 1000000 | tf_op jit(solution)/shard_map/forces/pallas_call | solution.py:683
  13.3 1.7 %collective-permute-done.3 = f32[16,1152]{1,0:T(8,128)S(1)} collective-permute-done((f32[16,1152]{1,0:T(8,128)S(1)}, f32[16,1152]{1,0:T(8,128)S(1)}, u32[]{:S(2)}, u32[]{:S(2)}) %collective-permute-start.3) | collective-permute-done | bytes 73760 | tf_op jit(solution)/shard_map/ppermute | solution.py:693
  15.1 3.5 %collective-permute-start.4 = (f32[16,1152]{1,0:T(8,128)S(1)}, f32[16,1152]{1,0:T(8,128)S(1)}, u32[]{:S(2)}, u32[]{:S(2)}) collective-permute-start(f32[16,1152]{1,0:T(8,128)S(1)} %add.3.after_ref.own_ref), channel_id=1, source_target_pairs={{0,15},{1,2},{2,1},{3,4},{4,3},{5,6},{6,5},{7,8},{8,7},{9,10},{10,... | collective-permute-start | bytes 221192 | tf_op jit(solution)/shard_map/ppermute | solution.py:698
  18.6 0.0 collective-permute-start.5
  18.6 0.0 copy-start.5
  18.6 0.0 copy-start.6
  18.6 1.2 %near_forces.1.line_ref = f32[2,144,128]{2,1,0:T(8,128)S(1)} custom-call(f32[2,144,128]{2,1,0:T(8,128)S(1)} %forces.1.force_ref, f32[2,128,128]{2,1,0:T(8,128)S(1)} %get-tuple-element.73.near_half_ref, f32[200,128]{1,0:T(8,128)S(1)} %get-tuple-element.66.flux_in_ref.near_flux_ref, f32[144,128]{1,0:T(8,128)S(1)} %collective-permute-done.prev_ref, ...), custom_call_target="tpu_custom_call" | custom-call | flops 200000000 | bytes 1000000 | tf_op jit(solution)/shard_map/near_forces/pallas_call | solution.py:701
  19.9 0.0 copy-start.3
  19.9 0.7 %step.1 = (f32[1,17424]{1,0:T(1,128)}, f32[1,17424]{1,0:T(1,128)}, f32[1,17424]{1,0:T(1,128)}, f32[1,17424]{1,0:T(1,128)}) custom-call(f32[2,144,128]{2,1,0:T(8,128)S(1)} %near_forces.1.line_ref, f32[1,17424]{1,0:T(1,128)S(1)} %copy-done.1, f32[1,17424]{1,0:T(1,128)S(1)} %copy-done.5, f32[1,17424]{1,0:T(1,128)S(1)} %copy-done.2, f32[1,17424]{1,0:T(1,128)S(1)} %copy-done.6, ...), custom_call_target="tpu_custom_call" | custom-call | flops 200000000 | bytes 1000000 | tf_op jit(solution)/shard_map/step/pallas_call | solution.py:720
  20.6 1.0 %collective-permute-done.4.first_ref = f32[16,1152]{1,0:T(8,128)S(1)} collective-permute-done((f32[16,1152]{1,0:T(8,128)S(1)}, f32[16,1152]{1,0:T(8,128)S(1)}, u32[]{:S(2)}, u32[]{:S(2)}) %collective-permute-start.4) | collective-permute-done | bytes 73760 | tf_op jit(solution)/shard_map/ppermute | solution.py:698
  21.6 0.0 collective-permute-done.5.second_ref
  21.6 0.8 %band.1 = f32[16,1089]{1,0:T(8,128)} custom-call(s32[1]{0:T(128)} %bitcast.1.cut_ref, f32[16,1152]{1,0:T(8,128)S(1)} %add.3.after_ref.own_ref, f32[16,1152]{1,0:T(8,128)S(1)} %collective-permute-done.4.first_ref, f32[16,1152]{1,0:T(8,128)S(1)} %collective-permute-done.5.second_ref, bf16[2,16,288]{2,1,0:T(8,128)(2,1)S(1)} %copy-done.3), custom_call_target="tpu_custom_call" | custom-call | flops 20000000 | bytes 1000000 | tf_op jit(solution)/shard_map/band/pallas_call | solution.py:734
  (12 shorter events, 0.0 us)
Async XLA Ops:
  0.6 5.2 %copy-start = (f32[24,1152]{1,0:T(8,128)S(1)}, f32[24,1152]{1,0:T(8,128)}, u32[]{:S(2)}) copy-start(f32[24,1152]{1,0:T(8,128)} %constant.8.clone.cross_ref) | copy-start | bytes 331780
  1.9 7.8 %collective-permute-start = (f32[144,128]{1,0:T(8,128)S(1)}, f32[144,128]{1,0:T(8,128)S(1)}, u32[]{:S(2)}, u32[]{:S(2)}) collective-permute-start(f32[144,128]{1,0:T(8,128)S(1)} %get-tuple-element.42), channel_id=1, source_target_pairs={{0,1},{1,2},{2,3},{3,4},{4,5},{5,6},{6,7},{7,8},{8,9},{9,10},{10,1... | collective-permute-start | bytes 221192 | tf_op jit(solution)/shard_map/ppermute | solution.py:637
  3.1 6.5 %collective-permute-start.2 = (s32[8,128]{1,0:T(8,128)S(1)}, s32[8,128]{1,0:T(8,128)S(1)}, u32[]{:S(2)}, u32[]{:S(2)}) collective-permute-start(s32[8,128]{1,0:T(8,128)S(1)} %broadcast_in_dim.8.count_ref), channel_id=1, source_target_pairs={{0,1},{1,2},{2,3},{3,4},{4,5},{5,6},{6,7},{7,8},{8,9},{9,10},{10,1... | collective-permute-start | bytes 12296 | tf_op jit(solution)/shard_map/ppermute | solution.py:640
  7.4 2.3 %collective-permute-start.1 = (f32[32,128]{1,0:T(8,128)S(1)}, f32[32,128]{1,0:T(8,128)S(1)}, u32[]{:S(2)}, u32[]{:S(2)}) collective-permute-start(f32[32,128]{1,0:T(8,128)S(1)} %get-tuple-element.58), channel_id=1, source_target_pairs={{1,0},{2,1},{3,2},{4,3},{5,4},{6,5},{7,6},{8,7},{9,8},{10,9},{11,1... | collective-permute-start | bytes 49160 | tf_op jit(solution)/shard_map/ppermute | solution.py:664
  10.6 4.4 %collective-permute-start.3 = (f32[16,1152]{1,0:T(8,128)S(1)}, f32[16,1152]{1,0:T(8,128)S(1)}, u32[]{:S(2)}, u32[]{:S(2)}) collective-permute-start(f32[16,1152]{1,0:T(8,128)S(1)} %near_layers.1), channel_id=1, source_target_pairs={{0,16},{16,0},{1,17},{17,1},{2,18},{18,2},{3,19},{19,3},{4,20},{20... | collective-permute-start | bytes 221192 | tf_op jit(solution)/shard_map/ppermute | solution.py:693
  15.1 6.5 %collective-permute-start.4 = (f32[16,1152]{1,0:T(8,128)S(1)}, f32[16,1152]{1,0:T(8,128)S(1)}, u32[]{:S(2)}, u32[]{:S(2)}) collective-permute-start(f32[16,1152]{1,0:T(8,128)S(1)} %add.3.after_ref.own_ref), channel_id=1, source_target_pairs={{0,15},{1,2},{2,1},{3,4},{4,3},{5,6},{6,5},{7,8},{8,7},{9,10},{10,... | collective-permute-start | bytes 221192 | tf_op jit(solution)/shard_map/ppermute | solution.py:698
  18.6 3.0 %collective-permute-start.5 = (f32[16,1152]{1,0:T(8,128)S(1)}, f32[16,1152]{1,0:T(8,128)S(1)}, u32[]{:S(2)}, u32[]{:S(2)}) collective-permute-start(f32[16,1152]{1,0:T(8,128)S(1)} %add.3.after_ref.own_ref), channel_id=1, source_target_pairs={{0,1},{1,0},{2,3},{3,2},{4,5},{5,4},{6,7},{7,6},{8,9},{9,8},{10,11... | collective-permute-start | bytes 221192 | tf_op jit(solution)/shard_map/ppermute | solution.py:699
  18.6 1.2 %copy-start.1 = (f32[1,17424]{1,0:T(1,128)S(1)}, f32[1,17424]{1,0:T(1,128)}, u32[]{:S(2)}) copy-start(f32[1,17424]{1,0:T(1,128)} %fwd_ref.1) | copy-start | bytes 209092
  18.6 1.2 %copy-start.2 = (f32[1,17424]{1,0:T(1,128)S(1)}, f32[1,17424]{1,0:T(1,128)}, u32[]{:S(2)}) copy-start(f32[1,17424]{1,0:T(1,128)} %adj_ref.1) | copy-start | bytes 209092
  18.6 1.3 %copy-start.4 = (f32[17424]{0:T(1024)S(1)}, f32[17424]{0:T(1024)}, u32[]{:S(2)}) copy-start(f32[17424]{0:T(1024)} %mass_ref.1) | copy-start | bytes 209092
  18.6 1.3 %copy-start.5 = (f32[1,17424]{1,0:T(1,128)S(1)}, f32[1,17424]{1,0:T(1,128)}, u32[]{:S(2)}) copy-start(f32[1,17424]{1,0:T(1,128)} %fwd_speed_ref.1) | copy-start | bytes 209092
  18.6 1.3 %copy-start.6 = (f32[1,17424]{1,0:T(1,128)S(1)}, f32[1,17424]{1,0:T(1,128)}, u32[]{:S(2)}) copy-start(f32[1,17424]{1,0:T(1,128)} %adj_speed_ref.1) | copy-start | bytes 209092
  19.9 1.7 %copy-start.3 = (bf16[2,16,288]{2,1,0:T(8,128)(2,1)S(1)}, bf16[2,16,288]{2,1,0:T(8,128)(2,1)}, u32[]{:S(2)}) copy-start(bf16[2,16,288]{2,1,0:T(8,128)(2,1)} %constant.9.clone.band_ref) | copy-start | bytes 55300

commit v15 on v14

--- a/solution.py
+++ b/solution.py
@@ -492,7 +492,15 @@
         line_ref[f, r0 + 1 : r0 + 10, :] = line_ref[f, r0 + 1 : r0 + 10, :] + spill
 
 
-def force_kernel(elem_ref, flux_ref, out_ref, win_ref, fold_ref, force_ref, plane_ref):
+def force_kernel(turn, cut_ref, elem_ref, flux_ref, before_ref, *refs):
+    mine = (cut_ref[0] == 1) if turn == 0 else (cut_ref[0] != 1)
+
+    @pl.when(mine)
+    def _():
+        own_forces(elem_ref, flux_ref, refs[0], *refs[len(refs) - 4 :])
+
+
+def own_forces(elem_ref, flux_ref, out_ref, win_ref, fold_ref, force_ref, plane_ref):
     out_ref[...] = jnp.zeros(out_ref.shape, F32)
     for f in range(2):
         force_terms(elem_ref, f, 2 + f, flux_ref, fold_ref, win_ref, 0)
@@ -680,14 +688,21 @@
         name="near_layers",
     )(held(prev), held(after), held(prev_count), held(near_flux), held(near_slope), held(near_kern), held(kern), cross)
 
-    force = pl.pallas_call(
-        force_kernel,
-        out_shape=pltpu.VMEM((2, ROWS, LANES), F32),
-        in_specs=[vmem] * 2,
-        scratch_shapes=[windows(2), line_block, windows(1), pltpu.VMEM((144, LANES), F32)],
-        cost_estimate=cost(200000000),
-        name="forces",
-    )(held(elem), held(flux))
+    point_block = pltpu.VMEM((2, ROWS, LANES), F32)
+
+    def force_part(turn, before, outs, aliases):
+        return pl.pallas_call(
+            functools.partial(force_kernel, turn),
+            out_shape=outs,
+            in_specs=[smem] + [vmem] * 3,
+            scratch_shapes=[windows(2), line_block, windows(1), pltpu.VMEM((144, LANES), F32)],
+            input_output_aliases=aliases,
+            cost_estimate=cost(200000000),
+            name="forces",
+        )(cut, held(elem), held(flux), held(before))
+
+    force, kern = force_part(0, kern, [point_block, kern_block], {3: 1})
+    (force,) = force_part(1, force, [point_block], {3: 0})
 
     if events == 2:
         other = lax.ppermute(kern, "event", [(0, 1), (1, 0)])

time: 22.6 us -> 23.3 us (1.031)
  waiting for transfers between devices: 4.15 us -> 5.43 us
  starting transfers between devices: 9.56 us -> 8.93 us
    ppermute x1, waiting for transfers between devices: 1.71 us -> 2.35 us  [on_device(): other = lax.ppermute(kern, 'event', [(0, 1), (1, 0)])]
    ppermute x1, starting transfers between devices: 3.52 us -> 2.88 us  [on_device(): kern_first = lax.ppermute(kern, 'cuts', pairs_first)]
    ppermute x1, waiting for transfers between devices: 1 us -> 1.62 us  [on_device(): kern_first = lax.ppermute(kern, 'cuts', pairs_first)]
    pallas_call x1 -> x2, Pallas kernels: 0.71 us -> 0.71 us  [force_part(): pl.pallas_call(functools.partial(force_kernel, turn), out_shape=outs, in_...]
  transfers between devices with their start and end apart: 6 -> 6, of which waited for: 4 -> 4; matrix products, arithmetic and copies ran while one was open for 0% -> 0% of each run, Pallas kernels for 19% -> 18%
where the time goes in v15:
time: 23.3 us; the launch traced here: 23.1 us
  starting transfers between devices  8.93 us (38%)
  Pallas kernels  7.28 us (31%)
  waiting for transfers between devices  5.43 us (23%)
  between operations  1.43 us (6%)
    ppermute x1, starting transfers between devices, on_device(): kern_first = lax.ppermute(kern, 'cuts', pairs_first)  2.88 us
    ppermute x1, starting transfers between devices, on_device(): prev_count = lax.ppermute(count, 'cuts', to_next)  2.68 us
    ppermute x1, waiting for transfers between devices, on_device(): other = lax.ppermute(kern, 'event', [(0, 1), (1, 0)])  2.35 us
    ppermute x1, starting transfers between devices, on_device(): other = lax.ppermute(kern, 'event', [(0, 1), (1, 0)])  1.99 us
    ppermute x1, waiting for transfers between devices, on_device(): kern_first = lax.ppermute(kern, 'cuts', pairs_first)  1.62 us
    pallas_call x2, Pallas kernels, own_part(): pl.pallas_call(functools.partial(own_kernel, turn), out_shape=own_blocks,...  1.6 us
    ppermute x1, waiting for transfers between devices, on_device(): prev_count = lax.ppermute(count, 'cuts', to_next)  1.31 us
    pallas_call x1, Pallas kernels, on_device(): pl.pallas_call(pack_kernel, out_shape=[pltpu.VMEM((144, LANES), F32), plt...  1.28 us
  transfers between devices with their start and end apart: 6, of which 4 were waited for; matrix products, arithmetic and copies ran while one was open for 0% of the time, Pallas kernels for 18%

profile of v15, /device:TPU:0, one launch (start us, length us, event | category | flops | bytes accessed | tf_op | source)
XLA Modules:
  0.0 23.1 jit_solution(1006173307223137326)
XLA Ops:
  0.6 0.0 copy-start
  0.6 1.3 %pack.1 = (f32[144,128]{1,0:T(8,128)S(1)}, f32[32,128]{1,0:T(8,128)S(1)}, f32[288,128]{1,0:T(8,128)S(1)}, s32[8,256]{1,0:T(8,128)S(1)}, bf16[384,256]{1,0:T(8,128)(2,1)S(1)}) custom-call(s32[125,256]{1,0:T(8,128)} %conn_hbm.1, f32[125,256]{1,0:T(8,128)} %shear_hbm.1, f32[1,17424]{1,0:T(1,128)} %fwd_ref.1, f32[1,17424]{1,0:T(1,128)} %adj_ref.1), custom_call_target="tpu_custom_call" | custom-call | flops 100000000 | bytes 1000000 | tf_op jit(solution)/shard_map/pack/pallas_call | solution.py:623
  1.9 0.5 %collective-permute-start = (f32[144,128]{1,0:T(8,128)S(1)}, f32[144,128]{1,0:T(8,128)S(1)}, u32[]{:S(2)}, u32[]{:S(2)}) collective-permute-start(f32[144,128]{1,0:T(8,128)S(1)} %get-tuple-element.68), channel_id=1, source_target_pairs={{0,1},{1,2},{2,3},{3,4},{4,5},{5,6},{6,7},{7,8},{8,9},{9,10},{10,1... | collective-permute-start | bytes 221192 | tf_op jit(solution)/shard_map/ppermute | solution.py:645
  3.1 2.7 %collective-permute-start.2 = (s32[8,128]{1,0:T(8,128)S(1)}, s32[8,128]{1,0:T(8,128)S(1)}, u32[]{:S(2)}, u32[]{:S(2)}) collective-permute-start(s32[8,128]{1,0:T(8,128)S(1)} %broadcast_in_dim.8.count_ref), channel_id=1, source_target_pairs={{0,1},{1,2},{2,3},{3,4},{4,5},{5,6},{6,7},{7,8},{8,9},{9,10},{10,1... | collective-permute-start | bytes 12296 | tf_op jit(solution)/shard_map/ppermute | solution.py:648
  5.8 0.0 copy-done
  5.8 1.6 %own_layers.2 = (f32[4,168,128]{2,1,0:T(8,128)S(1)}, f32[200,128]{1,0:T(8,128)S(1)}, f32[200,128]{1,0:T(8,128)S(1)}, f32[2,128,128]{2,1,0:T(8,128)S(1)}, f32[2,1...) custom-call(s32[1]{0:T(128)} %bitcast.cut_ref, s32[8,128]{1,0:T(8,128)S(1)} %broadcast_in_dim.8.count_ref, ...), custom_call_target="tpu_custom_call" | custom-call | flops 300000000 | bytes 1000000 | tf_op jit(solution)/shard_map/own_layers/pallas_call | solution.py:655
  7.4 0.9 %collective-permute-start.1 = (f32[32,128]{1,0:T(8,128)S(1)}, f32[32,128]{1,0:T(8,128)S(1)}, u32[]{:S(2)}, u32[]{:S(2)}) collective-permute-start(f32[32,128]{1,0:T(8,128)S(1)} %get-tuple-element.69), channel_id=1, source_target_pairs={{1,0},{2,1},{3,2},{4,3},{5,4},{6,5},{7,6},{8,7},{9,8},{10,9},{11,1... | collective-permute-start | bytes 49160 | tf_op jit(solution)/shard_map/ppermute | solution.py:672
  8.3 1.3 %collective-permute-done.2.count_ref = s32[8,128]{1,0:T(8,128)S(1)} collective-permute-done((s32[8,128]{1,0:T(8,128)S(1)}, s32[8,128]{1,0:T(8,128)S(1)}, u32[]{:S(2)}, u32[]{:S(2)}) %collective-permute-start.2) | collective-permute-done | bytes 4128 | tf_op jit(solution)/shard_map/ppermute | solution.py:648
  9.6 0.1 collective-permute-done.1.next_ref
  9.7 0.0 collective-permute-done.prev_ref
  9.7 0.9 %near_layers.1.before_ref = f32[16,1152]{1,0:T(8,128)S(1)} custom-call(f32[144,128]{1,0:T(8,128)S(1)} %collective-permute-done.prev_ref, f32[32,128]{1,0:T(8,128)S(1)} %collective-permute-done.1.next_ref, s32[8,128]{1,0:T(8,128)S(1)} %collective-permute-done.2.count_ref, f32[200,128]{1,0:T(8,128)S(1)} %get-tuple-element.70.flux_in_ref.near_flux_ref, ...), custom_call_target="tpu_custom_call" | custom-call | flops 200000000 | bytes 1000000 | tf_op jit(solution)/shard_map/near_layers/pallas_call | solution.py:674
  10.7 2.0 %collective-permute-start.3 = (f32[16,1152]{1,0:T(8,128)S(1)}, f32[16,1152]{1,0:T(8,128)S(1)}, u32[]{:S(2)}, u32[]{:S(2)}) collective-permute-start(f32[16,1152]{1,0:T(8,128)S(1)} %get-tuple-element.74), channel_id=1, source_target_pairs={{0,16},{16,0},{1,17},{17,1},{2,18},{18,2},{3,19},{19,3},{4,20},{20... | collective-permute-start | bytes 221192 | tf_op jit(solution)/shard_map/ppermute | solution.py:708
  12.6 0.7 %forces.3.force_ref = f32[2,144,128]{2,1,0:T(8,128)S(1)} custom-call(s32[1]{0:T(128)} %bitcast.cut_ref, f32[4,168,128]{2,1,0:T(8,128)S(1)} %get-tuple-element.66.elem_ref, f32[200,128]{1,0:T(8,128)S(1)} %get-tuple-element.67.flux_ref, f32[2,144,128]{2,1,0:T(8,128)S(1)} %get-tuple-element.75.before_ref), custom_call_target="tpu_custom_call", output_to_operand_aliasing={{}: (3, {})} | custom-call | flops 200000000 | bytes 1000000 | tf_op jit(solution)/shard_map/forces/pallas_call | solution.py:694
  13.4 2.4 %collective-permute-done.3 = f32[16,1152]{1,0:T(8,128)S(1)} collective-permute-done((f32[16,1152]{1,0:T(8,128)S(1)}, f32[16,1152]{1,0:T(8,128)S(1)}, u32[]{:S(2)}, u32[]{:S(2)}) %collective-permute-start.3) | collective-permute-done | bytes 73760 | tf_op jit(solution)/shard_map/ppermute | solution.py:708
  15.7 2.9 %collective-permute-start.4 = (f32[16,1152]{1,0:T(8,128)S(1)}, f32[16,1152]{1,0:T(8,128)S(1)}, u32[]{:S(2)}, u32[]{:S(2)}) collective-permute-start(f32[16,1152]{1,0:T(8,128)S(1)} %add.3.after_ref.own_ref), channel_id=1, source_target_pairs={{0,15},{1,2},{2,1},{3,4},{4,3},{5,6},{6,5},{7,8},{8,7},{9,10},{10,... | collective-permute-start | bytes 221192 | tf_op jit(solution)/shard_map/ppermute | solution.py:713
  18.6 0.0 collective-permute-start.5
  18.6 0.0 copy-start.5
  18.6 0.0 copy-start.6
  18.6 1.2 %near_forces.1.line_ref = f32[2,144,128]{2,1,0:T(8,128)S(1)} custom-call(f32[2,144,128]{2,1,0:T(8,128)S(1)} %forces.3.force_ref, f32[2,128,128]{2,1,0:T(8,128)S(1)} %get-tuple-element.77.near_half_ref, f32[200,128]{1,0:T(8,128)S(1)} %get-tuple-element.70.flux_in_ref.near_flux_ref, f32[144,128]{1,0:T(8,128)S(1)} %collective-permute-done.prev_ref, ...), custom_call_target="tpu_custom_call" | custom-call | flops 200000000 | bytes 1000000 | tf_op jit(solution)/shard_map/near_forces/pallas_call | solution.py:716
  19.9 0.0 copy-start.3
  19.9 0.7 %step.1 = (f32[1,17424]{1,0:T(1,128)}, f32[1,17424]{1,0:T(1,128)}, f32[1,17424]{1,0:T(1,128)}, f32[1,17424]{1,0:T(1,128)}) custom-call(f32[2,144,128]{2,1,0:T(8,128)S(1)} %near_forces.1.line_ref, f32[1,17424]{1,0:T(1,128)S(1)} %copy-done.1, f32[1,17424]{1,0:T(1,128)S(1)} %copy-done.5, f32[1,17424]{1,0:T(1,128)S(1)} %copy-done.2, f32[1,17424]{1,0:T(1,128)S(1)} %copy-done.6, ...), custom_call_target="tpu_custom_call" | custom-call | flops 200000000 | bytes 1000000 | tf_op jit(solution)/shard_map/step/pallas_call | solution.py:735
  20.6 1.6 %collective-permute-done.4.first_ref = f32[16,1152]{1,0:T(8,128)S(1)} collective-permute-done((f32[16,1152]{1,0:T(8,128)S(1)}, f32[16,1152]{1,0:T(8,128)S(1)}, u32[]{:S(2)}, u32[]{:S(2)}) %collective-permute-start.4) | collective-permute-done | bytes 73760 | tf_op jit(solution)/shard_map/ppermute | solution.py:713
  22.3 0.0 collective-permute-done.5.second_ref
  22.3 0.8 %band.1 = f32[16,1089]{1,0:T(8,128)} custom-call(s32[1]{0:T(128)} %bitcast.cut_ref, f32[16,1152]{1,0:T(8,128)S(1)} %add.3.after_ref.own_ref, f32[16,1152]{1,0:T(8,128)S(1)} %collective-permute-done.4.first_ref, f32[16,1152]{1,0:T(8,128)S(1)} %collective-permute-done.5.second_ref, bf16[2,16,288]{2,1,0:T(8,128)(2,1)S(1)} %copy-done.3), custom_call_target="tpu_custom_call" | custom-call | flops 20000000 | bytes 1000000 | tf_op jit(solution)/shard_map/band/pallas_call | solution.py:749
  (13 shorter events, 0.0 us)
Async XLA Ops:
  0.6 5.2 %copy-start = (f32[24,1152]{1,0:T(8,128)S(1)}, f32[24,1152]{1,0:T(8,128)}, u32[]{:S(2)}) copy-start(f32[24,1152]{1,0:T(8,128)} %constant.8.clone.cross_ref) | copy-start | bytes 331780
  1.9 7.8 %collective-permute-start = (f32[144,128]{1,0:T(8,128)S(1)}, f32[144,128]{1,0:T(8,128)S(1)}, u32[]{:S(2)}, u32[]{:S(2)}) collective-permute-start(f32[144,128]{1,0:T(8,128)S(1)} %get-tuple-element.68), channel_id=1, source_target_pairs={{0,1},{1,2},{2,3},{3,4},{4,5},{5,6},{6,7},{7,8},{8,9},{9,10},{10,1... | collective-permute-start | bytes 221192 | tf_op jit(solution)/shard_map/ppermute | solution.py:645
  3.1 6.5 %collective-permute-start.2 = (s32[8,128]{1,0:T(8,128)S(1)}, s32[8,128]{1,0:T(8,128)S(1)}, u32[]{:S(2)}, u32[]{:S(2)}) collective-permute-start(s32[8,128]{1,0:T(8,128)S(1)} %broadcast_in_dim.8.count_ref), channel_id=1, source_target_pairs={{0,1},{1,2},{2,3},{3,4},{4,5},{5,6},{6,7},{7,8},{8,9},{9,10},{10,1... | collective-permute-start | bytes 12296 | tf_op jit(solution)/shard_map/ppermute | solution.py:648
  7.4 2.3 %collective-permute-start.1 = (f32[32,128]{1,0:T(8,128)S(1)}, f32[32,128]{1,0:T(8,128)S(1)}, u32[]{:S(2)}, u32[]{:S(2)}) collective-permute-start(f32[32,128]{1,0:T(8,128)S(1)} %get-tuple-element.69), channel_id=1, source_target_pairs={{1,0},{2,1},{3,2},{4,3},{5,4},{6,5},{7,6},{8,7},{9,8},{10,9},{11,1... | collective-permute-start | bytes 49160 | tf_op jit(solution)/shard_map/ppermute | solution.py:672
  10.7 5.1 %collective-permute-start.3 = (f32[16,1152]{1,0:T(8,128)S(1)}, f32[16,1152]{1,0:T(8,128)S(1)}, u32[]{:S(2)}, u32[]{:S(2)}) collective-permute-start(f32[16,1152]{1,0:T(8,128)S(1)} %get-tuple-element.74), channel_id=1, source_target_pairs={{0,16},{16,0},{1,17},{17,1},{2,18},{18,2},{3,19},{19,3},{4,20},{20... | collective-permute-start | bytes 221192 | tf_op jit(solution)/shard_map/ppermute | solution.py:708
  15.7 6.5 %collective-permute-start.4 = (f32[16,1152]{1,0:T(8,128)S(1)}, f32[16,1152]{1,0:T(8,128)S(1)}, u32[]{:S(2)}, u32[]{:S(2)}) collective-permute-start(f32[16,1152]{1,0:T(8,128)S(1)} %add.3.after_ref.own_ref), channel_id=1, source_target_pairs={{0,15},{1,2},{2,1},{3,4},{4,3},{5,6},{6,5},{7,8},{8,7},{9,10},{10,... | collective-permute-start | bytes 221192 | tf_op jit(solution)/shard_map/ppermute | solution.py:713
  18.6 3.7 %collective-permute-start.5 = (f32[16,1152]{1,0:T(8,128)S(1)}, f32[16,1152]{1,0:T(8,128)S(1)}, u32[]{:S(2)}, u32[]{:S(2)}) collective-permute-start(f32[16,1152]{1,0:T(8,128)S(1)} %add.3.after_ref.own_ref), channel_id=1, source_target_pairs={{0,1},{1,0},{2,3},{3,2},{4,5},{5,4},{6,7},{7,6},{8,9},{9,8},{10,11... | collective-permute-start | bytes 221192 | tf_op jit(solution)/shard_map/ppermute | solution.py:714
  18.6 1.2 %copy-start.1 = (f32[1,17424]{1,0:T(1,128)S(1)}, f32[1,17424]{1,0:T(1,128)}, u32[]{:S(2)}) copy-start(f32[1,17424]{1,0:T(1,128)} %fwd_ref.1) | copy-start | bytes 209092
  18.6 1.2 %copy-start.2 = (f32[1,17424]{1,0:T(1,128)S(1)}, f32[1,17424]{1,0:T(1,128)}, u32[]{:S(2)}) copy-start(f32[1,17424]{1,0:T(1,128)} %adj_ref.1) | copy-start | bytes 209092
  18.6 1.3 %copy-start.4 = (f32[17424]{0:T(1024)S(1)}, f32[17424]{0:T(1024)}, u32[]{:S(2)}) copy-start(f32[17424]{0:T(1024)} %mass_ref.1) | copy-start | bytes 209092
  18.6 1.3 %copy-start.5 = (f32[1,17424]{1,0:T(1,128)S(1)}, f32[1,17424]{1,0:T(1,128)}, u32[]{:S(2)}) copy-start(f32[1,17424]{1,0:T(1,128)} %fwd_speed_ref.1) | copy-start | bytes 209092
  18.6 1.3 %copy-start.6 = (f32[1,17424]{1,0:T(1,128)S(1)}, f32[1,17424]{1,0:T(1,128)}, u32[]{:S(2)}) copy-start(f32[1,17424]{1,0:T(1,128)} %adj_speed_ref.1) | copy-start | bytes 209092
  19.9 2.4 %copy-start.3 = (bf16[2,16,288]{2,1,0:T(8,128)(2,1)S(1)}, bf16[2,16,288]{2,1,0:T(8,128)(2,1)}, u32[]{:S(2)}) copy-start(bf16[2,16,288]{2,1,0:T(8,128)(2,1)} %constant.9.clone.band_ref) | copy-start | bytes 55300

commit v16 on v14

--- a/solution.py
+++ b/solution.py
@@ -318,7 +318,7 @@
 
 def own_kernel(turn, cut_ref, count_ref, own_ref, code_ref, parts_ref, cross_ref, *refs):
     refs = refs[-OWN_OUTS - OWN_SCRATCH :]
-    mine = (cut_ref[0] == 0) if turn == 0 else (cut_ref[0] != 0)
+    mine = (cut_ref[0] < 2) if turn == 0 else (cut_ref[0] >= 2)
 
     @pl.when(mine)
     def _():

time: 22.6 us -> 23.4 us (1.035)
  waiting for transfers between devices: 4.15 us -> 5.66 us
  starting transfers between devices: 9.56 us -> 8.81 us
    ppermute x1, starting transfers between devices: 3.52 us -> 2.76 us  [on_device(): kern_first = lax.ppermute(kern, 'cuts', pairs_first)]
    ppermute x1, waiting for transfers between devices: 1.71 us -> 2.46 us  [on_device(): other = lax.ppermute(kern, 'event', [(0, 1), (1, 0)])]
    ppermute x1, waiting for transfers between devices: 1 us -> 1.75 us  [on_device(): kern_first = lax.ppermute(kern, 'cuts', pairs_first)]
  transfers between devices with their start and end apart: 6 -> 6, of which waited for: 4 -> 4; matrix products, arithmetic and copies ran while one was open for 0% -> 0% of each run, Pallas kernels for 19% -> 18%
where the time goes in v16:
time: 23.4 us; the launch traced here: 23.2 us
  starting transfers between devices  8.81 us (38%)
  Pallas kernels  7.28 us (31%)
  waiting for transfers between devices  5.66 us (24%)
  between operations  1.42 us (6%)
    ppermute x1, starting transfers between devices, on_device(): kern_first = lax.ppermute(kern, 'cuts', pairs_first)  2.76 us
    ppermute x1, starting transfers between devices, on_device(): prev_count = lax.ppermute(count, 'cuts', to_next)  2.68 us
    ppermute x1, waiting for transfers between devices, on_device(): other = lax.ppermute(kern, 'event', [(0, 1), (1, 0)])  2.46 us
    ppermute x1, starting transfers between devices, on_device(): other = lax.ppermute(kern, 'event', [(0, 1), (1, 0)])  1.99 us
    ppermute x1, waiting for transfers between devices, on_device(): kern_first = lax.ppermute(kern, 'cuts', pairs_first)  1.75 us
    pallas_call x2, Pallas kernels, own_part(): pl.pallas_call(functools.partial(own_kernel, turn), out_shape=own_blocks,...  1.6 us
    pallas_call x1, Pallas kernels, on_device(): pl.pallas_call(pack_kernel, out_shape=[pltpu.VMEM((144, LANES), F32), plt...  1.28 us
    ppermute x1, waiting for transfers between devices, on_device(): prev_count = lax.ppermute(count, 'cuts', to_next)  1.26 us
  transfers between devices with their start and end apart: 6, of which 4 were waited for; matrix products, arithmetic and copies ran while one was open for 0% of the time, Pallas kernels for 18%

profile of v16, /device:TPU:0, one launch (start us, length us, event | category | flops | bytes accessed | tf_op | source)
XLA Modules:
  0.0 23.2 jit_solution(4144085529364011584)
XLA Ops:
  0.6 0.0 copy-start
  0.6 1.3 %pack.1 = (f32[144,128]{1,0:T(8,128)S(1)}, f32[32,128]{1,0:T(8,128)S(1)}, f32[288,128]{1,0:T(8,128)S(1)}, s32[8,256]{1,0:T(8,128)S(1)}, bf16[384,256]{1,0:T(8,128)(2,1)S(1)}) custom-call(s32[125,256]{1,0:T(8,128)} %conn_hbm.1, f32[125,256]{1,0:T(8,128)} %shear_hbm.1, f32[1,17424]{1,0:T(1,128)} %fwd_ref.1, f32[1,17424]{1,0:T(1,128)} %adj_ref.1), custom_call_target="tpu_custom_call" | custom-call | flops 100000000 | bytes 1000000 | tf_op jit(solution)/shard_map/pack/pallas_call | solution.py:615
  1.9 0.5 %collective-permute-start = (f32[144,128]{1,0:T(8,128)S(1)}, f32[144,128]{1,0:T(8,128)S(1)}, u32[]{:S(2)}, u32[]{:S(2)}) collective-permute-start(f32[144,128]{1,0:T(8,128)S(1)} %get-tuple-element.42), channel_id=1, source_target_pairs={{0,1},{1,2},{2,3},{3,4},{4,5},{5,6},{6,7},{7,8},{8,9},{9,10},{10,1... | collective-permute-start | bytes 221192 | tf_op jit(solution)/shard_map/ppermute | solution.py:637
  3.1 2.7 %collective-permute-start.2 = (s32[8,128]{1,0:T(8,128)S(1)}, s32[8,128]{1,0:T(8,128)S(1)}, u32[]{:S(2)}, u32[]{:S(2)}) collective-permute-start(s32[8,128]{1,0:T(8,128)S(1)} %broadcast_in_dim.8.count_ref), channel_id=1, source_target_pairs={{0,1},{1,2},{2,3},{3,4},{4,5},{5,6},{6,7},{7,8},{8,9},{9,10},{10,1... | collective-permute-start | bytes 12296 | tf_op jit(solution)/shard_map/ppermute | solution.py:640
  5.8 0.0 copy-done
  5.8 1.6 %own_layers.2 = (f32[4,168,128]{2,1,0:T(8,128)S(1)}, f32[200,128]{1,0:T(8,128)S(1)}, f32[200,128]{1,0:T(8,128)S(1)}, f32[2,128,128]{2,1,0:T(8,128)S(1)}, f32[2,1...) custom-call(s32[1]{0:T(128)} %bitcast.1.cut_ref, s32[8,128]{1,0:T(8,128)S(1)} %broadcast_in_dim.8.count_ref, ...), custom_call_target="tpu_custom_call" | custom-call | flops 300000000 | bytes 1000000 | tf_op jit(solution)/shard_map/own_layers/pallas_call | solution.py:647
  7.4 0.9 %collective-permute-start.1 = (f32[32,128]{1,0:T(8,128)S(1)}, f32[32,128]{1,0:T(8,128)S(1)}, u32[]{:S(2)}, u32[]{:S(2)}) collective-permute-start(f32[32,128]{1,0:T(8,128)S(1)} %get-tuple-element.58), channel_id=1, source_target_pairs={{1,0},{2,1},{3,2},{4,3},{5,4},{6,5},{7,6},{8,7},{9,8},{10,9},{11,1... | collective-permute-start | bytes 49160 | tf_op jit(solution)/shard_map/ppermute | solution.py:664
  8.3 1.3 %collective-permute-done.2.count_ref = s32[8,128]{1,0:T(8,128)S(1)} collective-permute-done((s32[8,128]{1,0:T(8,128)S(1)}, s32[8,128]{1,0:T(8,128)S(1)}, u32[]{:S(2)}, u32[]{:S(2)}) %collective-permute-start.2) | collective-permute-done | bytes 4128 | tf_op jit(solution)/shard_map/ppermute | solution.py:640
  9.5 0.2 collective-permute-done.1.next_ref
  9.7 0.0 collective-permute-done.prev_ref
  9.7 0.9 %near_layers.1 = f32[16,1152]{1,0:T(8,128)S(1)} custom-call(f32[144,128]{1,0:T(8,128)S(1)} %collective-permute-done.prev_ref, f32[32,128]{1,0:T(8,128)S(1)} %collective-permute-done.1.next_ref, s32[8,128]{1,0:T(8,128)S(1)} %collective-permute-done.2.count_ref, f32[200,128]{1,0:T(8,128)S(1)} %get-tuple-element.66.flux_in_ref.near_flux_ref, ...), custom_call_target="tpu_custom_call" | custom-call | flops 200000000 | bytes 1000000 | tf_op jit(solution)/shard_map/near_layers/pallas_call | solution.py:666
  10.6 2.0 %collective-permute-start.3 = (f32[16,1152]{1,0:T(8,128)S(1)}, f32[16,1152]{1,0:T(8,128)S(1)}, u32[]{:S(2)}, u32[]{:S(2)}) collective-permute-start(f32[16,1152]{1,0:T(8,128)S(1)} %near_layers.1), channel_id=1, source_target_pairs={{0,16},{16,0},{1,17},{17,1},{2,18},{18,2},{3,19},{19,3},{4,20},{20... | collective-permute-start | bytes 221192 | tf_op jit(solution)/shard_map/ppermute | solution.py:693
  12.6 0.7 %forces.1.force_ref = f32[2,144,128]{2,1,0:T(8,128)S(1)} custom-call(f32[4,168,128]{2,1,0:T(8,128)S(1)} %get-tuple-element.70.elem_ref, f32[200,128]{1,0:T(8,128)S(1)} %get-tuple-element.71.flux_ref), custom_call_target="tpu_custom_call" | custom-call | flops 200000000 | bytes 1000000 | tf_op jit(solution)/shard_map/forces/pallas_call | solution.py:683
  13.3 2.5 %collective-permute-done.3 = f32[16,1152]{1,0:T(8,128)S(1)} collective-permute-done((f32[16,1152]{1,0:T(8,128)S(1)}, f32[16,1152]{1,0:T(8,128)S(1)}, u32[]{:S(2)}, u32[]{:S(2)}) %collective-permute-start.3) | collective-permute-done | bytes 73760 | tf_op jit(solution)/shard_map/ppermute | solution.py:693
  15.8 2.8 %collective-permute-start.4 = (f32[16,1152]{1,0:T(8,128)S(1)}, f32[16,1152]{1,0:T(8,128)S(1)}, u32[]{:S(2)}, u32[]{:S(2)}) collective-permute-start(f32[16,1152]{1,0:T(8,128)S(1)} %add.3.after_ref.own_ref), channel_id=1, source_target_pairs={{0,15},{1,2},{2,1},{3,4},{4,3},{5,6},{6,5},{7,8},{8,7},{9,10},{10,... | collective-permute-start | bytes 221192 | tf_op jit(solution)/shard_map/ppermute | solution.py:698
  18.6 0.0 collective-permute-start.5
  18.6 0.0 copy-start.5
  18.6 0.0 copy-start.6
  18.6 1.2 %near_forces.1.line_ref = f32[2,144,128]{2,1,0:T(8,128)S(1)} custom-call(f32[2,144,128]{2,1,0:T(8,128)S(1)} %forces.1.force_ref, f32[2,128,128]{2,1,0:T(8,128)S(1)} %get-tuple-element.73.near_half_ref, f32[200,128]{1,0:T(8,128)S(1)} %get-tuple-element.66.flux_in_ref.near_flux_ref, f32[144,128]{1,0:T(8,128)S(1)} %collective-permute-done.prev_ref, ...), custom_call_target="tpu_custom_call" | custom-call | flops 200000000 | bytes 1000000 | tf_op jit(solution)/shard_map/near_forces/pallas_call | solution.py:701
  19.9 0.0 copy-start.3
  19.9 0.7 %step.1 = (f32[1,17424]{1,0:T(1,128)}, f32[1,17424]{1,0:T(1,128)}, f32[1,17424]{1,0:T(1,128)}, f32[1,17424]{1,0:T(1,128)}) custom-call(f32[2,144,128]{2,1,0:T(8,128)S(1)} %near_forces.1.line_ref, f32[1,17424]{1,0:T(1,128)S(1)} %copy-done.1, f32[1,17424]{1,0:T(1,128)S(1)} %copy-done.5, f32[1,17424]{1,0:T(1,128)S(1)} %copy-done.2, f32[1,17424]{1,0:T(1,128)S(1)} %copy-done.6, ...), custom_call_target="tpu_custom_call" | custom-call | flops 200000000 | bytes 1000000 | tf_op jit(solution)/shard_map/step/pallas_call | solution.py:720
  20.6 1.7 %collective-permute-done.4.first_ref = f32[16,1152]{1,0:T(8,128)S(1)} collective-permute-done((f32[16,1152]{1,0:T(8,128)S(1)}, f32[16,1152]{1,0:T(8,128)S(1)}, u32[]{:S(2)}, u32[]{:S(2)}) %collective-permute-start.4) | collective-permute-done | bytes 73760 | tf_op jit(solution)/shard_map/ppermute | solution.py:698
  22.4 0.0 collective-permute-done.5.second_ref
  22.4 0.8 %band.1 = f32[16,1089]{1,0:T(8,128)} custom-call(s32[1]{0:T(128)} %bitcast.1.cut_ref, f32[16,1152]{1,0:T(8,128)S(1)} %add.3.after_ref.own_ref, f32[16,1152]{1,0:T(8,128)S(1)} %collective-permute-done.4.first_ref, f32[16,1152]{1,0:T(8,128)S(1)} %collective-permute-done.5.second_ref, bf16[2,16,288]{2,1,0:T(8,128)(2,1)S(1)} %copy-done.3), custom_call_target="tpu_custom_call" | custom-call | flops 20000000 | bytes 1000000 | tf_op jit(solution)/shard_map/band/pallas_call | solution.py:734
  (12 shorter events, 0.0 us)
Async XLA Ops:
  0.6 5.2 %copy-start = (f32[24,1152]{1,0:T(8,128)S(1)}, f32[24,1152]{1,0:T(8,128)}, u32[]{:S(2)}) copy-start(f32[24,1152]{1,0:T(8,128)} %constant.8.clone.cross_ref) | copy-start | bytes 331780
  1.9 7.8 %collective-permute-start = (f32[144,128]{1,0:T(8,128)S(1)}, f32[144,128]{1,0:T(8,128)S(1)}, u32[]{:S(2)}, u32[]{:S(2)}) collective-permute-start(f32[144,128]{1,0:T(8,128)S(1)} %get-tuple-element.42), channel_id=1, source_target_pairs={{0,1},{1,2},{2,3},{3,4},{4,5},{5,6},{6,7},{7,8},{8,9},{9,10},{10,1... | collective-permute-start | bytes 221192 | tf_op jit(solution)/shard_map/ppermute | solution.py:637
  3.1 6.4 %collective-permute-start.2 = (s32[8,128]{1,0:T(8,128)S(1)}, s32[8,128]{1,0:T(8,128)S(1)}, u32[]{:S(2)}, u32[]{:S(2)}) collective-permute-start(s32[8,128]{1,0:T(8,128)S(1)} %broadcast_in_dim.8.count_ref), channel_id=1, source_target_pairs={{0,1},{1,2},{2,3},{3,4},{4,5},{5,6},{6,7},{7,8},{8,9},{9,10},{10,1... | collective-permute-start | bytes 12296 | tf_op jit(solution)/shard_map/ppermute | solution.py:640
  7.4 2.3 %collective-permute-start.1 = (f32[32,128]{1,0:T(8,128)S(1)}, f32[32,128]{1,0:T(8,128)S(1)}, u32[]{:S(2)}, u32[]{:S(2)}) collective-permute-start(f32[32,128]{1,0:T(8,128)S(1)} %get-tuple-element.58), channel_id=1, source_target_pairs={{1,0},{2,1},{3,2},{4,3},{5,4},{6,5},{7,6},{8,7},{9,8},{10,9},{11,1... | collective-permute-start | bytes 49160 | tf_op jit(solution)/shard_map/ppermute | solution.py:664
  10.6 5.2 %collective-permute-start.3 = (f32[16,1152]{1,0:T(8,128)S(1)}, f32[16,1152]{1,0:T(8,128)S(1)}, u32[]{:S(2)}, u32[]{:S(2)}) collective-permute-start(f32[16,1152]{1,0:T(8,128)S(1)} %near_layers.1), channel_id=1, source_target_pairs={{0,16},{16,0},{1,17},{17,1},{2,18},{18,2},{3,19},{19,3},{4,20},{20... | collective-permute-start | bytes 221192 | tf_op jit(solution)/shard_map/ppermute | solution.py:693
  15.8 6.5 %collective-permute-start.4 = (f32[16,1152]{1,0:T(8,128)S(1)}, f32[16,1152]{1,0:T(8,128)S(1)}, u32[]{:S(2)}, u32[]{:S(2)}) collective-permute-start(f32[16,1152]{1,0:T(8,128)S(1)} %add.3.after_ref.own_ref), channel_id=1, source_target_pairs={{0,15},{1,2},{2,1},{3,4},{4,3},{5,6},{6,5},{7,8},{8,7},{9,10},{10,... | collective-permute-start | bytes 221192 | tf_op jit(solution)/shard_map/ppermute | solution.py:698
  18.6 3.8 %collective-permute-start.5 = (f32[16,1152]{1,0:T(8,128)S(1)}, f32[16,1152]{1,0:T(8,128)S(1)}, u32[]{:S(2)}, u32[]{:S(2)}) collective-permute-start(f32[16,1152]{1,0:T(8,128)S(1)} %add.3.after_ref.own_ref), channel_id=1, source_target_pairs={{0,1},{1,0},{2,3},{3,2},{4,5},{5,4},{6,7},{7,6},{8,9},{9,8},{10,11... | collective-permute-start | bytes 221192 | tf_op jit(solution)/shard_map/ppermute | solution.py:699
  18.6 1.2 %copy-start.1 = (f32[1,17424]{1,0:T(1,128)S(1)}, f32[1,17424]{1,0:T(1,128)}, u32[]{:S(2)}) copy-start(f32[1,17424]{1,0:T(1,128)} %fwd_ref.1) | copy-start | bytes 209092
  18.6 1.2 %copy-start.2 = (f32[1,17424]{1,0:T(1,128)S(1)}, f32[1,17424]{1,0:T(1,128)}, u32[]{:S(2)}) copy-start(f32[1,17424]{1,0:T(1,128)} %adj_ref.1) | copy-start | bytes 209092
  18.6 1.3 %copy-start.4 = (f32[17424]{0:T(1024)S(1)}, f32[17424]{0:T(1024)}, u32[]{:S(2)}) copy-start(f32[17424]{0:T(1024)} %mass_ref.1) | copy-start | bytes 209092
  18.6 1.3 %copy-start.5 = (f32[1,17424]{1,0:T(1,128)S(1)}, f32[1,17424]{1,0:T(1,128)}, u32[]{:S(2)}) copy-start(f32[1,17424]{1,0:T(1,128)} %fwd_speed_ref.1) | copy-start | bytes 209092
  18.6 1.3 %copy-start.6 = (f32[1,17424]{1,0:T(1,128)S(1)}, f32[1,17424]{1,0:T(1,128)}, u32[]{:S(2)}) copy-start(f32[1,17424]{1,0:T(1,128)} %adj_speed_ref.1) | copy-start | bytes 209092
  19.9 2.5 %copy-start.3 = (bf16[2,16,288]{2,1,0:T(8,128)(2,1)S(1)}, bf16[2,16,288]{2,1,0:T(8,128)(2,1)}, u32[]{:S(2)}) copy-start(bf16[2,16,288]{2,1,0:T(8,128)(2,1)} %constant.9.clone.band_ref) | copy-start | bytes 55300

commit v17 on v15

--- a/solution.py
+++ b/solution.py
@@ -515,8 +515,16 @@
             add_plane(out_ref, f, x, sum(flat[1:], flat[0]))
 
 
-def near_force_kernel(
-    force_ref, near_half_ref, near_flux_ref, prev_ref, next_ref, count_ref, after_ref,
+def near_force_kernel(turn, cut_ref, *refs):
+    mine = (cut_ref[0] == 1) if turn == 0 else (cut_ref[0] != 1)
+
+    @pl.when(mine)
+    def _():
+        near_forces(*refs[:6], refs[len(refs) - 11 + turn], *refs[len(refs) - 9 :])
+
+
+def near_forces(
+    force_ref, near_half_ref, near_flux_ref, prev_ref, next_ref, count_ref,
     out_ref,
     win_ref, fold_ref, near_force_ref, plane_ref, flux_ref, elem_ref, near_win_ref, near_plane_ref, spread_ref,
 ):
@@ -701,7 +709,39 @@
             name="forces",
         )(cut, held(elem), held(flux), held(before))
 
+    def near_force_part(turn, force, before, outs, aliases, waits=()):
+        return pl.pallas_call(
+            functools.partial(near_force_kernel, turn),
+            out_shape=outs,
+            in_specs=[smem] + [vmem] * (7 + len(waits)),
+            scratch_shapes=[
+                windows(2),
+                line_block,
+                windows(1),
+                pltpu.VMEM((144, LANES), F32),
+                flux_block,
+                elements(2),
+                windows(2),
+                pltpu.VMEM((2 * 72, LANES), F32),
+                pltpu.VMEM((136, LANES), F32),
+            ],
+            input_output_aliases=aliases,
+            cost_estimate=cost(200000000),
+            name="near_forces",
+        )(
+            cut,
+            held(force),
+            held(near_win),
+            held(near_flux),
+            held(prev),
+            held(after),
+            held(prev_count),
+            held(before),
+            *[held(block) for block in waits],
+        )
+
     force, kern = force_part(0, kern, [point_block, kern_block], {3: 1})
+    whole, kern = near_force_part(0, force, kern, [point_block, kern_block], {7: 1})
     (force,) = force_part(1, force, [point_block], {3: 0})
 
     if events == 2:
@@ -713,24 +753,7 @@
     kern_first = lax.ppermute(kern, "cuts", pairs_first)
     kern_second = lax.ppermute(kern, "cuts", pairs_second)
 
-    force = pl.pallas_call(
-        near_force_kernel,
-        out_shape=pltpu.VMEM((2, ROWS, LANES), F32),
-        in_specs=[vmem] * 7,
-        scratch_shapes=[
-            windows(2),
-            line_block,
-            windows(1),
-            pltpu.VMEM((144, LANES), F32),
-            flux_block,
-            elements(2),
-            windows(2),
-            pltpu.VMEM((2 * 72, LANES), F32),
-            pltpu.VMEM((136, LANES), F32),
-        ],
-        cost_estimate=cost(200000000),
-        name="near_forces",
-    )(held(force), held(near_win), held(near_flux), held(prev), held(after), held(prev_count), held(kern))
+    (force,) = near_force_part(1, force, whole, [point_block], {7: 0}, [kern])
     points = jax.ShapeDtypeStruct((1, NPTS), F32)
     outs = pl.pallas_call(
         step_kernel,

time: 23.3 us -> 22.7 us (0.974)
  waiting for transfers between devices: 5.43 us -> 4.16 us
  starting transfers between devices: 8.93 us -> 9.56 us
    ppermute x1, waiting for transfers between devices: 2.35 us -> 1.72 us  [on_device(): other = lax.ppermute(kern, 'event', [(0, 1), (1, 0)])]
    ppermute x1, waiting for transfers between devices: 1.62 us -> 0.99 us  [on_device(): kern_first = lax.ppermute(kern, 'cuts', pairs_first)]
    ppermute x1, starting transfers between devices: 2.88 us -> 3.52 us  [on_device(): kern_first = lax.ppermute(kern, 'cuts', pairs_first)]
    pallas_call x1 -> x2, Pallas kernels: 1.19 us -> 1.21 us  [near_force_part(): pl.pallas_call(functools.partial(near_force_kernel, turn), out_shape=outs...]
  transfers between devices with their start and end apart: 6 -> 6, of which waited for: 4 -> 4; matrix products, arithmetic and copies ran while one was open for 0% -> 0% of each run, Pallas kernels for 18% -> 19%
where the time goes in v17:
time: 22.7 us; the launch traced here: 22.5 us
  starting transfers between devices  9.56 us (42%)
  Pallas kernels  7.3 us (32%)
  waiting for transfers between devices  4.16 us (18%)
  between operations  1.43 us (6%)
    ppermute x1, starting transfers between devices, on_device(): kern_first = lax.ppermute(kern, 'cuts', pairs_first)  3.52 us
    ppermute x1, starting transfers between devices, on_device(): prev_count = lax.ppermute(count, 'cuts', to_next)  2.68 us
    ppermute x1, starting transfers between devices, on_device(): other = lax.ppermute(kern, 'event', [(0, 1), (1, 0)])  1.99 us
    ppermute x1, waiting for transfers between devices, on_device(): other = lax.ppermute(kern, 'event', [(0, 1), (1, 0)])  1.72 us
    pallas_call x2, Pallas kernels, own_part(): pl.pallas_call(functools.partial(own_kernel, turn), out_shape=own_blocks,...  1.6 us
    ppermute x1, waiting for transfers between devices, on_device(): prev_count = lax.ppermute(count, 'cuts', to_next)  1.31 us
    pallas_call x1, Pallas kernels, on_device(): pl.pallas_call(pack_kernel, out_shape=[pltpu.VMEM((144, LANES), F32), plt...  1.28 us
    pallas_call x2, Pallas kernels, near_force_part(): pl.pallas_call(functools.partial(near_force_kernel, turn), out_shape=outs...  1.21 us
  transfers between devices with their start and end apart: 6, of which 4 were waited for; matrix products, arithmetic and copies ran while one was open for 0% of the time, Pallas kernels for 19%

profile of v17, /device:TPU:0, one launch (start us, length us, event | category | flops | bytes accessed | tf_op | source)
XLA Modules:
  0.0 22.5 jit_solution(9282988965824804665)
XLA Ops:
  0.6 0.0 copy-start
  0.6 1.3 %pack.1 = (f32[144,128]{1,0:T(8,128)S(1)}, f32[32,128]{1,0:T(8,128)S(1)}, f32[288,128]{1,0:T(8,128)S(1)}, s32[8,256]{1,0:T(8,128)S(1)}, bf16[384,256]{1,0:T(8,128)(2,1)S(1)}) custom-call(s32[125,256]{1,0:T(8,128)} %conn_hbm.1, f32[125,256]{1,0:T(8,128)} %shear_hbm.1, f32[1,17424]{1,0:T(1,128)} %fwd_ref.1, f32[1,17424]{1,0:T(1,128)} %adj_ref.1), custom_call_target="tpu_custom_call" | custom-call | flops 100000000 | bytes 1000000 | tf_op jit(solution)/shard_map/pack/pallas_call | solution.py:631
  1.9 0.5 %collective-permute-start = (f32[144,128]{1,0:T(8,128)S(1)}, f32[144,128]{1,0:T(8,128)S(1)}, u32[]{:S(2)}, u32[]{:S(2)}) collective-permute-start(f32[144,128]{1,0:T(8,128)S(1)} %get-tuple-element.70), channel_id=1, source_target_pairs={{0,1},{1,2},{2,3},{3,4},{4,5},{5,6},{6,7},{7,8},{8,9},{9,10},{10,1... | collective-permute-start | bytes 221192 | tf_op jit(solution)/shard_map/ppermute | solution.py:653
  3.1 2.7 %collective-permute-start.2 = (s32[8,128]{1,0:T(8,128)S(1)}, s32[8,128]{1,0:T(8,128)S(1)}, u32[]{:S(2)}, u32[]{:S(2)}) collective-permute-start(s32[8,128]{1,0:T(8,128)S(1)} %broadcast_in_dim.8.count_ref), channel_id=1, source_target_pairs={{0,1},{1,2},{2,3},{3,4},{4,5},{5,6},{6,7},{7,8},{8,9},{9,10},{10,1... | collective-permute-start | bytes 12296 | tf_op jit(solution)/shard_map/ppermute | solution.py:656
  5.8 0.0 copy-done
  5.8 1.6 %own_layers.2 = (f32[4,168,128]{2,1,0:T(8,128)S(1)}, f32[200,128]{1,0:T(8,128)S(1)}, f32[200,128]{1,0:T(8,128)S(1)}, f32[2,128,128]{2,1,0:T(8,128)S(1)}, f32[2,1...) custom-call(s32[1]{0:T(128)} %bitcast.cut_ref, s32[8,128]{1,0:T(8,128)S(1)} %broadcast_in_dim.8.count_ref, ...), custom_call_target="tpu_custom_call" | custom-call | flops 300000000 | bytes 1000000 | tf_op jit(solution)/shard_map/own_layers/pallas_call | solution.py:663
  7.4 0.9 %collective-permute-start.1 = (f32[32,128]{1,0:T(8,128)S(1)}, f32[32,128]{1,0:T(8,128)S(1)}, u32[]{:S(2)}, u32[]{:S(2)}) collective-permute-start(f32[32,128]{1,0:T(8,128)S(1)} %get-tuple-element.71), channel_id=1, source_target_pairs={{1,0},{2,1},{3,2},{4,3},{5,4},{6,5},{7,6},{8,7},{9,8},{10,9},{11,1... | collective-permute-start | bytes 49160 | tf_op jit(solution)/shard_map/ppermute | solution.py:680
  8.3 1.3 %collective-permute-done.2.count_ref.refs_5_ = s32[8,128]{1,0:T(8,128)S(1)} collective-permute-done((s32[8,128]{1,0:T(8,128)S(1)}, s32[8,128]{1,0:T(8,128)S(1)}, u32[]{:S(2)}, u32[]{:S(2)}) %collective-permute-start.2) | collective-permute-done | bytes 4128 | tf_op jit(solution)/shard_map/ppermute | solution.py:656
  9.6 0.1 collective-permute-done.1.next_ref.refs_4_
  9.7 0.0 collective-permute-done.prev_ref.refs_3_
  9.7 0.9 %near_layers.1.before_ref = f32[16,1152]{1,0:T(8,128)S(1)} custom-call(f32[144,128]{1,0:T(8,128)S(1)} %collective-permute-done.prev_ref.refs_3_, f32[32,128]{1,0:T(8,128)S(1)} %collective-permute-done.1.next_ref.refs_4_, s32[8,128]{1,0:T(8,128)S(1)} %collective-permute-done.2.count_ref.refs_5_, f32[200,128]{1,0:T(8,128)S(1)} %get-tuple-element.72.flux_in_ref.refs_2_, ...), custom_call_target="tpu_custom_call" | custom-call | flops 200000000 | bytes 1000000 | tf_op jit(solution)/shard_map/near_layers/pallas_call | solution.py:682
  10.7 2.0 %collective-permute-start.3 = (f32[16,1152]{1,0:T(8,128)S(1)}, f32[16,1152]{1,0:T(8,128)S(1)}, u32[]{:S(2)}, u32[]{:S(2)}) collective-permute-start(f32[16,1152]{1,0:T(8,128)S(1)} %get-tuple-element.79), channel_id=1, source_target_pairs={{0,16},{16,0},{1,17},{17,1},{2,18},{18,2},{3,19},{19,3},{4,20},{20... | collective-permute-start | bytes 221192 | tf_op jit(solution)/shard_map/ppermute | solution.py:748
  12.7 0.7 %forces.3.refs_0_ = f32[2,144,128]{2,1,0:T(8,128)S(1)} custom-call(s32[1]{0:T(128)} %bitcast.cut_ref, f32[4,168,128]{2,1,0:T(8,128)S(1)} %get-tuple-element.68.elem_ref, f32[200,128]{1,0:T(8,128)S(1)} %get-tuple-element.69.flux_ref, f32[2,144,128]{2,1,0:T(8,128)S(1)} %get-tuple-element.76.refs_0_.before_ref), custom_call_target="tpu_custom_call", output_to_operand_aliasing={{}: (3, {})} | custom-call | flops 200000000 | bytes 1000000 | tf_op jit(solution)/shard_map/forces/pallas_call | solution.py:702
  13.4 1.7 %collective-permute-done.3 = f32[16,1152]{1,0:T(8,128)S(1)} collective-permute-done((f32[16,1152]{1,0:T(8,128)S(1)}, f32[16,1152]{1,0:T(8,128)S(1)}, u32[]{:S(2)}, u32[]{:S(2)}) %collective-permute-start.3) | collective-permute-done | bytes 73760 | tf_op jit(solution)/shard_map/ppermute | solution.py:748
  15.1 3.5 %collective-permute-start.4 = (f32[16,1152]{1,0:T(8,128)S(1)}, f32[16,1152]{1,0:T(8,128)S(1)}, u32[]{:S(2)}, u32[]{:S(2)}) collective-permute-start(f32[16,1152]{1,0:T(8,128)S(1)} %add.3.refs_7_.own_ref), channel_id=1, source_target_pairs={{0,15},{1,2},{2,1},{3,4},{4,3},{5,6},{6,5},{7,8},{8,7},{9,10},{10,... | collective-permute-start | bytes 221192 | tf_op jit(solution)/shard_map/ppermute | solution.py:753
  18.6 0.0 collective-permute-start.5
  18.6 0.0 copy-start.5
  18.6 0.0 copy-start.6
  18.7 1.2 %near_forces.3.line_ref = f32[2,144,128]{2,1,0:T(8,128)S(1)} custom-call(s32[1]{0:T(128)} %bitcast.cut_ref, f32[2,144,128]{2,1,0:T(8,128)S(1)} %forces.3.refs_0_, f32[2,128,128]{2,1,0:T(8,128)S(1)} %get-tuple-element.77.refs_1_, f32[200,128]{1,0:T(8,128)S(1)} %get-tuple-element.72.flux_in_ref.refs_2_, ...), custom_call_target="tpu_custom_call", output_to_operand_aliasing={{}: (7, {})} | custom-call | flops 200000000 | bytes 1000000 | tf_op jit(solution)/shard_map/near_forces/pallas_call | solution.py:713
  19.9 0.0 copy-start.3
  19.9 0.7 %step.1 = (f32[1,17424]{1,0:T(1,128)}, f32[1,17424]{1,0:T(1,128)}, f32[1,17424]{1,0:T(1,128)}, f32[1,17424]{1,0:T(1,128)}) custom-call(f32[2,144,128]{2,1,0:T(8,128)S(1)} %near_forces.3.line_ref, f32[1,17424]{1,0:T(1,128)S(1)} %copy-done.1, f32[1,17424]{1,0:T(1,128)S(1)} %copy-done.5, f32[1,17424]{1,0:T(1,128)S(1)} %copy-done.2, f32[1,17424]{1,0:T(1,128)S(1)} %copy-done.6, ...), custom_call_target="tpu_custom_call" | custom-call | flops 200000000 | bytes 1000000 | tf_op jit(solution)/shard_map/step/pallas_call | solution.py:758
  20.7 1.0 %collective-permute-done.4.first_ref = f32[16,1152]{1,0:T(8,128)S(1)} collective-permute-done((f32[16,1152]{1,0:T(8,128)S(1)}, f32[16,1152]{1,0:T(8,128)S(1)}, u32[]{:S(2)}, u32[]{:S(2)}) %collective-permute-start.4) | collective-permute-done | bytes 73760 | tf_op jit(solution)/shard_map/ppermute | solution.py:753
  21.6 0.0 collective-permute-done.5.second_ref
  21.7 0.8 %band.1 = f32[16,1089]{1,0:T(8,128)} custom-call(s32[1]{0:T(128)} %bitcast.cut_ref, f32[16,1152]{1,0:T(8,128)S(1)} %add.3.refs_7_.own_ref, f32[16,1152]{1,0:T(8,128)S(1)} %collective-permute-done.4.first_ref, f32[16,1152]{1,0:T(8,128)S(1)} %collective-permute-done.5.second_ref, bf16[2,16,288]{2,1,0:T(8,128)(2,1)S(1)} %copy-done.3), custom_call_target="tpu_custom_call" | custom-call | flops 20000000 | bytes 1000000 | tf_op jit(solution)/shard_map/band/pallas_call | solution.py:772
  (14 shorter events, 0.1 us)
Async XLA Ops:
  0.6 5.2 %copy-start = (f32[24,1152]{1,0:T(8,128)S(1)}, f32[24,1152]{1,0:T(8,128)}, u32[]{:S(2)}) copy-start(f32[24,1152]{1,0:T(8,128)} %constant.8.clone.cross_ref) | copy-start | bytes 331780
  1.9 7.8 %collective-permute-start = (f32[144,128]{1,0:T(8,128)S(1)}, f32[144,128]{1,0:T(8,128)S(1)}, u32[]{:S(2)}, u32[]{:S(2)}) collective-permute-start(f32[144,128]{1,0:T(8,128)S(1)} %get-tuple-element.70), channel_id=1, source_target_pairs={{0,1},{1,2},{2,3},{3,4},{4,5},{5,6},{6,7},{7,8},{8,9},{9,10},{10,1... | collective-permute-start | bytes 221192 | tf_op jit(solution)/shard_map/ppermute | solution.py:653
  3.1 6.5 %collective-permute-start.2 = (s32[8,128]{1,0:T(8,128)S(1)}, s32[8,128]{1,0:T(8,128)S(1)}, u32[]{:S(2)}, u32[]{:S(2)}) collective-permute-start(s32[8,128]{1,0:T(8,128)S(1)} %broadcast_in_dim.8.count_ref), channel_id=1, source_target_pairs={{0,1},{1,2},{2,3},{3,4},{4,5},{5,6},{6,7},{7,8},{8,9},{9,10},{10,1... | collective-permute-start | bytes 12296 | tf_op jit(solution)/shard_map/ppermute | solution.py:656
  7.4 2.3 %collective-permute-start.1 = (f32[32,128]{1,0:T(8,128)S(1)}, f32[32,128]{1,0:T(8,128)S(1)}, u32[]{:S(2)}, u32[]{:S(2)}) collective-permute-start(f32[32,128]{1,0:T(8,128)S(1)} %get-tuple-element.71), channel_id=1, source_target_pairs={{1,0},{2,1},{3,2},{4,3},{5,4},{6,5},{7,6},{8,7},{9,8},{10,9},{11,1... | collective-permute-start | bytes 49160 | tf_op jit(solution)/shard_map/ppermute | solution.py:680
  10.7 4.4 %collective-permute-start.3 = (f32[16,1152]{1,0:T(8,128)S(1)}, f32[16,1152]{1,0:T(8,128)S(1)}, u32[]{:S(2)}, u32[]{:S(2)}) collective-permute-start(f32[16,1152]{1,0:T(8,128)S(1)} %get-tuple-element.79), channel_id=1, source_target_pairs={{0,16},{16,0},{1,17},{17,1},{2,18},{18,2},{3,19},{19,3},{4,20},{20... | collective-permute-start | bytes 221192 | tf_op jit(solution)/shard_map/ppermute | solution.py:748
  15.1 6.5 %collective-permute-start.4 = (f32[16,1152]{1,0:T(8,128)S(1)}, f32[16,1152]{1,0:T(8,128)S(1)}, u32[]{:S(2)}, u32[]{:S(2)}) collective-permute-start(f32[16,1152]{1,0:T(8,128)S(1)} %add.3.refs_7_.own_ref), channel_id=1, source_target_pairs={{0,15},{1,2},{2,1},{3,4},{4,3},{5,6},{6,5},{7,8},{8,7},{9,10},{10,... | collective-permute-start | bytes 221192 | tf_op jit(solution)/shard_map/ppermute | solution.py:753
  18.6 3.0 %collective-permute-start.5 = (f32[16,1152]{1,0:T(8,128)S(1)}, f32[16,1152]{1,0:T(8,128)S(1)}, u32[]{:S(2)}, u32[]{:S(2)}) collective-permute-start(f32[16,1152]{1,0:T(8,128)S(1)} %add.3.refs_7_.own_ref), channel_id=1, source_target_pairs={{0,1},{1,0},{2,3},{3,2},{4,5},{5,4},{6,7},{7,6},{8,9},{9,8},{10,11... | collective-permute-start | bytes 221192 | tf_op jit(solution)/shard_map/ppermute | solution.py:754
  18.6 1.2 %copy-start.1 = (f32[1,17424]{1,0:T(1,128)S(1)}, f32[1,17424]{1,0:T(1,128)}, u32[]{:S(2)}) copy-start(f32[1,17424]{1,0:T(1,128)} %fwd_ref.1) | copy-start | bytes 209092
  18.6 1.3 %copy-start.2 = (f32[1,17424]{1,0:T(1,128)S(1)}, f32[1,17424]{1,0:T(1,128)}, u32[]{:S(2)}) copy-start(f32[1,17424]{1,0:T(1,128)} %adj_ref.1) | copy-start | bytes 209092
  18.6 1.3 %copy-start.4 = (f32[17424]{0:T(1024)S(1)}, f32[17424]{0:T(1024)}, u32[]{:S(2)}) copy-start(f32[17424]{0:T(1024)} %mass_ref.1) | copy-start | bytes 209092
  18.6 1.3 %copy-start.5 = (f32[1,17424]{1,0:T(1,128)S(1)}, f32[1,17424]{1,0:T(1,128)}, u32[]{:S(2)}) copy-start(f32[1,17424]{1,0:T(1,128)} %fwd_speed_ref.1) | copy-start | bytes 209092
  18.6 1.3 %copy-start.6 = (f32[1,17424]{1,0:T(1,128)S(1)}, f32[1,17424]{1,0:T(1,128)}, u32[]{:S(2)}) copy-start(f32[1,17424]{1,0:T(1,128)} %adj_speed_ref.1) | copy-start | bytes 209092
  19.9 1.7 %copy-start.3 = (bf16[2,16,288]{2,1,0:T(8,128)(2,1)S(1)}, bf16[2,16,288]{2,1,0:T(8,128)(2,1)}, u32[]{:S(2)}) copy-start(bf16[2,16,288]{2,1,0:T(8,128)(2,1)} %constant.9.clone.band_ref) | copy-start | bytes 55300
